TPU v7x, 256 devices: a whole 4x4x8 slice. The times are simulated.
256 devices in a mesh: rows: 32 (over z, y_hi, core), cols: 8 (over x, y_lo).
Axes of the slice: x: 4, y: 4 (y_hi: 2, y_lo: 2; y = y_hi * 2 + y_lo), z: 8, core: 2. Of those that a mesh axis runs over, the one named last changes fastest.
Arguments:
- latent: bfloat16 [256, 1024, 128], P('rows', 'cols'), may hold values from -36 to 36, as said below
- cotangent: bfloat16 [256, 1024, 128], P('rows', 'cols'), may hold values from -6 to 6
- w_qkv: bfloat16 [2, 128, 384], replicated, may hold values from -0.5 to 0.5
- w_proj: bfloat16 [2, 128, 128], replicated, may hold values from -0.5 to 0.5
- w_up: bfloat16 [2, 128, 512], replicated, may hold values from -0.5 to 0.5
- w_down: bfloat16 [2, 512, 128], replicated, may hold values from -0.25 to 0.25
- gains: float32 [2, 2, 128], replicated, may hold values from 0.5 to 1.5
- attn_bias: float32 [2, 4, 64, 64], replicated, may hold values from -4 to 300
Outputs:
- latent_grad: bfloat16 [256, 1024, 128], P('rows', 'cols')
- qkv_grad: float32 [2, 128, 384], replicated
- proj_grad: float32 [2, 128, 128], replicated
- up_grad: float32 [2, 128, 512], replicated
- down_grad: float32 [2, 512, 128], replicated
- gains_grad: float32 [2, 2, 128], replicated
- bias_grad: float32 [2, 4, 64, 64], replicated
Inputs may be any that keep to these rules, and one draw needn't show every extreme that they name: `latent`: token and channel scales vary.
All inputs are finite; a program needn't handle non-finite values.
Results may differ from a plain program's by a relative error of at most 0.03.
Values may be sent and summed in bfloat16 or wider, within the bound.
No kernel may reach another device: no remote copies, remote signals or barrier semaphores. Data moves between devices by JAX's collectives and lax.ppermute only.
A program may use at most 64 MiB of HBM per device.

v0:
```python
from functools import partial

import jax
import jax.numpy as jnp
from jax import lax
from jax.sharding import PartitionSpec as P

WINDOW = 8


NORM_EPS = 1e-05


def shifted(value, axis, by):
    peers = lax.axis_size(axis)
    return lax.ppermute(value, axis, [(i, (i + by) % peers) for i in range(peers)])


def norm(values, gain_vec):
    centre = values - jnp.mean(values, axis=-1, keepdims=True)
    spread = jnp.mean(centre * centre, axis=-1, keepdims=True)
    return centre * lax.rsqrt(spread + NORM_EPS) * gain_vec


def product(pattern, left_op, right_op):
    return jnp.einsum(pattern, left_op, right_op, preferred_element_type=jnp.float32)


def forward(inputs, w_qkv, w_proj, w_up, w_down, gain_attn, gain_mlp, bias):
    win_count, length, channels = inputs.shape
    head_count = bias.shape[0]
    head_size = channels // head_count
    score_scale = head_size ** (-0.5)
    stream = inputs.astype(jnp.float32)
    normed = norm(stream, gain_attn).astype(jnp.bfloat16)
    packed = product("wlc,cd->wld", normed, w_qkv).astype(jnp.bfloat16)
    queries = packed[..., :channels].reshape(win_count, length, head_count, head_size)
    key_rows = packed[..., channels : 2 * channels].reshape(
        win_count, length, head_count, head_size
    )
    value_rows = packed[..., 2 * channels :].reshape(win_count, length, head_count, head_size)
    scores = product("wihd,wjhd->whij", queries, key_rows) * score_scale + bias
    probabilities = jax.nn.softmax(scores, axis=-1)
    weights = probabilities.astype(jnp.bfloat16)
    mixed_out = (
        product("whij,wjhd->wihd", weights, value_rows)
        .reshape(win_count, length, channels)
        .astype(jnp.bfloat16)
    )
    middle = (stream + product("wlc,cd->wld", mixed_out, w_proj)).astype(jnp.bfloat16)
    middle_f = middle.astype(jnp.float32)
    normed_two = norm(middle_f, gain_mlp).astype(jnp.bfloat16)
    hidden_pre = product("wlc,cf->wlf", normed_two, w_up)
    hidden = jax.nn.gelu(hidden_pre, approximate=True).astype(jnp.bfloat16)
    result = (middle_f + product("wlf,fc->wlc", hidden, w_down)).astype(jnp.bfloat16)
    stored = (
        stream,
        normed,
        queries,
        key_rows,
        value_rows,
        probabilities,
        weights,
        mixed_out,
        middle_f,
        normed_two,
        hidden_pre,
        hidden,
    )
    return (result, stored)


def backward(stored, grad_out, w_qkv, w_proj, w_up, w_down, gain_attn, gain_mlp, bias):
    (
        stream,
        normed,
        queries,
        key_rows,
        value_rows,
        probabilities,
        weights,
        mixed_out,
        middle_f,
        normed_two,
        hidden_pre,
        hidden,
    ) = stored
    win_count, length, head_count, head_size = queries.shape
    channels = head_count * head_size
    score_scale = head_size ** (-0.5)
    grad_f = grad_out.astype(jnp.float32)
    d_hidden = product("wlc,fc->wlf", grad_out, w_down)
    g_down = product("wlf,wlc->fc", hidden, grad_out)
    _, gelu_pull = jax.vjp(partial(jax.nn.gelu, approximate=True), hidden_pre)
    d_pre = gelu_pull(d_hidden)[0].astype(jnp.bfloat16)
    g_up = product("wlc,wlf->cf", normed_two, d_pre)
    d_normed_two = product("wlf,cf->wlc", d_pre, w_up)
    _, pull_two = jax.vjp(norm, middle_f, gain_mlp)
    d_middle_part, g_gain_mlp = pull_two(d_normed_two)
    d_middle = grad_f + d_middle_part
    d_middle_b = d_middle.astype(jnp.bfloat16)
    g_proj = product("wlc,wld->cd", mixed_out, d_middle_b)
    d_mixed = (
        product("wld,cd->wlc", d_middle_b, w_proj)
        .astype(jnp.bfloat16)
        .reshape(win_count, length, head_count, head_size)
    )
    d_values = product("whij,wihd->wjhd", weights, d_mixed)
    d_weights = product("wihd,wjhd->whij", d_mixed, value_rows)
    d_scores = probabilities * (
        d_weights - jnp.sum(d_weights * probabilities, axis=-1, keepdims=True)
    )
    g_bias = jnp.sum(d_scores, axis=0)
    d_scores_b = d_scores.astype(jnp.bfloat16)
    d_queries = product("whij,wjhd->wihd", d_scores_b, key_rows) * score_scale
    d_keys = product("whij,wihd->wjhd", d_scores_b, queries) * score_scale
    d_packed = jnp.concatenate(
        [
            d_queries.reshape(win_count, length, channels),
            d_keys.reshape(win_count, length, channels),
            d_values.reshape(win_count, length, channels),
        ],
        axis=-1,
    ).astype(jnp.bfloat16)
    g_qkv = product("wlc,wld->cd", normed, d_packed)
    d_normed = product("wld,cd->wlc", d_packed, w_qkv)
    _, pull_one = jax.vjp(norm, stream, gain_attn)
    d_stream_part, g_gain_attn = pull_one(d_normed)
    d_input = (d_middle + d_stream_part).astype(jnp.bfloat16)
    return (d_input, (g_qkv, g_proj, g_up, g_down, g_gain_attn, g_gain_mlp, g_bias))


def split_tile(tile):
    row_count, col_count, channels = tile.shape
    return (
        tile.reshape(row_count // WINDOW, WINDOW, col_count // WINDOW, WINDOW, channels)
        .transpose(0, 2, 1, 3, 4)
        .reshape(-1, WINDOW * WINDOW, channels)
    )


def join_tile(windows, row_count, col_count):
    channels = windows.shape[2]
    return (
        windows.reshape(row_count // WINDOW, col_count // WINDOW, WINDOW, WINDOW, channels)
        .transpose(0, 2, 1, 3, 4)
        .reshape(row_count, col_count, channels)
    )


def body(latent, cotangent, w_qkv, w_proj, w_up, w_down, gains, attn_bias):
    row_count, col_count, channels = latent.shape
    half_win = WINDOW // 2
    first_params = (w_qkv[0], w_proj[0], w_up[0], w_down[0], gains[0, 0], gains[0, 1], attn_bias[0])
    second_params = (
        w_qkv[1],
        w_proj[1],
        w_up[1],
        w_down[1],
        gains[1, 0],
        gains[1, 1],
        attn_bias[1],
    )
    result_one, stored_one = forward(split_tile(latent), *first_params)
    after_first = join_tile(result_one, row_count, col_count)
    below_x, below_g = shifted((after_first[:half_win], cotangent[:half_win]), "rows", -1)
    rowed_x = jnp.concatenate([after_first[half_win:], below_x], axis=0)
    rowed_g = jnp.concatenate([cotangent[half_win:], below_g], axis=0)
    right_x, right_g = shifted((rowed_x[:, :half_win], rowed_g[:, :half_win]), "cols", -1)
    moved_x = jnp.concatenate([rowed_x[:, half_win:], right_x], axis=1)
    moved_g = jnp.concatenate([rowed_g[:, half_win:], right_g], axis=1)
    _, stored_two = forward(split_tile(moved_x), *second_params)
    d_moved, grads_two = backward(stored_two, split_tile(moved_g), *second_params)
    d_tile = join_tile(d_moved, row_count, col_count)
    from_left = shifted(d_tile[:, col_count - half_win :], "cols", 1)
    d_cols = jnp.concatenate([from_left, d_tile[:, : col_count - half_win]], axis=1)
    from_above = shifted(d_cols[row_count - half_win :], "rows", 1)
    d_after = jnp.concatenate([from_above, d_cols[: row_count - half_win]], axis=0)
    d_windows, grads_one = backward(stored_one, split_tile(d_after), *first_params)
    summed = lax.psum(
        (
            grads_one[0],
            grads_one[1],
            grads_one[2],
            grads_one[3],
            grads_one[4],
            grads_one[5],
            grads_one[6],
            grads_two[0],
            grads_two[1],
            grads_two[2],
            grads_two[3],
            grads_two[4],
            grads_two[5],
            grads_two[6],
        ),
        ("rows", "cols"),
    )
    grads_one = summed[:7]
    grads_two = summed[7:]
    latent_grad = join_tile(d_windows, row_count, col_count)
    gains_grad = jnp.stack(
        [jnp.stack([grads_one[4], grads_one[5]]), jnp.stack([grads_two[4], grads_two[5]])]
    )
    return (
        latent_grad,
        jnp.stack([grads_one[0], grads_two[0]]),
        jnp.stack([grads_one[1], grads_two[1]]),
        jnp.stack([grads_one[2], grads_two[2]]),
        jnp.stack([grads_one[3], grads_two[3]]),
        gains_grad,
        jnp.stack([grads_one[6], grads_two[6]]),
    )


def solution(mesh):
    in_specs = (P("rows", "cols", None), P("rows", "cols", None), P(), P(), P(), P(), P(), P())
    out_specs = (P("rows", "cols", None), P(), P(), P(), P(), P(), P())
    return jax.shard_map(body, mesh=mesh, in_specs=in_specs, out_specs=out_specs, check_vma=False)
```

profile of v0, /device:TPU:1, one launch (start us, length us, event | category | flops | bytes accessed | tf_op | source)
XLA Modules:
  0.0 392.7 jit_solution(2637865286650832610)
XLA Ops:
  7.2 1.7 fusion.133
  8.9 3.2 collective-permute-start
  17.6 1.6 slice_bitcast_fusion.2
  22.3 2.5 fusion.134
  24.9 1.9 convolution_convert_fusion.5
  29.6 6.3 %collective-permute-start.2 = (bf16[4,128,128]{2,1,0:T(8,128)(2,1)S(1)}, bf16[4,128,128]{2,1,0:T(8,128)(2,1)S(1)}, u32[]{:S(2)}, u32[]{:S(2)}) collective-permute-start(bf16[4,128,128]{2,1,0:T(8,128)(2,1)S(1)} %get-tuple-element.62), channel_id=1, source_target_pairs={{0,248},{8,0},{16,8},{24,16},{32,24},{40,32},{48,40},{56,48},{64,5... | collective-permute-start | bytes 393224 | tf_op jit(solution)/shard_map/ppermute | solution.py:16
  39.3 2.6 collective-permute-start.1
  51.0 3.4 fusion.136
  54.5 2.2 convolution_convert_fusion.4
  58.1 2.3 fusion.15
  60.4 1.4 convolution_bitcast_fusion.2
  65.7 3.3 convolution_convert_fusion.3
  69.6 1.4 fusion.32
  71.0 1.5 fusion.19
  75.1 2.0 copy.245
  77.1 1.9 copy.246
  79.1 1.5 multiply_reduce_fusion.8
  82.0 1.6 copy_bitcast_fusion.1
  84.0 2.3 convolution_bitcast_fusion
  88.6 1.4 convolution_bitcast_fusion.4
  90.0 2.5 collective-permute-done.5
  92.5 1.6 fusion.8
  94.1 1.4 convolution_bitcast_fusion.3
  98.9 3.2 convolution_convert_fusion.2
  107.6 1.5 multiply_reduce_fusion.6
  110.0 2.1 convolution_bitcast_fusion.5
  112.1 1.6 convolution_bitcast_fusion.1
  114.4 79.5 %all-reduce = (f32[1,128]{1,0:T(1,128)S(1)}, f32[1,128]{1,0:T(1,128)S(1)}, f32[1,128]{1,0:T(1,128)S(1)}, f32[1,128]{1,0:T(1,128)S(1)}) all-reduce(f32[1,128]{1,0:T(1,128)S(1)} %bitcast.370, f32[1,128]{1,0:T(1,128)S(1)} %bitcast.368, f32[1,128]{1,0:T(1,128)S(1)} %bitcast.371, ...), channel_id=1, replica_groups=mesh['rows'=32,'cols'=8] {'rows','cols'}, use_global_device_ids=true, to_apply=%region_37.0 | all-reduce | flops 512 | bytes 4096 | tf_op jit(solution)/shard_map/psum | solution.py:180
  194.4 1.5 copy_bitcast_fusion
  195.9 183.0 %all-reduce.4.cloned.1.call-done = (f32[1,128,384]{2,1,0:T(8,128)}, f32[1,128,384]{2,1,0:T(8,128)}, f32[1,128,128]{2,1,0:T(8,128)}, f32[1,128,128]{2,1,0:T(8,128...) async-done(((f32[1,128,384]{2,1,0:T(8,128)}, ...) | async-done | bytes 1703952 | tf_op jit(solution)/shard_map/psum | solution.py:180
  380.9 1.8 pad_maximum_fusion.4
  382.7 1.5 pad_maximum_fusion.11
  (232 shorter events, 50.5 us)
Async XLA Ops:
  7.2 12.8 %copy-start = (bf16[8,128,128]{2,1,0:T(8,128)(2,1)S(1)}, bf16[8,128,128]{2,1,0:T(8,128)(2,1)}, u32[]{:S(2)}) copy-start(bf16[8,128,128]{2,1,0:T(8,128)(2,1)} %param.8) | copy-start | bytes 786436
  7.2 12.8 %copy-start.63 = (bf16[2,128,384]{2,1,0:T(8,128)(2,1)S(1)}, bf16[2,128,384]{2,1,0:T(8,128)(2,1)}, u32[]{:S(2)}) copy-start(bf16[2,128,384]{2,1,0:T(8,128)(2,1)} %param.10) | copy-start | bytes 589828
  7.2 371.8 %all-reduce.4.cloned.1.call-start = ((), (), s32[]{:S(2)}) async-start(), calls=%async_computation | async-start | bytes 3670016 | tf_op jit(solution)/shard_map/psum | solution.py:180
  8.9 29.1 %collective-permute-start = (bf16[4,128,128]{2,1,0:T(8,128)(2,1)}, bf16[4,128,128]{2,1,0:T(8,128)(2,1)}, u32[]{:S(2)}, u32[]{:S(2)}) collective-permute-start(bf16[4,128,128]{2,1,0:T(8,128)(2,1)} %get-tuple-element.58), channel_id=1, source_target_pairs={{0,248},{8,0},{16,8},{24,16},{32,24},{40,32},{48,40},{56,48},{64,5... | collective-permute-start | bytes 393224 | tf_op jit(solution)/shard_map/ppermute | solution.py:16
  13.5 6.5 %copy-start.52 = (f32[128]{0:T(128)}, f32[128]{0:T(128)S(1)}, u32[]{:S(2)}) copy-start(f32[128]{0:T(128)S(1)} %get-tuple-element.77) | copy-start | bytes 1540
  21.3 3.5 copy-start.6
  28.2 7.7 %copy-start.39 = (f32[16,64]{0,1:T(8,128)S(1)}, f32[16,64]{0,1:T(8,128)}, u32[]{:S(2)}) copy-start(f32[16,64]{0,1:T(8,128)} %get-tuple-element.65) | copy-start | bytes 12292
  28.2 8.4 %copy-start.40 = (f32[16,64]{0,1:T(8,128)S(1)}, f32[16,64]{0,1:T(8,128)}, u32[]{:S(2)}) copy-start(f32[16,64]{0,1:T(8,128)} %get-tuple-element.63) | copy-start | bytes 12292
  28.2 9.0 %copy-start.24 = (f32[4,64,64]{2,1,0:T(8,128)S(1)}, f32[4,64,64]{2,1,0:T(8,128)}, u32[]{:S(2)}) copy-start(f32[4,64,64]{2,1,0:T(8,128)} %get-tuple-element.59) | copy-start | bytes 196612
  29.6 16.7 %copy-start.54 = (f32[128]{0:T(128)S(1)}, f32[128]{0:T(128)}, u32[]{:S(2)}) copy-start(f32[128]{0:T(128)} %get-tuple-element.78) | copy-start | bytes 1540
  29.6 16.7 %copy-start.64 = (bf16[2,128,384]{2,1,0:T(8,128)(2,1)S(1)}, bf16[2,128,384]{2,1,0:T(8,128)(2,1)}, u32[]{:S(2)}) copy-start(bf16[2,128,384]{2,1,0:T(8,128)(2,1)} %param.10) | copy-start | bytes 589828
  29.6 12.3 %collective-permute-start.2 = (bf16[4,128,128]{2,1,0:T(8,128)(2,1)S(1)}, bf16[4,128,128]{2,1,0:T(8,128)(2,1)S(1)}, u32[]{:S(2)}, u32[]{:S(2)}) collective-permute-start(bf16[4,128,128]{2,1,0:T(8,128)(2,1)S(1)} %get-tuple-element.62), channel_id=1, source_target_pairs={{0,248},{8,0},{16,8},{24,16},{32,24},{40,32},{48,40},{56,48},{64,5... | collective-permute-start | bytes 393224 | tf_op jit(solution)/shard_map/ppermute | solution.py:16
  39.3 18.7 %collective-permute-start.1 = (bf16[8,4,128]{2,1,0:T(4,128)(2,1)}, bf16[8,4,128]{2,1,0:T(4,128)(2,1)}, u32[]{:S(2)}, u32[]{:S(2)}) collective-permute-start(bf16[8,4,128]{2,1,0:T(4,128)(2,1)} %pad_maximum_fusion.13), channel_id=1, source_target_pairs={{0,7},{1,0},{2,1},{3,2},{4,3},{5,4},{6,5},{7,6},{8,15},{9,8},{10,9... | collective-permute-start | bytes 24584 | tf_op jit(solution)/shard_map/ppermute | solution.py:16
  41.9 2.8 collective-permute-start.3
  49.0 5.4 %copy-start.8 = (bf16[16,64,128]{1,2,0:T(8,128)(2,1)}, bf16[16,64,128]{1,2,0:T(8,128)(2,1)S(1)}, u32[]{:S(2)}) copy-start(bf16[16,64,128]{1,2,0:T(8,128)(2,1)S(1)} %copy.237) | copy-start | bytes 786436
  72.5 6.6 %copy-start.55 = (f32[128]{0:T(128)S(1)}, f32[128]{0:T(128)}, u32[]{:S(2)}) copy-start(f32[128]{0:T(128)} %get-tuple-element.78) | copy-start | bytes 1540
  75.1 5.5 %copy-start.25 = (bf16[16,64,128]{2,1,0:T(8,128)(2,1)}, bf16[16,64,128]{2,1,0:T(8,128)(2,1)S(1)}, u32[]{:S(2)}) copy-start(bf16[16,64,128]{2,1,0:T(8,128)(2,1)S(1)} %copy.247) | copy-start | bytes 786436
  77.1 3.5 copy-start.56
  83.6 5.0 %copy-start.26 = (bf16[16,64,128]{2,1,0:T(8,128)(2,1)S(1)}, bf16[16,64,128]{2,1,0:T(8,128)(2,1)}, u32[]{:S(2)}) copy-start(bf16[16,64,128]{2,1,0:T(8,128)(2,1)} %copy-done.25) | copy-start | bytes 786436
  83.6 5.0 %copy-start.27 = (bf16[16,64,128]{2,1,0:T(8,128)(2,1)S(1)}, bf16[16,64,128]{2,1,0:T(8,128)(2,1)}, u32[]{:S(2)}) copy-start(bf16[16,64,128]{2,1,0:T(8,128)(2,1)} %copy.245) | copy-start | bytes 786436
  83.6 5.0 %copy-start.28 = (bf16[16,64,128]{2,1,0:T(8,128)(2,1)S(1)}, bf16[16,64,128]{2,1,0:T(8,128)(2,1)}, u32[]{:S(2)}) copy-start(bf16[16,64,128]{2,1,0:T(8,128)(2,1)} %copy.246) | copy-start | bytes 786436
  83.6 4.8 %collective-permute-start.4 = (bf16[8,4,128]{2,1,0:T(4,128)(2,1)S(1)}, bf16[8,4,128]{2,1,0:T(4,128)(2,1)S(1)}, u32[]{:S(2)}, u32[]{:S(2)}) collective-permute-start(bf16[8,4,128]{2,1,0:T(4,128)(2,1)S(1)} %slice.148), channel_id=1, source_target_pairs={{0,1},{1,2},{2,3},{3,4},{4,5},{5,6},{6,7},{7,0},{8,9},{9,10},{10,1... | collective-permute-start | bytes 24584 | tf_op jit(solution)/shard_map/ppermute | solution.py:16
  86.3 6.3 %copy-start.2 = (f32[16,64,512]{2,1,0:T(8,128)S(1)}, f32[16,64,512]{2,1,0:T(8,128)}, u32[]{:S(2)}) copy-start(f32[16,64,512]{2,1,0:T(8,128)} %copy-done.1) | copy-start | bytes 6291460
  86.3 6.3 %copy-start.62 = (bf16[2,512,128]{2,1,0:T(8,128)(2,1)S(1)}, bf16[2,512,128]{2,1,0:T(8,128)(2,1)}, u32[]{:S(2)}) copy-start(bf16[2,512,128]{2,1,0:T(8,128)(2,1)} %param.13) | copy-start | bytes 786436
  88.4 8.8 %copy-start.42 = (bf16[8,4,128]{2,1,0:T(4,128)(2,1)}, bf16[8,4,128]{2,1,0:T(4,128)(2,1)S(1)}, u32[]{:S(2)}) copy-start(bf16[8,4,128]{2,1,0:T(4,128)(2,1)S(1)} %collective-permute-done.4) | copy-start | bytes 24580
  88.4 4.1 %collective-permute-start.5 = (bf16[4,128,128]{2,1,0:T(8,128)(2,1)S(1)}, bf16[4,128,128]{2,1,0:T(8,128)(2,1)S(1)}, u32[]{:S(2)}, u32[]{:S(2)}) collective-permute-start(bf16[4,128,128]{2,1,0:T(8,128)(2,1)S(1)} %fusion.70), channel_id=1, source_target_pairs={{0,8},{8,16},{16,24},{24,32},{32,40},{40,48},{48,56},{56,64},{64,7... | collective-permute-start | bytes 393224 | tf_op jit(solution)/shard_map/ppermute | solution.py:16
  90.0 4.1 %copy-start.50 = (f32[128]{0:T(128)S(1)}, f32[128]{0:T(128)}, u32[]{:S(2)}) copy-start(f32[128]{0:T(128)} %get-tuple-element.76) | copy-start | bytes 1540
  90.0 5.6 %copy-start.20 = (bf16[2,128,512]{2,1,0:T(8,128)(2,1)S(1)}, bf16[2,128,512]{2,1,0:T(8,128)(2,1)}, u32[]{:S(2)}) copy-start(bf16[2,128,512]{2,1,0:T(8,128)(2,1)} %param.12) | copy-start | bytes 786436
  379.0 5.3 %copy-start.32 = (f32[1,128,512]{2,1,0:T(8,128)S(1)}, f32[1,128,512]{2,1,0:T(8,128)}, u32[]{:S(2)}) copy-start(f32[1,128,512]{2,1,0:T(8,128)} %get-tuple-element.37) | copy-start | bytes 786436
  379.0 5.3 %copy-start.33 = (f32[1,128,512]{2,1,0:T(8,128)S(1)}, f32[1,128,512]{2,1,0:T(8,128)}, u32[]{:S(2)}) copy-start(f32[1,128,512]{2,1,0:T(8,128)} %get-tuple-element.38) | copy-start | bytes 786436
  379.0 6.1 %copy-start.30 = (f32[1,512,128]{2,1,0:T(8,128)S(1)}, f32[1,512,128]{2,1,0:T(8,128)}, u32[]{:S(2)}) copy-start(f32[1,512,128]{2,1,0:T(8,128)} %get-tuple-element.39) | copy-start | bytes 786436
  379.0 6.1 %copy-start.31 = (f32[1,512,128]{2,1,0:T(8,128)S(1)}, f32[1,512,128]{2,1,0:T(8,128)}, u32[]{:S(2)}) copy-start(f32[1,512,128]{2,1,0:T(8,128)} %get-tuple-element.40) | copy-start | bytes 786436
  (40 other events, 88.9 us)
Sparse Core Ops, SparseCore 0:
  113.8 265.0 all-reduce.3
where the time goes:
time: 394 us; the launch traced here: 393 us
  waiting for transfers between devices  187 us (47%)
  blocking collectives  79.5 us (20%)
  matrix products  46.5 us (12%)
  other arithmetic  25.9 us (7%)
  local copies, waits for them, and re-layouts  24.8 us (6%)
  between operations  15 us (4%)
  starting transfers between devices  13.9 us (4%)
    psum x1, waiting for transfers between devices, body(): lax.psum((grads_one[0], grads_one[1], grads_one[2], grads_one[3], grads_o...  183 us
    psum x1, blocking collectives, body(): lax.psum((grads_one[0], grads_one[1], grads_one[2], grads_one[3], grads_o...  79.5 us
    dot_general x33, matrix products, product(): jnp.einsum(pattern, left_op, right_op, preferred_element_type=jnp.float32)  40.7 us
    ppermute x6, starting transfers between devices, shifted(): lax.ppermute(value, axis, [(i, (i + by) % peers) for i in range(peers)])  13.8 us
  transfers between devices with their start and end apart: 7, of which 4 were waited for; matrix products, arithmetic and copies ran while one was open for 11% of the time, Pallas kernels for 0%

commit v1 on v0

v1 whole, which is shorter than its diff:
```python
import functools

import jax
import jax.numpy as jnp
from jax import lax
from jax.experimental import pallas as pl
from jax.experimental.pallas import tpu as pltpu
from jax.sharding import PartitionSpec as P

WIN = 8
HALF = 4
LEN = 64
CH = 128
HEADS = 4
FFN = 512
EPS = 1e-05
SCALE = (CH // HEADS) ** -0.5
F32 = jnp.float32
BF16 = jnp.bfloat16
VMEM_LIMIT = 32 * 1024 * 1024
FIRST_LIMIT = 55 * 1000 * 1000

ROW_QKV, ROW_PROJ, ROW_UP, ROW_DOWN, ROW_BIAS, ROW_GAIN, ROWS = 0, 384, 512, 1024, 1536, 1664, 1792
AXES = ("z", "yh", "core", "x", "yl")
PLANE = ("yh", "x", "yl")


def nn(a, b):
    return lax.dot_general(a, b, (((1,), (0,)), ((), ())), preferred_element_type=F32)


def nt(a, b):
    return lax.dot_general(a, b, (((1,), (1,)), ((), ())), preferred_element_type=F32)


def tn(a, b):
    return lax.dot_general(a, b, (((0,), (0,)), ((), ())), preferred_element_type=F32)


def lane_means(parts):
    width = len(parts) * CH
    block = lax.broadcasted_iota(jnp.int32, (width, width), 0) // CH == lax.broadcasted_iota(jnp.int32, (width, width), 1) // CH
    ones = (block.astype(F32) * (1.0 / CH)).astype(BF16)
    sums = nn(jnp.concatenate([p.astype(BF16) for p in parts], axis=1), ones)
    return [sums[:, CH * i : CH * (i + 1)] for i in range(len(parts))]


def normalise(v):
    centre = v - jnp.mean(v, axis=-1, keepdims=True)
    spread = jnp.mean(centre * centre, axis=-1, keepdims=True)
    inv = lax.rsqrt(spread + EPS)
    return centre * inv, inv


def normalise_back(dn, hat, inv, gain):
    d_hat = dn * gain
    mean, along = lane_means([d_hat, d_hat * hat])
    return inv * (d_hat - mean - hat * along)


def head_mask():
    rows = lax.broadcasted_iota(jnp.int32, (HEADS * LEN, CH), 0) // LEN
    lanes = lax.broadcasted_iota(jnp.int32, (HEADS * LEN, CH), 1) // (CH // HEADS)
    return (rows == lanes).astype(F32).astype(BF16)


def spread_heads(v, mask):
    return jnp.concatenate([v] * HEADS, axis=0) * mask


def gather_heads(v):
    lane = lax.broadcasted_iota(jnp.int32, (LEN, CH), 1)
    size = CH // HEADS
    out = v[3 * LEN :]
    for h in (2, 1, 0):
        out = jnp.where(lane < (h + 1) * size, v[h * LEN : (h + 1) * LEN], out)
    return out


def attention(qkv, bias_t, mask):
    q, k, v = qkv[:, :CH], qkv[:, CH : 2 * CH], qkv[:, 2 * CH :]
    scores = nt(k, spread_heads(q, mask)) * SCALE + bias_t
    top = jnp.max(scores, axis=0, keepdims=True)
    e = jnp.exp(scores - top)
    p = (e * (1.0 / jnp.sum(e, axis=0, keepdims=True))).astype(BF16)
    return gather_heads(tn(p, v)).astype(BF16), p


def attention_back(d_o, qkv, p, mask):
    q, k, v = qkv[:, :CH], qkv[:, CH : 2 * CH], qkv[:, 2 * CH :]
    do_spread = spread_heads(d_o, mask)
    dv = nn(p, do_spread)
    dp = nt(v, do_spread)
    pf = p.astype(F32)
    ds = pf * (dp - jnp.sum(dp * pf, axis=0, keepdims=True))
    dsb = ds.astype(BF16)
    dk = nn(dsb, spread_heads(q, mask)) * SCALE
    dq = gather_heads(tn(dsb, k)) * SCALE
    return jnp.concatenate([dq, dk, dv], axis=1).astype(BF16), ds


def gelu_and_slope(u):
    c = 0.7978845608028654
    sq = u * u
    s = 0.5 * jnp.tanh(u * (c + (c * 0.044715) * sq)) + 0.5
    m = u * s
    return m, s + m * (1.0 - s) * (2.0 * c + (6.0 * c * 0.044715) * sq)


def forward(x, w_qkv, w_proj, g1, g2, bias_t, mask):
    hat1, inv1 = normalise(x)
    a1 = (hat1 * g1).astype(BF16)
    qkv = nn(a1, w_qkv).astype(BF16)
    outs, weights = [], []
    for w in range(x.shape[0] // LEN):
        o, p = attention(qkv[w * LEN : (w + 1) * LEN], bias_t, mask)
        outs.append(o)
        weights.append(p)
    o = jnp.concatenate(outs, axis=0)
    h = (x + nn(o, w_proj)).astype(BF16).astype(F32)
    hat2, inv2 = normalise(h)
    a2 = (hat2 * g2).astype(BF16)
    return h, (hat1, inv1, a1, jnp.concatenate(weights, axis=0), o, hat2, inv2, a2), qkv


def backward(gy, kept, qkv, w_qkv, w_proj, w_up, w_down, g1, g2, mask):
    hat1, inv1, a1, p, o, hat2, inv2, a2 = kept
    m, slope = gelu_and_slope(nn(a2, w_up))
    m = m.astype(BF16)
    du = (nt(gy, w_down) * slope).astype(BF16)
    da2 = nt(du, w_up)
    gain2 = jnp.sum(da2 * hat2, axis=0, keepdims=True)
    dh = gy.astype(F32) + normalise_back(da2, hat2, inv2, g2)
    dhb = dh.astype(BF16)
    d_o = nt(dhb, w_proj).astype(BF16)
    parts, bias = [], None
    for w in range(gy.shape[0] // LEN):
        at = slice(w * LEN, (w + 1) * LEN)
        part, ds = attention_back(d_o[at], qkv[at], p[at], mask)
        parts.append(part)
        bias = ds if bias is None else bias + ds
    dqkv = jnp.concatenate(parts, axis=0)
    da1 = nt(dqkv, w_qkv)
    gain1 = jnp.sum(da1 * hat1, axis=0, keepdims=True)
    dx = dh + normalise_back(da1, hat1, inv1, g1)
    return dx, (gy, m, a2, du, o, dhb, a1, dqkv), bias, gain1, gain2


def pack(pack_ref, pairs, bias, gain1, gain2):
    gy, m, a2, du, o, dhb, a1, dqkv = pairs
    down, up, qkv = tn(gy, m), tn(a2, du), tn(a1, dqkv)
    for j in range(3):
        pack_ref[ROW_QKV + CH * j : ROW_QKV + CH * (j + 1)] = qkv[:, CH * j : CH * (j + 1)]
    pack_ref[ROW_PROJ : ROW_PROJ + CH] = tn(o, dhb)
    for j in range(4):
        pack_ref[ROW_UP + CH * j : ROW_UP + CH * (j + 1)] = up[:, CH * j : CH * (j + 1)]
        pack_ref[ROW_DOWN + CH * j : ROW_DOWN + CH * (j + 1)] = down[:, CH * j : CH * (j + 1)].T
    pack_ref[ROW_BIAS : ROW_BIAS + LEN] = bias[:, :CH]
    pack_ref[ROW_BIAS + LEN : ROW_BIAS + 2 * LEN] = bias[:, CH:]
    pack_ref[ROW_GAIN : ROW_GAIN + 1] = gain1
    pack_ref[ROW_GAIN + 1 : ROW_GAIN + 2] = gain2
    pack_ref[ROW_GAIN + 2 :] = jnp.zeros((ROWS - ROW_GAIN - 2, CH), F32)


def to_windows(tile):
    rows, cols, ch = tile.shape
    return tile.reshape(WIN, cols // WIN, WIN, ch).transpose(1, 0, 2, 3).reshape(-1, ch)


def from_windows(tokens):
    count = tokens.shape[0] // LEN
    return tokens.reshape(count, WIN, WIN, CH).transpose(1, 0, 2, 3).reshape(WIN, count * WIN, CH)


def turned_bias(bias):
    return jnp.concatenate([bias[h].T for h in range(HEADS)], axis=1)


def first_kernel(*refs):
    (latent_hbm, bias_hbm), weights_hbm, refs = refs[:2], refs[2:7], refs[7:]
    (top_ref, low_ref), kept_refs, refs = refs[:2], refs[2:10], refs[10:]
    (x_ref, bias_ref, sem), weight_refs = refs[:3], refs[3:]
    w_qkv_ref, w_proj_ref, w_up_ref, w_down_ref, gain_ref = weight_refs
    moves = [(latent_hbm, x_ref), (bias_hbm.at[0], bias_ref)]
    moves += [(source.at[0], target) for source, target in zip(weights_hbm, weight_refs)]
    copies = [pltpu.make_async_copy(source, target, sem.at[i]) for i, (source, target) in enumerate(moves)]
    for copy in copies:
        copy.start()
    mask = head_mask()
    for copy in copies:
        copy.wait()
    x = to_windows(x_ref[...].astype(F32))
    h, kept, _ = forward(
        x, w_qkv_ref[...], w_proj_ref[...], gain_ref[0:1], gain_ref[1:2], turned_bias(bias_ref), mask
    )
    for ref, value in zip(kept_refs, kept):
        ref[...] = jnp.broadcast_to(value, ref.shape).astype(ref.dtype)
    m, _ = gelu_and_slope(nn(kept[7], w_up_ref[...]))
    tile = from_windows(h + nn(m.astype(BF16), w_down_ref[...]))
    top_ref[...] = tile[:HALF].astype(BF16)
    low_ref[...] = tile[HALF:].astype(BF16)


def second_kernel(*refs):
    x_own_ref, x_low_ref, g_own_ref, g_low_ref, edge_ref = refs[:5]
    w_qkv_ref, w_proj_ref, w_up_ref, w_down_ref, gain_ref, bias_ref = refs[5:11]
    (dtop_ref, dlow_ref), pair_refs, (bias_out_ref, gain_out_ref, frame_ref) = refs[11:13], refs[13:21], refs[21:]
    cols = x_own_ref.shape[1]

    def shifted(own, low, right):
        frame_ref[0:HALF, 0:cols] = own[...].astype(F32)
        frame_ref[HALF:, 0:cols] = low[...].astype(F32)
        frame_ref[:, cols : cols + WIN] = right.astype(F32)
        return to_windows(frame_ref[:, HALF : HALF + cols])

    mask = head_mask()
    x = shifted(x_own_ref, x_low_ref, edge_ref[0:WIN])
    gy = shifted(g_own_ref, g_low_ref, edge_ref[WIN:]).astype(BF16)
    w_qkv, w_proj, w_up, g1, g2 = w_qkv_ref[1], w_proj_ref[1], w_up_ref[1], gain_ref[1, 0:1], gain_ref[1, 1:2]
    _, kept, qkv = forward(x, w_qkv, w_proj, g1, g2, turned_bias(bias_ref[1]), mask)
    dx, pairs, bias, gain1, gain2 = backward(gy, kept, qkv, w_qkv, w_proj, w_up, w_down_ref[1], g1, g2, mask)
    for ref, value in zip(pair_refs, pairs):
        ref[...] = value
    bias_out_ref[...] = bias
    gain_out_ref[0:1] = gain1
    gain_out_ref[1:2] = gain2
    tile = from_windows(dx)
    dtop_ref[...] = tile[:HALF].astype(BF16)
    dlow_ref[...] = tile[HALF:].astype(BF16)


def weights_kernel(*refs):
    pairs, (bias_ref, gain_ref, pack_ref) = refs[:8], refs[8:]
    pack(pack_ref, [ref[...] for ref in pairs], bias_ref[...], gain_ref[0:1], gain_ref[1:2])


def last_kernel(*refs):
    (own, above, left), kept_refs, refs = refs[:3], refs[3:11], refs[11:]
    w_qkv_ref, w_proj_ref, w_up_ref, w_down_ref, gain_ref, other_ref, core_ref = refs[:7]
    dx_ref, keep_ref, send_ref, frame_ref, pack_ref = refs[7:]
    cols = own.shape[1]
    frame_ref[:, 0:WIN] = left[...].astype(F32)
    first = frame_ref[:, HALF:WIN]
    frame_ref[:, 0:HALF] = first
    frame_ref[HALF:, HALF : HALF + cols] = own[...].astype(F32)
    frame_ref[0:HALF, HALF : HALF + cols] = above[...].astype(F32)
    gy = to_windows(frame_ref[:, 0:cols]).astype(BF16)
    kept = [ref[...].astype(F32) if i in (0, 1, 5, 6) else ref[...] for i, ref in enumerate(kept_refs)]
    g1, g2 = gain_ref[0, 0:1], gain_ref[0, 1:2]
    dx, pairs, bias, gain1, gain2 = backward(
        gy, kept, nn(kept[2], w_qkv_ref[0]).astype(BF16), w_qkv_ref[0], w_proj_ref[0], w_up_ref[0], w_down_ref[0], g1, g2, head_mask()
    )
    dx_ref[...] = from_windows(dx).astype(BF16)
    pack(pack_ref, pairs, bias, gain1, gain2)
    first_core = core_ref[0] == 0

    @pl.when(first_core)
    def _():
        keep_ref[...] = pack_ref[...]
        send_ref[...] = other_ref[...].astype(BF16)

    @pl.when(jnp.logical_not(first_core))
    def _():
        keep_ref[...] = other_ref[...]
        send_ref[...] = pack_ref[...].astype(BF16)


def unpack_kernel(core_ref, own_ref, other_ref, *refs):
    qkv_ref, proj_ref, up_ref, down_ref, gain_ref, bias_ref, whole_ref = refs
    at = pl.multiple_of(core_ref[0] * ROWS, ROWS)
    whole_ref[pl.ds(at, ROWS)] = own_ref[...].astype(F32)
    whole_ref[pl.ds(ROWS - at, ROWS)] = other_ref[...].astype(F32)
    for b in range(2):
        at = b * ROWS
        for j in range(3):
            qkv_ref[b, :, CH * j : CH * (j + 1)] = whole_ref[at + ROW_QKV + CH * j : at + ROW_QKV + CH * (j + 1)]
        proj_ref[b] = whole_ref[at + ROW_PROJ : at + ROW_PROJ + CH]
        for j in range(4):
            up_ref[b, :, CH * j : CH * (j + 1)] = whole_ref[at + ROW_UP + CH * j : at + ROW_UP + CH * (j + 1)]
        down_ref[b] = whole_ref[at + ROW_DOWN : at + ROW_DOWN + FFN]
        for j in range(2):
            turned = whole_ref[at + ROW_BIAS + LEN * j : at + ROW_BIAS + LEN * (j + 1)].T
            bias_ref[b, 2 * j] = turned[:LEN]
            bias_ref[b, 2 * j + 1] = turned[LEN:]
        gain_ref[b] = whole_ref[at + ROW_GAIN : at + ROW_GAIN + 2]


def vmem(count):
    return [pl.BlockSpec(memory_space=pltpu.VMEM)] * count


def cost(flops, moved):
    return pl.CostEstimate(flops=flops, bytes_accessed=moved, transcendentals=0)


def shift(value, down, right):
    tall, wide = 32, 8
    pairs = []
    for r in range(tall):
        for c in range(wide):
            pairs.append((r * wide + c, (r + down) % tall * wide + (c + right) % wide))
    return lax.ppermute(value, AXES, pairs)


def swap_core(value):
    return lax.ppermute(value, "core", [(0, 1), (1, 0)])


def scatter_sum(value, axis, count):
    pieces = value.astype(BF16).reshape(count, value.shape[0] // count, CH)
    return jnp.sum(lax.all_to_all(pieces, axis, 0, 0).astype(F32), axis=0)


def collect(value, axis, count):
    spread = jnp.broadcast_to(value[None], (count, *value.shape))
    return lax.all_to_all(spread, axis, 0, 0)


def sum_over_devices(keep, send):
    total = keep + swap_core(send).astype(F32)
    total = scatter_sum(total, PLANE, 16)
    total = jnp.sum(collect(total.astype(BF16), "z", 8).astype(F32), axis=0).astype(BF16)
    total = collect(total, PLANE, 16).reshape(ROWS, CH)
    return total, swap_core(total)


def body(latent, cotangent, w_qkv, w_proj, w_up, w_down, gains, attn_bias):
    cols = latent.shape[1]
    half = jax.ShapeDtypeStruct((HALF, cols, CH), BF16)
    params = pltpu.CompilerParams(vmem_limit_bytes=VMEM_LIMIT)
    packed = jax.ShapeDtypeStruct((ROWS, CH), F32)
    core = lax.axis_index("core").reshape(1)
    weights = (w_qkv, w_proj, w_up, w_down, gains)
    g_low = cotangent[HALF:]
    g_below = shift(cotangent[:HALF], -1, 0)
    tokens = WIN * cols

    def table(width):
        return jax.ShapeDtypeStruct((tokens, width), BF16)

    kept_shapes = [table(CH), table(CH), table(CH), table(HEADS * LEN), table(CH)]
    kept_shapes += [table(CH), table(CH), table(CH)]
    pair_shapes = [table(CH), table(FFN), table(CH), table(FFN), table(CH), table(CH), table(CH), table(3 * CH)]
    top, low, *kept = pl.pallas_call(
        first_kernel,
        out_shape=(half, half, *kept_shapes),
        in_specs=[pl.BlockSpec(memory_space=pltpu.HBM)] * 7,
        out_specs=vmem(10),
        scratch_shapes=[
            pltpu.VMEM(latent.shape, BF16),
            pltpu.VMEM(attn_bias.shape[1:], F32),
            pltpu.SemaphoreType.DMA((7,)),
        ]
        + [pltpu.VMEM(w.shape[1:], w.dtype) for w in weights],
        compiler_params=pltpu.CompilerParams(vmem_limit_bytes=FIRST_LIMIT),
        cost_estimate=cost(500_000_000, 1_500_000),
        name="forward_first",
    )(latent, attn_bias, *weights)
    top, g_below = lax.optimization_barrier((top, g_below))
    x_below = shift(top, -1, 0)
    edge = jnp.concatenate([v[:, :WIN] for v in (low, x_below, g_low, g_below)], axis=0)
    edge = shift(edge, 0, -1)
    frame = pltpu.VMEM((WIN, cols + 2 * WIN, CH), F32)
    d_top, d_low, *pairs = pl.pallas_call(
        second_kernel,
        out_shape=(
            half,
            half,
            *pair_shapes,
            jax.ShapeDtypeStruct((LEN, HEADS * LEN), F32),
            jax.ShapeDtypeStruct((2, CH), F32),
        ),
        in_specs=vmem(11),
        out_specs=vmem(12),
        scratch_shapes=[frame],
        compiler_params=params,
        cost_estimate=cost(1_500_000_000, 3_000_000),
        name="backward_second",
    )(low, x_below, g_low, g_below, edge, *weights, attn_bias)
    pack_two = pl.pallas_call(
        weights_kernel,
        out_shape=packed,
        in_specs=vmem(10),
        out_specs=vmem(1)[0],
        compiler_params=params,
        cost_estimate=cost(500_000_000, 5_000_000),
        name="weights_second",
    )(*pairs)
    d_above = shift(d_low, 1, 0)
    d_above, pack_two = lax.optimization_barrier((d_above, pack_two))
    d_left = shift(jnp.concatenate([v[:, cols - WIN :] for v in (d_above, d_top)], axis=0), 0, 1)
    dx, keep, send = pl.pallas_call(
        last_kernel,
        out_shape=(
            jax.ShapeDtypeStruct(latent.shape, BF16),
            packed,
            jax.ShapeDtypeStruct((ROWS, CH), BF16),
        ),
        in_specs=vmem(17) + [pl.BlockSpec(memory_space=pltpu.SMEM)],
        out_specs=vmem(3),
        scratch_shapes=[frame, pltpu.VMEM((ROWS, CH), F32)],
        compiler_params=params,
        cost_estimate=cost(1_500_000_000, 4_000_000),
        name="backward_first",
    )(d_top, d_above, d_left, *kept, *weights, pack_two, core)
    parts = sum_over_devices(keep, send)
    qkv, proj, up, down, gain, bias = pl.pallas_call(
        unpack_kernel,
        out_shape=(
            jax.ShapeDtypeStruct((2, CH, 3 * CH), F32),
            jax.ShapeDtypeStruct((2, CH, CH), F32),
            jax.ShapeDtypeStruct((2, CH, FFN), F32),
            jax.ShapeDtypeStruct((2, FFN, CH), F32),
            jax.ShapeDtypeStruct((2, 2, CH), F32),
            jax.ShapeDtypeStruct((2, HEADS, LEN, LEN), F32),
        ),
        in_specs=[pl.BlockSpec(memory_space=pltpu.SMEM)] + vmem(2),
        out_specs=vmem(6),
        scratch_shapes=[pltpu.VMEM((2 * ROWS, CH), F32)],
        compiler_params=params,
        cost_estimate=cost(1_000_000, 4_000_000),
        name="unpack",
    )(core, *parts)
    return dx, qkv, proj, up, down, gain, bias


def solution(mesh):
    fine = jax.sharding.Mesh(mesh.devices.reshape(8, 2, 2, 4, 2), AXES)
    tiles = P(("z", "yh", "core"), ("x", "yl"), None)
    in_specs = (tiles, tiles, P(), P(), P(), P(), P(), P())
    out_specs = (tiles, P(), P(), P(), P(), P(), P())
    return jax.shard_map(body, mesh=fine, in_specs=in_specs, out_specs=out_specs, check_vma=False)
```

time: 394 us -> 108 us (0.27)
  waiting for transfers between devices: 187 us -> 13.4 us
  matrix products: 46.5 us -> 0 us
  blocking collectives: 79.5 us -> 36.1 us
  other arithmetic: 25.9 us -> 0.25 us
  Pallas kernels: 0 us -> 25.5 us
  local copies, waits for them, and re-layouts: 24.8 us -> 5.68 us
  between operations: 15 us -> 0.77 us
  starting transfers between devices: 13.9 us -> 25.9 us
    psum x1 -> x0, waiting for transfers between devices: 183 us -> none  [body(): lax.psum((grads_one[0], grads_one[1], grads_one[2], grads_one[3], grads_o...]
    psum x1 -> x0, blocking collectives: 79.5 us -> none  [body(): lax.psum((grads_one[0], grads_one[1], grads_one[2], grads_one[3], grads_o...]
    dot_general x33 -> x0, matrix products: 40.7 us -> none  [product(): jnp.einsum(pattern, left_op, right_op, preferred_element_type=jnp.float32)]
    all_to_all x0 -> x3, blocking collectives: none -> 36.1 us  [the longest x2 23 us: collect(): return lax.all_to_all(spread, axis, 0, 0)]
    pallas_call x0 -> x5, Pallas kernels: none -> 25.5 us  [the longest x1 9.7 us: body(): pl.pallas_call(second_kernel, out_shape=(half, half, *pair_shapes, jax.Sh...]
    ppermute x6 -> x7, starting transfers between devices: 13.8 us -> 25.9 us  [the longest x5 13.6 us: shift(): return lax.ppermute(value, AXES, pairs)]
    reduce_sum x12 -> x2, other arithmetic: 9.79 us -> 0.11 us  [the longest x1 0.07 us: scatter_sum(): return jnp.sum(lax.all_to_all(pieces, axis, 0, 0).astype(F32), axis=0)]
    ppermute x6 -> x7, waiting for transfers between devices: 4.12 us -> 13.4 us  [the longest x5 10.5 us: shift(): return lax.ppermute(value, AXES, pairs)]
  transfers between devices with their start and end apart: 7 -> 7, of which waited for: 4 -> 6; matrix products, arithmetic and copies ran while one was open for 11% -> 1% of each run, Pallas kernels for 0% -> 6%
where the time goes in v1:
time: 108 us
  blocking collectives  36.1 us (33%)
  starting transfers between devices  25.9 us (24%)
  Pallas kernels  25.5 us (24%)
  waiting for transfers between devices  13.4 us (12%)
  local copies, waits for them, and re-layouts  5.68 us (5%)
    all_to_all x2, blocking collectives, collect(): return lax.all_to_all(spread, axis, 0, 0)  23 us
    ppermute x5, starting transfers between devices, shift(): return lax.ppermute(value, AXES, pairs)  13.6 us
    all_to_all x1, blocking collectives, scatter_sum(): return jnp.sum(lax.all_to_all(pieces, axis, 0, 0).astype(F32), axis=0)  13 us
    ppermute x2, starting transfers between devices, swap_core(): return lax.ppermute(value, 'core', [(0, 1), (1, 0)])  12.3 us
    ppermute x5, waiting for transfers between devices, shift(): return lax.ppermute(value, AXES, pairs)  10.5 us
    pallas_call x1, Pallas kernels, body(): pl.pallas_call(second_kernel, out_shape=(half, half, *pair_shapes, jax.Sh...  9.7 us
    pallas_call x1, Pallas kernels, body(): pl.pallas_call(last_kernel, out_shape=(jax.ShapeDtypeStruct(latent.shape,...  7.75 us
    pallas_call x1, Pallas kernels, body(): pl.pallas_call(first_kernel, out_shape=(half, half, *kept_shapes), in_spe...  5.96 us
  transfers between devices with their start and end apart: 7, of which 6 were waited for; matrix products, arithmetic and copies ran while one was open for 1% of the time, Pallas kernels for 6%

profile of v1, /device:TPU:1, one launch (start us, length us, event | category | flops | bytes accessed | tf_op | source)
XLA Modules:
  0.0 107.6 jit_solution(6814518198648934907)
XLA Ops:
  0.7 1.0 fusion
  1.7 0.0 copy-start
  1.7 3.3 %collective-permute-start = (bf16[4,128,128]{2,1,0:T(8,128)(2,1)S(1)}, bf16[4,128,128]{2,1,0:T(8,128)(2,1)S(1)}, u32[]{:S(2)}, u32[]{:S(2)}) collective-permute-start(bf16[4,128,128]{2,1,0:T(8,128)(2,1)S(1)} %get-tuple-element.78), channel_id=1, source_target_pairs={{0,248},{1,249},{2,250},{3,251},{4,252},{5,253},{6,254},{7,255},{8... | collective-permute-start | bytes 393224 | tf_op jit(solution)/shard_map/ppermute | solution.py:302
  5.1 6.0 %forward_first.1 = (bf16[4,128,128]{2,1,0:T(8,128)(2,1)S(1)}, bf16[4,128,128]{2,1,0:T(8,128)(2,1)S(1)}, bf16[1024,128]{1,0:T(8,128)(2,1)S(1)}, bf16[1024,128]{1,...) custom-call(bf16[8,128,128]{2,1,0:T(8,128)(2,1)} %refs_0_.1, ...), custom_call_target="tpu_custom_call" | custom-call | flops 500000000 | bytes 1500000 | tf_op jit(solution)/shard_map/forward_first/pallas_call | solution.py:344
  11.0 6.3 %collective-permute-start.1 = (bf16[4,128,128]{2,1,0:T(8,128)(2,1)S(1)}, bf16[4,128,128]{2,1,0:T(8,128)(2,1)S(1)}, u32[]{:S(2)}, u32[]{:S(2)}) collective-permute-start(bf16[4,128,128]{2,1,0:T(8,128)(2,1)S(1)} %get-tuple-element.44), channel_id=1, source_target_pairs={{0,248},{1,249},{2,250},{3,251},{4,252},{5,253},{6,254},{7,255},{8... | collective-permute-start | bytes 393224 | tf_op jit(solution)/shard_map/ppermute | solution.py:302
  17.3 0.7 slice.29
  18.0 0.3 collective-permute-done.1.refs_1_
  18.3 2.8 %collective-permute-start.2 = (bf16[16,8,128]{2,1,0:T(8,128)(2,1)S(1)}, bf16[16,8,128]{2,1,0:T(8,128)(2,1)S(1)}, u32[]{:S(2)}, u32[]{:S(2)}) collective-permute-start(bf16[16,8,128]{2,1,0:T(8,128)(2,1)S(1)} %pad_maximum_fusion), channel_id=1, source_target_pairs={{0,7},{1,0},{2,1},{3,2},{4,3},{5,4},{6,5},{7,6},{8,15},{9,8},{10,9... | collective-permute-start | bytes 98312 | tf_op jit(solution)/shard_map/ppermute | solution.py:302
  21.2 1.0 collective-permute-done.2.refs_4_
  22.2 9.7 %backward_second.1 = (bf16[4,128,128]{2,1,0:T(8,128)(2,1)S(1)}, bf16[4,128,128]{2,1,0:T(8,128)(2,1)S(1)}, bf16[1024,128]{1,0:T(8,128)(2,1)S(1)}, bf16[1024,512]{...) custom-call(bf16[4,128,128]{2,1,0:T(8,128)(2,1)S(1)} %get-tuple-elem, ...), custom_call_target="tpu_custom_call" | custom-call | flops 1500000000 | bytes 3000000 | tf_op jit(solution)/shard_map/backward_second/pallas_call | solution.py:364
  31.9 0.1 collective-permute-start.3
  32.0 0.0 copy-start.6
  32.0 0.7 weights_second.1.refs_16_
  32.8 4.4 %collective-permute-done.3.refs_1_ = bf16[4,128,128]{2,1,0:T(8,128)(2,1)S(1)} collective-permute-done((bf16[4,128,128]{2,1,0:T(8,128)(2,1)S(1)}, bf16[4,128,128]{2,1,0:T(8,128)(2,1)S(1)}, u32[]{:S(2)}, u32[]{:S(2)}) %collective-permute-start.3) | collective-permute-done | bytes 131104 | tf_op jit(solution)/shard_map/ppermute | solution.py:302
  37.2 1.1 collective-permute-start.4
  38.2 4.8 %collective-permute-done.4.refs_2_ = bf16[8,8,128]{2,1,0:T(8,128)(2,1)S(1)} collective-permute-done((bf16[8,8,128]{2,1,0:T(8,128)(2,1)S(1)}, bf16[8,8,128]{2,1,0:T(8,128)(2,1)S(1)}, u32[]{:S(2)}, u32[]{:S(2)}) %collective-permute-start.4) | collective-permute-done | bytes 16416 | tf_op jit(solution)/shard_map/ppermute | solution.py:302
  43.0 0.9 copy-done.7
  44.0 0.9 copy-done.8
  45.0 0.9 copy-done.9
  45.9 0.9 copy-done.10
  46.9 7.7 %backward_first.1 = (bf16[8,128,128]{2,1,0:T(8,128)(2,1)}, f32[1792,128]{1,0:T(8,128)S(1)}, bf16[1792,128]{1,0:T(8,128)(2,1)S(1)}) custom-call(bf16[4,128,128]{2,1,0:T(8,128)(2,1)S(1)} %get-tuple-element.46.refs_0_, bf16[4,128,128]{2,1,0:T(8,128)(2,1)S(1)} %collective-permute-done.3.refs_1_, bf16[8,8,128]{2,1,0:T(8,128)(2,1)S(1)} %collective-permute-done.4.refs_2_, ...), custom_call_target="tpu_custom_call" | custom-call | flops 1500000000 | bytes 4000000 | tf_op jit(solution)/shard_map/backward_first/pallas_call | solution.py:392
  54.6 7.7 %collective-permute-start.5 = (bf16[1792,128]{1,0:T(8,128)(2,1)S(1)}, bf16[1792,128]{1,0:T(8,128)(2,1)S(1)}, u32[]{:S(2)}, u32[]{:S(2)}) collective-permute-start(bf16[1792,128]{1,0:T(8,128)(2,1)S(1)} %get-tuple-element.70), channel_id=1, source_target_pairs={{0,8},{8,0},{1,9},{9,1},{2,10},{10,2},{3,11},{11,3},{4,12},{12,4},... | collective-permute-start | bytes 1376264 | tf_op jit(solution)/shard_map/ppermute | solution.py:306
  62.3 1.4 %collective-permute-done.5 = bf16[1792,128]{1,0:T(8,128)(2,1)S(1)} collective-permute-done((bf16[1792,128]{1,0:T(8,128)(2,1)S(1)}, bf16[1792,128]{1,0:T(8,128)(2,1)S(1)}, u32[]{:S(2)}, u32[]{:S(2)}) %collective-permute-start.5) | collective-permute-done | bytes 458784 | tf_op jit(solution)/shard_map/ppermute | solution.py:306
  63.8 0.1 add_convert_fusion
  63.9 13.0 %all_to_all.15 = bf16[16,112,128]{2,1,0:T(8,128)(2,1)S(1)} all-to-all(bf16[16,112,128]{2,1,0:T(8,128)(2,1)S(1)} %bitcast.5), channel_id=1, replica_groups=mesh['z'=8,'yh'=2,'core'=2,'x'=4,'yl'=2] {'yh','x','yl'}, dimensions={0} | all-to-all | bytes 917504 | tf_op jit(solution)/shard_map/all_to_all | solution.py:311
  76.9 0.1 reduce_sum.24
  77.1 11.3 %all_to_all.16 = bf16[8,112,128]{2,1,0:T(8,128)(2,1)S(1)} all-to-all(bf16[8,112,128]{2,1,0:T(8,128)(2,1)S(1)} %broadcast_in_dim.4), channel_id=1, replica_groups=mesh['z'=8,'yh'=2,'core'=2,'x'=4,'yl'=2] {'z'}, dimensions={0} | all-to-all | bytes 458752 | tf_op jit(solution)/shard_map/all_to_all | solution.py:316
  88.4 0.1 broadcast_in_dim.5
  88.5 11.7 %all_to_all.17 = bf16[16,112,128]{2,1,0:T(8,128)(2,1)S(1)} all-to-all(bf16[16,112,128]{2,1,0:T(8,128)(2,1)S(1)} %broadcast_in_dim.5), channel_id=1, replica_groups=mesh['z'=8,'yh'=2,'core'=2,'x'=4,'yl'=2] {'yh','x','yl'}, dimensions={0} | all-to-all | bytes 917504 | tf_op jit(solution)/shard_map/all_to_all | solution.py:316
  100.2 4.6 %collective-permute-start.6 = (bf16[1792,128]{1,0:T(8,128)(2,1)S(1)}, bf16[1792,128]{1,0:T(8,128)(2,1)S(1)}, u32[]{:S(2)}, u32[]{:S(2)}) collective-permute-start(bf16[1792,128]{1,0:T(8,128)(2,1)S(1)} %bitcast.3), channel_id=1, source_target_pairs={{0,8},{8,0},{1,9},{9,1},{2,10},{10,2},{3,11},{11,3},{4,12},{12,4},... | collective-permute-start | bytes 1376264 | tf_op jit(solution)/shard_map/ppermute | solution.py:306
  104.8 1.4 %collective-permute-done.6.other_ref = bf16[1792,128]{1,0:T(8,128)(2,1)S(1)} collective-permute-done((bf16[1792,128]{1,0:T(8,128)(2,1)S(1)}, bf16[1792,128]{1,0:T(8,128)(2,1)S(1)}, u32[]{:S(2)}, u32[]{:S(2)}) %collective-permute-start.6) | collective-permute-done | bytes 458784 | tf_op jit(solution)/shard_map/ppermute | solution.py:306
  106.2 1.4 %unpack.1 = (f32[2,128,384]{2,1,0:T(8,128)}, f32[2,128,128]{2,1,0:T(8,128)}, f32[2,128,512]{2,1,0:T(8,128)}, f32[2,512,128]{2,1,0:T(8,128)}, f32[2,2,128]{2,1,0:T(2,128)}, /*index=5*/f32[2,4,64,64]{3,2,1,0:T(8,128)}) custom-call(s32[1]{0:T(128)} %bitcast.refs_17_.core_ref, bf16[1792,128]{1,0:T(8,128)(2,1)S(1)} %bitcast.4, ...), custom_call_target="tpu_custom_call" | custom-call | flops 1000000 | bytes 4000000 | tf_op jit(solution)/shard_map/unpack/pallas_call | solution.py:407
  (26 shorter events, 0.1 us)
Async XLA Ops:
  0.6 4.4 %copy-start.3 = (bf16[2,128,384]{2,1,0:T(8,128)(2,1)S(1)}, bf16[2,128,384]{2,1,0:T(8,128)(2,1)}, u32[]{:S(2)}) copy-start(bf16[2,128,384]{2,1,0:T(8,128)(2,1)} %refs_11_.1) | copy-start | bytes 589828
  0.6 4.4 %copy-start.4 = (bf16[2,128,128]{2,1,0:T(8,128)(2,1)S(1)}, bf16[2,128,128]{2,1,0:T(8,128)(2,1)}, u32[]{:S(2)}) copy-start(bf16[2,128,128]{2,1,0:T(8,128)(2,1)} %refs_12_.1) | copy-start | bytes 196612
  0.7 4.4 %copy-start.5 = (f32[2,2,128]{2,1,0:T(2,128)S(1)}, f32[2,2,128]{2,1,0:T(2,128)}, u32[]{:S(2)}) copy-start(f32[2,2,128]{2,1,0:T(2,128)} %refs_15_.1) | copy-start | bytes 6148
  1.7 20.5 %copy-start = (f32[2,4,64,64]{3,2,1,0:T(8,128)S(1)}, f32[2,4,64,64]{3,2,1,0:T(8,128)}, u32[]{:S(2)}) copy-start(f32[2,4,64,64]{3,2,1,0:T(8,128)} %refs_10_.1) | copy-start | bytes 393220
  1.7 20.5 %copy-start.1 = (bf16[2,128,512]{2,1,0:T(8,128)(2,1)S(1)}, bf16[2,128,512]{2,1,0:T(8,128)(2,1)}, u32[]{:S(2)}) copy-start(bf16[2,128,512]{2,1,0:T(8,128)(2,1)} %refs_13_.1) | copy-start | bytes 786436
  1.7 20.5 %copy-start.2 = (bf16[2,512,128]{2,1,0:T(8,128)(2,1)S(1)}, bf16[2,512,128]{2,1,0:T(8,128)(2,1)}, u32[]{:S(2)}) copy-start(bf16[2,512,128]{2,1,0:T(8,128)(2,1)} %refs_14_.1) | copy-start | bytes 786436
  1.7 9.3 %collective-permute-start = (bf16[4,128,128]{2,1,0:T(8,128)(2,1)S(1)}, bf16[4,128,128]{2,1,0:T(8,128)(2,1)S(1)}, u32[]{:S(2)}, u32[]{:S(2)}) collective-permute-start(bf16[4,128,128]{2,1,0:T(8,128)(2,1)S(1)} %get-tuple-element.78), channel_id=1, source_target_pairs={{0,248},{1,249},{2,250},{3,251},{4,252},{5,253},{6,254},{7,255},{8... | collective-permute-start | bytes 393224 | tf_op jit(solution)/shard_map/ppermute | solution.py:302
  11.0 7.3 %collective-permute-start.1 = (bf16[4,128,128]{2,1,0:T(8,128)(2,1)S(1)}, bf16[4,128,128]{2,1,0:T(8,128)(2,1)S(1)}, u32[]{:S(2)}, u32[]{:S(2)}) collective-permute-start(bf16[4,128,128]{2,1,0:T(8,128)(2,1)S(1)} %get-tuple-element.44), channel_id=1, source_target_pairs={{0,248},{1,249},{2,250},{3,251},{4,252},{5,253},{6,254},{7,255},{8... | collective-permute-start | bytes 393224 | tf_op jit(solution)/shard_map/ppermute | solution.py:302
  18.3 3.9 %collective-permute-start.2 = (bf16[16,8,128]{2,1,0:T(8,128)(2,1)S(1)}, bf16[16,8,128]{2,1,0:T(8,128)(2,1)S(1)}, u32[]{:S(2)}, u32[]{:S(2)}) collective-permute-start(bf16[16,8,128]{2,1,0:T(8,128)(2,1)S(1)} %pad_maximum_fusion), channel_id=1, source_target_pairs={{0,7},{1,0},{2,1},{3,2},{4,3},{5,4},{6,5},{7,6},{8,15},{9,8},{10,9... | collective-permute-start | bytes 98312 | tf_op jit(solution)/shard_map/ppermute | solution.py:302
  31.9 5.2 %collective-permute-start.3 = (bf16[4,128,128]{2,1,0:T(8,128)(2,1)S(1)}, bf16[4,128,128]{2,1,0:T(8,128)(2,1)S(1)}, u32[]{:S(2)}, u32[]{:S(2)}) collective-permute-start(bf16[4,128,128]{2,1,0:T(8,128)(2,1)S(1)} %get-tuple-element.47), channel_id=1, source_target_pairs={{0,8},{1,9},{2,10},{3,11},{4,12},{5,13},{6,14},{7,15},{8,16},{9,17... | collective-permute-start | bytes 393224 | tf_op jit(solution)/shard_map/ppermute | solution.py:302
  32.0 11.0 %copy-start.6 = (bf16[1024,256]{1,0:T(8,128)(2,1)S(1)}, bf16[1024,256]{1,0:T(8,128)(2,1)}, u32[]{:S(2)}) copy-start(bf16[1024,256]{1,0:T(8,128)(2,1)} %get-tuple-element.62.refs_6_) | copy-start | bytes 1572868
  37.2 5.9 %collective-permute-start.4 = (bf16[8,8,128]{2,1,0:T(8,128)(2,1)S(1)}, bf16[8,8,128]{2,1,0:T(8,128)(2,1)S(1)}, u32[]{:S(2)}, u32[]{:S(2)}) collective-permute-start(bf16[8,8,128]{2,1,0:T(8,128)(2,1)S(1)} %pad_maximum_fusion.1), channel_id=1, source_target_pairs={{0,1},{1,2},{2,3},{3,4},{4,5},{5,6},{6,7},{7,0},{8,9},{9,10},{10,1... | collective-permute-start | bytes 49160 | tf_op jit(solution)/shard_map/ppermute | solution.py:302
  43.0 1.0 copy-start.7
  44.0 0.9 copy-start.8
  45.0 0.9 copy-start.9
  45.9 0.9 copy-start.10
  54.6 9.2 %collective-permute-start.5 = (bf16[1792,128]{1,0:T(8,128)(2,1)S(1)}, bf16[1792,128]{1,0:T(8,128)(2,1)S(1)}, u32[]{:S(2)}, u32[]{:S(2)}) collective-permute-start(bf16[1792,128]{1,0:T(8,128)(2,1)S(1)} %get-tuple-element.70), channel_id=1, source_target_pairs={{0,8},{8,0},{1,9},{9,1},{2,10},{10,2},{3,11},{11,3},{4,12},{12,4},... | collective-permute-start | bytes 1376264 | tf_op jit(solution)/shard_map/ppermute | solution.py:306
  100.2 6.0 %collective-permute-start.6 = (bf16[1792,128]{1,0:T(8,128)(2,1)S(1)}, bf16[1792,128]{1,0:T(8,128)(2,1)S(1)}, u32[]{:S(2)}, u32[]{:S(2)}) collective-permute-start(bf16[1792,128]{1,0:T(8,128)(2,1)S(1)} %bitcast.3), channel_id=1, source_target_pairs={{0,8},{8,0},{1,9},{9,1},{2,10},{10,2},{3,11},{11,3},{4,12},{12,4},... | collective-permute-start | bytes 1376264 | tf_op jit(solution)/shard_map/ppermute | solution.py:306

commit v2 on v1

--- a/solution.py
+++ b/solution.py
@@ -18,7 +18,7 @@
 F32 = jnp.float32
 BF16 = jnp.bfloat16
 VMEM_LIMIT = 32 * 1024 * 1024
-FIRST_LIMIT = 55 * 1000 * 1000
+FIRST_LIMIT = 57 * 1000 * 1000
 
 ROW_QKV, ROW_PROJ, ROW_UP, ROW_DOWN, ROW_BIAS, ROW_GAIN, ROWS = 0, 384, 512, 1024, 1536, 1664, 1792
 AXES = ("z", "yh", "core", "x", "yl")
@@ -176,66 +176,107 @@
     return jnp.concatenate([bias[h].T for h in range(HEADS)], axis=1)
 
 
+def first_half(x, w_qkv, w_proj, w_up, w_down, gain_ref, bias, top_ref, low_ref):
+    h, kept, _ = forward(to_windows(x.astype(F32)), w_qkv, w_proj, gain_ref[0:1], gain_ref[1:2], turned_bias(bias), head_mask())
+    m, _ = gelu_and_slope(nn(kept[7], w_up))
+    tile = from_windows(h + nn(m.astype(BF16), w_down))
+    top_ref[...] = tile[:HALF].astype(BF16)
+    low_ref[...] = tile[HALF:].astype(BF16)
+
+
 def first_kernel(*refs):
     (latent_hbm, bias_hbm), weights_hbm, refs = refs[:2], refs[2:7], refs[7:]
-    (top_ref, low_ref), kept_refs, refs = refs[:2], refs[2:10], refs[10:]
+    (top_ref, low_ref), refs = refs[:2], refs[2:]
     (x_ref, bias_ref, sem), weight_refs = refs[:3], refs[3:]
     w_qkv_ref, w_proj_ref, w_up_ref, w_down_ref, gain_ref = weight_refs
-    moves = [(latent_hbm, x_ref), (bias_hbm.at[0], bias_ref)]
+    wide = latent_hbm.shape[1] // 2
+    moves = [(latent_hbm.at[:, 0:wide], x_ref), (bias_hbm.at[0], bias_ref)]
     moves += [(source.at[0], target) for source, target in zip(weights_hbm, weight_refs)]
     copies = [pltpu.make_async_copy(source, target, sem.at[i]) for i, (source, target) in enumerate(moves)]
     for copy in copies:
         copy.start()
-    mask = head_mask()
     for copy in copies:
         copy.wait()
-    x = to_windows(x_ref[...].astype(F32))
-    h, kept, _ = forward(
-        x, w_qkv_ref[...], w_proj_ref[...], gain_ref[0:1], gain_ref[1:2], turned_bias(bias_ref), mask
-    )
+    weights = (w_qkv_ref[...], w_proj_ref[...], w_up_ref[...], w_down_ref[...])
+    first_half(x_ref[...], *weights, gain_ref, bias_ref, top_ref, low_ref)
+
+
+def next_kernel(x_ref, w_qkv_ref, w_proj_ref, w_up_ref, w_down_ref, gain_ref, bias_ref, top_ref, low_ref):
+    wide = x_ref.shape[1] // 2
+    weights = (w_qkv_ref[0], w_proj_ref[0], w_up_ref[0], w_down_ref[0])
+    first_half(x_ref[:, wide:], *weights, gain_ref.at[0], bias_ref.at[0], top_ref, low_ref)
+
+
+def keep_kernel(part, x_ref, w_qkv_ref, w_proj_ref, gain_ref, bias_ref, *kept_refs):
+    wide = x_ref.shape[1] // 2
+    x = to_windows(x_ref[:, part * wide : (part + 1) * wide].astype(F32))
+    g1, g2 = gain_ref[0, 0:1], gain_ref[0, 1:2]
+    _, kept, _ = forward(x, w_qkv_ref[0], w_proj_ref[0], g1, g2, turned_bias(bias_ref[0]), head_mask())
     for ref, value in zip(kept_refs, kept):
         ref[...] = jnp.broadcast_to(value, ref.shape).astype(ref.dtype)
-    m, _ = gelu_and_slope(nn(kept[7], w_up_ref[...]))
-    tile = from_windows(h + nn(m.astype(BF16), w_down_ref[...]))
-    top_ref[...] = tile[:HALF].astype(BF16)
-    low_ref[...] = tile[HALF:].astype(BF16)
+
+
+def second_half(x, gy, w_qkv_ref, w_proj_ref, w_up_ref, w_down_ref, gain_ref, bias_ref):
+    mask = head_mask()
+    w_qkv, w_proj, w_up, g1, g2 = w_qkv_ref[1], w_proj_ref[1], w_up_ref[1], gain_ref[1, 0:1], gain_ref[1, 1:2]
+    _, kept, qkv = forward(to_windows(x), w_qkv, w_proj, g1, g2, turned_bias(bias_ref[1]), mask)
+    return backward(to_windows(gy).astype(BF16), kept, qkv, w_qkv, w_proj, w_up, w_down_ref[1], g1, g2, mask)
 
 
 def second_kernel(*refs):
-    x_own_ref, x_low_ref, g_own_ref, g_low_ref, edge_ref = refs[:5]
-    w_qkv_ref, w_proj_ref, w_up_ref, w_down_ref, gain_ref, bias_ref = refs[5:11]
-    (dtop_ref, dlow_ref), pair_refs, (bias_out_ref, gain_out_ref, frame_ref) = refs[11:13], refs[13:21], refs[21:]
-    cols = x_own_ref.shape[1]
-
-    def shifted(own, low, right):
-        frame_ref[0:HALF, 0:cols] = own[...].astype(F32)
-        frame_ref[HALF:, 0:cols] = low[...].astype(F32)
-        frame_ref[:, cols : cols + WIN] = right.astype(F32)
-        return to_windows(frame_ref[:, HALF : HALF + cols])
-
-    mask = head_mask()
-    x = shifted(x_own_ref, x_low_ref, edge_ref[0:WIN])
-    gy = shifted(g_own_ref, g_low_ref, edge_ref[WIN:]).astype(BF16)
-    w_qkv, w_proj, w_up, g1, g2 = w_qkv_ref[1], w_proj_ref[1], w_up_ref[1], gain_ref[1, 0:1], gain_ref[1, 1:2]
-    _, kept, qkv = forward(x, w_qkv, w_proj, g1, g2, turned_bias(bias_ref[1]), mask)
-    dx, pairs, bias, gain1, gain2 = backward(gy, kept, qkv, w_qkv, w_proj, w_up, w_down_ref[1], g1, g2, mask)
+    low_ref, below_ref, g_own_ref, g_below_ref = refs[:4]
+    weights, (dx_ref, *pair_refs), (bias_out_ref, gain_out_ref, frame_ref) = refs[4:10], refs[10:19], refs[19:]
+    wide = low_ref.shape[1]
+    frame_ref[0:HALF, 0:wide] = low_ref[...].astype(F32)
+    frame_ref[HALF:, 0:wide] = below_ref[...].astype(F32)
+    x = frame_ref[:, HALF : wide - HALF]
+    frame_ref[0:HALF, 0:wide] = g_own_ref[HALF:, 0:wide].astype(F32)
+    frame_ref[HALF:, 0:wide] = g_below_ref[0:HALF, 0:wide].astype(F32)
+    gy = frame_ref[:, HALF : wide - HALF]
+    dx, pairs, bias, gain1, gain2 = second_half(x, gy, *weights)
+    dx_ref[...] = dx
     for ref, value in zip(pair_refs, pairs):
         ref[...] = value
     bias_out_ref[...] = bias
     gain_out_ref[0:1] = gain1
     gain_out_ref[1:2] = gain2
-    tile = from_windows(dx)
+
+
+def third_kernel(*refs):
+    low_a_ref, low_b_ref, below_a_ref, below_b_ref, g_own_ref, g_below_ref, edge_ref = refs[:7]
+    weights, (dx_ref, bias_ref, gain_ref) = refs[7:13], refs[13:16]
+    (dtop_ref, dlow_ref), pair_refs, (bias_out_ref, gain_out_ref, frame_ref) = refs[16:18], refs[18:26], refs[26:]
+    wide, cols = low_a_ref.shape[1], g_own_ref.shape[1]
+    span = cols - wide + WIN
+    frame_ref[0:HALF, 0:WIN] = low_a_ref[:, wide - WIN :].astype(F32)
+    frame_ref[HALF:, 0:WIN] = below_a_ref[:, wide - WIN :].astype(F32)
+    frame_ref[0:HALF, WIN:span] = low_b_ref[...].astype(F32)
+    frame_ref[HALF:, WIN:span] = below_b_ref[...].astype(F32)
+    frame_ref[:, span : span + WIN] = edge_ref[0:WIN].astype(F32)
+    x = frame_ref[:, HALF : span + HALF]
+    frame_ref[0:HALF, 0:span] = g_own_ref[HALF:, wide - WIN :].astype(F32)
+    frame_ref[HALF:, 0:span] = g_below_ref[0:HALF, wide - WIN :].astype(F32)
+    frame_ref[:, span : span + WIN] = edge_ref[WIN:].astype(F32)
+    gy = frame_ref[:, HALF : span + HALF]
+    dx, pairs, bias, gain1, gain2 = second_half(x, gy, *weights)
+    for ref, value in zip(pair_refs, pairs):
+        ref[...] = value
+    bias_out_ref[...] = bias_ref[...] + bias
+    gain_out_ref[0:1] = gain_ref[0:1] + gain1
+    gain_out_ref[1:2] = gain_ref[1:2] + gain2
+    tile = from_windows(jnp.concatenate([dx_ref[...], dx], axis=0))
     dtop_ref[...] = tile[:HALF].astype(BF16)
     dlow_ref[...] = tile[HALF:].astype(BF16)
 
 
 def weights_kernel(*refs):
-    pairs, (bias_ref, gain_ref, pack_ref) = refs[:8], refs[8:]
-    pack(pack_ref, [ref[...] for ref in pairs], bias_ref[...], gain_ref[0:1], gain_ref[1:2])
+    first, second, (bias_ref, gain_ref, pack_ref) = refs[:8], refs[8:16], refs[16:]
+    pairs = [jnp.concatenate([a[...], b[...]], axis=0) for a, b in zip(first, second)]
+    pack(pack_ref, pairs, bias_ref[...], gain_ref[0:1], gain_ref[1:2])
 
 
 def last_kernel(*refs):
-    (own, above, left), kept_refs, refs = refs[:3], refs[3:11], refs[11:]
+    (own, above, left), kept_refs, refs = refs[:3], refs[3:19], refs[19:]
     w_qkv_ref, w_proj_ref, w_up_ref, w_down_ref, gain_ref, other_ref, core_ref = refs[:7]
     dx_ref, keep_ref, send_ref, frame_ref, pack_ref = refs[7:]
     cols = own.shape[1]
@@ -245,7 +286,8 @@
     frame_ref[HALF:, HALF : HALF + cols] = own[...].astype(F32)
     frame_ref[0:HALF, HALF : HALF + cols] = above[...].astype(F32)
     gy = to_windows(frame_ref[:, 0:cols]).astype(BF16)
-    kept = [ref[...].astype(F32) if i in (0, 1, 5, 6) else ref[...] for i, ref in enumerate(kept_refs)]
+    kept = [jnp.concatenate([a[...], b[...]], axis=0) for a, b in zip(kept_refs[:8], kept_refs[8:])]
+    kept = [v.astype(F32) if i in (0, 1, 5, 6) else v for i, v in enumerate(kept)]
     g1, g2 = gain_ref[0, 0:1], gain_ref[0, 1:2]
     dx, pairs, bias, gain1, gain2 = backward(
         gy, kept, nn(kept[2], w_qkv_ref[0]).astype(BF16), w_qkv_ref[0], w_proj_ref[0], w_up_ref[0], w_down_ref[0], g1, g2, head_mask()
@@ -331,64 +373,101 @@
     packed = jax.ShapeDtypeStruct((ROWS, CH), F32)
     core = lax.axis_index("core").reshape(1)
     weights = (w_qkv, w_proj, w_up, w_down, gains)
-    g_low = cotangent[HALF:]
-    g_below = shift(cotangent[:HALF], -1, 0)
+    g_below = shift(cotangent, -1, 0)
     tokens = WIN * cols
 
-    def table(width):
-        return jax.ShapeDtypeStruct((tokens, width), BF16)
-
-    kept_shapes = [table(CH), table(CH), table(CH), table(HEADS * LEN), table(CH)]
-    kept_shapes += [table(CH), table(CH), table(CH)]
-    pair_shapes = [table(CH), table(FFN), table(CH), table(FFN), table(CH), table(CH), table(CH), table(3 * CH)]
-    top, low, *kept = pl.pallas_call(
+    def table(width, share=1):
+        return jax.ShapeDtypeStruct((tokens // share, width), BF16)
+
+    kept_shapes = [table(width, 2) for width in (CH, CH, CH, HEADS * LEN, CH, CH, CH, CH)]
+    pair_widths = (CH, FFN, CH, FFN, CH, CH, CH, 3 * CH)
+    wide = cols // 2
+    part_a, part_b = WIN * (wide - WIN), WIN * (cols - wide + WIN)
+    small = [jax.ShapeDtypeStruct((LEN, HEADS * LEN), F32), jax.ShapeDtypeStruct((2, CH), F32)]
+    side = jax.ShapeDtypeStruct((HALF, wide, CH), BF16)
+    top_a, low_a = pl.pallas_call(
         first_kernel,
-        out_shape=(half, half, *kept_shapes),
+        out_shape=(side, side),
         in_specs=[pl.BlockSpec(memory_space=pltpu.HBM)] * 7,
-        out_specs=vmem(10),
+        out_specs=vmem(2),
         scratch_shapes=[
-            pltpu.VMEM(latent.shape, BF16),
+            pltpu.VMEM((WIN, wide, CH), BF16),
             pltpu.VMEM(attn_bias.shape[1:], F32),
             pltpu.SemaphoreType.DMA((7,)),
         ]
         + [pltpu.VMEM(w.shape[1:], w.dtype) for w in weights],
         compiler_params=pltpu.CompilerParams(vmem_limit_bytes=FIRST_LIMIT),
-        cost_estimate=cost(500_000_000, 1_500_000),
+        cost_estimate=cost(300_000_000, 1_500_000),
         name="forward_first",
     )(latent, attn_bias, *weights)
-    top, g_below = lax.optimization_barrier((top, g_below))
-    x_below = shift(top, -1, 0)
-    edge = jnp.concatenate([v[:, :WIN] for v in (low, x_below, g_low, g_below)], axis=0)
-    edge = shift(edge, 0, -1)
+    below_a = shift(top_a, -1, 0)
+    top_b, low_b = pl.pallas_call(
+        next_kernel,
+        out_shape=(side, side),
+        in_specs=vmem(7),
+        out_specs=vmem(2),
+        compiler_params=params,
+        cost_estimate=cost(300_000_000, 1_500_000),
+        name="forward_next",
+    )(latent, *weights, attn_bias)
+    top_b, below_a, g_below = lax.optimization_barrier((top_b, below_a, g_below))
+    below_b = shift(top_b, -1, 0)
+    rows = (low_a, below_a, cotangent[HALF:], g_below[:HALF])
+    edge = shift(jnp.concatenate([v[:, :WIN] for v in rows], axis=0), 0, -1)
+    weights = (*weights, attn_bias)
     frame = pltpu.VMEM((WIN, cols + 2 * WIN, CH), F32)
-    d_top, d_low, *pairs = pl.pallas_call(
+    dx_a, *pairs_a, bias_a, gain_a = pl.pallas_call(
         second_kernel,
         out_shape=(
-            half,
-            half,
-            *pair_shapes,
-            jax.ShapeDtypeStruct((LEN, HEADS * LEN), F32),
-            jax.ShapeDtypeStruct((2, CH), F32),
+            jax.ShapeDtypeStruct((part_a, CH), F32),
+            *[jax.ShapeDtypeStruct((part_a, width), BF16) for width in pair_widths],
+            *small,
         ),
-        in_specs=vmem(11),
+        in_specs=vmem(10),
+        out_specs=vmem(11),
+        scratch_shapes=[frame],
+        compiler_params=params,
+        cost_estimate=cost(700_000_000, 3_000_000),
+        name="backward_second",
+    )(low_a, below_a, cotangent, g_below, *weights)
+    edge, below_b, dx_a = lax.optimization_barrier((edge, below_b, dx_a))
+    d_top, d_low, *pairs_b, bias_b, gain_b = pl.pallas_call(
+        third_kernel,
+        out_shape=(half, half, *[jax.ShapeDtypeStruct((part_b, width), BF16) for width in pair_widths], *small),
+        in_specs=vmem(16),
         out_specs=vmem(12),
         scratch_shapes=[frame],
         compiler_params=params,
-        cost_estimate=cost(1_500_000_000, 3_000_000),
-        name="backward_second",
-    )(low, x_below, g_low, g_below, edge, *weights, attn_bias)
+        cost_estimate=cost(800_000_000, 3_000_000),
+        name="backward_third",
+    )(low_a, low_b, below_a, below_b, cotangent, g_below, edge, *weights, dx_a, bias_a, gain_a)
     pack_two = pl.pallas_call(
         weights_kernel,
         out_shape=packed,
-        in_specs=vmem(10),
+        in_specs=vmem(18),
         out_specs=vmem(1)[0],
         compiler_params=params,
         cost_estimate=cost(500_000_000, 5_000_000),
         name="weights_second",
-    )(*pairs)
+    )(*pairs_a, *pairs_b, bias_b, gain_b)
     d_above = shift(d_low, 1, 0)
-    d_above, pack_two = lax.optimization_barrier((d_above, pack_two))
-    d_left = shift(jnp.concatenate([v[:, cols - WIN :] for v in (d_above, d_top)], axis=0), 0, 1)
+    kept = []
+    for part in range(2):
+        made = pl.pallas_call(
+            functools.partial(keep_kernel, part),
+            out_shape=kept_shapes,
+            in_specs=vmem(5),
+            out_specs=vmem(8),
+            compiler_params=params,
+            cost_estimate=cost(300_000_000, 2_000_000),
+            name="keep_first",
+        )(latent, w_qkv, w_proj, gains, attn_bias)
+        if part == 0:
+            d_above, pack_two, made = lax.optimization_barrier((d_above, pack_two, made))
+            d_left = shift(jnp.concatenate([v[:, cols - WIN :] for v in (d_above, d_top)], axis=0), 0, 1)
+        else:
+            d_left, made = lax.optimization_barrier((d_left, made))
+        kept += made
     dx, keep, send = pl.pallas_call(
         last_kernel,
         out_shape=(
@@ -396,13 +475,13 @@
             packed,
             jax.ShapeDtypeStruct((ROWS, CH), BF16),
         ),
-        in_specs=vmem(17) + [pl.BlockSpec(memory_space=pltpu.SMEM)],
+        in_specs=vmem(25) + [pl.BlockSpec(memory_space=pltpu.SMEM)],
         out_specs=vmem(3),
         scratch_shapes=[frame, pltpu.VMEM((ROWS, CH), F32)],
         compiler_params=params,
         cost_estimate=cost(1_500_000_000, 4_000_000),
         name="backward_first",
-    )(d_top, d_above, d_left, *kept, *weights, pack_two, core)
+    )(d_top, d_above, d_left, *kept, *weights[:5], pack_two, core)
     parts = sum_over_devices(keep, send)
     qkv, proj, up, down, gain, bias = pl.pallas_call(
         unpack_kernel,

time: 108 us -> 115 us (1.065)
  local copies, waits for them, and re-layouts: 5.68 us -> 16.2 us
  waiting for transfers between devices: 13.4 us -> 5.7 us
  Pallas kernels: 25.5 us -> 30.5 us
  starting transfers between devices: 25.9 us -> 23.6 us
  blocking collectives: 36.1 us -> 37.5 us
    unnamed x22 -> x78, local copies, waits for them, and re-layouts: 3.84 us -> 13.3 us
    ppermute x5 -> x6, waiting for transfers between devices: 10.5 us -> 2.81 us  [shift(): return lax.ppermute(value, AXES, pairs)]
    ppermute x2, starting transfers between devices: 12.3 us -> 7.82 us  [swap_core(): return lax.ppermute(value, 'core', [(0, 1), (1, 0)])]
    pallas_call x3 -> x7, Pallas kernels: 16.4 us -> 20.5 us  [the longest x1 6.53 us: body(): pl.pallas_call(third_kernel, out_shape=(half, half, *[jax.ShapeDtypeStruc...]
    ppermute x5 -> x6, starting transfers between devices: 13.6 us -> 15.8 us  [shift(): return lax.ppermute(value, AXES, pairs)]
    all_to_all x2, blocking collectives: 23 us -> 24.6 us  [collect(): return lax.all_to_all(spread, axis, 0, 0)]
    slice x2, local copies, waits for them, and re-layouts: 0.01 us -> 1.4 us  [body(): v[:, cols - WIN:]]
  transfers between devices with their start and end apart: 7 -> 8, of which waited for: 6 -> 3; matrix products, arithmetic and copies ran while one was open for 1% -> 2% of each run, Pallas kernels for 6% -> 12%
where the time goes in v2:
time: 115 us
  blocking collectives  37.5 us (33%)
  Pallas kernels  30.5 us (27%)
  starting transfers between devices  23.6 us (21%)
  local copies, waits for them, and re-layouts  16.2 us (14%)
  waiting for transfers between devices  5.7 us (5%)
    all_to_all x2, blocking collectives, collect(): return lax.all_to_all(spread, axis, 0, 0)  24.6 us
    ppermute x6, starting transfers between devices, shift(): return lax.ppermute(value, AXES, pairs)  15.8 us
    unnamed x78, local copies, waits for them, and re-layouts  13.3 us
    all_to_all x1, blocking collectives, scatter_sum(): return jnp.sum(lax.all_to_all(pieces, axis, 0, 0).astype(F32), axis=0)  12.9 us
    pallas_call x1, Pallas kernels, body(): pl.pallas_call(last_kernel, out_shape=(jax.ShapeDtypeStruct(latent.shape,...  8.67 us
    ppermute x2, starting transfers between devices, swap_core(): return lax.ppermute(value, 'core', [(0, 1), (1, 0)])  7.82 us
    pallas_call x1, Pallas kernels, body(): pl.pallas_call(third_kernel, out_shape=(half, half, *[jax.ShapeDtypeStruc...  6.53 us
    pallas_call x1, Pallas kernels, body(): pl.pallas_call(second_kernel, out_shape=(jax.ShapeDtypeStruct((part_a, CH...  4.48 us
  transfers between devices with their start and end apart: 8, of which 3 were waited for; matrix products, arithmetic and copies ran while one was open for 2% of the time, Pallas kernels for 12%

profile of v2, /device:TPU:1, one launch (start us, length us, event | category | flops | bytes accessed | tf_op | source)
XLA Modules:
  0.0 114.8 jit_solution(9782948282900111142)
XLA Ops:
  0.7 3.3 %collective-permute-start.1 = (bf16[8,128,128]{2,1,0:T(8,128)(2,1)}, bf16[8,128,128]{2,1,0:T(8,128)(2,1)S(1)}, u32[]{:S(2)}, u32[]{:S(2)}) collective-permute-start(bf16[8,128,128]{2,1,0:T(8,128)(2,1)} %refs_4_.5), channel_id=1, source_target_pairs={{0,248},{1,249},{2,250},{3,251},{4,252},{5,253},{6,254},{7,255},{8... | collective-permute-start | bytes 786440 | tf_op jit(solution)/shard_map/ppermute | solution.py:344
  4.0 3.8 %forward_first.1 = (bf16[4,64,128]{2,1,0:T(8,128)(2,1)}, bf16[4,64,128]{2,1,0:T(8,128)(2,1)}) custom-call(bf16[8,128,128]{2,1,0:T(8,128)(2,1)} %x_ref.5, f32[2,4,64,64]{3,2,1,0:T(8,128)} %bias_ref.5, bf16[2,128,384]{2,1,0:T(8,128)(2,1)} %refs_19_.1, bf16[2,128,128]{2,1,0:T(8,128)(2,1)} %refs_20_.1, bf16[2,128,512]{2,1,0:T(8,128)(2,1)} %refs_21_.1, ...), custom_call_target="tpu_custom_call" | custom-call | flops 300000000 | bytes 1500000 | tf_op jit(solution)/shard_map/forward_first/pallas_call | solution.py:388
  7.8 6.3 %collective-permute-start = (bf16[4,64,128]{2,1,0:T(8,128)(2,1)}, bf16[4,64,128]{2,1,0:T(8,128)(2,1)S(1)}, u32[]{:S(2)}, u32[]{:S(2)}) collective-permute-start(bf16[4,64,128]{2,1,0:T(8,128)(2,1)} %get-tuple-element.87), channel_id=1, source_target_pairs={{0,248},{1,249},{2,250},{3,251},{4,252},{5,253},{6,254},{7,255},{8... | collective-permute-start | bytes 196616 | tf_op jit(solution)/shard_map/ppermute | solution.py:344
  14.8 0.7 slice.22
  15.6 1.9 %forward_next.1 = (bf16[4,64,128]{2,1,0:T(8,128)(2,1)S(1)}, bf16[4,64,128]{2,1,0:T(8,128)(2,1)S(1)}) custom-call(bf16[8,128,128]{2,1,0:T(8,128)(2,1)S(1)} %copy-done, bf16[2,128,384]{2,1,0:T(8,128)(2,1)S(1)} %copy-done.4, bf16[2,128,128]{2,1,0:T(8,128)(2,1)S(1)} %copy-done.9, bf16[2,128,512]{2,1,0:T(8,128)(2,1)S(1)} %copy-done.2, ...), custom_call_target="tpu_custom_call" | custom-call | flops 300000000 | bytes 1500000 | tf_op jit(solution)/shard_map/forward_next/pallas_call | solution.py:404
  17.6 2.7 %collective-permute-start.2 = (bf16[16,8,128]{2,1,0:T(8,128)(2,1)S(1)}, bf16[16,8,128]{2,1,0:T(8,128)(2,1)S(1)}, u32[]{:S(2)}, u32[]{:S(2)}) collective-permute-start(bf16[16,8,128]{2,1,0:T(8,128)(2,1)S(1)} %pad_maximum_fusion), channel_id=1, source_target_pairs={{0,7},{1,0},{2,1},{3,2},{4,3},{5,4},{6,5},{7,6},{8,15},{9,8},{10,9... | collective-permute-start | bytes 98312 | tf_op jit(solution)/shard_map/ppermute | solution.py:344
  20.2 1.0 collective-permute-start.3
  21.2 4.5 %backward_second.1 = (f32[448,128]{1,0:T(8,128)S(1)}, bf16[448,128]{1,0:T(8,128)(2,1)S(1)}, bf16[448,512]{1,0:T(8,128)(2,1)S(1)}, bf16[448,128]{1,0:T(8,128)(2,1...) custom-call(bf16[4,64,128]{2,1,0:T(8,128)(2,1)S(1)} %copy-done.33, ...), custom_call_target="tpu_custom_call" | custom-call | flops 700000000 | bytes 3000000 | tf_op jit(solution)/shard_map/backward_second/pallas_call | solution.py:419
  25.8 6.5 %backward_third.1 = (bf16[4,128,128]{2,1,0:T(8,128)(2,1)S(1)}, bf16[4,128,128]{2,1,0:T(8,128)(2,1)}, bf16[576,128]{1,0:T(8,128)(2,1)S(1)}, bf16[576,512]{1,0:T(8...) custom-call(bf16[4,64,128]{2,1,0:T(8,128)(2,1)S(1)} %copy-done.33, ...), custom_call_target="tpu_custom_call" | custom-call | flops 800000000 | bytes 3000000 | tf_op jit(solution)/shard_map/backward_third/pallas_call | solution.py:434
  32.3 0.8 copy-done.5
  37.6 2.3 %collective-permute-start.4 = (bf16[4,128,128]{2,1,0:T(8,128)(2,1)}, bf16[4,128,128]{2,1,0:T(8,128)(2,1)}, u32[]{:S(2)}, u32[]{:S(2)}) collective-permute-start(bf16[4,128,128]{2,1,0:T(8,128)(2,1)} %get-tuple-element.98), channel_id=1, source_target_pairs={{0,8},{1,9},{2,10},{3,11},{4,12},{5,13},{6,14},{7,15},{8,16},{9,17... | collective-permute-start | bytes 393224 | tf_op jit(solution)/shard_map/ppermute | solution.py:344
  40.6 1.5 %keep_first.2 = (bf16[512,128]{1,0:T(8,128)(2,1)S(1)}, bf16[512,128]{1,0:T(8,128)(2,1)S(1)}, bf16[512,128]{1,0:T(8,128)(2,1)S(1)}, bf16[512,256]{1,0:T(8,128)(2,...) custom-call(bf16[8,128,128]{2,1,0:T(8,128)(2,1)S(1)} %copy-done, ...), custom_call_target="tpu_custom_call" | custom-call | flops 300000000 | bytes 2000000 | tf_op jit(solution)/shard_map/keep_first/pallas_call | solution.py:456
  42.1 0.7 slice.27
  43.5 0.9 copy-done.15
  44.4 0.9 copy-done.17
  45.3 0.9 copy-done.19
  46.2 0.9 copy-done.21
  47.1 0.9 copy-done.23
  48.0 0.9 copy-done.25
  48.9 0.9 copy-done.27
  50.5 0.7 slice.26
  51.9 1.5 %keep_first.3 = (bf16[512,128]{1,0:T(8,128)(2,1)S(1)}, bf16[512,128]{1,0:T(8,128)(2,1)S(1)}, bf16[512,128]{1,0:T(8,128)(2,1)S(1)}, bf16[512,256]{1,0:T(8,128)(2,...) custom-call(bf16[8,128,128]{2,1,0:T(8,128)(2,1)S(1)} %copy-done, ...), custom_call_target="tpu_custom_call" | custom-call | flops 300000000 | bytes 2000000 | tf_op jit(solution)/shard_map/keep_first/pallas_call | solution.py:456
  53.4 2.8 %collective-permute-done.5.refs_2_ = bf16[8,8,128]{2,1,0:T(8,128)(2,1)S(1)} collective-permute-done((bf16[8,8,128]{2,1,0:T(8,128)(2,1)S(1)}, bf16[8,8,128]{2,1,0:T(8,128)(2,1)S(1)}, u32[]{:S(2)}, u32[]{:S(2)}) %collective-permute-start.5) | collective-permute-done | bytes 16416 | tf_op jit(solution)/shard_map/ppermute | solution.py:344
  56.2 8.7 %backward_first.1 = (bf16[8,128,128]{2,1,0:T(8,128)(2,1)}, f32[1792,128]{1,0:T(8,128)S(1)}, bf16[1792,128]{1,0:T(8,128)(2,1)S(1)}) custom-call(bf16[4,128,128]{2,1,0:T(8,128)(2,1)S(1)} %copy-done.37, bf16[4,128,128]{2,1,0:T(8,128)(2,1)} %collective-permute-done.4.refs_1_, bf16[8,8,128]{2,1,0:T(8,128)(2,1)S(1)} %collective-permute-done.5.refs_2_, ...), custom_call_target="tpu_custom_call" | custom-call | flops 1500000000 | bytes 4000000 | tf_op jit(solution)/shard_map/backward_first/pallas_call | solution.py:471
  64.9 3.2 %collective-permute-start.6 = (bf16[1792,128]{1,0:T(8,128)(2,1)S(1)}, bf16[1792,128]{1,0:T(8,128)(2,1)S(1)}, u32[]{:S(2)}, u32[]{:S(2)}) collective-permute-start(bf16[1792,128]{1,0:T(8,128)(2,1)S(1)} %get-tuple-element.154), channel_id=1, source_target_pairs={{0,8},{8,0},{1,9},{9,1},{2,10},{10,2},{3,11},{11,3},{4,12},{12,4},... | collective-permute-start | bytes 1376264 | tf_op jit(solution)/shard_map/ppermute | solution.py:348
  68.1 1.4 %collective-permute-done.6 = bf16[1792,128]{1,0:T(8,128)(2,1)S(1)} collective-permute-done((bf16[1792,128]{1,0:T(8,128)(2,1)S(1)}, bf16[1792,128]{1,0:T(8,128)(2,1)S(1)}, u32[]{:S(2)}, u32[]{:S(2)}) %collective-permute-start.6) | collective-permute-done | bytes 458784 | tf_op jit(solution)/shard_map/ppermute | solution.py:348
  69.7 12.9 %all_to_all.15 = bf16[16,112,128]{2,1,0:T(8,128)(2,1)S(1)} all-to-all(bf16[16,112,128]{2,1,0:T(8,128)(2,1)S(1)} %bitcast.5), channel_id=1, replica_groups=mesh['z'=8,'yh'=2,'core'=2,'x'=4,'yl'=2] {'yh','x','yl'}, dimensions={0} | all-to-all | bytes 917504 | tf_op jit(solution)/shard_map/all_to_all | solution.py:353
  82.7 13.0 %all_to_all.16 = bf16[8,112,128]{2,1,0:T(8,128)(2,1)S(1)} all-to-all(bf16[8,112,128]{2,1,0:T(8,128)(2,1)S(1)} %broadcast_in_dim.4), channel_id=1, replica_groups=mesh['z'=8,'yh'=2,'core'=2,'x'=4,'yl'=2] {'z'}, dimensions={0} | all-to-all | bytes 458752 | tf_op jit(solution)/shard_map/all_to_all | solution.py:358
  95.8 11.6 %all_to_all.17 = bf16[16,112,128]{2,1,0:T(8,128)(2,1)S(1)} all-to-all(bf16[16,112,128]{2,1,0:T(8,128)(2,1)S(1)} %broadcast_in_dim.5), channel_id=1, replica_groups=mesh['z'=8,'yh'=2,'core'=2,'x'=4,'yl'=2] {'yh','x','yl'}, dimensions={0} | all-to-all | bytes 917504 | tf_op jit(solution)/shard_map/all_to_all | solution.py:358
  107.4 4.6 %collective-permute-start.7 = (bf16[1792,128]{1,0:T(8,128)(2,1)S(1)}, bf16[1792,128]{1,0:T(8,128)(2,1)S(1)}, u32[]{:S(2)}, u32[]{:S(2)}) collective-permute-start(bf16[1792,128]{1,0:T(8,128)(2,1)S(1)} %bitcast.3), channel_id=1, source_target_pairs={{0,8},{8,0},{1,9},{9,1},{2,10},{10,2},{3,11},{11,3},{4,12},{12,4},... | collective-permute-start | bytes 1376264 | tf_op jit(solution)/shard_map/ppermute | solution.py:348
  111.9 1.4 %collective-permute-done.7.other_ref = bf16[1792,128]{1,0:T(8,128)(2,1)S(1)} collective-permute-done((bf16[1792,128]{1,0:T(8,128)(2,1)S(1)}, bf16[1792,128]{1,0:T(8,128)(2,1)S(1)}, u32[]{:S(2)}, u32[]{:S(2)}) %collective-permute-start.7) | collective-permute-done | bytes 458784 | tf_op jit(solution)/shard_map/ppermute | solution.py:348
  113.4 1.4 %unpack.1 = (f32[2,128,384]{2,1,0:T(8,128)}, f32[2,128,128]{2,1,0:T(8,128)}, f32[2,128,512]{2,1,0:T(8,128)}, f32[2,512,128]{2,1,0:T(8,128)}, f32[2,2,128]{2,1,0:T(2,128)}, /*index=5*/f32[2,4,64,64]{3,2,1,0:T(8,128)}) custom-call(s32[1]{0:T(128)} %bitcast.refs_25_.core_ref, bf16[1792,128]{1,0:T(8,128)(2,1)S(1)} %bitcast.4, ...), custom_call_target="tpu_custom_call" | custom-call | flops 1000000 | bytes 4000000 | tf_op jit(solution)/shard_map/unpack/pallas_call | solution.py:486
  (87 shorter events, 8.3 us)
Async XLA Ops:
  0.6 14.9 %copy-start = (bf16[8,128,128]{2,1,0:T(8,128)(2,1)S(1)}, bf16[8,128,128]{2,1,0:T(8,128)(2,1)}, u32[]{:S(2)}) copy-start(bf16[8,128,128]{2,1,0:T(8,128)(2,1)} %x_ref.5) | copy-start | bytes 786436
  0.6 14.9 %copy-start.1 = (f32[2,4,64,64]{3,2,1,0:T(8,128)S(1)}, f32[2,4,64,64]{3,2,1,0:T(8,128)}, u32[]{:S(2)}) copy-start(f32[2,4,64,64]{3,2,1,0:T(8,128)} %bias_ref.5) | copy-start | bytes 393220
  0.7 14.8 %copy-start.4 = (bf16[2,128,384]{2,1,0:T(8,128)(2,1)S(1)}, bf16[2,128,384]{2,1,0:T(8,128)(2,1)}, u32[]{:S(2)}) copy-start(bf16[2,128,384]{2,1,0:T(8,128)(2,1)} %refs_19_.1) | copy-start | bytes 589828
  0.7 14.8 %copy-start.2 = (bf16[2,128,512]{2,1,0:T(8,128)(2,1)S(1)}, bf16[2,128,512]{2,1,0:T(8,128)(2,1)}, u32[]{:S(2)}) copy-start(bf16[2,128,512]{2,1,0:T(8,128)(2,1)} %refs_21_.1) | copy-start | bytes 786436
  0.7 14.8 %copy-start.3 = (bf16[2,512,128]{2,1,0:T(8,128)(2,1)S(1)}, bf16[2,512,128]{2,1,0:T(8,128)(2,1)}, u32[]{:S(2)}) copy-start(bf16[2,512,128]{2,1,0:T(8,128)(2,1)} %refs_22_.1) | copy-start | bytes 786436
  0.7 16.8 %collective-permute-start.1 = (bf16[8,128,128]{2,1,0:T(8,128)(2,1)}, bf16[8,128,128]{2,1,0:T(8,128)(2,1)S(1)}, u32[]{:S(2)}, u32[]{:S(2)}) collective-permute-start(bf16[8,128,128]{2,1,0:T(8,128)(2,1)} %refs_4_.5), channel_id=1, source_target_pairs={{0,248},{1,249},{2,250},{3,251},{4,252},{5,253},{6,254},{7,255},{8... | collective-permute-start | bytes 786440 | tf_op jit(solution)/shard_map/ppermute | solution.py:344
  4.0 11.5 %copy-start.9 = (bf16[2,128,128]{2,1,0:T(8,128)(2,1)S(1)}, bf16[2,128,128]{2,1,0:T(8,128)(2,1)}, u32[]{:S(2)}) copy-start(bf16[2,128,128]{2,1,0:T(8,128)(2,1)} %refs_20_.1) | copy-start | bytes 196612
  7.8 9.7 %collective-permute-start = (bf16[4,64,128]{2,1,0:T(8,128)(2,1)}, bf16[4,64,128]{2,1,0:T(8,128)(2,1)S(1)}, u32[]{:S(2)}, u32[]{:S(2)}) collective-permute-start(bf16[4,64,128]{2,1,0:T(8,128)(2,1)} %get-tuple-element.87), channel_id=1, source_target_pairs={{0,248},{1,249},{2,250},{3,251},{4,252},{5,253},{6,254},{7,255},{8... | collective-permute-start | bytes 196616 | tf_op jit(solution)/shard_map/ppermute | solution.py:344
  15.5 5.6 %copy-start.38 = (bf16[8,128,128]{2,1,0:T(8,128)(2,1)S(1)}, bf16[8,128,128]{2,1,0:T(8,128)(2,1)}, u32[]{:S(2)}) copy-start(bf16[8,128,128]{2,1,0:T(8,128)(2,1)} %refs_4_.5) | copy-start | bytes 786436
  17.5 3.7 %copy-start.33 = (bf16[4,64,128]{2,1,0:T(8,128)(2,1)S(1)}, bf16[4,64,128]{2,1,0:T(8,128)(2,1)}, u32[]{:S(2)}) copy-start(bf16[4,64,128]{2,1,0:T(8,128)(2,1)} %get-tuple-element.84.refs_0_) | copy-start | bytes 196612
  17.6 8.2 %collective-permute-start.2 = (bf16[16,8,128]{2,1,0:T(8,128)(2,1)S(1)}, bf16[16,8,128]{2,1,0:T(8,128)(2,1)S(1)}, u32[]{:S(2)}, u32[]{:S(2)}) collective-permute-start(bf16[16,8,128]{2,1,0:T(8,128)(2,1)S(1)} %pad_maximum_fusion), channel_id=1, source_target_pairs={{0,7},{1,0},{2,1},{3,2},{4,3},{5,4},{6,5},{7,6},{8,15},{9,8},{10,9... | collective-permute-start | bytes 98312 | tf_op jit(solution)/shard_map/ppermute | solution.py:344
  20.2 5.5 %collective-permute-start.3 = (bf16[4,64,128]{2,1,0:T(8,128)(2,1)S(1)}, bf16[4,64,128]{2,1,0:T(8,128)(2,1)S(1)}, u32[]{:S(2)}, u32[]{:S(2)}) collective-permute-start(bf16[4,64,128]{2,1,0:T(8,128)(2,1)S(1)} %get-tuple-element.90), channel_id=1, source_target_pairs={{0,248},{1,249},{2,250},{3,251},{4,252},{5,253},{6,254},{7,255},{8... | collective-permute-start | bytes 196616 | tf_op jit(solution)/shard_map/ppermute | solution.py:344
  25.7 6.6 %copy-start.7 = (bf16[448,384]{1,0:T(8,128)(2,1)}, bf16[448,384]{1,0:T(8,128)(2,1)S(1)}, u32[]{:S(2)}) copy-start(bf16[448,384]{1,0:T(8,128)(2,1)S(1)} %get-tuple-element.106.refs_7_) | copy-start | bytes 1032196
  25.7 6.6 %copy-start.18 = (bf16[448,128]{1,0:T(8,128)(2,1)}, bf16[448,128]{1,0:T(8,128)(2,1)S(1)}, u32[]{:S(2)}) copy-start(bf16[448,128]{1,0:T(8,128)(2,1)S(1)} %get-tuple-element.99.refs_0_) | copy-start | bytes 344068
  25.7 6.6 %copy-start.20 = (bf16[448,128]{1,0:T(8,128)(2,1)}, bf16[448,128]{1,0:T(8,128)(2,1)S(1)}, u32[]{:S(2)}) copy-start(bf16[448,128]{1,0:T(8,128)(2,1)S(1)} %get-tuple-element.101.refs_2_) | copy-start | bytes 344068
  25.7 6.6 %copy-start.22 = (bf16[448,128]{1,0:T(8,128)(2,1)}, bf16[448,128]{1,0:T(8,128)(2,1)S(1)}, u32[]{:S(2)}) copy-start(bf16[448,128]{1,0:T(8,128)(2,1)S(1)} %get-tuple-element.103.refs_4_) | copy-start | bytes 344068
  25.7 6.6 %copy-start.24 = (bf16[448,128]{1,0:T(8,128)(2,1)}, bf16[448,128]{1,0:T(8,128)(2,1)S(1)}, u32[]{:S(2)}) copy-start(bf16[448,128]{1,0:T(8,128)(2,1)S(1)} %get-tuple-element.104.refs_5_) | copy-start | bytes 344068
  25.7 6.6 %copy-start.26 = (bf16[448,128]{1,0:T(8,128)(2,1)}, bf16[448,128]{1,0:T(8,128)(2,1)S(1)}, u32[]{:S(2)}) copy-start(bf16[448,128]{1,0:T(8,128)(2,1)S(1)} %get-tuple-element.105.refs_6_) | copy-start | bytes 344068
  37.6 12.9 %collective-permute-start.4 = (bf16[4,128,128]{2,1,0:T(8,128)(2,1)}, bf16[4,128,128]{2,1,0:T(8,128)(2,1)}, u32[]{:S(2)}, u32[]{:S(2)}) collective-permute-start(bf16[4,128,128]{2,1,0:T(8,128)(2,1)} %get-tuple-element.98), channel_id=1, source_target_pairs={{0,8},{1,9},{2,10},{3,11},{4,12},{5,13},{6,14},{7,15},{8,16},{9,17... | collective-permute-start | bytes 393224 | tf_op jit(solution)/shard_map/ppermute | solution.py:344
  40.5 2.3 %copy-start.6 = (bf16[576,384]{1,0:T(8,128)(2,1)S(1)}, bf16[576,384]{1,0:T(8,128)(2,1)}, u32[]{:S(2)}) copy-start(bf16[576,384]{1,0:T(8,128)(2,1)} %copy-done.5) | copy-start | bytes 1327108
  40.5 2.3 %copy-start.8 = (bf16[448,384]{1,0:T(8,128)(2,1)S(1)}, bf16[448,384]{1,0:T(8,128)(2,1)}, u32[]{:S(2)}) copy-start(bf16[448,384]{1,0:T(8,128)(2,1)} %copy-done.7) | copy-start | bytes 1032196
  40.5 2.3 %copy-start.11 = (bf16[576,128]{1,0:T(8,128)(2,1)S(1)}, bf16[576,128]{1,0:T(8,128)(2,1)}, u32[]{:S(2)}) copy-start(bf16[576,128]{1,0:T(8,128)(2,1)} %copy-done.10) | copy-start | bytes 442372
  40.5 2.3 %copy-start.13 = (bf16[576,128]{1,0:T(8,128)(2,1)S(1)}, bf16[576,128]{1,0:T(8,128)(2,1)}, u32[]{:S(2)}) copy-start(bf16[576,128]{1,0:T(8,128)(2,1)} %copy-done.12) | copy-start | bytes 442372
  40.6 2.3 %copy-start.29 = (f32[64,256]{1,0:T(8,128)S(1)}, f32[64,256]{1,0:T(8,128)}, u32[]{:S(2)}) copy-start(f32[64,256]{1,0:T(8,128)} %copy-done.28) | copy-start | bytes 196612
  43.5 0.9 copy-start.15
  44.4 0.9 copy-start.17
  45.3 0.9 copy-start.19
  46.2 0.9 copy-start.21
  51.2 5.0 %copy-start.37 = (bf16[4,128,128]{2,1,0:T(8,128)(2,1)S(1)}, bf16[4,128,128]{2,1,0:T(8,128)(2,1)}, u32[]{:S(2)}) copy-start(bf16[4,128,128]{2,1,0:T(8,128)(2,1)} %copy-done.36) | copy-start | bytes 393220
  51.2 5.0 %collective-permute-start.5 = (bf16[8,8,128]{2,1,0:T(8,128)(2,1)S(1)}, bf16[8,8,128]{2,1,0:T(8,128)(2,1)S(1)}, u32[]{:S(2)}, u32[]{:S(2)}) collective-permute-start(bf16[8,8,128]{2,1,0:T(8,128)(2,1)S(1)} %pad_maximum_fusion.1), channel_id=1, source_target_pairs={{0,1},{1,2},{2,3},{3,4},{4,5},{5,6},{6,7},{7,0},{8,9},{9,10},{10,1... | collective-permute-start | bytes 49160 | tf_op jit(solution)/shard_map/ppermute | solution.py:344
  64.9 4.7 %collective-permute-start.6 = (bf16[1792,128]{1,0:T(8,128)(2,1)S(1)}, bf16[1792,128]{1,0:T(8,128)(2,1)S(1)}, u32[]{:S(2)}, u32[]{:S(2)}) collective-permute-start(bf16[1792,128]{1,0:T(8,128)(2,1)S(1)} %get-tuple-element.154), channel_id=1, source_target_pairs={{0,8},{8,0},{1,9},{9,1},{2,10},{10,2},{3,11},{11,3},{4,12},{12,4},... | collective-permute-start | bytes 1376264 | tf_op jit(solution)/shard_map/ppermute | solution.py:348
  107.4 6.0 %collective-permute-start.7 = (bf16[1792,128]{1,0:T(8,128)(2,1)S(1)}, bf16[1792,128]{1,0:T(8,128)(2,1)S(1)}, u32[]{:S(2)}, u32[]{:S(2)}) collective-permute-start(bf16[1792,128]{1,0:T(8,128)(2,1)S(1)} %bitcast.3), channel_id=1, source_target_pairs={{0,8},{8,0},{1,9},{9,1},{2,10},{10,2},{3,11},{11,3},{4,12},{12,4},... | collective-permute-start | bytes 1376264 | tf_op jit(solution)/shard_map/ppermute | solution.py:348
  (15 other events, 10.7 us)

commit v3 on v2

--- a/solution.py
+++ b/solution.py
@@ -107,19 +107,21 @@
     return m, s + m * (1.0 - s) * (2.0 * c + (6.0 * c * 0.044715) * sq)
 
 
-def forward(x, w_qkv, w_proj, g1, g2, bias_t, mask):
+def forward(x, w_qkv, w_proj, gains, bias, mask):
     hat1, inv1 = normalise(x)
-    a1 = (hat1 * g1).astype(BF16)
-    qkv = nn(a1, w_qkv).astype(BF16)
+    gain = gains()
+    a1 = (hat1 * gain[0:1]).astype(BF16)
+    qkv = nn(a1, w_qkv()).astype(BF16)
+    bias_t = turned_bias(bias())
     outs, weights = [], []
     for w in range(x.shape[0] // LEN):
         o, p = attention(qkv[w * LEN : (w + 1) * LEN], bias_t, mask)
         outs.append(o)
         weights.append(p)
     o = jnp.concatenate(outs, axis=0)
-    h = (x + nn(o, w_proj)).astype(BF16).astype(F32)
+    h = (x + nn(o, w_proj())).astype(BF16).astype(F32)
     hat2, inv2 = normalise(h)
-    a2 = (hat2 * g2).astype(BF16)
+    a2 = (hat2 * gain[1:2]).astype(BF16)
     return h, (hat1, inv1, a1, jnp.concatenate(weights, axis=0), o, hat2, inv2, a2), qkv
 
 
@@ -146,20 +148,23 @@
     return dx, (gy, m, a2, du, o, dhb, a1, dqkv), bias, gain1, gain2
 
 
-def pack(pack_ref, pairs, bias, gain1, gain2):
+def pack(pack_ref, pairs, bias, gain1, gain2, old=None):
     gy, m, a2, du, o, dhb, a1, dqkv = pairs
+
+    def put(at, value):
+        rows = slice(at, at + value.shape[0])
+        pack_ref[rows] = value if old is None else value + old[rows].astype(F32)
+
     down, up, qkv = tn(gy, m), tn(a2, du), tn(a1, dqkv)
     for j in range(3):
-        pack_ref[ROW_QKV + CH * j : ROW_QKV + CH * (j + 1)] = qkv[:, CH * j : CH * (j + 1)]
-    pack_ref[ROW_PROJ : ROW_PROJ + CH] = tn(o, dhb)
+        put(ROW_QKV + CH * j, qkv[:, CH * j : CH * (j + 1)])
+    put(ROW_PROJ, tn(o, dhb))
     for j in range(4):
-        pack_ref[ROW_UP + CH * j : ROW_UP + CH * (j + 1)] = up[:, CH * j : CH * (j + 1)]
-        pack_ref[ROW_DOWN + CH * j : ROW_DOWN + CH * (j + 1)] = down[:, CH * j : CH * (j + 1)].T
-    pack_ref[ROW_BIAS : ROW_BIAS + LEN] = bias[:, :CH]
-    pack_ref[ROW_BIAS + LEN : ROW_BIAS + 2 * LEN] = bias[:, CH:]
-    pack_ref[ROW_GAIN : ROW_GAIN + 1] = gain1
-    pack_ref[ROW_GAIN + 1 : ROW_GAIN + 2] = gain2
-    pack_ref[ROW_GAIN + 2 :] = jnp.zeros((ROWS - ROW_GAIN - 2, CH), F32)
+        put(ROW_UP + CH * j, up[:, CH * j : CH * (j + 1)])
+        put(ROW_DOWN + CH * j, down[:, CH * j : CH * (j + 1)].T)
+    put(ROW_BIAS, bias[:, :CH])
+    put(ROW_BIAS + LEN, bias[:, CH:])
+    put(ROW_GAIN, jnp.concatenate([gain1, gain2, jnp.zeros((ROWS - ROW_GAIN - 2, CH), F32)], axis=0))
 
 
 def to_windows(tile):
@@ -176,56 +181,76 @@
     return jnp.concatenate([bias[h].T for h in range(HEADS)], axis=1)
 
 
-def first_half(x, w_qkv, w_proj, w_up, w_down, gain_ref, bias, top_ref, low_ref):
-    h, kept, _ = forward(to_windows(x.astype(F32)), w_qkv, w_proj, gain_ref[0:1], gain_ref[1:2], turned_bias(bias), head_mask())
-    m, _ = gelu_and_slope(nn(kept[7], w_up))
-    tile = from_windows(h + nn(m.astype(BF16), w_down))
-    top_ref[...] = tile[:HALF].astype(BF16)
-    low_ref[...] = tile[HALF:].astype(BF16)
+def first_half(x, w_qkv, w_proj, w_up, w_down, gains, bias):
+    h, kept, _ = forward(to_windows(x.astype(F32)), w_qkv, w_proj, gains, bias, head_mask())
+    m, _ = gelu_and_slope(nn(kept[7], w_up()))
+    return from_windows(h + nn(m.astype(BF16), w_down()))
 
 
 def first_kernel(*refs):
-    (latent_hbm, bias_hbm), weights_hbm, refs = refs[:2], refs[2:7], refs[7:]
-    (top_ref, low_ref), refs = refs[:2], refs[2:]
-    (x_ref, bias_ref, sem), weight_refs = refs[:3], refs[3:]
-    w_qkv_ref, w_proj_ref, w_up_ref, w_down_ref, gain_ref = weight_refs
-    wide = latent_hbm.shape[1] // 2
-    moves = [(latent_hbm.at[:, 0:wide], x_ref), (bias_hbm.at[0], bias_ref)]
-    moves += [(source.at[0], target) for source, target in zip(weights_hbm, weight_refs)]
+    sources, (top_ref, low_ref, edge_ref), refs = refs[:8], refs[8:11], refs[11:]
+    targets, sem = refs[:8], refs[8]
+    wide = sources[0].shape[1] // 2
+    moves = [(sources[0].at[:, 0:wide], targets[0])]
+    moves += [(source.at[0], target) for source, target in zip(sources[1:7], targets[1:7])]
+    moves += [(sources[7].at[HALF:, 0:WIN], targets[7])]
     copies = [pltpu.make_async_copy(source, target, sem.at[i]) for i, (source, target) in enumerate(moves)]
     for copy in copies:
         copy.start()
-    for copy in copies:
-        copy.wait()
-    weights = (w_qkv_ref[...], w_proj_ref[...], w_up_ref[...], w_down_ref[...])
-    first_half(x_ref[...], *weights, gain_ref, bias_ref, top_ref, low_ref)
+
+    def fetched(i):
+        copies[i].wait()
+        return targets[i][...]
+
+    parts = [functools.partial(fetched, i) for i in range(1, 7)]
+    tile = first_half(fetched(0), *parts)
+    top_ref[...] = tile[:HALF].astype(BF16)
+    low_ref[...] = tile[HALF:].astype(BF16)
+    edge_ref[0:HALF] = tile[HALF:, 0:WIN].astype(BF16)
+    edge_ref[HALF:] = fetched(7)
+
+
+def at(ref, i):
+    return lambda: ref[i]
 
 
 def next_kernel(x_ref, w_qkv_ref, w_proj_ref, w_up_ref, w_down_ref, gain_ref, bias_ref, top_ref, low_ref):
     wide = x_ref.shape[1] // 2
-    weights = (w_qkv_ref[0], w_proj_ref[0], w_up_ref[0], w_down_ref[0])
-    first_half(x_ref[:, wide:], *weights, gain_ref.at[0], bias_ref.at[0], top_ref, low_ref)
-
-
-def keep_kernel(part, x_ref, w_qkv_ref, w_proj_ref, gain_ref, bias_ref, *kept_refs):
+    parts = [at(ref, 0) for ref in (w_qkv_ref, w_proj_ref, w_up_ref, w_down_ref, gain_ref, bias_ref)]
+    tile = first_half(x_ref[:, wide:], *parts)
+    top_ref[...] = tile[:HALF].astype(BF16)
+    low_ref[...] = tile[HALF:].astype(BF16)
+
+
+KEPT = (CH, CH, CH, HEADS * LEN, CH, CH, CH, CH)
+
+
+def kept_slices():
+    starts = [sum(KEPT[:i]) for i in range(len(KEPT))]
+    return [slice(start, start + width) for start, width in zip(starts, KEPT)]
+
+
+def keep_kernel(part, x_ref, w_qkv_ref, w_proj_ref, gain_ref, bias_ref, kept_ref):
     wide = x_ref.shape[1] // 2
     x = to_windows(x_ref[:, part * wide : (part + 1) * wide].astype(F32))
-    g1, g2 = gain_ref[0, 0:1], gain_ref[0, 1:2]
-    _, kept, _ = forward(x, w_qkv_ref[0], w_proj_ref[0], g1, g2, turned_bias(bias_ref[0]), head_mask())
-    for ref, value in zip(kept_refs, kept):
-        ref[...] = jnp.broadcast_to(value, ref.shape).astype(ref.dtype)
+    _, kept, _ = forward(x, at(w_qkv_ref, 0), at(w_proj_ref, 0), at(gain_ref, 0), at(bias_ref, 0), head_mask())
+    for place, value, width in zip(kept_slices(), kept, KEPT):
+        kept_ref[:, place] = jnp.broadcast_to(value, (x.shape[0], width)).astype(BF16)
 
 
 def second_half(x, gy, w_qkv_ref, w_proj_ref, w_up_ref, w_down_ref, gain_ref, bias_ref):
     mask = head_mask()
-    w_qkv, w_proj, w_up, g1, g2 = w_qkv_ref[1], w_proj_ref[1], w_up_ref[1], gain_ref[1, 0:1], gain_ref[1, 1:2]
-    _, kept, qkv = forward(to_windows(x), w_qkv, w_proj, g1, g2, turned_bias(bias_ref[1]), mask)
-    return backward(to_windows(gy).astype(BF16), kept, qkv, w_qkv, w_proj, w_up, w_down_ref[1], g1, g2, mask)
+    _, kept, qkv = forward(
+        to_windows(x), at(w_qkv_ref, 1), at(w_proj_ref, 1), at(gain_ref, 1), at(bias_ref, 1), mask
+    )
+    w_qkv, w_proj, w_up, w_down = w_qkv_ref[1], w_proj_ref[1], w_up_ref[1], w_down_ref[1]
+    g1, g2 = gain_ref[1, 0:1], gain_ref[1, 1:2]
+    return backward(to_windows(gy).astype(BF16), kept, qkv, w_qkv, w_proj, w_up, w_down, g1, g2, mask)
 
 
 def second_kernel(*refs):
     low_ref, below_ref, g_own_ref, g_below_ref = refs[:4]
-    weights, (dx_ref, *pair_refs), (bias_out_ref, gain_out_ref, frame_ref) = refs[4:10], refs[10:19], refs[19:]
+    weights, (dx_ref, pack_ref, frame_ref) = refs[4:10], refs[10:]
     wide = low_ref.shape[1]
     frame_ref[0:HALF, 0:wide] = low_ref[...].astype(F32)
     frame_ref[HALF:, 0:wide] = below_ref[...].astype(F32)
@@ -233,50 +258,38 @@
     frame_ref[0:HALF, 0:wide] = g_own_ref[HALF:, 0:wide].astype(F32)
     frame_ref[HALF:, 0:wide] = g_below_ref[0:HALF, 0:wide].astype(F32)
     gy = frame_ref[:, HALF : wide - HALF]
-    dx, pairs, bias, gain1, gain2 = second_half(x, gy, *weights)
-    dx_ref[...] = dx
-    for ref, value in zip(pair_refs, pairs):
-        ref[...] = value
-    bias_out_ref[...] = bias
-    gain_out_ref[0:1] = gain1
-    gain_out_ref[1:2] = gain2
+    dx, *sums = second_half(x, gy, *weights)
+    dx_ref[...] = dx.astype(BF16)
+    pack(pack_ref, *sums)
 
 
 def third_kernel(*refs):
     low_a_ref, low_b_ref, below_a_ref, below_b_ref, g_own_ref, g_below_ref, edge_ref = refs[:7]
-    weights, (dx_ref, bias_ref, gain_ref) = refs[7:13], refs[13:16]
-    (dtop_ref, dlow_ref), pair_refs, (bias_out_ref, gain_out_ref, frame_ref) = refs[16:18], refs[18:26], refs[26:]
+    weights, (dx_ref, old_ref, dtop_ref, dlow_ref, dedge_ref, pack_ref, frame_ref) = refs[7:13], refs[13:]
     wide, cols = low_a_ref.shape[1], g_own_ref.shape[1]
     span = cols - wide + WIN
     frame_ref[0:HALF, 0:WIN] = low_a_ref[:, wide - WIN :].astype(F32)
     frame_ref[HALF:, 0:WIN] = below_a_ref[:, wide - WIN :].astype(F32)
     frame_ref[0:HALF, WIN:span] = low_b_ref[...].astype(F32)
     frame_ref[HALF:, WIN:span] = below_b_ref[...].astype(F32)
-    frame_ref[:, span : span + WIN] = edge_ref[0:WIN].astype(F32)
+    frame_ref[0:HALF, span : span + WIN] = edge_ref[0:HALF].astype(F32)
+    frame_ref[HALF:, span : span + WIN] = edge_ref[WIN : WIN + HALF].astype(F32)
     x = frame_ref[:, HALF : span + HALF]
     frame_ref[0:HALF, 0:span] = g_own_ref[HALF:, wide - WIN :].astype(F32)
     frame_ref[HALF:, 0:span] = g_below_ref[0:HALF, wide - WIN :].astype(F32)
-    frame_ref[:, span : span + WIN] = edge_ref[WIN:].astype(F32)
+    frame_ref[0:HALF, span : span + WIN] = edge_ref[HALF:WIN].astype(F32)
+    frame_ref[HALF:, span : span + WIN] = edge_ref[WIN + HALF :].astype(F32)
     gy = frame_ref[:, HALF : span + HALF]
-    dx, pairs, bias, gain1, gain2 = second_half(x, gy, *weights)
-    for ref, value in zip(pair_refs, pairs):
-        ref[...] = value
-    bias_out_ref[...] = bias_ref[...] + bias
-    gain_out_ref[0:1] = gain_ref[0:1] + gain1
-    gain_out_ref[1:2] = gain_ref[1:2] + gain2
-    tile = from_windows(jnp.concatenate([dx_ref[...], dx], axis=0))
+    dx, *sums = second_half(x, gy, *weights)
+    pack(pack_ref, *sums, old_ref)
+    tile = from_windows(jnp.concatenate([dx_ref[...].astype(F32), dx], axis=0))
     dtop_ref[...] = tile[:HALF].astype(BF16)
     dlow_ref[...] = tile[HALF:].astype(BF16)
-
-
-def weights_kernel(*refs):
-    first, second, (bias_ref, gain_ref, pack_ref) = refs[:8], refs[8:16], refs[16:]
-    pairs = [jnp.concatenate([a[...], b[...]], axis=0) for a, b in zip(first, second)]
-    pack(pack_ref, pairs, bias_ref[...], gain_ref[0:1], gain_ref[1:2])
+    dedge_ref[...] = tile[:HALF, cols - WIN :].astype(BF16)
 
 
 def last_kernel(*refs):
-    (own, above, left), kept_refs, refs = refs[:3], refs[3:19], refs[19:]
+    (own, above, left), kept_refs, refs = refs[:3], refs[3:5], refs[5:]
     w_qkv_ref, w_proj_ref, w_up_ref, w_down_ref, gain_ref, other_ref, core_ref = refs[:7]
     dx_ref, keep_ref, send_ref, frame_ref, pack_ref = refs[7:]
     cols = own.shape[1]
@@ -286,7 +299,7 @@
     frame_ref[HALF:, HALF : HALF + cols] = own[...].astype(F32)
     frame_ref[0:HALF, HALF : HALF + cols] = above[...].astype(F32)
     gy = to_windows(frame_ref[:, 0:cols]).astype(BF16)
-    kept = [jnp.concatenate([a[...], b[...]], axis=0) for a, b in zip(kept_refs[:8], kept_refs[8:])]
+    kept = [jnp.concatenate([ref[:, place] for ref in kept_refs], axis=0) for place in kept_slices()]
     kept = [v.astype(F32) if i in (0, 1, 5, 6) else v for i, v in enumerate(kept)]
     g1, g2 = gain_ref[0, 0:1], gain_ref[0, 1:2]
     dx, pairs, bias, gain1, gain2 = backward(
@@ -376,30 +389,22 @@
     g_below = shift(cotangent, -1, 0)
     tokens = WIN * cols
 
-    def table(width, share=1):
-        return jax.ShapeDtypeStruct((tokens // share, width), BF16)
-
-    kept_shapes = [table(width, 2) for width in (CH, CH, CH, HEADS * LEN, CH, CH, CH, CH)]
-    pair_widths = (CH, FFN, CH, FFN, CH, CH, CH, 3 * CH)
     wide = cols // 2
-    part_a, part_b = WIN * (wide - WIN), WIN * (cols - wide + WIN)
-    small = [jax.ShapeDtypeStruct((LEN, HEADS * LEN), F32), jax.ShapeDtypeStruct((2, CH), F32)]
+    part_a = WIN * (wide - WIN)
     side = jax.ShapeDtypeStruct((HALF, wide, CH), BF16)
-    top_a, low_a = pl.pallas_call(
+    corner = jax.ShapeDtypeStruct((WIN, WIN, CH), BF16)
+    top_a, low_a, edge_own = pl.pallas_call(
         first_kernel,
-        out_shape=(side, side),
-        in_specs=[pl.BlockSpec(memory_space=pltpu.HBM)] * 7,
-        out_specs=vmem(2),
-        scratch_shapes=[
-            pltpu.VMEM((WIN, wide, CH), BF16),
-            pltpu.VMEM(attn_bias.shape[1:], F32),
-            pltpu.SemaphoreType.DMA((7,)),
-        ]
-        + [pltpu.VMEM(w.shape[1:], w.dtype) for w in weights],
+        out_shape=(side, side, corner),
+        in_specs=[pl.BlockSpec(memory_space=pltpu.HBM)] * 8,
+        out_specs=vmem(3),
+        scratch_shapes=[pltpu.VMEM((WIN, wide, CH), BF16)]
+        + [pltpu.VMEM(w.shape[1:], w.dtype) for w in (*weights, attn_bias)]
+        + [pltpu.VMEM((HALF, WIN, CH), BF16), pltpu.SemaphoreType.DMA((8,))],
         compiler_params=pltpu.CompilerParams(vmem_limit_bytes=FIRST_LIMIT),
         cost_estimate=cost(300_000_000, 1_500_000),
         name="forward_first",
-    )(latent, attn_bias, *weights)
+    )(latent, *weights, attn_bias, cotangent)
     below_a = shift(top_a, -1, 0)
     top_b, low_b = pl.pallas_call(
         next_kernel,
@@ -412,62 +417,48 @@
     )(latent, *weights, attn_bias)
     top_b, below_a, g_below = lax.optimization_barrier((top_b, below_a, g_below))
     below_b = shift(top_b, -1, 0)
-    rows = (low_a, below_a, cotangent[HALF:], g_below[:HALF])
-    edge = shift(jnp.concatenate([v[:, :WIN] for v in rows], axis=0), 0, -1)
+    edge = shift(jnp.concatenate([edge_own, below_a[:, :WIN], g_below[:HALF, :WIN]], axis=0), 0, -1)
     weights = (*weights, attn_bias)
     frame = pltpu.VMEM((WIN, cols + 2 * WIN, CH), F32)
-    dx_a, *pairs_a, bias_a, gain_a = pl.pallas_call(
+    dx_a, pack_a = pl.pallas_call(
         second_kernel,
-        out_shape=(
-            jax.ShapeDtypeStruct((part_a, CH), F32),
-            *[jax.ShapeDtypeStruct((part_a, width), BF16) for width in pair_widths],
-            *small,
-        ),
+        out_shape=(jax.ShapeDtypeStruct((part_a, CH), BF16), packed),
         in_specs=vmem(10),
-        out_specs=vmem(11),
+        out_specs=vmem(2),
         scratch_shapes=[frame],
         compiler_params=params,
         cost_estimate=cost(700_000_000, 3_000_000),
         name="backward_second",
     )(low_a, below_a, cotangent, g_below, *weights)
     edge, below_b, dx_a = lax.optimization_barrier((edge, below_b, dx_a))
-    d_top, d_low, *pairs_b, bias_b, gain_b = pl.pallas_call(
+    d_top, d_low, d_edge, pack_two = pl.pallas_call(
         third_kernel,
-        out_shape=(half, half, *[jax.ShapeDtypeStruct((part_b, width), BF16) for width in pair_widths], *small),
-        in_specs=vmem(16),
-        out_specs=vmem(12),
+        out_shape=(half, half, jax.ShapeDtypeStruct((HALF, WIN, CH), BF16), packed),
+        in_specs=vmem(15),
+        out_specs=vmem(4),
         scratch_shapes=[frame],
         compiler_params=params,
         cost_estimate=cost(800_000_000, 3_000_000),
         name="backward_third",
-    )(low_a, low_b, below_a, below_b, cotangent, g_below, edge, *weights, dx_a, bias_a, gain_a)
-    pack_two = pl.pallas_call(
-        weights_kernel,
-        out_shape=packed,
-        in_specs=vmem(18),
-        out_specs=vmem(1)[0],
-        compiler_params=params,
-        cost_estimate=cost(500_000_000, 5_000_000),
-        name="weights_second",
-    )(*pairs_a, *pairs_b, bias_b, gain_b)
+    )(low_a, low_b, below_a, below_b, cotangent, g_below, edge, *weights, dx_a, pack_a)
     d_above = shift(d_low, 1, 0)
     kept = []
     for part in range(2):
         made = pl.pallas_call(
             functools.partial(keep_kernel, part),
-            out_shape=kept_shapes,
+            out_shape=jax.ShapeDtypeStruct((WIN * wide, sum(KEPT)), BF16),
             in_specs=vmem(5),
-            out_specs=vmem(8),
+            out_specs=vmem(1)[0],
             compiler_params=params,
             cost_estimate=cost(300_000_000, 2_000_000),
             name="keep_first",
         )(latent, w_qkv, w_proj, gains, attn_bias)
         if part == 0:
-            d_above, pack_two, made = lax.optimization_barrier((d_above, pack_two, made))
-            d_left = shift(jnp.concatenate([v[:, cols - WIN :] for v in (d_above, d_top)], axis=0), 0, 1)
+            d_above, made = lax.optimization_barrier((d_above, made))
+            d_left = shift(jnp.concatenate([d_above[:, cols - WIN :], d_edge], axis=0), 0, 1)
         else:
             d_left, made = lax.optimization_barrier((d_left, made))
-        kept += made
+        kept.append(made)
     dx, keep, send = pl.pallas_call(
         last_kernel,
         out_shape=(
@@ -475,7 +466,7 @@
             packed,
             jax.ShapeDtypeStruct((ROWS, CH), BF16),
         ),
-        in_specs=vmem(25) + [pl.BlockSpec(memory_space=pltpu.SMEM)],
+        in_specs=vmem(11) + [pl.BlockSpec(memory_space=pltpu.SMEM)],
         out_specs=vmem(3),
         scratch_shapes=[frame, pltpu.VMEM((ROWS, CH), F32)],
         compiler_params=params,

time: 115 us -> 104 us (0.904)
  local copies, waits for them, and re-layouts: 16.2 us -> 0.15 us
  starting transfers between devices: 23.6 us -> 28.6 us
  waiting for transfers between devices: 5.7 us -> 8.92 us
  Pallas kernels: 30.5 us -> 29 us
  blocking collectives: 37.5 us -> 36 us
    unnamed x78 -> x20, local copies, waits for them, and re-layouts: 13.3 us -> 0.05 us
    ppermute x2, starting transfers between devices: 7.82 us -> 12.7 us  [swap_core(): return lax.ppermute(value, 'core', [(0, 1), (1, 0)])]
    ppermute x6, waiting for transfers between devices: 2.81 us -> 6.03 us  [shift(): return lax.ppermute(value, AXES, pairs)]
    slice x6 -> x3, local copies, waits for them, and re-layouts: 2.82 us -> 0.01 us  [the longest x1 0.01 us: body(): below_a[:, :WIN]]
    all_to_all x2, blocking collectives: 24.6 us -> 23.1 us  [collect(): return lax.all_to_all(spread, axis, 0, 0)]
    pallas_call x5 -> x4, Pallas kernels: 14.1 us -> 13.4 us  [the longest x1 6.17 us: body(): pl.pallas_call(third_kernel, out_shape=(half, half, jax.ShapeDtypeStruct(...]
  transfers between devices with their start and end apart: 8 -> 8, of which waited for: 3 -> 4; matrix products, arithmetic and copies ran while one was open for 2% -> 0% of each run, Pallas kernels for 12% -> 13%
where the time goes in v3:
time: 104 us
  blocking collectives  36 us (35%)
  Pallas kernels  29 us (28%)
  starting transfers between devices  28.6 us (28%)
  waiting for transfers between devices  8.92 us (9%)
    all_to_all x2, blocking collectives, collect(): return lax.all_to_all(spread, axis, 0, 0)  23.1 us
    ppermute x6, starting transfers between devices, shift(): return lax.ppermute(value, AXES, pairs)  15.9 us
    all_to_all x1, blocking collectives, scatter_sum(): return jnp.sum(lax.all_to_all(pieces, axis, 0, 0).astype(F32), axis=0)  12.9 us
    ppermute x2, starting transfers between devices, swap_core(): return lax.ppermute(value, 'core', [(0, 1), (1, 0)])  12.7 us
    pallas_call x1, Pallas kernels, body(): pl.pallas_call(last_kernel, out_shape=(jax.ShapeDtypeStruct(latent.shape,...  7.77 us
    pallas_call x1, Pallas kernels, body(): pl.pallas_call(third_kernel, out_shape=(half, half, jax.ShapeDtypeStruct(...  6.17 us
    ppermute x6, waiting for transfers between devices, shift(): return lax.ppermute(value, AXES, pairs)  6.03 us
    pallas_call x1, Pallas kernels, body(): pl.pallas_call(second_kernel, out_shape=(jax.ShapeDtypeStruct((part_a, CH...  4.57 us
  transfers between devices with their start and end apart: 8, of which 4 were waited for; matrix products, arithmetic and copies ran while one was open for 0% of the time, Pallas kernels for 13%

profile of v3, /device:TPU:1, one launch (start us, length us, event | category | flops | bytes accessed | tf_op | source)
XLA Modules:
  0.0 103.8 jit_solution(17010232351301838534)
XLA Ops:
  0.7 3.3 %collective-permute-start.1 = (bf16[8,128,128]{2,1,0:T(8,128)(2,1)}, bf16[8,128,128]{2,1,0:T(8,128)(2,1)S(1)}, u32[]{:S(2)}, u32[]{:S(2)}) collective-permute-start(bf16[8,128,128]{2,1,0:T(8,128)(2,1)} %refs_4_.5), channel_id=1, source_target_pairs={{0,248},{1,249},{2,250},{3,251},{4,252},{5,253},{6,254},{7,255},{8... | collective-permute-start | bytes 786440 | tf_op jit(solution)/shard_map/ppermute | solution.py:357
  4.0 4.2 %forward_first.1 = (bf16[4,64,128]{2,1,0:T(8,128)(2,1)}, bf16[4,64,128]{2,1,0:T(8,128)(2,1)}, bf16[8,8,128]{2,1,0:T(8,128)(2,1)}) custom-call(bf16[8,128,128]{2,1,0:T(8,128)(2,1)} %x_ref.5, bf16[2,128,384]{2,1,0:T(8,128)(2,1)} %refs_5_.5, bf16[2,128,128]{2,1,0:T(8,128)(2,1)} %refs_6_.5, bf16[2,128,512]{2,1,0:T(8,128)(2,1)} %refs_7_.7, ...), custom_call_target="tpu_custom_call" | custom-call | flops 300000000 | bytes 1500000 | tf_op jit(solution)/shard_map/forward_first/pallas_call | solution.py:396
  8.2 0.0 copy-start.9
  8.3 0.0 copy-start.8
  8.3 6.3 %collective-permute-start = (bf16[4,64,128]{2,1,0:T(8,128)(2,1)}, bf16[4,64,128]{2,1,0:T(8,128)(2,1)S(1)}, u32[]{:S(2)}, u32[]{:S(2)}) collective-permute-start(bf16[4,64,128]{2,1,0:T(8,128)(2,1)} %get-tuple-element.40), channel_id=1, source_target_pairs={{0,248},{1,249},{2,250},{3,251},{4,252},{5,253},{6,254},{7,255},{8... | collective-permute-start | bytes 196616 | tf_op jit(solution)/shard_map/ppermute | solution.py:357
  14.6 1.9 %forward_next.1 = (bf16[4,64,128]{2,1,0:T(8,128)(2,1)S(1)}, bf16[4,64,128]{2,1,0:T(8,128)(2,1)S(1)}) custom-call(bf16[8,128,128]{2,1,0:T(8,128)(2,1)S(1)} %copy-done, bf16[2,128,384]{2,1,0:T(8,128)(2,1)S(1)} %copy-done.2, bf16[2,128,128]{2,1,0:T(8,128)(2,1)S(1)} %copy-done.3, bf16[2,128,512]{2,1,0:T(8,128)(2,1)S(1)} %copy-done.4, ...), custom_call_target="tpu_custom_call" | custom-call | flops 300000000 | bytes 1500000 | tf_op jit(solution)/shard_map/forward_next/pallas_call | solution.py:409
  16.5 0.0 collective-permute-done.refs_1_.refs_2_
  16.5 0.0 collective-permute-done.1.refs_3_.refs_5_
  16.6 2.7 %collective-permute-start.2 = (bf16[16,8,128]{2,1,0:T(8,128)(2,1)S(1)}, bf16[16,8,128]{2,1,0:T(8,128)(2,1)S(1)}, u32[]{:S(2)}, u32[]{:S(2)}) collective-permute-start(bf16[16,8,128]{2,1,0:T(8,128)(2,1)S(1)} %pad_maximum_fusion), channel_id=1, source_target_pairs={{0,7},{1,0},{2,1},{3,2},{4,3},{5,4},{6,5},{7,6},{8,15},{9,8},{10,9... | collective-permute-start | bytes 98312 | tf_op jit(solution)/shard_map/ppermute | solution.py:357
  19.2 1.2 %collective-permute-start.3 = (bf16[4,64,128]{2,1,0:T(8,128)(2,1)S(1)}, bf16[4,64,128]{2,1,0:T(8,128)(2,1)S(1)}, u32[]{:S(2)}, u32[]{:S(2)}) collective-permute-start(bf16[4,64,128]{2,1,0:T(8,128)(2,1)S(1)} %get-tuple-element.44), channel_id=1, source_target_pairs={{0,248},{1,249},{2,250},{3,251},{4,252},{5,253},{6,254},{7,255},{8... | collective-permute-start | bytes 196616 | tf_op jit(solution)/shard_map/ppermute | solution.py:357
  20.4 4.6 %backward_second.1 = (bf16[448,128]{1,0:T(8,128)(2,1)S(1)}, f32[1792,128]{1,0:T(8,128)S(1)}) custom-call(bf16[4,64,128]{2,1,0:T(8,128)(2,1)S(1)} %copy-done.8, bf16[4,64,128]{2,1,0:T(8,128)(2,1)S(1)} %collective-permute-done.refs_1_.refs_2_, bf16[8,128,128]{2,1,0:T(8,128)(2,1)S(1)} %copy-done.6, ...), custom_call_target="tpu_custom_call" | custom-call | flops 700000000 | bytes 3000000 | tf_op jit(solution)/shard_map/backward_second/pallas_call | solution.py:423
  25.0 0.0 collective-permute-done.2.refs_6_
  25.0 0.0 collective-permute-done.3.refs_3_
  25.0 6.2 %backward_third.1 = (bf16[4,128,128]{2,1,0:T(8,128)(2,1)S(1)}, bf16[4,128,128]{2,1,0:T(8,128)(2,1)S(1)}, bf16[4,8,128]{2,1,0:T(8,128)(2,1)S(1)}, f32[1792,128]{1,0:T(8,128)S(1)}) custom-call(bf16[4,64,128]{2,1,0:T(8,128)(2,1)S(1)} %copy-done.8, bf16[4,64,128]{2,1,0:T(8,128)(2,1)S(1)} %get-tuple-element.38.refs_1_, ...), custom_call_target="tpu_custom_call" | custom-call | flops 800000000 | bytes 3000000 | tf_op jit(solution)/shard_map/backward_third/pallas_call | solution.py:434
  31.2 2.2 %collective-permute-start.4 = (bf16[4,128,128]{2,1,0:T(8,128)(2,1)S(1)}, bf16[4,128,128]{2,1,0:T(8,128)(2,1)S(1)}, u32[]{:S(2)}, u32[]{:S(2)}) collective-permute-start(bf16[4,128,128]{2,1,0:T(8,128)(2,1)S(1)} %get-tuple-element.51), channel_id=1, source_target_pairs={{0,8},{1,9},{2,10},{3,11},{4,12},{5,13},{6,14},{7,15},{8,16},{9,17... | collective-permute-start | bytes 393224 | tf_op jit(solution)/shard_map/ppermute | solution.py:357
  33.4 1.5 %keep_first.2.refs_3_ = bf16[512,1152]{1,0:T(8,128)(2,1)S(1)} custom-call(bf16[8,128,128]{2,1,0:T(8,128)(2,1)S(1)} %copy-done, bf16[2,128,384]{2,1,0:T(8,128)(2,1)S(1)} %copy-done.2, bf16[2,128,128]{2,1,0:T(8,128)(2,1)S(1)} %copy-done.3, f32[2,2,128]{2,1,0:T(2,128)S(1)} %copy-done.7, f32[2,4,64,64]{3,2,1,0:T(8,128)S(1)} %copy-done.1), custom_call_target="tpu_custom_call" | custom-call | flops 300000000 | bytes 2000000 | tf_op jit(solution)/shard_map/keep_first/pallas_call | solution.py:447
  34.9 2.9 %collective-permute-done.4.refs_1_ = bf16[4,128,128]{2,1,0:T(8,128)(2,1)S(1)} collective-permute-done((bf16[4,128,128]{2,1,0:T(8,128)(2,1)S(1)}, bf16[4,128,128]{2,1,0:T(8,128)(2,1)S(1)}, u32[]{:S(2)}, u32[]{:S(2)}) %collective-permute-start.4) | collective-permute-done | bytes 131104 | tf_op jit(solution)/shard_map/ppermute | solution.py:357
  37.8 0.3 collective-permute-start.5
  38.1 1.5 %keep_first.3.refs_4_ = bf16[512,1152]{1,0:T(8,128)(2,1)S(1)} custom-call(bf16[8,128,128]{2,1,0:T(8,128)(2,1)S(1)} %copy-done, bf16[2,128,384]{2,1,0:T(8,128)(2,1)S(1)} %copy-done.2, bf16[2,128,128]{2,1,0:T(8,128)(2,1)S(1)} %copy-done.3, f32[2,2,128]{2,1,0:T(2,128)S(1)} %copy-done.7, f32[2,4,64,64]{3,2,1,0:T(8,128)S(1)} %copy-done.1), custom_call_target="tpu_custom_call" | custom-call | flops 300000000 | bytes 2000000 | tf_op jit(solution)/shard_map/keep_first/pallas_call | solution.py:447
  39.6 3.2 %collective-permute-done.5.refs_2_ = bf16[8,8,128]{2,1,0:T(8,128)(2,1)S(1)} collective-permute-done((bf16[8,8,128]{2,1,0:T(8,128)(2,1)S(1)}, bf16[8,8,128]{2,1,0:T(8,128)(2,1)S(1)}, u32[]{:S(2)}, u32[]{:S(2)}) %collective-permute-start.5) | collective-permute-done | bytes 16416 | tf_op jit(solution)/shard_map/ppermute | solution.py:357
  42.7 7.8 %backward_first.1 = (bf16[8,128,128]{2,1,0:T(8,128)(2,1)}, f32[1792,128]{1,0:T(8,128)S(1)}, bf16[1792,128]{1,0:T(8,128)(2,1)S(1)}) custom-call(bf16[4,128,128]{2,1,0:T(8,128)(2,1)S(1)} %get-tuple-element.50.refs_0_, bf16[4,128,128]{2,1,0:T(8,128)(2,1)S(1)} %collective-permute-done.4.refs_1_, bf16[8,8,128]{2,1,0:T(8,128)(2,1)S(1)} %collective-permute-done.5.refs_2_, ...), custom_call_target="tpu_custom_call" | custom-call | flops 1500000000 | bytes 4000000 | tf_op jit(solution)/shard_map/backward_first/pallas_call | solution.py:462
  50.5 8.3 %collective-permute-start.6 = (bf16[1792,128]{1,0:T(8,128)(2,1)S(1)}, bf16[1792,128]{1,0:T(8,128)(2,1)S(1)}, u32[]{:S(2)}, u32[]{:S(2)}) collective-permute-start(bf16[1792,128]{1,0:T(8,128)(2,1)S(1)} %get-tuple-element.60), channel_id=1, source_target_pairs={{0,8},{8,0},{1,9},{9,1},{2,10},{10,2},{3,11},{11,3},{4,12},{12,4},... | collective-permute-start | bytes 1376264 | tf_op jit(solution)/shard_map/ppermute | solution.py:361
  58.8 1.4 %collective-permute-done.6 = bf16[1792,128]{1,0:T(8,128)(2,1)S(1)} collective-permute-done((bf16[1792,128]{1,0:T(8,128)(2,1)S(1)}, bf16[1792,128]{1,0:T(8,128)(2,1)S(1)}, u32[]{:S(2)}, u32[]{:S(2)}) %collective-permute-start.6) | collective-permute-done | bytes 458784 | tf_op jit(solution)/shard_map/ppermute | solution.py:361
  60.3 0.1 add_convert_fusion
  60.4 12.9 %all_to_all.15 = bf16[16,112,128]{2,1,0:T(8,128)(2,1)S(1)} all-to-all(bf16[16,112,128]{2,1,0:T(8,128)(2,1)S(1)} %bitcast.5), channel_id=1, replica_groups=mesh['z'=8,'yh'=2,'core'=2,'x'=4,'yl'=2] {'yh','x','yl'}, dimensions={0} | all-to-all | bytes 917504 | tf_op jit(solution)/shard_map/all_to_all | solution.py:366
  73.3 0.1 reduce_sum.24
  73.4 11.3 %all_to_all.16 = bf16[8,112,128]{2,1,0:T(8,128)(2,1)S(1)} all-to-all(bf16[8,112,128]{2,1,0:T(8,128)(2,1)S(1)} %broadcast_in_dim.4), channel_id=1, replica_groups=mesh['z'=8,'yh'=2,'core'=2,'x'=4,'yl'=2] {'z'}, dimensions={0} | all-to-all | bytes 458752 | tf_op jit(solution)/shard_map/all_to_all | solution.py:371
  84.7 0.1 broadcast_in_dim.5
  84.8 11.8 %all_to_all.17 = bf16[16,112,128]{2,1,0:T(8,128)(2,1)S(1)} all-to-all(bf16[16,112,128]{2,1,0:T(8,128)(2,1)S(1)} %broadcast_in_dim.5), channel_id=1, replica_groups=mesh['z'=8,'yh'=2,'core'=2,'x'=4,'yl'=2] {'yh','x','yl'}, dimensions={0} | all-to-all | bytes 917504 | tf_op jit(solution)/shard_map/all_to_all | solution.py:371
  96.5 4.4 %collective-permute-start.7 = (bf16[1792,128]{1,0:T(8,128)(2,1)S(1)}, bf16[1792,128]{1,0:T(8,128)(2,1)S(1)}, u32[]{:S(2)}, u32[]{:S(2)}) collective-permute-start(bf16[1792,128]{1,0:T(8,128)(2,1)S(1)} %bitcast.3), channel_id=1, source_target_pairs={{0,8},{8,0},{1,9},{9,1},{2,10},{10,2},{3,11},{11,3},{4,12},{12,4},... | collective-permute-start | bytes 1376264 | tf_op jit(solution)/shard_map/ppermute | solution.py:361
  101.0 1.4 %collective-permute-done.7.other_ref = bf16[1792,128]{1,0:T(8,128)(2,1)S(1)} collective-permute-done((bf16[1792,128]{1,0:T(8,128)(2,1)S(1)}, bf16[1792,128]{1,0:T(8,128)(2,1)S(1)}, u32[]{:S(2)}, u32[]{:S(2)}) %collective-permute-start.7) | collective-permute-done | bytes 458784 | tf_op jit(solution)/shard_map/ppermute | solution.py:361
  102.4 1.4 %unpack.1 = (f32[2,128,384]{2,1,0:T(8,128)}, f32[2,128,128]{2,1,0:T(8,128)}, f32[2,128,512]{2,1,0:T(8,128)}, f32[2,512,128]{2,1,0:T(8,128)}, f32[2,2,128]{2,1,0:T(2,128)}, /*index=5*/f32[2,4,64,64]{3,2,1,0:T(8,128)}) custom-call(s32[1]{0:T(128)} %bitcast.refs_11_.core_ref, bf16[1792,128]{1,0:T(8,128)(2,1)S(1)} %bitcast.4, ...), custom_call_target="tpu_custom_call" | custom-call | flops 1000000 | bytes 4000000 | tf_op jit(solution)/shard_map/unpack/pallas_call | solution.py:477
  (25 shorter events, 0.1 us)
Async XLA Ops:
  0.6 19.8 %copy-start.6 = (bf16[8,128,128]{2,1,0:T(8,128)(2,1)S(1)}, bf16[8,128,128]{2,1,0:T(8,128)(2,1)}, u32[]{:S(2)}) copy-start(bf16[8,128,128]{2,1,0:T(8,128)(2,1)} %refs_4_.5) | copy-start | bytes 786436
  0.6 13.9 %copy-start.7 = (f32[2,2,128]{2,1,0:T(2,128)S(1)}, f32[2,2,128]{2,1,0:T(2,128)}, u32[]{:S(2)}) copy-start(f32[2,2,128]{2,1,0:T(2,128)} %refs_9_.5) | copy-start | bytes 6148
  0.7 13.9 %copy-start.3 = (bf16[2,128,128]{2,1,0:T(8,128)(2,1)S(1)}, bf16[2,128,128]{2,1,0:T(8,128)(2,1)}, u32[]{:S(2)}) copy-start(bf16[2,128,128]{2,1,0:T(8,128)(2,1)} %refs_6_.5) | copy-start | bytes 196612
  0.7 13.9 %copy-start.2 = (bf16[2,128,384]{2,1,0:T(8,128)(2,1)S(1)}, bf16[2,128,384]{2,1,0:T(8,128)(2,1)}, u32[]{:S(2)}) copy-start(bf16[2,128,384]{2,1,0:T(8,128)(2,1)} %refs_5_.5) | copy-start | bytes 589828
  0.7 13.9 %copy-start.1 = (f32[2,4,64,64]{3,2,1,0:T(8,128)S(1)}, f32[2,4,64,64]{3,2,1,0:T(8,128)}, u32[]{:S(2)}) copy-start(f32[2,4,64,64]{3,2,1,0:T(8,128)} %bias_ref.5) | copy-start | bytes 393220
  0.7 13.9 %copy-start.5 = (bf16[2,512,128]{2,1,0:T(8,128)(2,1)S(1)}, bf16[2,512,128]{2,1,0:T(8,128)(2,1)}, u32[]{:S(2)}) copy-start(bf16[2,512,128]{2,1,0:T(8,128)(2,1)} %refs_8_.5) | copy-start | bytes 786436
  0.7 13.9 %copy-start.4 = (bf16[2,128,512]{2,1,0:T(8,128)(2,1)S(1)}, bf16[2,128,512]{2,1,0:T(8,128)(2,1)}, u32[]{:S(2)}) copy-start(bf16[2,128,512]{2,1,0:T(8,128)(2,1)} %refs_7_.7) | copy-start | bytes 786436
  0.7 13.9 %copy-start = (bf16[8,128,128]{2,1,0:T(8,128)(2,1)S(1)}, bf16[8,128,128]{2,1,0:T(8,128)(2,1)}, u32[]{:S(2)}) copy-start(bf16[8,128,128]{2,1,0:T(8,128)(2,1)} %x_ref.5) | copy-start | bytes 786436
  0.7 15.8 %collective-permute-start.1 = (bf16[8,128,128]{2,1,0:T(8,128)(2,1)}, bf16[8,128,128]{2,1,0:T(8,128)(2,1)S(1)}, u32[]{:S(2)}, u32[]{:S(2)}) collective-permute-start(bf16[8,128,128]{2,1,0:T(8,128)(2,1)} %refs_4_.5), channel_id=1, source_target_pairs={{0,248},{1,249},{2,250},{3,251},{4,252},{5,253},{6,254},{7,255},{8... | collective-permute-start | bytes 786440 | tf_op jit(solution)/shard_map/ppermute | solution.py:357
  8.2 8.3 %copy-start.9 = (bf16[8,8,128]{2,1,0:T(8,128)(2,1)S(1)}, bf16[8,8,128]{2,1,0:T(8,128)(2,1)}, u32[]{:S(2)}) copy-start(bf16[8,8,128]{2,1,0:T(8,128)(2,1)} %get-tuple-element.42) | copy-start | bytes 49156
  8.3 12.2 %copy-start.8 = (bf16[4,64,128]{2,1,0:T(8,128)(2,1)S(1)}, bf16[4,64,128]{2,1,0:T(8,128)(2,1)}, u32[]{:S(2)}) copy-start(bf16[4,64,128]{2,1,0:T(8,128)(2,1)} %get-tuple-element.37.refs_0_) | copy-start | bytes 196612
  8.3 8.2 %collective-permute-start = (bf16[4,64,128]{2,1,0:T(8,128)(2,1)}, bf16[4,64,128]{2,1,0:T(8,128)(2,1)S(1)}, u32[]{:S(2)}, u32[]{:S(2)}) collective-permute-start(bf16[4,64,128]{2,1,0:T(8,128)(2,1)} %get-tuple-element.40), channel_id=1, source_target_pairs={{0,248},{1,249},{2,250},{3,251},{4,252},{5,253},{6,254},{7,255},{8... | collective-permute-start | bytes 196616 | tf_op jit(solution)/shard_map/ppermute | solution.py:357
  16.6 8.4 %collective-permute-start.2 = (bf16[16,8,128]{2,1,0:T(8,128)(2,1)S(1)}, bf16[16,8,128]{2,1,0:T(8,128)(2,1)S(1)}, u32[]{:S(2)}, u32[]{:S(2)}) collective-permute-start(bf16[16,8,128]{2,1,0:T(8,128)(2,1)S(1)} %pad_maximum_fusion), channel_id=1, source_target_pairs={{0,7},{1,0},{2,1},{3,2},{4,3},{5,4},{6,5},{7,6},{8,15},{9,8},{10,9... | collective-permute-start | bytes 98312 | tf_op jit(solution)/shard_map/ppermute | solution.py:357
  19.2 5.8 %collective-permute-start.3 = (bf16[4,64,128]{2,1,0:T(8,128)(2,1)S(1)}, bf16[4,64,128]{2,1,0:T(8,128)(2,1)S(1)}, u32[]{:S(2)}, u32[]{:S(2)}) collective-permute-start(bf16[4,64,128]{2,1,0:T(8,128)(2,1)S(1)} %get-tuple-element.44), channel_id=1, source_target_pairs={{0,248},{1,249},{2,250},{3,251},{4,252},{5,253},{6,254},{7,255},{8... | collective-permute-start | bytes 196616 | tf_op jit(solution)/shard_map/ppermute | solution.py:357
  31.2 6.5 %collective-permute-start.4 = (bf16[4,128,128]{2,1,0:T(8,128)(2,1)S(1)}, bf16[4,128,128]{2,1,0:T(8,128)(2,1)S(1)}, u32[]{:S(2)}, u32[]{:S(2)}) collective-permute-start(bf16[4,128,128]{2,1,0:T(8,128)(2,1)S(1)} %get-tuple-element.51), channel_id=1, source_target_pairs={{0,8},{1,9},{2,10},{3,11},{4,12},{5,13},{6,14},{7,15},{8,16},{9,17... | collective-permute-start | bytes 393224 | tf_op jit(solution)/shard_map/ppermute | solution.py:357
  37.8 5.0 %collective-permute-start.5 = (bf16[8,8,128]{2,1,0:T(8,128)(2,1)S(1)}, bf16[8,8,128]{2,1,0:T(8,128)(2,1)S(1)}, u32[]{:S(2)}, u32[]{:S(2)}) collective-permute-start(bf16[8,8,128]{2,1,0:T(8,128)(2,1)S(1)} %pad_maximum_fusion.1), channel_id=1, source_target_pairs={{0,1},{1,2},{2,3},{3,4},{4,5},{5,6},{6,7},{7,0},{8,9},{9,10},{10,1... | collective-permute-start | bytes 49160 | tf_op jit(solution)/shard_map/ppermute | solution.py:357
  50.5 9.7 %collective-permute-start.6 = (bf16[1792,128]{1,0:T(8,128)(2,1)S(1)}, bf16[1792,128]{1,0:T(8,128)(2,1)S(1)}, u32[]{:S(2)}, u32[]{:S(2)}) collective-permute-start(bf16[1792,128]{1,0:T(8,128)(2,1)S(1)} %get-tuple-element.60), channel_id=1, source_target_pairs={{0,8},{8,0},{1,9},{9,1},{2,10},{10,2},{3,11},{11,3},{4,12},{12,4},... | collective-permute-start | bytes 1376264 | tf_op jit(solution)/shard_map/ppermute | solution.py:361
  96.5 5.9 %collective-permute-start.7 = (bf16[1792,128]{1,0:T(8,128)(2,1)S(1)}, bf16[1792,128]{1,0:T(8,128)(2,1)S(1)}, u32[]{:S(2)}, u32[]{:S(2)}) collective-permute-start(bf16[1792,128]{1,0:T(8,128)(2,1)S(1)} %bitcast.3), channel_id=1, source_target_pairs={{0,8},{8,0},{1,9},{9,1},{2,10},{10,2},{3,11},{11,3},{4,12},{12,4},... | collective-permute-start | bytes 1376264 | tf_op jit(solution)/shard_map/ppermute | solution.py:361

commit v4 on v3

--- a/solution.py
+++ b/solution.py
@@ -97,6 +97,13 @@
     dk = nn(dsb, spread_heads(q, mask)) * SCALE
     dq = gather_heads(tn(dsb, k)) * SCALE
     return jnp.concatenate([dq, dk, dv], axis=1).astype(BF16), ds
+
+
+CHUNK = 32
+
+
+def mlp_scratch(tokens):
+    return [pltpu.VMEM((tokens, FFN), kind) for kind in (F32, F32, BF16, BF16)]
 
 
 def gelu_and_slope(u):
@@ -125,11 +132,18 @@
     return h, (hat1, inv1, a1, jnp.concatenate(weights, axis=0), o, hat2, inv2, a2), qkv
 
 
-def backward(gy, kept, qkv, w_qkv, w_proj, w_up, w_down, g1, g2, mask):
+def backward(gy, kept, qkv, w_qkv, w_proj, w_up, w_down, g1, g2, mask, scratch):
     hat1, inv1, a1, p, o, hat2, inv2, a2 = kept
-    m, slope = gelu_and_slope(nn(a2, w_up))
-    m = m.astype(BF16)
-    du = (nt(gy, w_down) * slope).astype(BF16)
+    u_ref, dm_ref, m_ref, du_ref = scratch
+    tokens = gy.shape[0]
+    u_ref[0:tokens] = nn(a2, w_up)
+    dm_ref[0:tokens] = nt(gy, w_down)
+    for start in range(0, tokens, CHUNK):
+        rows = slice(start, start + CHUNK)
+        part, slope = gelu_and_slope(u_ref[rows])
+        m_ref[rows] = part.astype(BF16)
+        du_ref[rows] = (dm_ref[rows] * slope).astype(BF16)
+    m, du = m_ref[0:tokens], du_ref[0:tokens]
     da2 = nt(du, w_up)
     gain2 = jnp.sum(da2 * hat2, axis=0, keepdims=True)
     dh = gy.astype(F32) + normalise_back(da2, hat2, inv2, g2)
@@ -195,8 +209,8 @@
     moves += [(source.at[0], target) for source, target in zip(sources[1:7], targets[1:7])]
     moves += [(sources[7].at[HALF:, 0:WIN], targets[7])]
     copies = [pltpu.make_async_copy(source, target, sem.at[i]) for i, (source, target) in enumerate(moves)]
-    for copy in copies:
-        copy.start()
+    for i in (0, 5, 1, 6, 2, 3, 4, 7):
+        copies[i].start(priority=1)
 
     def fetched(i):
         copies[i].wait()
@@ -238,19 +252,19 @@
         kept_ref[:, place] = jnp.broadcast_to(value, (x.shape[0], width)).astype(BF16)
 
 
-def second_half(x, gy, w_qkv_ref, w_proj_ref, w_up_ref, w_down_ref, gain_ref, bias_ref):
+def second_half(x, gy, scratch, w_qkv_ref, w_proj_ref, w_up_ref, w_down_ref, gain_ref, bias_ref):
     mask = head_mask()
     _, kept, qkv = forward(
         to_windows(x), at(w_qkv_ref, 1), at(w_proj_ref, 1), at(gain_ref, 1), at(bias_ref, 1), mask
     )
     w_qkv, w_proj, w_up, w_down = w_qkv_ref[1], w_proj_ref[1], w_up_ref[1], w_down_ref[1]
     g1, g2 = gain_ref[1, 0:1], gain_ref[1, 1:2]
-    return backward(to_windows(gy).astype(BF16), kept, qkv, w_qkv, w_proj, w_up, w_down, g1, g2, mask)
+    return backward(to_windows(gy).astype(BF16), kept, qkv, w_qkv, w_proj, w_up, w_down, g1, g2, mask, scratch)
 
 
 def second_kernel(*refs):
     low_ref, below_ref, g_own_ref, g_below_ref = refs[:4]
-    weights, (dx_ref, pack_ref, frame_ref) = refs[4:10], refs[10:]
+    weights, (dx_ref, pack_ref, frame_ref, *scratch) = refs[4:10], refs[10:]
     wide = low_ref.shape[1]
     frame_ref[0:HALF, 0:wide] = low_ref[...].astype(F32)
     frame_ref[HALF:, 0:wide] = below_ref[...].astype(F32)
@@ -258,14 +272,14 @@
     frame_ref[0:HALF, 0:wide] = g_own_ref[HALF:, 0:wide].astype(F32)
     frame_ref[HALF:, 0:wide] = g_below_ref[0:HALF, 0:wide].astype(F32)
     gy = frame_ref[:, HALF : wide - HALF]
-    dx, *sums = second_half(x, gy, *weights)
+    dx, *sums = second_half(x, gy, scratch, *weights)
     dx_ref[...] = dx.astype(BF16)
     pack(pack_ref, *sums)
 
 
 def third_kernel(*refs):
     low_a_ref, low_b_ref, below_a_ref, below_b_ref, g_own_ref, g_below_ref, edge_ref = refs[:7]
-    weights, (dx_ref, old_ref, dtop_ref, dlow_ref, dedge_ref, pack_ref, frame_ref) = refs[7:13], refs[13:]
+    weights, (dx_ref, old_ref, dtop_ref, dlow_ref, dedge_ref, pack_ref, frame_ref, *scratch) = refs[7:13], refs[13:]
     wide, cols = low_a_ref.shape[1], g_own_ref.shape[1]
     span = cols - wide + WIN
     frame_ref[0:HALF, 0:WIN] = low_a_ref[:, wide - WIN :].astype(F32)
@@ -280,7 +294,7 @@
     frame_ref[0:HALF, span : span + WIN] = edge_ref[HALF:WIN].astype(F32)
     frame_ref[HALF:, span : span + WIN] = edge_ref[WIN + HALF :].astype(F32)
     gy = frame_ref[:, HALF : span + HALF]
-    dx, *sums = second_half(x, gy, *weights)
+    dx, *sums = second_half(x, gy, scratch, *weights)
     pack(pack_ref, *sums, old_ref)
     tile = from_windows(jnp.concatenate([dx_ref[...].astype(F32), dx], axis=0))
     dtop_ref[...] = tile[:HALF].astype(BF16)
@@ -291,7 +305,7 @@
 def last_kernel(*refs):
     (own, above, left), kept_refs, refs = refs[:3], refs[3:5], refs[5:]
     w_qkv_ref, w_proj_ref, w_up_ref, w_down_ref, gain_ref, other_ref, core_ref = refs[:7]
-    dx_ref, keep_ref, send_ref, frame_ref, pack_ref = refs[7:]
+    dx_ref, keep_ref, send_ref, frame_ref, pack_ref, *scratch = refs[7:]
     cols = own.shape[1]
     frame_ref[:, 0:WIN] = left[...].astype(F32)
     first = frame_ref[:, HALF:WIN]
@@ -303,7 +317,7 @@
     kept = [v.astype(F32) if i in (0, 1, 5, 6) else v for i, v in enumerate(kept)]
     g1, g2 = gain_ref[0, 0:1], gain_ref[0, 1:2]
     dx, pairs, bias, gain1, gain2 = backward(
-        gy, kept, nn(kept[2], w_qkv_ref[0]).astype(BF16), w_qkv_ref[0], w_proj_ref[0], w_up_ref[0], w_down_ref[0], g1, g2, head_mask()
+        gy, kept, nn(kept[2], w_qkv_ref[0]).astype(BF16), w_qkv_ref[0], w_proj_ref[0], w_up_ref[0], w_down_ref[0], g1, g2, head_mask(), scratch
     )
     dx_ref[...] = from_windows(dx).astype(BF16)
     pack(pack_ref, pairs, bias, gain1, gain2)
@@ -415,7 +429,6 @@
         cost_estimate=cost(300_000_000, 1_500_000),
         name="forward_next",
     )(latent, *weights, attn_bias)
-    top_b, below_a, g_below = lax.optimization_barrier((top_b, below_a, g_below))
     below_b = shift(top_b, -1, 0)
     edge = shift(jnp.concatenate([edge_own, below_a[:, :WIN], g_below[:HALF, :WIN]], axis=0), 0, -1)
     weights = (*weights, attn_bias)
@@ -425,7 +438,7 @@
         out_shape=(jax.ShapeDtypeStruct((part_a, CH), BF16), packed),
         in_specs=vmem(10),
         out_specs=vmem(2),
-        scratch_shapes=[frame],
+        scratch_shapes=[frame, *mlp_scratch(part_a)],
         compiler_params=params,
         cost_estimate=cost(700_000_000, 3_000_000),
         name="backward_second",
@@ -436,7 +449,7 @@
         out_shape=(half, half, jax.ShapeDtypeStruct((HALF, WIN, CH), BF16), packed),
         in_specs=vmem(15),
         out_specs=vmem(4),
-        scratch_shapes=[frame],
+        scratch_shapes=[frame, *mlp_scratch(WIN * cols - part_a)],
         compiler_params=params,
         cost_estimate=cost(800_000_000, 3_000_000),
         name="backward_third",
@@ -468,7 +481,7 @@
         ),
         in_specs=vmem(11) + [pl.BlockSpec(memory_space=pltpu.SMEM)],
         out_specs=vmem(3),
-        scratch_shapes=[frame, pltpu.VMEM((ROWS, CH), F32)],
+        scratch_shapes=[frame, pltpu.VMEM((ROWS, CH), F32), *mlp_scratch(WIN * cols)],
         compiler_params=params,
         cost_estimate=cost(1_500_000_000, 4_000_000),
         name="backward_first",

time: 104 us -> 99.1 us (0.953)
  starting transfers between devices: 28.6 us -> 26 us
  waiting for transfers between devices: 8.92 us -> 6.49 us
    ppermute x2, starting transfers between devices: 12.7 us -> 9.13 us  [swap_core(): return lax.ppermute(value, 'core', [(0, 1), (1, 0)])]
    ppermute x6, waiting for transfers between devices: 6.03 us -> 3.6 us  [shift(): return lax.ppermute(value, AXES, pairs)]
  transfers between devices with their start and end apart: 8 -> 8, of which waited for: 4 -> 4; matrix products, arithmetic and copies ran while one was open for 0% -> 0% of each run, Pallas kernels for 13% -> 14%
where the time goes in v4:
time: 99.1 us; the launch traced here: 98.9 us
  blocking collectives  36.1 us (36%)
  Pallas kernels  29.1 us (29%)
  starting transfers between devices  26 us (26%)
  waiting for transfers between devices  6.49 us (7%)
    all_to_all x2, blocking collectives, collect(): return lax.all_to_all(spread, axis, 0, 0)  23.2 us
    ppermute x6, starting transfers between devices, shift(): return lax.ppermute(value, AXES, pairs)  16.9 us
    all_to_all x1, blocking collectives, scatter_sum(): return jnp.sum(lax.all_to_all(pieces, axis, 0, 0).astype(F32), axis=0)  12.9 us
    ppermute x2, starting transfers between devices, swap_core(): return lax.ppermute(value, 'core', [(0, 1), (1, 0)])  9.13 us
    pallas_call x1, Pallas kernels, body(): pl.pallas_call(last_kernel, out_shape=(jax.ShapeDtypeStruct(latent.shape,...  7.76 us
    pallas_call x1, Pallas kernels, body(): pl.pallas_call(third_kernel, out_shape=(half, half, jax.ShapeDtypeStruct(...  6.18 us
    pallas_call x1, Pallas kernels, body(): pl.pallas_call(second_kernel, out_shape=(jax.ShapeDtypeStruct((part_a, CH...  4.58 us
    pallas_call x1, Pallas kernels, body(): pl.pallas_call(first_kernel, out_shape=(side, side, corner), in_specs=[pl...  4.2 us
  transfers between devices with their start and end apart: 8, of which 4 were waited for; matrix products, arithmetic and copies ran while one was open for 0% of the time, Pallas kernels for 14%

profile of v4, /device:TPU:1, one launch (start us, length us, event | category | flops | bytes accessed | tf_op | source)
XLA Modules:
  0.0 98.9 jit_solution(1554643349117387668)
XLA Ops:
  0.7 3.3 %collective-permute-start.1 = (bf16[8,128,128]{2,1,0:T(8,128)(2,1)}, bf16[8,128,128]{2,1,0:T(8,128)(2,1)S(1)}, u32[]{:S(2)}, u32[]{:S(2)}) collective-permute-start(bf16[8,128,128]{2,1,0:T(8,128)(2,1)} %refs_4_.5), channel_id=1, source_target_pairs={{0,248},{1,249},{2,250},{3,251},{4,252},{5,253},{6,254},{7,255},{8... | collective-permute-start | bytes 786440 | tf_op jit(solution)/shard_map/ppermute | solution.py:371
  4.0 4.2 %forward_first.1 = (bf16[4,64,128]{2,1,0:T(8,128)(2,1)}, bf16[4,64,128]{2,1,0:T(8,128)(2,1)}, bf16[8,8,128]{2,1,0:T(8,128)(2,1)}) custom-call(bf16[8,128,128]{2,1,0:T(8,128)(2,1)} %x_ref.5, bf16[2,128,384]{2,1,0:T(8,128)(2,1)} %refs_5_.5, bf16[2,128,128]{2,1,0:T(8,128)(2,1)} %refs_6_.5, bf16[2,128,512]{2,1,0:T(8,128)(2,1)} %refs_7_.7, ...), custom_call_target="tpu_custom_call" | custom-call | flops 300000000 | bytes 1500000 | tf_op jit(solution)/shard_map/forward_first/pallas_call | solution.py:410
  8.2 0.0 copy-start.9
  8.3 0.0 copy-start.8
  8.3 6.3 %collective-permute-start = (bf16[4,64,128]{2,1,0:T(8,128)(2,1)}, bf16[4,64,128]{2,1,0:T(8,128)(2,1)S(1)}, u32[]{:S(2)}, u32[]{:S(2)}) collective-permute-start(bf16[4,64,128]{2,1,0:T(8,128)(2,1)} %get-tuple-element.36), channel_id=1, source_target_pairs={{0,248},{1,249},{2,250},{3,251},{4,252},{5,253},{6,254},{7,255},{8... | collective-permute-start | bytes 196616 | tf_op jit(solution)/shard_map/ppermute | solution.py:371
  14.6 1.9 %forward_next.1 = (bf16[4,64,128]{2,1,0:T(8,128)(2,1)S(1)}, bf16[4,64,128]{2,1,0:T(8,128)(2,1)S(1)}) custom-call(bf16[8,128,128]{2,1,0:T(8,128)(2,1)S(1)} %copy-done, bf16[2,128,384]{2,1,0:T(8,128)(2,1)S(1)} %copy-done.2, bf16[2,128,128]{2,1,0:T(8,128)(2,1)S(1)} %copy-done.3, bf16[2,128,512]{2,1,0:T(8,128)(2,1)S(1)} %copy-done.4, ...), custom_call_target="tpu_custom_call" | custom-call | flops 300000000 | bytes 1500000 | tf_op jit(solution)/shard_map/forward_next/pallas_call | solution.py:423
  16.5 0.8 collective-permute-start.3
  17.3 0.0 collective-permute-done.refs_1_.refs_2_
  17.3 0.0 collective-permute-done.1.refs_3_.refs_5_
  17.3 2.9 %collective-permute-start.2 = (bf16[16,8,128]{2,1,0:T(8,128)(2,1)S(1)}, bf16[16,8,128]{2,1,0:T(8,128)(2,1)S(1)}, u32[]{:S(2)}, u32[]{:S(2)}) collective-permute-start(bf16[16,8,128]{2,1,0:T(8,128)(2,1)S(1)} %pad_maximum_fusion), channel_id=1, source_target_pairs={{0,7},{1,0},{2,1},{3,2},{4,3},{5,4},{6,5},{7,6},{8,15},{9,8},{10,9... | collective-permute-start | bytes 98312 | tf_op jit(solution)/shard_map/ppermute | solution.py:371
  20.2 4.6 %backward_second.1 = (bf16[448,128]{1,0:T(8,128)(2,1)S(1)}, f32[1792,128]{1,0:T(8,128)S(1)}) custom-call(bf16[4,64,128]{2,1,0:T(8,128)(2,1)S(1)} %copy-done.8, bf16[4,64,128]{2,1,0:T(8,128)(2,1)S(1)} %collective-permute-done.refs_1_.refs_2_, bf16[8,128,128]{2,1,0:T(8,128)(2,1)S(1)} %copy-done.6, ...), custom_call_target="tpu_custom_call" | custom-call | flops 700000000 | bytes 3000000 | tf_op jit(solution)/shard_map/backward_second/pallas_call | solution.py:436
  24.7 0.0 collective-permute-done.3.refs_3_
  24.7 0.0 collective-permute-done.2.refs_6_
  24.8 6.2 %backward_third.1 = (bf16[4,128,128]{2,1,0:T(8,128)(2,1)S(1)}, bf16[4,128,128]{2,1,0:T(8,128)(2,1)S(1)}, bf16[4,8,128]{2,1,0:T(8,128)(2,1)S(1)}, f32[1792,128]{1,0:T(8,128)S(1)}) custom-call(bf16[4,64,128]{2,1,0:T(8,128)(2,1)S(1)} %copy-done.8, bf16[4,64,128]{2,1,0:T(8,128)(2,1)S(1)} %get-tuple-element.35.refs_1_, ...), custom_call_target="tpu_custom_call" | custom-call | flops 800000000 | bytes 3000000 | tf_op jit(solution)/shard_map/backward_third/pallas_call | solution.py:447
  30.9 3.5 %collective-permute-start.4 = (bf16[4,128,128]{2,1,0:T(8,128)(2,1)S(1)}, bf16[4,128,128]{2,1,0:T(8,128)(2,1)S(1)}, u32[]{:S(2)}, u32[]{:S(2)}) collective-permute-start(bf16[4,128,128]{2,1,0:T(8,128)(2,1)S(1)} %get-tuple-element.45), channel_id=1, source_target_pairs={{0,8},{1,9},{2,10},{3,11},{4,12},{5,13},{6,14},{7,15},{8,16},{9,17... | collective-permute-start | bytes 393224 | tf_op jit(solution)/shard_map/ppermute | solution.py:371
  34.5 1.5 %keep_first.2.refs_3_ = bf16[512,1152]{1,0:T(8,128)(2,1)S(1)} custom-call(bf16[8,128,128]{2,1,0:T(8,128)(2,1)S(1)} %copy-done, bf16[2,128,384]{2,1,0:T(8,128)(2,1)S(1)} %copy-done.2, bf16[2,128,128]{2,1,0:T(8,128)(2,1)S(1)} %copy-done.3, f32[2,2,128]{2,1,0:T(2,128)S(1)} %copy-done.7, f32[2,4,64,64]{3,2,1,0:T(8,128)S(1)} %copy-done.1), custom_call_target="tpu_custom_call" | custom-call | flops 300000000 | bytes 2000000 | tf_op jit(solution)/shard_map/keep_first/pallas_call | solution.py:460
  36.0 0.4 collective-permute-done.4.refs_1_
  36.4 0.2 collective-permute-start.5
  36.6 1.5 %keep_first.3.refs_4_ = bf16[512,1152]{1,0:T(8,128)(2,1)S(1)} custom-call(bf16[8,128,128]{2,1,0:T(8,128)(2,1)S(1)} %copy-done, bf16[2,128,384]{2,1,0:T(8,128)(2,1)S(1)} %copy-done.2, bf16[2,128,128]{2,1,0:T(8,128)(2,1)S(1)} %copy-done.3, f32[2,2,128]{2,1,0:T(2,128)S(1)} %copy-done.7, f32[2,4,64,64]{3,2,1,0:T(8,128)S(1)} %copy-done.1), custom_call_target="tpu_custom_call" | custom-call | flops 300000000 | bytes 2000000 | tf_op jit(solution)/shard_map/keep_first/pallas_call | solution.py:460
  38.2 3.2 %collective-permute-done.5.refs_2_ = bf16[8,8,128]{2,1,0:T(8,128)(2,1)S(1)} collective-permute-done((bf16[8,8,128]{2,1,0:T(8,128)(2,1)S(1)}, bf16[8,8,128]{2,1,0:T(8,128)(2,1)S(1)}, u32[]{:S(2)}, u32[]{:S(2)}) %collective-permute-start.5) | collective-permute-done | bytes 16416 | tf_op jit(solution)/shard_map/ppermute | solution.py:371
  41.3 7.8 %backward_first.1 = (bf16[8,128,128]{2,1,0:T(8,128)(2,1)}, f32[1792,128]{1,0:T(8,128)S(1)}, bf16[1792,128]{1,0:T(8,128)(2,1)S(1)}) custom-call(bf16[4,128,128]{2,1,0:T(8,128)(2,1)S(1)} %get-tuple-element.44.refs_0_, bf16[4,128,128]{2,1,0:T(8,128)(2,1)S(1)} %collective-permute-done.4.refs_1_, bf16[8,8,128]{2,1,0:T(8,128)(2,1)S(1)} %collective-permute-done.5.refs_2_, ...), custom_call_target="tpu_custom_call" | custom-call | flops 1500000000 | bytes 4000000 | tf_op jit(solution)/shard_map/backward_first/pallas_call | solution.py:475
  49.1 4.8 %collective-permute-start.6 = (bf16[1792,128]{1,0:T(8,128)(2,1)S(1)}, bf16[1792,128]{1,0:T(8,128)(2,1)S(1)}, u32[]{:S(2)}, u32[]{:S(2)}) collective-permute-start(bf16[1792,128]{1,0:T(8,128)(2,1)S(1)} %get-tuple-element.54), channel_id=1, source_target_pairs={{0,8},{8,0},{1,9},{9,1},{2,10},{10,2},{3,11},{11,3},{4,12},{12,4},... | collective-permute-start | bytes 1376264 | tf_op jit(solution)/shard_map/ppermute | solution.py:375
  53.9 1.4 %collective-permute-done.6 = bf16[1792,128]{1,0:T(8,128)(2,1)S(1)} collective-permute-done((bf16[1792,128]{1,0:T(8,128)(2,1)S(1)}, bf16[1792,128]{1,0:T(8,128)(2,1)S(1)}, u32[]{:S(2)}, u32[]{:S(2)}) %collective-permute-start.6) | collective-permute-done | bytes 458784 | tf_op jit(solution)/shard_map/ppermute | solution.py:375
  55.4 0.1 add_convert_fusion
  55.5 12.9 %all_to_all.15 = bf16[16,112,128]{2,1,0:T(8,128)(2,1)S(1)} all-to-all(bf16[16,112,128]{2,1,0:T(8,128)(2,1)S(1)} %bitcast.5), channel_id=1, replica_groups=mesh['z'=8,'yh'=2,'core'=2,'x'=4,'yl'=2] {'yh','x','yl'}, dimensions={0} | all-to-all | bytes 917504 | tf_op jit(solution)/shard_map/all_to_all | solution.py:380
  68.4 0.1 reduce_sum.24
  68.5 11.6 %all_to_all.16 = bf16[8,112,128]{2,1,0:T(8,128)(2,1)S(1)} all-to-all(bf16[8,112,128]{2,1,0:T(8,128)(2,1)S(1)} %broadcast_in_dim.4), channel_id=1, replica_groups=mesh['z'=8,'yh'=2,'core'=2,'x'=4,'yl'=2] {'z'}, dimensions={0} | all-to-all | bytes 458752 | tf_op jit(solution)/shard_map/all_to_all | solution.py:385
  80.1 0.1 broadcast_in_dim.5
  80.1 11.6 %all_to_all.17 = bf16[16,112,128]{2,1,0:T(8,128)(2,1)S(1)} all-to-all(bf16[16,112,128]{2,1,0:T(8,128)(2,1)S(1)} %broadcast_in_dim.5), channel_id=1, replica_groups=mesh['z'=8,'yh'=2,'core'=2,'x'=4,'yl'=2] {'yh','x','yl'}, dimensions={0} | all-to-all | bytes 917504 | tf_op jit(solution)/shard_map/all_to_all | solution.py:385
  91.8 4.3 %collective-permute-start.7 = (bf16[1792,128]{1,0:T(8,128)(2,1)S(1)}, bf16[1792,128]{1,0:T(8,128)(2,1)S(1)}, u32[]{:S(2)}, u32[]{:S(2)}) collective-permute-start(bf16[1792,128]{1,0:T(8,128)(2,1)S(1)} %bitcast.3), channel_id=1, source_target_pairs={{0,8},{8,0},{1,9},{9,1},{2,10},{10,2},{3,11},{11,3},{4,12},{12,4},... | collective-permute-start | bytes 1376264 | tf_op jit(solution)/shard_map/ppermute | solution.py:375
  96.1 1.4 %collective-permute-done.7.other_ref = bf16[1792,128]{1,0:T(8,128)(2,1)S(1)} collective-permute-done((bf16[1792,128]{1,0:T(8,128)(2,1)S(1)}, bf16[1792,128]{1,0:T(8,128)(2,1)S(1)}, u32[]{:S(2)}, u32[]{:S(2)}) %collective-permute-start.7) | collective-permute-done | bytes 458784 | tf_op jit(solution)/shard_map/ppermute | solution.py:375
  97.5 1.4 %unpack.1 = (f32[2,128,384]{2,1,0:T(8,128)}, f32[2,128,128]{2,1,0:T(8,128)}, f32[2,128,512]{2,1,0:T(8,128)}, f32[2,512,128]{2,1,0:T(8,128)}, f32[2,2,128]{2,1,0:T(2,128)}, /*index=5*/f32[2,4,64,64]{3,2,1,0:T(8,128)}) custom-call(s32[1]{0:T(128)} %bitcast.refs_11_.core_ref, bf16[1792,128]{1,0:T(8,128)(2,1)S(1)} %bitcast.4, ...), custom_call_target="tpu_custom_call" | custom-call | flops 1000000 | bytes 4000000 | tf_op jit(solution)/shard_map/unpack/pallas_call | solution.py:490
  (25 shorter events, 0.1 us)
Async XLA Ops:
  0.6 19.5 %copy-start.6 = (bf16[8,128,128]{2,1,0:T(8,128)(2,1)S(1)}, bf16[8,128,128]{2,1,0:T(8,128)(2,1)}, u32[]{:S(2)}) copy-start(bf16[8,128,128]{2,1,0:T(8,128)(2,1)} %refs_4_.5) | copy-start | bytes 786436
  0.6 13.9 %copy-start.7 = (f32[2,2,128]{2,1,0:T(2,128)S(1)}, f32[2,2,128]{2,1,0:T(2,128)}, u32[]{:S(2)}) copy-start(f32[2,2,128]{2,1,0:T(2,128)} %refs_9_.5) | copy-start | bytes 6148
  0.7 13.9 %copy-start.3 = (bf16[2,128,128]{2,1,0:T(8,128)(2,1)S(1)}, bf16[2,128,128]{2,1,0:T(8,128)(2,1)}, u32[]{:S(2)}) copy-start(bf16[2,128,128]{2,1,0:T(8,128)(2,1)} %refs_6_.5) | copy-start | bytes 196612
  0.7 13.9 %copy-start.2 = (bf16[2,128,384]{2,1,0:T(8,128)(2,1)S(1)}, bf16[2,128,384]{2,1,0:T(8,128)(2,1)}, u32[]{:S(2)}) copy-start(bf16[2,128,384]{2,1,0:T(8,128)(2,1)} %refs_5_.5) | copy-start | bytes 589828
  0.7 13.9 %copy-start.1 = (f32[2,4,64,64]{3,2,1,0:T(8,128)S(1)}, f32[2,4,64,64]{3,2,1,0:T(8,128)}, u32[]{:S(2)}) copy-start(f32[2,4,64,64]{3,2,1,0:T(8,128)} %bias_ref.5) | copy-start | bytes 393220
  0.7 13.9 %copy-start.5 = (bf16[2,512,128]{2,1,0:T(8,128)(2,1)S(1)}, bf16[2,512,128]{2,1,0:T(8,128)(2,1)}, u32[]{:S(2)}) copy-start(bf16[2,512,128]{2,1,0:T(8,128)(2,1)} %refs_8_.5) | copy-start | bytes 786436
  0.7 13.9 %copy-start.4 = (bf16[2,128,512]{2,1,0:T(8,128)(2,1)S(1)}, bf16[2,128,512]{2,1,0:T(8,128)(2,1)}, u32[]{:S(2)}) copy-start(bf16[2,128,512]{2,1,0:T(8,128)(2,1)} %refs_7_.7) | copy-start | bytes 786436
  0.7 13.9 %copy-start = (bf16[8,128,128]{2,1,0:T(8,128)(2,1)S(1)}, bf16[8,128,128]{2,1,0:T(8,128)(2,1)}, u32[]{:S(2)}) copy-start(bf16[8,128,128]{2,1,0:T(8,128)(2,1)} %x_ref.5) | copy-start | bytes 786436
  0.7 16.5 %collective-permute-start.1 = (bf16[8,128,128]{2,1,0:T(8,128)(2,1)}, bf16[8,128,128]{2,1,0:T(8,128)(2,1)S(1)}, u32[]{:S(2)}, u32[]{:S(2)}) collective-permute-start(bf16[8,128,128]{2,1,0:T(8,128)(2,1)} %refs_4_.5), channel_id=1, source_target_pairs={{0,248},{1,249},{2,250},{3,251},{4,252},{5,253},{6,254},{7,255},{8... | collective-permute-start | bytes 786440 | tf_op jit(solution)/shard_map/ppermute | solution.py:371
  8.2 9.0 %copy-start.9 = (bf16[8,8,128]{2,1,0:T(8,128)(2,1)S(1)}, bf16[8,8,128]{2,1,0:T(8,128)(2,1)}, u32[]{:S(2)}) copy-start(bf16[8,8,128]{2,1,0:T(8,128)(2,1)} %get-tuple-element.37) | copy-start | bytes 49156
  8.3 11.9 %copy-start.8 = (bf16[4,64,128]{2,1,0:T(8,128)(2,1)S(1)}, bf16[4,64,128]{2,1,0:T(8,128)(2,1)}, u32[]{:S(2)}) copy-start(bf16[4,64,128]{2,1,0:T(8,128)(2,1)} %get-tuple-element.34.refs_0_) | copy-start | bytes 196612
  8.3 9.0 %collective-permute-start = (bf16[4,64,128]{2,1,0:T(8,128)(2,1)}, bf16[4,64,128]{2,1,0:T(8,128)(2,1)S(1)}, u32[]{:S(2)}, u32[]{:S(2)}) collective-permute-start(bf16[4,64,128]{2,1,0:T(8,128)(2,1)} %get-tuple-element.36), channel_id=1, source_target_pairs={{0,248},{1,249},{2,250},{3,251},{4,252},{5,253},{6,254},{7,255},{8... | collective-permute-start | bytes 196616 | tf_op jit(solution)/shard_map/ppermute | solution.py:371
  16.5 8.2 %collective-permute-start.3 = (bf16[4,64,128]{2,1,0:T(8,128)(2,1)S(1)}, bf16[4,64,128]{2,1,0:T(8,128)(2,1)S(1)}, u32[]{:S(2)}, u32[]{:S(2)}) collective-permute-start(bf16[4,64,128]{2,1,0:T(8,128)(2,1)S(1)} %get-tuple-element.38), channel_id=1, source_target_pairs={{0,248},{1,249},{2,250},{3,251},{4,252},{5,253},{6,254},{7,255},{8... | collective-permute-start | bytes 196616 | tf_op jit(solution)/shard_map/ppermute | solution.py:371
  17.3 7.4 %collective-permute-start.2 = (bf16[16,8,128]{2,1,0:T(8,128)(2,1)S(1)}, bf16[16,8,128]{2,1,0:T(8,128)(2,1)S(1)}, u32[]{:S(2)}, u32[]{:S(2)}) collective-permute-start(bf16[16,8,128]{2,1,0:T(8,128)(2,1)S(1)} %pad_maximum_fusion), channel_id=1, source_target_pairs={{0,7},{1,0},{2,1},{3,2},{4,3},{5,4},{6,5},{7,6},{8,15},{9,8},{10,9... | collective-permute-start | bytes 98312 | tf_op jit(solution)/shard_map/ppermute | solution.py:371
  30.9 5.5 %collective-permute-start.4 = (bf16[4,128,128]{2,1,0:T(8,128)(2,1)S(1)}, bf16[4,128,128]{2,1,0:T(8,128)(2,1)S(1)}, u32[]{:S(2)}, u32[]{:S(2)}) collective-permute-start(bf16[4,128,128]{2,1,0:T(8,128)(2,1)S(1)} %get-tuple-element.45), channel_id=1, source_target_pairs={{0,8},{1,9},{2,10},{3,11},{4,12},{5,13},{6,14},{7,15},{8,16},{9,17... | collective-permute-start | bytes 393224 | tf_op jit(solution)/shard_map/ppermute | solution.py:371
  36.4 4.9 %collective-permute-start.5 = (bf16[8,8,128]{2,1,0:T(8,128)(2,1)S(1)}, bf16[8,8,128]{2,1,0:T(8,128)(2,1)S(1)}, u32[]{:S(2)}, u32[]{:S(2)}) collective-permute-start(bf16[8,8,128]{2,1,0:T(8,128)(2,1)S(1)} %pad_maximum_fusion.1), channel_id=1, source_target_pairs={{0,1},{1,2},{2,3},{3,4},{4,5},{5,6},{6,7},{7,0},{8,9},{9,10},{10,1... | collective-permute-start | bytes 49160 | tf_op jit(solution)/shard_map/ppermute | solution.py:371
  49.1 6.3 %collective-permute-start.6 = (bf16[1792,128]{1,0:T(8,128)(2,1)S(1)}, bf16[1792,128]{1,0:T(8,128)(2,1)S(1)}, u32[]{:S(2)}, u32[]{:S(2)}) collective-permute-start(bf16[1792,128]{1,0:T(8,128)(2,1)S(1)} %get-tuple-element.54), channel_id=1, source_target_pairs={{0,8},{8,0},{1,9},{9,1},{2,10},{10,2},{3,11},{11,3},{4,12},{12,4},... | collective-permute-start | bytes 1376264 | tf_op jit(solution)/shard_map/ppermute | solution.py:375
  91.8 5.8 %collective-permute-start.7 = (bf16[1792,128]{1,0:T(8,128)(2,1)S(1)}, bf16[1792,128]{1,0:T(8,128)(2,1)S(1)}, u32[]{:S(2)}, u32[]{:S(2)}) collective-permute-start(bf16[1792,128]{1,0:T(8,128)(2,1)S(1)} %bitcast.3), channel_id=1, source_target_pairs={{0,8},{8,0},{1,9},{9,1},{2,10},{10,2},{3,11},{11,3},{4,12},{12,4},... | collective-permute-start | bytes 1376264 | tf_op jit(solution)/shard_map/ppermute | solution.py:375

commit v5 on v3

--- a/solution.py
+++ b/solution.py
@@ -77,26 +77,45 @@
     return out
 
 
-def attention(qkv, bias_t, mask):
-    q, k, v = qkv[:, :CH], qkv[:, CH : 2 * CH], qkv[:, 2 * CH :]
-    scores = nt(k, spread_heads(q, mask)) * SCALE + bias_t
-    top = jnp.max(scores, axis=0, keepdims=True)
-    e = jnp.exp(scores - top)
-    p = (e * (1.0 / jnp.sum(e, axis=0, keepdims=True))).astype(BF16)
-    return gather_heads(tn(p, v)).astype(BF16), p
-
-
-def attention_back(d_o, qkv, p, mask):
-    q, k, v = qkv[:, :CH], qkv[:, CH : 2 * CH], qkv[:, 2 * CH :]
-    do_spread = spread_heads(d_o, mask)
-    dv = nn(p, do_spread)
-    dp = nt(v, do_spread)
-    pf = p.astype(F32)
-    ds = pf * (dp - jnp.sum(dp * pf, axis=0, keepdims=True))
-    dsb = ds.astype(BF16)
-    dk = nn(dsb, spread_heads(q, mask)) * SCALE
-    dq = gather_heads(tn(dsb, k)) * SCALE
-    return jnp.concatenate([dq, dk, dv], axis=1).astype(BF16), ds
+def rows_of(values, w):
+    return values[w * LEN : (w + 1) * LEN]
+
+
+def groups_of(tokens, group):
+    count = tokens // LEN
+    return [range(start, min(start + group, count)) for start in range(0, count, group)]
+
+
+def attention(qkv, bias_t, mask, group):
+    outs, weights = [], []
+    for windows in groups_of(qkv.shape[0], group):
+        parts = [rows_of(qkv, w) for w in windows]
+        scores = [nt(x[:, CH : 2 * CH], spread_heads(x[:, :CH], mask)) * SCALE + bias_t for x in parts]
+        e = [jnp.exp(x - jnp.max(x, axis=0, keepdims=True)) for x in scores]
+        p = [(x * (1.0 / jnp.sum(x, axis=0, keepdims=True))).astype(BF16) for x in e]
+        o = [tn(x, y[:, 2 * CH :]) for x, y in zip(p, parts)]
+        outs += [gather_heads(x).astype(BF16) for x in o]
+        weights += p
+    return jnp.concatenate(outs, axis=0), jnp.concatenate(weights, axis=0)
+
+
+def attention_back(d_o, qkv, p, mask, group):
+    done, bias = [], None
+    for windows in groups_of(qkv.shape[0], group):
+        parts = [rows_of(qkv, w) for w in windows]
+        weights = [rows_of(p, w) for w in windows]
+        do_spread = [spread_heads(rows_of(d_o, w), mask) for w in windows]
+        dp = [nt(x[:, 2 * CH :], y) for x, y in zip(parts, do_spread)]
+        dv = [nn(x, y) for x, y in zip(weights, do_spread)]
+        weights = [x.astype(F32) for x in weights]
+        ds = [x * (y - jnp.sum(y * x, axis=0, keepdims=True)) for x, y in zip(weights, dp)]
+        dsb = [x.astype(BF16) for x in ds]
+        dk = [nn(x, spread_heads(y[:, :CH], mask)) * SCALE for x, y in zip(dsb, parts)]
+        dq = [gather_heads(tn(x, y[:, CH : 2 * CH])) * SCALE for x, y in zip(dsb, parts)]
+        for x in ds:
+            bias = x if bias is None else bias + x
+        done += [jnp.concatenate(x, axis=1).astype(BF16) for x in zip(dq, dk, dv)]
+    return jnp.concatenate(done, axis=0), bias
 
 
 def gelu_and_slope(u):
@@ -107,25 +126,19 @@
     return m, s + m * (1.0 - s) * (2.0 * c + (6.0 * c * 0.044715) * sq)
 
 
-def forward(x, w_qkv, w_proj, gains, bias, mask):
+def forward(x, w_qkv, w_proj, gains, bias, mask, group):
     hat1, inv1 = normalise(x)
     gain = gains()
     a1 = (hat1 * gain[0:1]).astype(BF16)
     qkv = nn(a1, w_qkv()).astype(BF16)
-    bias_t = turned_bias(bias())
-    outs, weights = [], []
-    for w in range(x.shape[0] // LEN):
-        o, p = attention(qkv[w * LEN : (w + 1) * LEN], bias_t, mask)
-        outs.append(o)
-        weights.append(p)
-    o = jnp.concatenate(outs, axis=0)
+    o, p = attention(qkv, turned_bias(bias()), mask, group)
     h = (x + nn(o, w_proj())).astype(BF16).astype(F32)
     hat2, inv2 = normalise(h)
     a2 = (hat2 * gain[1:2]).astype(BF16)
-    return h, (hat1, inv1, a1, jnp.concatenate(weights, axis=0), o, hat2, inv2, a2), qkv
-
-
-def backward(gy, kept, qkv, w_qkv, w_proj, w_up, w_down, g1, g2, mask):
+    return h, (hat1, inv1, a1, p, o, hat2, inv2, a2), qkv
+
+
+def backward(gy, kept, qkv, w_qkv, w_proj, w_up, w_down, g1, g2, mask, group):
     hat1, inv1, a1, p, o, hat2, inv2, a2 = kept
     m, slope = gelu_and_slope(nn(a2, w_up))
     m = m.astype(BF16)
@@ -135,13 +148,7 @@
     dh = gy.astype(F32) + normalise_back(da2, hat2, inv2, g2)
     dhb = dh.astype(BF16)
     d_o = nt(dhb, w_proj).astype(BF16)
-    parts, bias = [], None
-    for w in range(gy.shape[0] // LEN):
-        at = slice(w * LEN, (w + 1) * LEN)
-        part, ds = attention_back(d_o[at], qkv[at], p[at], mask)
-        parts.append(part)
-        bias = ds if bias is None else bias + ds
-    dqkv = jnp.concatenate(parts, axis=0)
+    dqkv, bias = attention_back(d_o, qkv, p, mask, group)
     da1 = nt(dqkv, w_qkv)
     gain1 = jnp.sum(da1 * hat1, axis=0, keepdims=True)
     dx = dh + normalise_back(da1, hat1, inv1, g1)
@@ -181,8 +188,8 @@
     return jnp.concatenate([bias[h].T for h in range(HEADS)], axis=1)
 
 
-def first_half(x, w_qkv, w_proj, w_up, w_down, gains, bias):
-    h, kept, _ = forward(to_windows(x.astype(F32)), w_qkv, w_proj, gains, bias, head_mask())
+def first_half(x, group, w_qkv, w_proj, w_up, w_down, gains, bias):
+    h, kept, _ = forward(to_windows(x.astype(F32)), w_qkv, w_proj, gains, bias, head_mask(), group)
     m, _ = gelu_and_slope(nn(kept[7], w_up()))
     return from_windows(h + nn(m.astype(BF16), w_down()))
 
@@ -195,15 +202,15 @@
     moves += [(source.at[0], target) for source, target in zip(sources[1:7], targets[1:7])]
     moves += [(sources[7].at[HALF:, 0:WIN], targets[7])]
     copies = [pltpu.make_async_copy(source, target, sem.at[i]) for i, (source, target) in enumerate(moves)]
-    for copy in copies:
-        copy.start()
+    for i in (0, 5, 1, 6, 2, 3, 4, 7):
+        copies[i].start(priority=1)
 
     def fetched(i):
         copies[i].wait()
         return targets[i][...]
 
     parts = [functools.partial(fetched, i) for i in range(1, 7)]
-    tile = first_half(fetched(0), *parts)
+    tile = first_half(fetched(0), 2, *parts)
     top_ref[...] = tile[:HALF].astype(BF16)
     low_ref[...] = tile[HALF:].astype(BF16)
     edge_ref[0:HALF] = tile[HALF:, 0:WIN].astype(BF16)
@@ -217,7 +224,7 @@
 def next_kernel(x_ref, w_qkv_ref, w_proj_ref, w_up_ref, w_down_ref, gain_ref, bias_ref, top_ref, low_ref):
     wide = x_ref.shape[1] // 2
     parts = [at(ref, 0) for ref in (w_qkv_ref, w_proj_ref, w_up_ref, w_down_ref, gain_ref, bias_ref)]
-    tile = first_half(x_ref[:, wide:], *parts)
+    tile = first_half(x_ref[:, wide:], 4, *parts)
     top_ref[...] = tile[:HALF].astype(BF16)
     low_ref[...] = tile[HALF:].astype(BF16)
 
@@ -233,19 +240,19 @@
 def keep_kernel(part, x_ref, w_qkv_ref, w_proj_ref, gain_ref, bias_ref, kept_ref):
     wide = x_ref.shape[1] // 2
     x = to_windows(x_ref[:, part * wide : (part + 1) * wide].astype(F32))
-    _, kept, _ = forward(x, at(w_qkv_ref, 0), at(w_proj_ref, 0), at(gain_ref, 0), at(bias_ref, 0), head_mask())
+    _, kept, _ = forward(x, at(w_qkv_ref, 0), at(w_proj_ref, 0), at(gain_ref, 0), at(bias_ref, 0), head_mask(), (8, 2)[part])
     for place, value, width in zip(kept_slices(), kept, KEPT):
         kept_ref[:, place] = jnp.broadcast_to(value, (x.shape[0], width)).astype(BF16)
 
 
-def second_half(x, gy, w_qkv_ref, w_proj_ref, w_up_ref, w_down_ref, gain_ref, bias_ref):
+def second_half(x, gy, group, w_qkv_ref, w_proj_ref, w_up_ref, w_down_ref, gain_ref, bias_ref):
     mask = head_mask()
     _, kept, qkv = forward(
-        to_windows(x), at(w_qkv_ref, 1), at(w_proj_ref, 1), at(gain_ref, 1), at(bias_ref, 1), mask
+        to_windows(x), at(w_qkv_ref, 1), at(w_proj_ref, 1), at(gain_ref, 1), at(bias_ref, 1), mask, group
     )
     w_qkv, w_proj, w_up, w_down = w_qkv_ref[1], w_proj_ref[1], w_up_ref[1], w_down_ref[1]
     g1, g2 = gain_ref[1, 0:1], gain_ref[1, 1:2]
-    return backward(to_windows(gy).astype(BF16), kept, qkv, w_qkv, w_proj, w_up, w_down, g1, g2, mask)
+    return backward(to_windows(gy).astype(BF16), kept, qkv, w_qkv, w_proj, w_up, w_down, g1, g2, mask, group)
 
 
 def second_kernel(*refs):
@@ -258,7 +265,7 @@
     frame_ref[0:HALF, 0:wide] = g_own_ref[HALF:, 0:wide].astype(F32)
     frame_ref[HALF:, 0:wide] = g_below_ref[0:HALF, 0:wide].astype(F32)
     gy = frame_ref[:, HALF : wide - HALF]
-    dx, *sums = second_half(x, gy, *weights)
+    dx, *sums = second_half(x, gy, 7, *weights)
     dx_ref[...] = dx.astype(BF16)
     pack(pack_ref, *sums)
 
@@ -280,7 +287,7 @@
     frame_ref[0:HALF, span : span + WIN] = edge_ref[HALF:WIN].astype(F32)
     frame_ref[HALF:, span : span + WIN] = edge_ref[WIN + HALF :].astype(F32)
     gy = frame_ref[:, HALF : span + HALF]
-    dx, *sums = second_half(x, gy, *weights)
+    dx, *sums = second_half(x, gy, 3, *weights)
     pack(pack_ref, *sums, old_ref)
     tile = from_windows(jnp.concatenate([dx_ref[...].astype(F32), dx], axis=0))
     dtop_ref[...] = tile[:HALF].astype(BF16)
@@ -303,7 +310,7 @@
     kept = [v.astype(F32) if i in (0, 1, 5, 6) else v for i, v in enumerate(kept)]
     g1, g2 = gain_ref[0, 0:1], gain_ref[0, 1:2]
     dx, pairs, bias, gain1, gain2 = backward(
-        gy, kept, nn(kept[2], w_qkv_ref[0]).astype(BF16), w_qkv_ref[0], w_proj_ref[0], w_up_ref[0], w_down_ref[0], g1, g2, head_mask()
+        gy, kept, nn(kept[2], w_qkv_ref[0]).astype(BF16), w_qkv_ref[0], w_proj_ref[0], w_up_ref[0], w_down_ref[0], g1, g2, head_mask(), 4
     )
     dx_ref[...] = from_windows(dx).astype(BF16)
     pack(pack_ref, pairs, bias, gain1, gain2)
@@ -415,7 +422,6 @@
         cost_estimate=cost(300_000_000, 1_500_000),
         name="forward_next",
     )(latent, *weights, attn_bias)
-    top_b, below_a, g_below = lax.optimization_barrier((top_b, below_a, g_below))
     below_b = shift(top_b, -1, 0)
     edge = shift(jnp.concatenate([edge_own, below_a[:, :WIN], g_below[:HALF, :WIN]], axis=0), 0, -1)
     weights = (*weights, attn_bias)

time: 104 us -> 94 us (0.904)
  Pallas kernels: 29 us -> 24.2 us
  waiting for transfers between devices: 8.92 us -> 6.29 us
  starting transfers between devices: 28.6 us -> 26 us
    ppermute x2, starting transfers between devices: 12.7 us -> 9.22 us  [swap_core(): return lax.ppermute(value, 'core', [(0, 1), (1, 0)])]
    ppermute x6, waiting for transfers between devices: 6.03 us -> 3.4 us  [shift(): return lax.ppermute(value, AXES, pairs)]
    pallas_call x1, Pallas kernels: 7.77 us -> 5.27 us  [body(): pl.pallas_call(last_kernel, out_shape=(jax.ShapeDtypeStruct(latent.shape,...]
    pallas_call x1, Pallas kernels: 6.17 us -> 4.48 us  [body(): pl.pallas_call(third_kernel, out_shape=(half, half, jax.ShapeDtypeStruct(...]
    pallas_call x1, Pallas kernels: 4.57 us -> 3.25 us  [body(): pl.pallas_call(second_kernel, out_shape=(jax.ShapeDtypeStruct((part_a, CH...]
  transfers between devices with their start and end apart: 8 -> 8, of which waited for: 4 -> 4; matrix products, arithmetic and copies ran while one was open for 0% -> 0% of each run, Pallas kernels for 13% -> 14%
where the time goes in v5:
time: 94 us; the launch traced here: 93.8 us
  blocking collectives  36 us (38%)
  starting transfers between devices  26 us (28%)
  Pallas kernels  24.2 us (26%)
  waiting for transfers between devices  6.29 us (7%)
    all_to_all x2, blocking collectives, collect(): return lax.all_to_all(spread, axis, 0, 0)  23.1 us
    ppermute x6, starting transfers between devices, shift(): return lax.ppermute(value, AXES, pairs)  16.8 us
    all_to_all x1, blocking collectives, scatter_sum(): return jnp.sum(lax.all_to_all(pieces, axis, 0, 0).astype(F32), axis=0)  12.9 us
    ppermute x2, starting transfers between devices, swap_core(): return lax.ppermute(value, 'core', [(0, 1), (1, 0)])  9.22 us
    pallas_call x1, Pallas kernels, body(): pl.pallas_call(last_kernel, out_shape=(jax.ShapeDtypeStruct(latent.shape,...  5.27 us
    pallas_call x1, Pallas kernels, body(): pl.pallas_call(first_kernel, out_shape=(side, side, corner), in_specs=[pl...  4.56 us
    pallas_call x1, Pallas kernels, body(): pl.pallas_call(third_kernel, out_shape=(half, half, jax.ShapeDtypeStruct(...  4.48 us
    ppermute x6, waiting for transfers between devices, shift(): return lax.ppermute(value, AXES, pairs)  3.4 us
  transfers between devices with their start and end apart: 8, of which 4 were waited for; matrix products, arithmetic and copies ran while one was open for 0% of the time, Pallas kernels for 14%

profile of v5, /device:TPU:1, one launch (start us, length us, event | category | flops | bytes accessed | tf_op | source)
XLA Modules:
  0.0 93.8 jit_solution(15527637782482656363)
XLA Ops:
  0.7 3.3 %collective-permute-start.1 = (bf16[8,128,128]{2,1,0:T(8,128)(2,1)}, bf16[8,128,128]{2,1,0:T(8,128)(2,1)S(1)}, u32[]{:S(2)}, u32[]{:S(2)}) collective-permute-start(bf16[8,128,128]{2,1,0:T(8,128)(2,1)} %refs_4_.5), channel_id=1, source_target_pairs={{0,248},{1,249},{2,250},{3,251},{4,252},{5,253},{6,254},{7,255},{8... | collective-permute-start | bytes 786440 | tf_op jit(solution)/shard_map/ppermute | solution.py:364
  4.0 4.6 %forward_first.1 = (bf16[4,64,128]{2,1,0:T(8,128)(2,1)}, bf16[4,64,128]{2,1,0:T(8,128)(2,1)}, bf16[8,8,128]{2,1,0:T(8,128)(2,1)}) custom-call(bf16[8,128,128]{2,1,0:T(8,128)(2,1)} %x_ref.5, bf16[2,128,384]{2,1,0:T(8,128)(2,1)} %refs_5_.5, bf16[2,128,128]{2,1,0:T(8,128)(2,1)} %refs_6_.5, bf16[2,128,512]{2,1,0:T(8,128)(2,1)} %refs_7_.7, ...), custom_call_target="tpu_custom_call" | custom-call | flops 300000000 | bytes 1500000 | tf_op jit(solution)/shard_map/forward_first/pallas_call | solution.py:403
  8.6 0.0 copy-start.9
  8.6 0.0 copy-start.8
  8.6 6.3 %collective-permute-start = (bf16[4,64,128]{2,1,0:T(8,128)(2,1)}, bf16[4,64,128]{2,1,0:T(8,128)(2,1)S(1)}, u32[]{:S(2)}, u32[]{:S(2)}) collective-permute-start(bf16[4,64,128]{2,1,0:T(8,128)(2,1)} %get-tuple-element.36), channel_id=1, source_target_pairs={{0,248},{1,249},{2,250},{3,251},{4,252},{5,253},{6,254},{7,255},{8... | collective-permute-start | bytes 196616 | tf_op jit(solution)/shard_map/ppermute | solution.py:364
  14.9 2.0 %forward_next.1 = (bf16[4,64,128]{2,1,0:T(8,128)(2,1)S(1)}, bf16[4,64,128]{2,1,0:T(8,128)(2,1)S(1)}) custom-call(bf16[8,128,128]{2,1,0:T(8,128)(2,1)S(1)} %copy-done, bf16[2,128,384]{2,1,0:T(8,128)(2,1)S(1)} %copy-done.2, bf16[2,128,128]{2,1,0:T(8,128)(2,1)S(1)} %copy-done.3, bf16[2,128,512]{2,1,0:T(8,128)(2,1)S(1)} %copy-done.4, ...), custom_call_target="tpu_custom_call" | custom-call | flops 300000000 | bytes 1500000 | tf_op jit(solution)/shard_map/forward_next/pallas_call | solution.py:416
  16.9 0.8 collective-permute-start.3
  17.7 0.0 collective-permute-done.refs_1_.refs_2_
  17.7 0.0 collective-permute-done.1.refs_3_.refs_5_
  17.8 2.9 %collective-permute-start.2 = (bf16[16,8,128]{2,1,0:T(8,128)(2,1)S(1)}, bf16[16,8,128]{2,1,0:T(8,128)(2,1)S(1)}, u32[]{:S(2)}, u32[]{:S(2)}) collective-permute-start(bf16[16,8,128]{2,1,0:T(8,128)(2,1)S(1)} %pad_maximum_fusion), channel_id=1, source_target_pairs={{0,7},{1,0},{2,1},{3,2},{4,3},{5,4},{6,5},{7,6},{8,15},{9,8},{10,9... | collective-permute-start | bytes 98312 | tf_op jit(solution)/shard_map/ppermute | solution.py:364
  20.6 3.2 %backward_second.1 = (bf16[448,128]{1,0:T(8,128)(2,1)S(1)}, f32[1792,128]{1,0:T(8,128)S(1)}) custom-call(bf16[4,64,128]{2,1,0:T(8,128)(2,1)S(1)} %copy-done.8, bf16[4,64,128]{2,1,0:T(8,128)(2,1)S(1)} %collective-permute-done.refs_1_.refs_2_, bf16[8,128,128]{2,1,0:T(8,128)(2,1)S(1)} %copy-done.6, ...), custom_call_target="tpu_custom_call" | custom-call | flops 700000000 | bytes 3000000 | tf_op jit(solution)/shard_map/backward_second/pallas_call | solution.py:429
  23.9 0.0 collective-permute-done.3.refs_3_
  23.9 0.0 collective-permute-done.2.refs_6_
  23.9 4.5 %backward_third.1 = (bf16[4,128,128]{2,1,0:T(8,128)(2,1)S(1)}, bf16[4,128,128]{2,1,0:T(8,128)(2,1)S(1)}, bf16[4,8,128]{2,1,0:T(8,128)(2,1)S(1)}, f32[1792,128]{1,0:T(8,128)S(1)}) custom-call(bf16[4,64,128]{2,1,0:T(8,128)(2,1)S(1)} %copy-done.8, bf16[4,64,128]{2,1,0:T(8,128)(2,1)S(1)} %get-tuple-element.35.refs_1_, ...), custom_call_target="tpu_custom_call" | custom-call | flops 800000000 | bytes 3000000 | tf_op jit(solution)/shard_map/backward_third/pallas_call | solution.py:440
  28.4 3.5 %collective-permute-start.4 = (bf16[4,128,128]{2,1,0:T(8,128)(2,1)S(1)}, bf16[4,128,128]{2,1,0:T(8,128)(2,1)S(1)}, u32[]{:S(2)}, u32[]{:S(2)}) collective-permute-start(bf16[4,128,128]{2,1,0:T(8,128)(2,1)S(1)} %get-tuple-element.45), channel_id=1, source_target_pairs={{0,8},{1,9},{2,10},{3,11},{4,12},{5,13},{6,14},{7,15},{8,16},{9,17... | collective-permute-start | bytes 393224 | tf_op jit(solution)/shard_map/ppermute | solution.py:364
  31.9 1.2 %keep_first.2.refs_3_ = bf16[512,1152]{1,0:T(8,128)(2,1)S(1)} custom-call(bf16[8,128,128]{2,1,0:T(8,128)(2,1)S(1)} %copy-done, bf16[2,128,384]{2,1,0:T(8,128)(2,1)S(1)} %copy-done.2, bf16[2,128,128]{2,1,0:T(8,128)(2,1)S(1)} %copy-done.3, f32[2,2,128]{2,1,0:T(2,128)S(1)} %copy-done.7, f32[2,4,64,64]{3,2,1,0:T(8,128)S(1)} %copy-done.1), custom_call_target="tpu_custom_call" | custom-call | flops 300000000 | bytes 2000000 | tf_op jit(solution)/shard_map/keep_first/pallas_call | solution.py:453
  33.2 0.7 collective-permute-done.4.refs_1_
  33.9 0.1 collective-permute-start.5
  34.0 2.0 %keep_first.3.refs_4_ = bf16[512,1152]{1,0:T(8,128)(2,1)S(1)} custom-call(bf16[8,128,128]{2,1,0:T(8,128)(2,1)S(1)} %copy-done, bf16[2,128,384]{2,1,0:T(8,128)(2,1)S(1)} %copy-done.2, bf16[2,128,128]{2,1,0:T(8,128)(2,1)S(1)} %copy-done.3, f32[2,2,128]{2,1,0:T(2,128)S(1)} %copy-done.7, f32[2,4,64,64]{3,2,1,0:T(8,128)S(1)} %copy-done.1), custom_call_target="tpu_custom_call" | custom-call | flops 300000000 | bytes 2000000 | tf_op jit(solution)/shard_map/keep_first/pallas_call | solution.py:453
  36.0 2.7 %collective-permute-done.5.refs_2_ = bf16[8,8,128]{2,1,0:T(8,128)(2,1)S(1)} collective-permute-done((bf16[8,8,128]{2,1,0:T(8,128)(2,1)S(1)}, bf16[8,8,128]{2,1,0:T(8,128)(2,1)S(1)}, u32[]{:S(2)}, u32[]{:S(2)}) %collective-permute-start.5) | collective-permute-done | bytes 16416 | tf_op jit(solution)/shard_map/ppermute | solution.py:364
  38.7 5.3 %backward_first.1 = (bf16[8,128,128]{2,1,0:T(8,128)(2,1)}, f32[1792,128]{1,0:T(8,128)S(1)}, bf16[1792,128]{1,0:T(8,128)(2,1)S(1)}) custom-call(bf16[4,128,128]{2,1,0:T(8,128)(2,1)S(1)} %get-tuple-element.44.refs_0_, bf16[4,128,128]{2,1,0:T(8,128)(2,1)S(1)} %collective-permute-done.4.refs_1_, bf16[8,8,128]{2,1,0:T(8,128)(2,1)S(1)} %collective-permute-done.5.refs_2_, ...), custom_call_target="tpu_custom_call" | custom-call | flops 1500000000 | bytes 4000000 | tf_op jit(solution)/shard_map/backward_first/pallas_call | solution.py:468
  43.9 4.9 %collective-permute-start.6 = (bf16[1792,128]{1,0:T(8,128)(2,1)S(1)}, bf16[1792,128]{1,0:T(8,128)(2,1)S(1)}, u32[]{:S(2)}, u32[]{:S(2)}) collective-permute-start(bf16[1792,128]{1,0:T(8,128)(2,1)S(1)} %get-tuple-element.54), channel_id=1, source_target_pairs={{0,8},{8,0},{1,9},{9,1},{2,10},{10,2},{3,11},{11,3},{4,12},{12,4},... | collective-permute-start | bytes 1376264 | tf_op jit(solution)/shard_map/ppermute | solution.py:368
  48.8 1.4 %collective-permute-done.6 = bf16[1792,128]{1,0:T(8,128)(2,1)S(1)} collective-permute-done((bf16[1792,128]{1,0:T(8,128)(2,1)S(1)}, bf16[1792,128]{1,0:T(8,128)(2,1)S(1)}, u32[]{:S(2)}, u32[]{:S(2)}) %collective-permute-start.6) | collective-permute-done | bytes 458784 | tf_op jit(solution)/shard_map/ppermute | solution.py:368
  50.2 0.1 add_convert_fusion
  50.3 12.9 %all_to_all.15 = bf16[16,112,128]{2,1,0:T(8,128)(2,1)S(1)} all-to-all(bf16[16,112,128]{2,1,0:T(8,128)(2,1)S(1)} %bitcast.5), channel_id=1, replica_groups=mesh['z'=8,'yh'=2,'core'=2,'x'=4,'yl'=2] {'yh','x','yl'}, dimensions={0} | all-to-all | bytes 917504 | tf_op jit(solution)/shard_map/all_to_all | solution.py:373
  63.3 0.1 reduce_sum.24
  63.4 11.5 %all_to_all.16 = bf16[8,112,128]{2,1,0:T(8,128)(2,1)S(1)} all-to-all(bf16[8,112,128]{2,1,0:T(8,128)(2,1)S(1)} %broadcast_in_dim.4), channel_id=1, replica_groups=mesh['z'=8,'yh'=2,'core'=2,'x'=4,'yl'=2] {'z'}, dimensions={0} | all-to-all | bytes 458752 | tf_op jit(solution)/shard_map/all_to_all | solution.py:378
  74.9 0.1 broadcast_in_dim.5
  75.0 11.6 %all_to_all.17 = bf16[16,112,128]{2,1,0:T(8,128)(2,1)S(1)} all-to-all(bf16[16,112,128]{2,1,0:T(8,128)(2,1)S(1)} %broadcast_in_dim.5), channel_id=1, replica_groups=mesh['z'=8,'yh'=2,'core'=2,'x'=4,'yl'=2] {'yh','x','yl'}, dimensions={0} | all-to-all | bytes 917504 | tf_op jit(solution)/shard_map/all_to_all | solution.py:378
  86.6 4.3 %collective-permute-start.7 = (bf16[1792,128]{1,0:T(8,128)(2,1)S(1)}, bf16[1792,128]{1,0:T(8,128)(2,1)S(1)}, u32[]{:S(2)}, u32[]{:S(2)}) collective-permute-start(bf16[1792,128]{1,0:T(8,128)(2,1)S(1)} %bitcast.3), channel_id=1, source_target_pairs={{0,8},{8,0},{1,9},{9,1},{2,10},{10,2},{3,11},{11,3},{4,12},{12,4},... | collective-permute-start | bytes 1376264 | tf_op jit(solution)/shard_map/ppermute | solution.py:368
  91.0 1.4 %collective-permute-done.7.other_ref = bf16[1792,128]{1,0:T(8,128)(2,1)S(1)} collective-permute-done((bf16[1792,128]{1,0:T(8,128)(2,1)S(1)}, bf16[1792,128]{1,0:T(8,128)(2,1)S(1)}, u32[]{:S(2)}, u32[]{:S(2)}) %collective-permute-start.7) | collective-permute-done | bytes 458784 | tf_op jit(solution)/shard_map/ppermute | solution.py:368
  92.4 1.4 %unpack.1 = (f32[2,128,384]{2,1,0:T(8,128)}, f32[2,128,128]{2,1,0:T(8,128)}, f32[2,128,512]{2,1,0:T(8,128)}, f32[2,512,128]{2,1,0:T(8,128)}, f32[2,2,128]{2,1,0:T(2,128)}, /*index=5*/f32[2,4,64,64]{3,2,1,0:T(8,128)}) custom-call(s32[1]{0:T(128)} %bitcast.refs_11_.core_ref, bf16[1792,128]{1,0:T(8,128)(2,1)S(1)} %bitcast.4, ...), custom_call_target="tpu_custom_call" | custom-call | flops 1000000 | bytes 4000000 | tf_op jit(solution)/shard_map/unpack/pallas_call | solution.py:483
  (25 shorter events, 0.1 us)
Async XLA Ops:
  0.6 20.0 %copy-start.6 = (bf16[8,128,128]{2,1,0:T(8,128)(2,1)S(1)}, bf16[8,128,128]{2,1,0:T(8,128)(2,1)}, u32[]{:S(2)}) copy-start(bf16[8,128,128]{2,1,0:T(8,128)(2,1)} %refs_4_.5) | copy-start | bytes 786436
  0.6 14.2 %copy-start.7 = (f32[2,2,128]{2,1,0:T(2,128)S(1)}, f32[2,2,128]{2,1,0:T(2,128)}, u32[]{:S(2)}) copy-start(f32[2,2,128]{2,1,0:T(2,128)} %refs_9_.5) | copy-start | bytes 6148
  0.7 14.2 %copy-start.3 = (bf16[2,128,128]{2,1,0:T(8,128)(2,1)S(1)}, bf16[2,128,128]{2,1,0:T(8,128)(2,1)}, u32[]{:S(2)}) copy-start(bf16[2,128,128]{2,1,0:T(8,128)(2,1)} %refs_6_.5) | copy-start | bytes 196612
  0.7 14.2 %copy-start.2 = (bf16[2,128,384]{2,1,0:T(8,128)(2,1)S(1)}, bf16[2,128,384]{2,1,0:T(8,128)(2,1)}, u32[]{:S(2)}) copy-start(bf16[2,128,384]{2,1,0:T(8,128)(2,1)} %refs_5_.5) | copy-start | bytes 589828
  0.7 14.2 %copy-start.1 = (f32[2,4,64,64]{3,2,1,0:T(8,128)S(1)}, f32[2,4,64,64]{3,2,1,0:T(8,128)}, u32[]{:S(2)}) copy-start(f32[2,4,64,64]{3,2,1,0:T(8,128)} %bias_ref.5) | copy-start | bytes 393220
  0.7 14.2 %copy-start.5 = (bf16[2,512,128]{2,1,0:T(8,128)(2,1)S(1)}, bf16[2,512,128]{2,1,0:T(8,128)(2,1)}, u32[]{:S(2)}) copy-start(bf16[2,512,128]{2,1,0:T(8,128)(2,1)} %refs_8_.5) | copy-start | bytes 786436
  0.7 14.2 %copy-start.4 = (bf16[2,128,512]{2,1,0:T(8,128)(2,1)S(1)}, bf16[2,128,512]{2,1,0:T(8,128)(2,1)}, u32[]{:S(2)}) copy-start(bf16[2,128,512]{2,1,0:T(8,128)(2,1)} %refs_7_.7) | copy-start | bytes 786436
  0.7 14.2 %copy-start = (bf16[8,128,128]{2,1,0:T(8,128)(2,1)S(1)}, bf16[8,128,128]{2,1,0:T(8,128)(2,1)}, u32[]{:S(2)}) copy-start(bf16[8,128,128]{2,1,0:T(8,128)(2,1)} %x_ref.5) | copy-start | bytes 786436
  0.7 17.0 %collective-permute-start.1 = (bf16[8,128,128]{2,1,0:T(8,128)(2,1)}, bf16[8,128,128]{2,1,0:T(8,128)(2,1)S(1)}, u32[]{:S(2)}, u32[]{:S(2)}) collective-permute-start(bf16[8,128,128]{2,1,0:T(8,128)(2,1)} %refs_4_.5), channel_id=1, source_target_pairs={{0,248},{1,249},{2,250},{3,251},{4,252},{5,253},{6,254},{7,255},{8... | collective-permute-start | bytes 786440 | tf_op jit(solution)/shard_map/ppermute | solution.py:364
  8.6 9.1 %copy-start.9 = (bf16[8,8,128]{2,1,0:T(8,128)(2,1)S(1)}, bf16[8,8,128]{2,1,0:T(8,128)(2,1)}, u32[]{:S(2)}) copy-start(bf16[8,8,128]{2,1,0:T(8,128)(2,1)} %get-tuple-element.37) | copy-start | bytes 49156
  8.6 12.0 %copy-start.8 = (bf16[4,64,128]{2,1,0:T(8,128)(2,1)S(1)}, bf16[4,64,128]{2,1,0:T(8,128)(2,1)}, u32[]{:S(2)}) copy-start(bf16[4,64,128]{2,1,0:T(8,128)(2,1)} %get-tuple-element.34.refs_0_) | copy-start | bytes 196612
  8.6 9.1 %collective-permute-start = (bf16[4,64,128]{2,1,0:T(8,128)(2,1)}, bf16[4,64,128]{2,1,0:T(8,128)(2,1)S(1)}, u32[]{:S(2)}, u32[]{:S(2)}) collective-permute-start(bf16[4,64,128]{2,1,0:T(8,128)(2,1)} %get-tuple-element.36), channel_id=1, source_target_pairs={{0,248},{1,249},{2,250},{3,251},{4,252},{5,253},{6,254},{7,255},{8... | collective-permute-start | bytes 196616 | tf_op jit(solution)/shard_map/ppermute | solution.py:364
  16.9 6.9 %collective-permute-start.3 = (bf16[4,64,128]{2,1,0:T(8,128)(2,1)S(1)}, bf16[4,64,128]{2,1,0:T(8,128)(2,1)S(1)}, u32[]{:S(2)}, u32[]{:S(2)}) collective-permute-start(bf16[4,64,128]{2,1,0:T(8,128)(2,1)S(1)} %get-tuple-element.38), channel_id=1, source_target_pairs={{0,248},{1,249},{2,250},{3,251},{4,252},{5,253},{6,254},{7,255},{8... | collective-permute-start | bytes 196616 | tf_op jit(solution)/shard_map/ppermute | solution.py:364
  17.8 6.1 %collective-permute-start.2 = (bf16[16,8,128]{2,1,0:T(8,128)(2,1)S(1)}, bf16[16,8,128]{2,1,0:T(8,128)(2,1)S(1)}, u32[]{:S(2)}, u32[]{:S(2)}) collective-permute-start(bf16[16,8,128]{2,1,0:T(8,128)(2,1)S(1)} %pad_maximum_fusion), channel_id=1, source_target_pairs={{0,7},{1,0},{2,1},{3,2},{4,3},{5,4},{6,5},{7,6},{8,15},{9,8},{10,9... | collective-permute-start | bytes 98312 | tf_op jit(solution)/shard_map/ppermute | solution.py:364
  28.4 5.5 %collective-permute-start.4 = (bf16[4,128,128]{2,1,0:T(8,128)(2,1)S(1)}, bf16[4,128,128]{2,1,0:T(8,128)(2,1)S(1)}, u32[]{:S(2)}, u32[]{:S(2)}) collective-permute-start(bf16[4,128,128]{2,1,0:T(8,128)(2,1)S(1)} %get-tuple-element.45), channel_id=1, source_target_pairs={{0,8},{1,9},{2,10},{3,11},{4,12},{5,13},{6,14},{7,15},{8,16},{9,17... | collective-permute-start | bytes 393224 | tf_op jit(solution)/shard_map/ppermute | solution.py:364
  33.9 4.8 %collective-permute-start.5 = (bf16[8,8,128]{2,1,0:T(8,128)(2,1)S(1)}, bf16[8,8,128]{2,1,0:T(8,128)(2,1)S(1)}, u32[]{:S(2)}, u32[]{:S(2)}) collective-permute-start(bf16[8,8,128]{2,1,0:T(8,128)(2,1)S(1)} %pad_maximum_fusion.1), channel_id=1, source_target_pairs={{0,1},{1,2},{2,3},{3,4},{4,5},{5,6},{6,7},{7,0},{8,9},{9,10},{10,1... | collective-permute-start | bytes 49160 | tf_op jit(solution)/shard_map/ppermute | solution.py:364
  43.9 6.3 %collective-permute-start.6 = (bf16[1792,128]{1,0:T(8,128)(2,1)S(1)}, bf16[1792,128]{1,0:T(8,128)(2,1)S(1)}, u32[]{:S(2)}, u32[]{:S(2)}) collective-permute-start(bf16[1792,128]{1,0:T(8,128)(2,1)S(1)} %get-tuple-element.54), channel_id=1, source_target_pairs={{0,8},{8,0},{1,9},{9,1},{2,10},{10,2},{3,11},{11,3},{4,12},{12,4},... | collective-permute-start | bytes 1376264 | tf_op jit(solution)/shard_map/ppermute | solution.py:368
  86.6 5.8 %collective-permute-start.7 = (bf16[1792,128]{1,0:T(8,128)(2,1)S(1)}, bf16[1792,128]{1,0:T(8,128)(2,1)S(1)}, u32[]{:S(2)}, u32[]{:S(2)}) collective-permute-start(bf16[1792,128]{1,0:T(8,128)(2,1)S(1)} %bitcast.3), channel_id=1, source_target_pairs={{0,8},{8,0},{1,9},{9,1},{2,10},{10,2},{3,11},{11,3},{4,12},{12,4},... | collective-permute-start | bytes 1376264 | tf_op jit(solution)/shard_map/ppermute | solution.py:368

commit v6 on v5

--- a/solution.py
+++ b/solution.py
@@ -86,36 +86,58 @@
     return [range(start, min(start + group, count)) for start in range(0, count, group)]
 
 
+def in_stages(stages, groups):
+    state = [None] * len(groups)
+    for step in range(len(groups) + len(stages) - 1):
+        for s in reversed(range(len(stages))):
+            g = step - s
+            if 0 <= g < len(groups):
+                state[g] = stages[s](groups[g], state[g])
+    return state
+
+
 def attention(qkv, bias_t, mask, group):
-    outs, weights = [], []
-    for windows in groups_of(qkv.shape[0], group):
+    def scores(windows, _):
         parts = [rows_of(qkv, w) for w in windows]
-        scores = [nt(x[:, CH : 2 * CH], spread_heads(x[:, :CH], mask)) * SCALE + bias_t for x in parts]
-        e = [jnp.exp(x - jnp.max(x, axis=0, keepdims=True)) for x in scores]
-        p = [(x * (1.0 / jnp.sum(x, axis=0, keepdims=True))).astype(BF16) for x in e]
+        return parts, [nt(x[:, CH : 2 * CH], spread_heads(x[:, :CH], mask)) * SCALE + bias_t for x in parts]
+
+    def softmax(_, state):
+        parts, values = state
+        e = [jnp.exp(x - jnp.max(x, axis=0, keepdims=True)) for x in values]
+        return parts, [(x * (1.0 / jnp.sum(x, axis=0, keepdims=True))).astype(BF16) for x in e]
+
+    def mix(_, state):
+        parts, p = state
         o = [tn(x, y[:, 2 * CH :]) for x, y in zip(p, parts)]
-        outs += [gather_heads(x).astype(BF16) for x in o]
-        weights += p
-    return jnp.concatenate(outs, axis=0), jnp.concatenate(weights, axis=0)
+        return [gather_heads(x).astype(BF16) for x in o], p
+
+    done = in_stages((scores, softmax, mix), groups_of(qkv.shape[0], group))
+    return jnp.concatenate(sum((x for x, _ in done), []), axis=0), jnp.concatenate(sum((x for _, x in done), []), axis=0)
 
 
 def attention_back(d_o, qkv, p, mask, group):
-    done, bias = [], None
-    for windows in groups_of(qkv.shape[0], group):
+    def spread(windows, _):
         parts = [rows_of(qkv, w) for w in windows]
         weights = [rows_of(p, w) for w in windows]
         do_spread = [spread_heads(rows_of(d_o, w), mask) for w in windows]
         dp = [nt(x[:, 2 * CH :], y) for x, y in zip(parts, do_spread)]
-        dv = [nn(x, y) for x, y in zip(weights, do_spread)]
+        return parts, weights, dp, [nn(x, y) for x, y in zip(weights, do_spread)]
+
+    def softmax(_, state):
+        parts, weights, dp, dv = state
         weights = [x.astype(F32) for x in weights]
-        ds = [x * (y - jnp.sum(y * x, axis=0, keepdims=True)) for x, y in zip(weights, dp)]
+        return parts, [x * (y - jnp.sum(y * x, axis=0, keepdims=True)) for x, y in zip(weights, dp)], dv
+
+    def mix(_, state):
+        parts, ds, dv = state
         dsb = [x.astype(BF16) for x in ds]
         dk = [nn(x, spread_heads(y[:, :CH], mask)) * SCALE for x, y in zip(dsb, parts)]
         dq = [gather_heads(tn(x, y[:, CH : 2 * CH])) * SCALE for x, y in zip(dsb, parts)]
-        for x in ds:
-            bias = x if bias is None else bias + x
-        done += [jnp.concatenate(x, axis=1).astype(BF16) for x in zip(dq, dk, dv)]
-    return jnp.concatenate(done, axis=0), bias
+        return [jnp.concatenate(x, axis=1).astype(BF16) for x in zip(dq, dk, dv)], sum(ds[1:], ds[0])
+
+    done = in_stages((spread, softmax, mix), groups_of(qkv.shape[0], group))
+    bias = sum((x for _, x in done[1:]), done[0][1])
+    return jnp.concatenate(sum((x for x, _ in done), []), axis=0), bias
 
 
 def gelu_and_slope(u):
@@ -144,28 +166,30 @@
     m = m.astype(BF16)
     du = (nt(gy, w_down) * slope).astype(BF16)
     da2 = nt(du, w_up)
+    down, up = tn(gy, m), tn(a2, du)
     gain2 = jnp.sum(da2 * hat2, axis=0, keepdims=True)
     dh = gy.astype(F32) + normalise_back(da2, hat2, inv2, g2)
     dhb = dh.astype(BF16)
     d_o = nt(dhb, w_proj).astype(BF16)
+    proj = tn(o, dhb)
     dqkv, bias = attention_back(d_o, qkv, p, mask, group)
     da1 = nt(dqkv, w_qkv)
+    grads = (tn(a1, dqkv), proj, up, down)
     gain1 = jnp.sum(da1 * hat1, axis=0, keepdims=True)
     dx = dh + normalise_back(da1, hat1, inv1, g1)
-    return dx, (gy, m, a2, du, o, dhb, a1, dqkv), bias, gain1, gain2
-
-
-def pack(pack_ref, pairs, bias, gain1, gain2, old=None):
-    gy, m, a2, du, o, dhb, a1, dqkv = pairs
+    return dx, grads, bias, gain1, gain2
+
+
+def pack(pack_ref, grads, bias, gain1, gain2, old=None):
+    qkv, proj, up, down = grads
 
     def put(at, value):
         rows = slice(at, at + value.shape[0])
         pack_ref[rows] = value if old is None else value + old[rows].astype(F32)
 
-    down, up, qkv = tn(gy, m), tn(a2, du), tn(a1, dqkv)
     for j in range(3):
         put(ROW_QKV + CH * j, qkv[:, CH * j : CH * (j + 1)])
-    put(ROW_PROJ, tn(o, dhb))
+    put(ROW_PROJ, proj)
     for j in range(4):
         put(ROW_UP + CH * j, up[:, CH * j : CH * (j + 1)])
         put(ROW_DOWN + CH * j, down[:, CH * j : CH * (j + 1)].T)
@@ -210,7 +234,7 @@
         return targets[i][...]
 
     parts = [functools.partial(fetched, i) for i in range(1, 7)]
-    tile = first_half(fetched(0), 2, *parts)
+    tile = first_half(fetched(0), 8, *parts)
     top_ref[...] = tile[:HALF].astype(BF16)
     low_ref[...] = tile[HALF:].astype(BF16)
     edge_ref[0:HALF] = tile[HALF:, 0:WIN].astype(BF16)
@@ -287,7 +311,7 @@
     frame_ref[0:HALF, span : span + WIN] = edge_ref[HALF:WIN].astype(F32)
     frame_ref[HALF:, span : span + WIN] = edge_ref[WIN + HALF :].astype(F32)
     gy = frame_ref[:, HALF : span + HALF]
-    dx, *sums = second_half(x, gy, 3, *weights)
+    dx, *sums = second_half(x, gy, 9, *weights)
     pack(pack_ref, *sums, old_ref)
     tile = from_windows(jnp.concatenate([dx_ref[...].astype(F32), dx], axis=0))
     dtop_ref[...] = tile[:HALF].astype(BF16)
@@ -309,11 +333,11 @@
     kept = [jnp.concatenate([ref[:, place] for ref in kept_refs], axis=0) for place in kept_slices()]
     kept = [v.astype(F32) if i in (0, 1, 5, 6) else v for i, v in enumerate(kept)]
     g1, g2 = gain_ref[0, 0:1], gain_ref[0, 1:2]
-    dx, pairs, bias, gain1, gain2 = backward(
+    dx, grads, bias, gain1, gain2 = backward(
         gy, kept, nn(kept[2], w_qkv_ref[0]).astype(BF16), w_qkv_ref[0], w_proj_ref[0], w_up_ref[0], w_down_ref[0], g1, g2, head_mask(), 4
     )
     dx_ref[...] = from_windows(dx).astype(BF16)
-    pack(pack_ref, pairs, bias, gain1, gain2)
+    pack(pack_ref, grads, bias, gain1, gain2)
     first_core = core_ref[0] == 0
 
     @pl.when(first_core)

time: 94 us -> 92 us (0.979)
  Pallas kernels: 24.2 us -> 21.7 us
  transfers between devices with their start and end apart: 8 -> 8, of which waited for: 4 -> 4; matrix products, arithmetic and copies ran while one was open for 0% -> 0% of each run, Pallas kernels for 14% -> 12%
where the time goes in v6:
time: 92 us; the launch traced here: 91.8 us
  blocking collectives  36.1 us (39%)
  starting transfers between devices  26 us (28%)
  Pallas kernels  21.7 us (24%)
  waiting for transfers between devices  6.81 us (7%)
    all_to_all x2, blocking collectives, collect(): return lax.all_to_all(spread, axis, 0, 0)  23.1 us
    ppermute x6, starting transfers between devices, shift(): return lax.ppermute(value, AXES, pairs)  16.8 us
    all_to_all x1, blocking collectives, scatter_sum(): return jnp.sum(lax.all_to_all(pieces, axis, 0, 0).astype(F32), axis=0)  12.9 us
    ppermute x2, starting transfers between devices, swap_core(): return lax.ppermute(value, 'core', [(0, 1), (1, 0)])  9.21 us
    pallas_call x1, Pallas kernels, body(): pl.pallas_call(last_kernel, out_shape=(jax.ShapeDtypeStruct(latent.shape,...  5.21 us
    ppermute x6, waiting for transfers between devices, shift(): return lax.ppermute(value, AXES, pairs)  3.92 us
    pallas_call x1, Pallas kernels, body(): pl.pallas_call(first_kernel, out_shape=(side, side, corner), in_specs=[pl...  3.9 us
    pallas_call x1, Pallas kernels, body(): pl.pallas_call(third_kernel, out_shape=(half, half, jax.ShapeDtypeStruct(...  3.59 us
  transfers between devices with their start and end apart: 8, of which 4 were waited for; matrix products, arithmetic and copies ran while one was open for 0% of the time, Pallas kernels for 12%

profile of v6, /device:TPU:1, one launch (start us, length us, event | category | flops | bytes accessed | tf_op | source)
XLA Modules:
  0.0 91.8 jit_solution(1209742866919307070)
XLA Ops:
  0.7 3.3 %collective-permute-start.1 = (bf16[8,128,128]{2,1,0:T(8,128)(2,1)}, bf16[8,128,128]{2,1,0:T(8,128)(2,1)S(1)}, u32[]{:S(2)}, u32[]{:S(2)}) collective-permute-start(bf16[8,128,128]{2,1,0:T(8,128)(2,1)} %refs_4_.5), channel_id=1, source_target_pairs={{0,248},{1,249},{2,250},{3,251},{4,252},{5,253},{6,254},{7,255},{8... | collective-permute-start | bytes 786440 | tf_op jit(solution)/shard_map/ppermute | solution.py:388
  4.0 3.9 %forward_first.1 = (bf16[4,64,128]{2,1,0:T(8,128)(2,1)}, bf16[4,64,128]{2,1,0:T(8,128)(2,1)}, bf16[8,8,128]{2,1,0:T(8,128)(2,1)}) custom-call(bf16[8,128,128]{2,1,0:T(8,128)(2,1)} %x_ref.5, bf16[2,128,384]{2,1,0:T(8,128)(2,1)} %refs_5_.5, bf16[2,128,128]{2,1,0:T(8,128)(2,1)} %refs_6_.5, bf16[2,128,512]{2,1,0:T(8,128)(2,1)} %refs_7_.7, ...), custom_call_target="tpu_custom_call" | custom-call | flops 300000000 | bytes 1500000 | tf_op jit(solution)/shard_map/forward_first/pallas_call | solution.py:427
  7.9 0.0 copy-start.9
  8.0 0.0 copy-start.8
  8.0 6.3 %collective-permute-start = (bf16[4,64,128]{2,1,0:T(8,128)(2,1)}, bf16[4,64,128]{2,1,0:T(8,128)(2,1)S(1)}, u32[]{:S(2)}, u32[]{:S(2)}) collective-permute-start(bf16[4,64,128]{2,1,0:T(8,128)(2,1)} %get-tuple-element.36), channel_id=1, source_target_pairs={{0,248},{1,249},{2,250},{3,251},{4,252},{5,253},{6,254},{7,255},{8... | collective-permute-start | bytes 196616 | tf_op jit(solution)/shard_map/ppermute | solution.py:388
  14.3 1.8 %forward_next.1 = (bf16[4,64,128]{2,1,0:T(8,128)(2,1)S(1)}, bf16[4,64,128]{2,1,0:T(8,128)(2,1)S(1)}) custom-call(bf16[8,128,128]{2,1,0:T(8,128)(2,1)S(1)} %copy-done, bf16[2,128,384]{2,1,0:T(8,128)(2,1)S(1)} %copy-done.2, bf16[2,128,128]{2,1,0:T(8,128)(2,1)S(1)} %copy-done.3, bf16[2,128,512]{2,1,0:T(8,128)(2,1)S(1)} %copy-done.4, ...), custom_call_target="tpu_custom_call" | custom-call | flops 300000000 | bytes 1500000 | tf_op jit(solution)/shard_map/forward_next/pallas_call | solution.py:440
  16.0 0.8 collective-permute-start.3
  16.8 0.0 collective-permute-done.refs_1_.refs_2_
  16.8 0.0 collective-permute-done.1.refs_3_.refs_5_
  16.8 2.8 %collective-permute-start.2 = (bf16[16,8,128]{2,1,0:T(8,128)(2,1)S(1)}, bf16[16,8,128]{2,1,0:T(8,128)(2,1)S(1)}, u32[]{:S(2)}, u32[]{:S(2)}) collective-permute-start(bf16[16,8,128]{2,1,0:T(8,128)(2,1)S(1)} %pad_maximum_fusion), channel_id=1, source_target_pairs={{0,7},{1,0},{2,1},{3,2},{4,3},{5,4},{6,5},{7,6},{8,15},{9,8},{10,9... | collective-permute-start | bytes 98312 | tf_op jit(solution)/shard_map/ppermute | solution.py:388
  19.7 3.1 %backward_second.1 = (bf16[448,128]{1,0:T(8,128)(2,1)S(1)}, f32[1792,128]{1,0:T(8,128)S(1)}) custom-call(bf16[4,64,128]{2,1,0:T(8,128)(2,1)S(1)} %copy-done.8, bf16[4,64,128]{2,1,0:T(8,128)(2,1)S(1)} %collective-permute-done.refs_1_.refs_2_, bf16[8,128,128]{2,1,0:T(8,128)(2,1)S(1)} %copy-done.6, ...), custom_call_target="tpu_custom_call" | custom-call | flops 700000000 | bytes 3000000 | tf_op jit(solution)/shard_map/backward_second/pallas_call | solution.py:453
  22.8 0.0 collective-permute-done.3.refs_3_
  22.8 0.0 collective-permute-done.2.refs_6_
  22.8 3.6 %backward_third.1 = (bf16[4,128,128]{2,1,0:T(8,128)(2,1)S(1)}, bf16[4,128,128]{2,1,0:T(8,128)(2,1)S(1)}, bf16[4,8,128]{2,1,0:T(8,128)(2,1)S(1)}, f32[1792,128]{1,0:T(8,128)S(1)}) custom-call(bf16[4,64,128]{2,1,0:T(8,128)(2,1)S(1)} %copy-done.8, bf16[4,64,128]{2,1,0:T(8,128)(2,1)S(1)} %get-tuple-element.35.refs_1_, ...), custom_call_target="tpu_custom_call" | custom-call | flops 800000000 | bytes 3000000 | tf_op jit(solution)/shard_map/backward_third/pallas_call | solution.py:464
  26.4 3.5 %collective-permute-start.4 = (bf16[4,128,128]{2,1,0:T(8,128)(2,1)S(1)}, bf16[4,128,128]{2,1,0:T(8,128)(2,1)S(1)}, u32[]{:S(2)}, u32[]{:S(2)}) collective-permute-start(bf16[4,128,128]{2,1,0:T(8,128)(2,1)S(1)} %get-tuple-element.45), channel_id=1, source_target_pairs={{0,8},{1,9},{2,10},{3,11},{4,12},{5,13},{6,14},{7,15},{8,16},{9,17... | collective-permute-start | bytes 393224 | tf_op jit(solution)/shard_map/ppermute | solution.py:388
  30.0 1.2 %keep_first.2.refs_3_ = bf16[512,1152]{1,0:T(8,128)(2,1)S(1)} custom-call(bf16[8,128,128]{2,1,0:T(8,128)(2,1)S(1)} %copy-done, bf16[2,128,384]{2,1,0:T(8,128)(2,1)S(1)} %copy-done.2, bf16[2,128,128]{2,1,0:T(8,128)(2,1)S(1)} %copy-done.3, f32[2,2,128]{2,1,0:T(2,128)S(1)} %copy-done.7, f32[2,4,64,64]{3,2,1,0:T(8,128)S(1)} %copy-done.1), custom_call_target="tpu_custom_call" | custom-call | flops 300000000 | bytes 2000000 | tf_op jit(solution)/shard_map/keep_first/pallas_call | solution.py:477
  31.2 0.7 collective-permute-done.4.refs_1_
  31.9 0.1 collective-permute-start.5
  32.0 1.5 %keep_first.3.refs_4_ = bf16[512,1152]{1,0:T(8,128)(2,1)S(1)} custom-call(bf16[8,128,128]{2,1,0:T(8,128)(2,1)S(1)} %copy-done, bf16[2,128,384]{2,1,0:T(8,128)(2,1)S(1)} %copy-done.2, bf16[2,128,128]{2,1,0:T(8,128)(2,1)S(1)} %copy-done.3, f32[2,2,128]{2,1,0:T(2,128)S(1)} %copy-done.7, f32[2,4,64,64]{3,2,1,0:T(8,128)S(1)} %copy-done.1), custom_call_target="tpu_custom_call" | custom-call | flops 300000000 | bytes 2000000 | tf_op jit(solution)/shard_map/keep_first/pallas_call | solution.py:477
  33.5 3.2 %collective-permute-done.5.refs_2_ = bf16[8,8,128]{2,1,0:T(8,128)(2,1)S(1)} collective-permute-done((bf16[8,8,128]{2,1,0:T(8,128)(2,1)S(1)}, bf16[8,8,128]{2,1,0:T(8,128)(2,1)S(1)}, u32[]{:S(2)}, u32[]{:S(2)}) %collective-permute-start.5) | collective-permute-done | bytes 16416 | tf_op jit(solution)/shard_map/ppermute | solution.py:388
  36.7 5.2 %backward_first.1 = (bf16[8,128,128]{2,1,0:T(8,128)(2,1)}, f32[1792,128]{1,0:T(8,128)S(1)}, bf16[1792,128]{1,0:T(8,128)(2,1)S(1)}) custom-call(bf16[4,128,128]{2,1,0:T(8,128)(2,1)S(1)} %get-tuple-element.44.refs_0_, bf16[4,128,128]{2,1,0:T(8,128)(2,1)S(1)} %collective-permute-done.4.refs_1_, bf16[8,8,128]{2,1,0:T(8,128)(2,1)S(1)} %collective-permute-done.5.refs_2_, ...), custom_call_target="tpu_custom_call" | custom-call | flops 1500000000 | bytes 4000000 | tf_op jit(solution)/shard_map/backward_first/pallas_call | solution.py:492
  41.9 4.9 %collective-permute-start.6 = (bf16[1792,128]{1,0:T(8,128)(2,1)S(1)}, bf16[1792,128]{1,0:T(8,128)(2,1)S(1)}, u32[]{:S(2)}, u32[]{:S(2)}) collective-permute-start(bf16[1792,128]{1,0:T(8,128)(2,1)S(1)} %get-tuple-element.54), channel_id=1, source_target_pairs={{0,8},{8,0},{1,9},{9,1},{2,10},{10,2},{3,11},{11,3},{4,12},{12,4},... | collective-permute-start | bytes 1376264 | tf_op jit(solution)/shard_map/ppermute | solution.py:392
  46.8 1.4 %collective-permute-done.6 = bf16[1792,128]{1,0:T(8,128)(2,1)S(1)} collective-permute-done((bf16[1792,128]{1,0:T(8,128)(2,1)S(1)}, bf16[1792,128]{1,0:T(8,128)(2,1)S(1)}, u32[]{:S(2)}, u32[]{:S(2)}) %collective-permute-start.6) | collective-permute-done | bytes 458784 | tf_op jit(solution)/shard_map/ppermute | solution.py:392
  48.3 0.1 add_convert_fusion
  48.4 12.9 %all_to_all.15 = bf16[16,112,128]{2,1,0:T(8,128)(2,1)S(1)} all-to-all(bf16[16,112,128]{2,1,0:T(8,128)(2,1)S(1)} %bitcast.5), channel_id=1, replica_groups=mesh['z'=8,'yh'=2,'core'=2,'x'=4,'yl'=2] {'yh','x','yl'}, dimensions={0} | all-to-all | bytes 917504 | tf_op jit(solution)/shard_map/all_to_all | solution.py:397
  61.3 0.1 reduce_sum.24
  61.4 11.5 %all_to_all.16 = bf16[8,112,128]{2,1,0:T(8,128)(2,1)S(1)} all-to-all(bf16[8,112,128]{2,1,0:T(8,128)(2,1)S(1)} %broadcast_in_dim.4), channel_id=1, replica_groups=mesh['z'=8,'yh'=2,'core'=2,'x'=4,'yl'=2] {'z'}, dimensions={0} | all-to-all | bytes 458752 | tf_op jit(solution)/shard_map/all_to_all | solution.py:402
  72.9 0.1 broadcast_in_dim.5
  73.0 11.6 %all_to_all.17 = bf16[16,112,128]{2,1,0:T(8,128)(2,1)S(1)} all-to-all(bf16[16,112,128]{2,1,0:T(8,128)(2,1)S(1)} %broadcast_in_dim.5), channel_id=1, replica_groups=mesh['z'=8,'yh'=2,'core'=2,'x'=4,'yl'=2] {'yh','x','yl'}, dimensions={0} | all-to-all | bytes 917504 | tf_op jit(solution)/shard_map/all_to_all | solution.py:402
  84.6 4.3 %collective-permute-start.7 = (bf16[1792,128]{1,0:T(8,128)(2,1)S(1)}, bf16[1792,128]{1,0:T(8,128)(2,1)S(1)}, u32[]{:S(2)}, u32[]{:S(2)}) collective-permute-start(bf16[1792,128]{1,0:T(8,128)(2,1)S(1)} %bitcast.3), channel_id=1, source_target_pairs={{0,8},{8,0},{1,9},{9,1},{2,10},{10,2},{3,11},{11,3},{4,12},{12,4},... | collective-permute-start | bytes 1376264 | tf_op jit(solution)/shard_map/ppermute | solution.py:392
  89.0 1.4 %collective-permute-done.7.other_ref = bf16[1792,128]{1,0:T(8,128)(2,1)S(1)} collective-permute-done((bf16[1792,128]{1,0:T(8,128)(2,1)S(1)}, bf16[1792,128]{1,0:T(8,128)(2,1)S(1)}, u32[]{:S(2)}, u32[]{:S(2)}) %collective-permute-start.7) | collective-permute-done | bytes 458784 | tf_op jit(solution)/shard_map/ppermute | solution.py:392
  90.4 1.4 %unpack.1 = (f32[2,128,384]{2,1,0:T(8,128)}, f32[2,128,128]{2,1,0:T(8,128)}, f32[2,128,512]{2,1,0:T(8,128)}, f32[2,512,128]{2,1,0:T(8,128)}, f32[2,2,128]{2,1,0:T(2,128)}, /*index=5*/f32[2,4,64,64]{3,2,1,0:T(8,128)}) custom-call(s32[1]{0:T(128)} %bitcast.refs_11_.core_ref, bf16[1792,128]{1,0:T(8,128)(2,1)S(1)} %bitcast.4, ...), custom_call_target="tpu_custom_call" | custom-call | flops 1000000 | bytes 4000000 | tf_op jit(solution)/shard_map/unpack/pallas_call | solution.py:507
  (25 shorter events, 0.1 us)
Async XLA Ops:
  0.6 19.1 %copy-start.6 = (bf16[8,128,128]{2,1,0:T(8,128)(2,1)S(1)}, bf16[8,128,128]{2,1,0:T(8,128)(2,1)}, u32[]{:S(2)}) copy-start(bf16[8,128,128]{2,1,0:T(8,128)(2,1)} %refs_4_.5) | copy-start | bytes 786436
  0.6 13.6 %copy-start.7 = (f32[2,2,128]{2,1,0:T(2,128)S(1)}, f32[2,2,128]{2,1,0:T(2,128)}, u32[]{:S(2)}) copy-start(f32[2,2,128]{2,1,0:T(2,128)} %refs_9_.5) | copy-start | bytes 6148
  0.7 13.6 %copy-start.3 = (bf16[2,128,128]{2,1,0:T(8,128)(2,1)S(1)}, bf16[2,128,128]{2,1,0:T(8,128)(2,1)}, u32[]{:S(2)}) copy-start(bf16[2,128,128]{2,1,0:T(8,128)(2,1)} %refs_6_.5) | copy-start | bytes 196612
  0.7 13.6 %copy-start.2 = (bf16[2,128,384]{2,1,0:T(8,128)(2,1)S(1)}, bf16[2,128,384]{2,1,0:T(8,128)(2,1)}, u32[]{:S(2)}) copy-start(bf16[2,128,384]{2,1,0:T(8,128)(2,1)} %refs_5_.5) | copy-start | bytes 589828
  0.7 13.6 %copy-start.1 = (f32[2,4,64,64]{3,2,1,0:T(8,128)S(1)}, f32[2,4,64,64]{3,2,1,0:T(8,128)}, u32[]{:S(2)}) copy-start(f32[2,4,64,64]{3,2,1,0:T(8,128)} %bias_ref.5) | copy-start | bytes 393220
  0.7 13.6 %copy-start.5 = (bf16[2,512,128]{2,1,0:T(8,128)(2,1)S(1)}, bf16[2,512,128]{2,1,0:T(8,128)(2,1)}, u32[]{:S(2)}) copy-start(bf16[2,512,128]{2,1,0:T(8,128)(2,1)} %refs_8_.5) | copy-start | bytes 786436
  0.7 13.6 %copy-start.4 = (bf16[2,128,512]{2,1,0:T(8,128)(2,1)S(1)}, bf16[2,128,512]{2,1,0:T(8,128)(2,1)}, u32[]{:S(2)}) copy-start(bf16[2,128,512]{2,1,0:T(8,128)(2,1)} %refs_7_.7) | copy-start | bytes 786436
  0.7 13.6 %copy-start = (bf16[8,128,128]{2,1,0:T(8,128)(2,1)S(1)}, bf16[8,128,128]{2,1,0:T(8,128)(2,1)}, u32[]{:S(2)}) copy-start(bf16[8,128,128]{2,1,0:T(8,128)(2,1)} %x_ref.5) | copy-start | bytes 786436
  0.7 16.1 %collective-permute-start.1 = (bf16[8,128,128]{2,1,0:T(8,128)(2,1)}, bf16[8,128,128]{2,1,0:T(8,128)(2,1)S(1)}, u32[]{:S(2)}, u32[]{:S(2)}) collective-permute-start(bf16[8,128,128]{2,1,0:T(8,128)(2,1)} %refs_4_.5), channel_id=1, source_target_pairs={{0,248},{1,249},{2,250},{3,251},{4,252},{5,253},{6,254},{7,255},{8... | collective-permute-start | bytes 786440 | tf_op jit(solution)/shard_map/ppermute | solution.py:388
  7.9 8.9 %copy-start.9 = (bf16[8,8,128]{2,1,0:T(8,128)(2,1)S(1)}, bf16[8,8,128]{2,1,0:T(8,128)(2,1)}, u32[]{:S(2)}) copy-start(bf16[8,8,128]{2,1,0:T(8,128)(2,1)} %get-tuple-element.37) | copy-start | bytes 49156
  8.0 11.7 %copy-start.8 = (bf16[4,64,128]{2,1,0:T(8,128)(2,1)S(1)}, bf16[4,64,128]{2,1,0:T(8,128)(2,1)}, u32[]{:S(2)}) copy-start(bf16[4,64,128]{2,1,0:T(8,128)(2,1)} %get-tuple-element.34.refs_0_) | copy-start | bytes 196612
  8.0 8.8 %collective-permute-start = (bf16[4,64,128]{2,1,0:T(8,128)(2,1)}, bf16[4,64,128]{2,1,0:T(8,128)(2,1)S(1)}, u32[]{:S(2)}, u32[]{:S(2)}) collective-permute-start(bf16[4,64,128]{2,1,0:T(8,128)(2,1)} %get-tuple-element.36), channel_id=1, source_target_pairs={{0,248},{1,249},{2,250},{3,251},{4,252},{5,253},{6,254},{7,255},{8... | collective-permute-start | bytes 196616 | tf_op jit(solution)/shard_map/ppermute | solution.py:388
  16.0 6.8 %collective-permute-start.3 = (bf16[4,64,128]{2,1,0:T(8,128)(2,1)S(1)}, bf16[4,64,128]{2,1,0:T(8,128)(2,1)S(1)}, u32[]{:S(2)}, u32[]{:S(2)}) collective-permute-start(bf16[4,64,128]{2,1,0:T(8,128)(2,1)S(1)} %get-tuple-element.38), channel_id=1, source_target_pairs={{0,248},{1,249},{2,250},{3,251},{4,252},{5,253},{6,254},{7,255},{8... | collective-permute-start | bytes 196616 | tf_op jit(solution)/shard_map/ppermute | solution.py:388
  16.8 6.0 %collective-permute-start.2 = (bf16[16,8,128]{2,1,0:T(8,128)(2,1)S(1)}, bf16[16,8,128]{2,1,0:T(8,128)(2,1)S(1)}, u32[]{:S(2)}, u32[]{:S(2)}) collective-permute-start(bf16[16,8,128]{2,1,0:T(8,128)(2,1)S(1)} %pad_maximum_fusion), channel_id=1, source_target_pairs={{0,7},{1,0},{2,1},{3,2},{4,3},{5,4},{6,5},{7,6},{8,15},{9,8},{10,9... | collective-permute-start | bytes 98312 | tf_op jit(solution)/shard_map/ppermute | solution.py:388
  26.4 5.5 %collective-permute-start.4 = (bf16[4,128,128]{2,1,0:T(8,128)(2,1)S(1)}, bf16[4,128,128]{2,1,0:T(8,128)(2,1)S(1)}, u32[]{:S(2)}, u32[]{:S(2)}) collective-permute-start(bf16[4,128,128]{2,1,0:T(8,128)(2,1)S(1)} %get-tuple-element.45), channel_id=1, source_target_pairs={{0,8},{1,9},{2,10},{3,11},{4,12},{5,13},{6,14},{7,15},{8,16},{9,17... | collective-permute-start | bytes 393224 | tf_op jit(solution)/shard_map/ppermute | solution.py:388
  31.9 4.8 %collective-permute-start.5 = (bf16[8,8,128]{2,1,0:T(8,128)(2,1)S(1)}, bf16[8,8,128]{2,1,0:T(8,128)(2,1)S(1)}, u32[]{:S(2)}, u32[]{:S(2)}) collective-permute-start(bf16[8,8,128]{2,1,0:T(8,128)(2,1)S(1)} %pad_maximum_fusion.1), channel_id=1, source_target_pairs={{0,1},{1,2},{2,3},{3,4},{4,5},{5,6},{6,7},{7,0},{8,9},{9,10},{10,1... | collective-permute-start | bytes 49160 | tf_op jit(solution)/shard_map/ppermute | solution.py:388
  41.9 6.3 %collective-permute-start.6 = (bf16[1792,128]{1,0:T(8,128)(2,1)S(1)}, bf16[1792,128]{1,0:T(8,128)(2,1)S(1)}, u32[]{:S(2)}, u32[]{:S(2)}) collective-permute-start(bf16[1792,128]{1,0:T(8,128)(2,1)S(1)} %get-tuple-element.54), channel_id=1, source_target_pairs={{0,8},{8,0},{1,9},{9,1},{2,10},{10,2},{3,11},{11,3},{4,12},{12,4},... | collective-permute-start | bytes 1376264 | tf_op jit(solution)/shard_map/ppermute | solution.py:392
  84.6 5.8 %collective-permute-start.7 = (bf16[1792,128]{1,0:T(8,128)(2,1)S(1)}, bf16[1792,128]{1,0:T(8,128)(2,1)S(1)}, u32[]{:S(2)}, u32[]{:S(2)}) collective-permute-start(bf16[1792,128]{1,0:T(8,128)(2,1)S(1)} %bitcast.3), channel_id=1, source_target_pairs={{0,8},{8,0},{1,9},{9,1},{2,10},{10,2},{3,11},{11,3},{4,12},{12,4},... | collective-permute-start | bytes 1376264 | tf_op jit(solution)/shard_map/ppermute | solution.py:392

commit v7 on v6

--- a/solution.py
+++ b/solution.py
@@ -160,8 +160,8 @@
     return h, (hat1, inv1, a1, p, o, hat2, inv2, a2), qkv
 
 
-def backward(gy, kept, qkv, w_qkv, w_proj, w_up, w_down, g1, g2, mask, group):
-    hat1, inv1, a1, p, o, hat2, inv2, a2 = kept
+def backward(gy, kept, w_qkv, w_proj, w_up, w_down, g1, g2, mask, group):
+    hat1, inv1, a1, p, o, hat2, inv2, a2, qkv = kept
     m, slope = gelu_and_slope(nn(a2, w_up))
     m = m.astype(BF16)
     du = (nt(gy, w_down) * slope).astype(BF16)
@@ -248,12 +248,12 @@
 def next_kernel(x_ref, w_qkv_ref, w_proj_ref, w_up_ref, w_down_ref, gain_ref, bias_ref, top_ref, low_ref):
     wide = x_ref.shape[1] // 2
     parts = [at(ref, 0) for ref in (w_qkv_ref, w_proj_ref, w_up_ref, w_down_ref, gain_ref, bias_ref)]
-    tile = first_half(x_ref[:, wide:], 4, *parts)
+    tile = first_half(x_ref[:, wide:], 8, *parts)
     top_ref[...] = tile[:HALF].astype(BF16)
     low_ref[...] = tile[HALF:].astype(BF16)
 
 
-KEPT = (CH, CH, CH, HEADS * LEN, CH, CH, CH, CH)
+KEPT = (CH, CH, CH, HEADS * LEN, CH, CH, CH, CH, 3 * CH)
 
 
 def kept_slices():
@@ -264,7 +264,8 @@
 def keep_kernel(part, x_ref, w_qkv_ref, w_proj_ref, gain_ref, bias_ref, kept_ref):
     wide = x_ref.shape[1] // 2
     x = to_windows(x_ref[:, part * wide : (part + 1) * wide].astype(F32))
-    _, kept, _ = forward(x, at(w_qkv_ref, 0), at(w_proj_ref, 0), at(gain_ref, 0), at(bias_ref, 0), head_mask(), (8, 2)[part])
+    _, kept, qkv = forward(x, at(w_qkv_ref, 0), at(w_proj_ref, 0), at(gain_ref, 0), at(bias_ref, 0), head_mask(), 8)
+    kept += (qkv,)
     for place, value, width in zip(kept_slices(), kept, KEPT):
         kept_ref[:, place] = jnp.broadcast_to(value, (x.shape[0], width)).astype(BF16)
 
@@ -276,7 +277,7 @@
     )
     w_qkv, w_proj, w_up, w_down = w_qkv_ref[1], w_proj_ref[1], w_up_ref[1], w_down_ref[1]
     g1, g2 = gain_ref[1, 0:1], gain_ref[1, 1:2]
-    return backward(to_windows(gy).astype(BF16), kept, qkv, w_qkv, w_proj, w_up, w_down, g1, g2, mask, group)
+    return backward(to_windows(gy).astype(BF16), (*kept, qkv), w_qkv, w_proj, w_up, w_down, g1, g2, mask, group)
 
 
 def second_kernel(*refs):
@@ -296,7 +297,7 @@
 
 def third_kernel(*refs):
     low_a_ref, low_b_ref, below_a_ref, below_b_ref, g_own_ref, g_below_ref, edge_ref = refs[:7]
-    weights, (dx_ref, old_ref, dtop_ref, dlow_ref, dedge_ref, pack_ref, frame_ref) = refs[7:13], refs[13:]
+    weights, (dx_ref, old_ref, dtop_ref, dlow_ref, dedge_ref, dcorner_ref, pack_ref, frame_ref) = refs[7:13], refs[13:]
     wide, cols = low_a_ref.shape[1], g_own_ref.shape[1]
     span = cols - wide + WIN
     frame_ref[0:HALF, 0:WIN] = low_a_ref[:, wide - WIN :].astype(F32)
@@ -317,14 +318,16 @@
     dtop_ref[...] = tile[:HALF].astype(BF16)
     dlow_ref[...] = tile[HALF:].astype(BF16)
     dedge_ref[...] = tile[:HALF, cols - WIN :].astype(BF16)
+    dcorner_ref[...] = tile[HALF:, cols - WIN :].astype(BF16)
 
 
 def last_kernel(*refs):
-    (own, above, left), kept_refs, refs = refs[:3], refs[3:5], refs[5:]
+    (own, above, left, corner), kept_refs, refs = refs[:4], refs[4:6], refs[6:]
     w_qkv_ref, w_proj_ref, w_up_ref, w_down_ref, gain_ref, other_ref, core_ref = refs[:7]
     dx_ref, keep_ref, send_ref, frame_ref, pack_ref = refs[7:]
     cols = own.shape[1]
-    frame_ref[:, 0:WIN] = left[...].astype(F32)
+    frame_ref[HALF:, 0:WIN] = left[...].astype(F32)
+    frame_ref[0:HALF, 0:WIN] = corner[...].astype(F32)
     first = frame_ref[:, HALF:WIN]
     frame_ref[:, 0:HALF] = first
     frame_ref[HALF:, HALF : HALF + cols] = own[...].astype(F32)
@@ -334,7 +337,7 @@
     kept = [v.astype(F32) if i in (0, 1, 5, 6) else v for i, v in enumerate(kept)]
     g1, g2 = gain_ref[0, 0:1], gain_ref[0, 1:2]
     dx, grads, bias, gain1, gain2 = backward(
-        gy, kept, nn(kept[2], w_qkv_ref[0]).astype(BF16), w_qkv_ref[0], w_proj_ref[0], w_up_ref[0], w_down_ref[0], g1, g2, head_mask(), 4
+        gy, kept, w_qkv_ref[0], w_proj_ref[0], w_up_ref[0], w_down_ref[0], g1, g2, head_mask(), 16
     )
     dx_ref[...] = from_windows(dx).astype(BF16)
     pack(pack_ref, grads, bias, gain1, gain2)
@@ -422,6 +425,7 @@
 
     wide = cols // 2
     part_a = WIN * (wide - WIN)
+    small = jax.ShapeDtypeStruct((HALF, WIN, CH), BF16)
     side = jax.ShapeDtypeStruct((HALF, wide, CH), BF16)
     corner = jax.ShapeDtypeStruct((WIN, WIN, CH), BF16)
     top_a, low_a, edge_own = pl.pallas_call(
@@ -461,17 +465,17 @@
         name="backward_second",
     )(low_a, below_a, cotangent, g_below, *weights)
     edge, below_b, dx_a = lax.optimization_barrier((edge, below_b, dx_a))
-    d_top, d_low, d_edge, pack_two = pl.pallas_call(
+    d_top, d_low, d_edge, d_corner, pack_two = pl.pallas_call(
         third_kernel,
-        out_shape=(half, half, jax.ShapeDtypeStruct((HALF, WIN, CH), BF16), packed),
+        out_shape=(half, half, small, small, packed),
         in_specs=vmem(15),
-        out_specs=vmem(4),
+        out_specs=vmem(5),
         scratch_shapes=[frame],
         compiler_params=params,
         cost_estimate=cost(800_000_000, 3_000_000),
         name="backward_third",
     )(low_a, low_b, below_a, below_b, cotangent, g_below, edge, *weights, dx_a, pack_a)
-    d_above = shift(d_low, 1, 0)
+    d_above, d_left, d_corner = shift(d_low, 1, 0), shift(d_edge, 0, 1), shift(d_corner, 1, 1)
     kept = []
     for part in range(2):
         made = pl.pallas_call(
@@ -483,11 +487,6 @@
             cost_estimate=cost(300_000_000, 2_000_000),
             name="keep_first",
         )(latent, w_qkv, w_proj, gains, attn_bias)
-        if part == 0:
-            d_above, made = lax.optimization_barrier((d_above, made))
-            d_left = shift(jnp.concatenate([d_above[:, cols - WIN :], d_edge], axis=0), 0, 1)
-        else:
-            d_left, made = lax.optimization_barrier((d_left, made))
         kept.append(made)
     dx, keep, send = pl.pallas_call(
         last_kernel,
@@ -496,13 +495,13 @@
             packed,
             jax.ShapeDtypeStruct((ROWS, CH), BF16),
         ),
-        in_specs=vmem(11) + [pl.BlockSpec(memory_space=pltpu.SMEM)],
+        in_specs=vmem(12) + [pl.BlockSpec(memory_space=pltpu.SMEM)],
         out_specs=vmem(3),
         scratch_shapes=[frame, pltpu.VMEM((ROWS, CH), F32)],
         compiler_params=params,
         cost_estimate=cost(1_500_000_000, 4_000_000),
         name="backward_first",
-    )(d_top, d_above, d_left, *kept, *weights[:5], pack_two, core)
+    )(d_top, d_above, d_left, d_corner, *kept, *weights[:5], pack_two, core)
     parts = sum_over_devices(keep, send)
     qkv, proj, up, down, gain, bias = pl.pallas_call(
         unpack_kernel,

time: 92 us -> 95.5 us (1.038)
  local copies, waits for them, and re-layouts: 0.15 us -> 4.97 us
  starting transfers between devices: 26 us -> 22.1 us
    unnamed x20 -> x30, local copies, waits for them, and re-layouts: 0.05 us -> 4.87 us
    ppermute x2, starting transfers between devices: 9.21 us -> 5.36 us  [swap_core(): return lax.ppermute(value, 'core', [(0, 1), (1, 0)])]
    ppermute x6 -> x7, waiting for transfers between devices: 3.92 us -> 4.31 us  [shift(): return lax.ppermute(value, AXES, pairs)]
    ppermute x6 -> x7, starting transfers between devices: 16.8 us -> 16.8 us  [shift(): return lax.ppermute(value, AXES, pairs)]
  transfers between devices with their start and end apart: 8 -> 9, of which waited for: 4 -> 4; matrix products, arithmetic and copies ran while one was open for 0% -> 1% of each run, Pallas kernels for 12% -> 12%
where the time goes in v7:
time: 95.5 us; the launch traced here: 95.1 us
  blocking collectives  36.6 us (38%)
  Pallas kernels  22.3 us (23%)
  starting transfers between devices  22.1 us (23%)
  waiting for transfers between devices  7.19 us (8%)
  local copies, waits for them, and re-layouts  4.97 us (5%)
  other arithmetic  0.96 us (1%)
    all_to_all x2, blocking collectives, collect(): return lax.all_to_all(spread, axis, 0, 0)  23.7 us
    ppermute x7, starting transfers between devices, shift(): return lax.ppermute(value, AXES, pairs)  16.8 us
    all_to_all x1, blocking collectives, scatter_sum(): return jnp.sum(lax.all_to_all(pieces, axis, 0, 0).astype(F32), axis=0)  12.9 us
    pallas_call x1, Pallas kernels, body(): pl.pallas_call(last_kernel, out_shape=(jax.ShapeDtypeStruct(latent.shape,...  5.54 us
    ppermute x2, starting transfers between devices, swap_core(): return lax.ppermute(value, 'core', [(0, 1), (1, 0)])  5.36 us
    unnamed x30, local copies, waits for them, and re-layouts  4.87 us
    ppermute x7, waiting for transfers between devices, shift(): return lax.ppermute(value, AXES, pairs)  4.31 us
    pallas_call x1, Pallas kernels, body(): pl.pallas_call(third_kernel, out_shape=(half, half, small, small, packed)...  4.16 us
  transfers between devices with their start and end apart: 9, of which 4 were waited for; matrix products, arithmetic and copies ran while one was open for 1% of the time, Pallas kernels for 12%

profile of v7, /device:TPU:1, one launch (start us, length us, event | category | flops | bytes accessed | tf_op | source)
XLA Modules:
  0.0 95.1 jit_solution(14280612804682980693)
XLA Ops:
  0.7 3.3 %collective-permute-start.1 = (bf16[8,128,128]{2,1,0:T(8,128)(2,1)}, bf16[8,128,128]{2,1,0:T(8,128)(2,1)S(1)}, u32[]{:S(2)}, u32[]{:S(2)}) collective-permute-start(bf16[8,128,128]{2,1,0:T(8,128)(2,1)} %refs_4_.5), channel_id=1, source_target_pairs={{0,248},{1,249},{2,250},{3,251},{4,252},{5,253},{6,254},{7,255},{8... | collective-permute-start | bytes 786440 | tf_op jit(solution)/shard_map/ppermute | solution.py:391
  4.0 3.9 %forward_first.1 = (bf16[4,64,128]{2,1,0:T(8,128)(2,1)}, bf16[4,64,128]{2,1,0:T(8,128)(2,1)}, bf16[8,8,128]{2,1,0:T(8,128)(2,1)}) custom-call(bf16[8,128,128]{2,1,0:T(8,128)(2,1)} %x_ref.5, bf16[2,128,384]{2,1,0:T(8,128)(2,1)} %refs_6_.5, bf16[2,128,128]{2,1,0:T(8,128)(2,1)} %refs_7_.7, bf16[2,128,512]{2,1,0:T(8,128)(2,1)} %refs_8_.5, ...), custom_call_target="tpu_custom_call" | custom-call | flops 300000000 | bytes 1500000 | tf_op jit(solution)/shard_map/forward_first/pallas_call | solution.py:431
  7.9 6.3 %collective-permute-start = (bf16[4,64,128]{2,1,0:T(8,128)(2,1)}, bf16[4,64,128]{2,1,0:T(8,128)(2,1)S(1)}, u32[]{:S(2)}, u32[]{:S(2)}) collective-permute-start(bf16[4,64,128]{2,1,0:T(8,128)(2,1)} %get-tuple-element.33), channel_id=1, source_target_pairs={{0,248},{1,249},{2,250},{3,251},{4,252},{5,253},{6,254},{7,255},{8... | collective-permute-start | bytes 196616 | tf_op jit(solution)/shard_map/ppermute | solution.py:391
  14.3 1.8 %forward_next.1 = (bf16[4,64,128]{2,1,0:T(8,128)(2,1)S(1)}, bf16[4,64,128]{2,1,0:T(8,128)(2,1)S(1)}) custom-call(bf16[8,128,128]{2,1,0:T(8,128)(2,1)S(1)} %copy-done, bf16[2,128,384]{2,1,0:T(8,128)(2,1)S(1)} %copy-done.2, bf16[2,128,128]{2,1,0:T(8,128)(2,1)S(1)} %copy-done.3, bf16[2,128,512]{2,1,0:T(8,128)(2,1)S(1)} %copy-done.4, ...), custom_call_target="tpu_custom_call" | custom-call | flops 300000000 | bytes 1500000 | tf_op jit(solution)/shard_map/forward_next/pallas_call | solution.py:444
  16.0 0.8 collective-permute-start.3
  16.8 0.7 pad_maximum_fusion
  17.5 2.6 %collective-permute-start.2 = (bf16[16,8,128]{2,1,0:T(8,128)(2,1)S(1)}, bf16[16,8,128]{2,1,0:T(8,128)(2,1)S(1)}, u32[]{:S(2)}, u32[]{:S(2)}) collective-permute-start(bf16[16,8,128]{2,1,0:T(8,128)(2,1)S(1)} %pad_maximum_fusion), channel_id=1, source_target_pairs={{0,7},{1,0},{2,1},{3,2},{4,3},{5,4},{6,5},{7,6},{8,15},{9,8},{10,9... | collective-permute-start | bytes 98312 | tf_op jit(solution)/shard_map/ppermute | solution.py:391
  20.1 0.8 copy-done.10
  21.0 3.1 %backward_second.1 = (bf16[448,128]{1,0:T(8,128)(2,1)S(1)}, f32[1792,128]{1,0:T(8,128)S(1)}) custom-call(bf16[4,64,128]{2,1,0:T(8,128)(2,1)S(1)} %copy-done.10, bf16[4,64,128]{2,1,0:T(8,128)(2,1)S(1)} %collective-permute-done.refs_1_.refs_2_, bf16[8,128,128]{2,1,0:T(8,128)(2,1)S(1)} %copy-done.8, ...), custom_call_target="tpu_custom_call" | custom-call | flops 700000000 | bytes 3000000 | tf_op jit(solution)/shard_map/backward_second/pallas_call | solution.py:457
  24.1 4.2 %backward_third.1 = (bf16[4,128,128]{2,1,0:T(8,128)(2,1)S(1)}, bf16[4,128,128]{2,1,0:T(8,128)(2,1)S(1)}, bf16[4,8,128]{2,1,0:T(8,128)(2,1)}, bf16[4,8,128]{2,1,0:T(8,128)(2,1)S(1)}, f32[1792,128]{1,0:T(8,128)S(1)}) custom-call(bf16[4,64,128]{2,1,0:T(8,128)(2,1)S(1)} %copy-done.10, bf16[4,64,128]{2,1,0:T(8,128)(2,1)S(1)} %get-tuple-element.32.refs_1_, ...), custom_call_target="tpu_custom_call" | custom-call | flops 800000000 | bytes 3000000 | tf_op jit(solution)/shard_map/backward_third/pallas_call | solution.py:468
  28.3 3.5 %collective-permute-start.4 = (bf16[4,128,128]{2,1,0:T(8,128)(2,1)S(1)}, bf16[4,128,128]{2,1,0:T(8,128)(2,1)}, u32[]{:S(2)}, u32[]{:S(2)}) collective-permute-start(bf16[4,128,128]{2,1,0:T(8,128)(2,1)S(1)} %get-tuple-element.42), channel_id=1, source_target_pairs={{0,8},{1,9},{2,10},{3,11},{4,12},{5,13},{6,14},{7,15},{8,16},{9,17... | collective-permute-start | bytes 393224 | tf_op jit(solution)/shard_map/ppermute | solution.py:391
  31.7 1.2 %keep_first.3.refs_5_ = bf16[512,1536]{1,0:T(8,128)(2,1)S(1)} custom-call(bf16[8,128,128]{2,1,0:T(8,128)(2,1)S(1)} %copy-done, bf16[2,128,384]{2,1,0:T(8,128)(2,1)S(1)} %copy-done.2, bf16[2,128,128]{2,1,0:T(8,128)(2,1)S(1)} %copy-done.3, f32[2,2,128]{2,1,0:T(2,128)S(1)} %copy-done.9, f32[2,4,64,64]{3,2,1,0:T(8,128)S(1)} %copy-done.1), custom_call_target="tpu_custom_call" | custom-call | flops 300000000 | bytes 2000000 | tf_op jit(solution)/shard_map/keep_first/pallas_call | solution.py:481
  33.0 0.1 collective-permute-start.5
  33.1 0.3 collective-permute-start.6
  33.4 1.2 %keep_first.2.refs_4_ = bf16[512,1536]{1,0:T(8,128)(2,1)S(1)} custom-call(bf16[8,128,128]{2,1,0:T(8,128)(2,1)S(1)} %copy-done, bf16[2,128,384]{2,1,0:T(8,128)(2,1)S(1)} %copy-done.2, bf16[2,128,128]{2,1,0:T(8,128)(2,1)S(1)} %copy-done.3, f32[2,2,128]{2,1,0:T(2,128)S(1)} %copy-done.9, f32[2,4,64,64]{3,2,1,0:T(8,128)S(1)} %copy-done.1), custom_call_target="tpu_custom_call" | custom-call | flops 300000000 | bytes 2000000 | tf_op jit(solution)/shard_map/keep_first/pallas_call | solution.py:481
  34.6 3.6 %collective-permute-done.5.refs_2_ = bf16[4,8,128]{2,1,0:T(8,128)(2,1)} collective-permute-done((bf16[4,8,128]{2,1,0:T(8,128)(2,1)}, bf16[4,8,128]{2,1,0:T(8,128)(2,1)}, u32[]{:S(2)}, u32[]{:S(2)}) %collective-permute-start.5) | collective-permute-done | bytes 8224 | tf_op jit(solution)/shard_map/ppermute | solution.py:391
  38.3 0.7 collective-permute-done.6.refs_3_
  38.9 0.9 copy-done.5
  39.9 0.9 copy-done.7
  40.8 1.2 %copy-done.12 = f32[1792,128]{1,0:T(8,128)S(1)} copy-done((f32[1792,128]{1,0:T(8,128)S(1)}, f32[1792,128]{1,0:T(8,128)}, u32[]{:S(2)}) %copy-start.12) | copy-done | bytes 917528
  42.0 0.9 copy-done.14
  42.9 5.5 %backward_first.1 = (bf16[8,128,128]{2,1,0:T(8,128)(2,1)}, f32[1792,128]{1,0:T(8,128)S(1)}, bf16[1792,128]{1,0:T(8,128)(2,1)S(1)}) custom-call(bf16[4,128,128]{2,1,0:T(8,128)(2,1)S(1)} %copy-done.14, bf16[4,128,128]{2,1,0:T(8,128)(2,1)} %collective-permute-done.4.refs_1_, bf16[4,8,128]{2,1,0:T(8,128)(2,1)} %collective-permute-done.5.refs_2_, ...), custom_call_target="tpu_custom_call" | custom-call | flops 1500000000 | bytes 4000000 | tf_op jit(solution)/shard_map/backward_first/pallas_call | solution.py:491
  48.5 0.8 collective-permute-start.7
  49.3 1.4 %collective-permute-done.7 = bf16[1792,128]{1,0:T(8,128)(2,1)S(1)} collective-permute-done((bf16[1792,128]{1,0:T(8,128)(2,1)S(1)}, bf16[1792,128]{1,0:T(8,128)(2,1)S(1)}, u32[]{:S(2)}, u32[]{:S(2)}) %collective-permute-start.7) | collective-permute-done | bytes 458784 | tf_op jit(solution)/shard_map/ppermute | solution.py:395
  50.7 0.1 add_convert_fusion
  50.8 12.9 %all_to_all.15 = bf16[16,112,128]{2,1,0:T(8,128)(2,1)S(1)} all-to-all(bf16[16,112,128]{2,1,0:T(8,128)(2,1)S(1)} %bitcast.5), channel_id=1, replica_groups=mesh['z'=8,'yh'=2,'core'=2,'x'=4,'yl'=2] {'yh','x','yl'}, dimensions={0} | all-to-all | bytes 917504 | tf_op jit(solution)/shard_map/all_to_all | solution.py:400
  63.7 0.1 reduce_sum.24
  63.8 12.0 %all_to_all.16 = bf16[8,112,128]{2,1,0:T(8,128)(2,1)S(1)} all-to-all(bf16[8,112,128]{2,1,0:T(8,128)(2,1)S(1)} %broadcast_in_dim.4), channel_id=1, replica_groups=mesh['z'=8,'yh'=2,'core'=2,'x'=4,'yl'=2] {'z'}, dimensions={0} | all-to-all | bytes 458752 | tf_op jit(solution)/shard_map/all_to_all | solution.py:405
  76.0 11.7 %all_to_all.17 = bf16[16,112,128]{2,1,0:T(8,128)(2,1)S(1)} all-to-all(bf16[16,112,128]{2,1,0:T(8,128)(2,1)S(1)} %broadcast_in_dim.5), channel_id=1, replica_groups=mesh['z'=8,'yh'=2,'core'=2,'x'=4,'yl'=2] {'yh','x','yl'}, dimensions={0} | all-to-all | bytes 917504 | tf_op jit(solution)/shard_map/all_to_all | solution.py:405
  87.7 4.6 %collective-permute-start.8 = (bf16[1792,128]{1,0:T(8,128)(2,1)S(1)}, bf16[1792,128]{1,0:T(8,128)(2,1)S(1)}, u32[]{:S(2)}, u32[]{:S(2)}) collective-permute-start(bf16[1792,128]{1,0:T(8,128)(2,1)S(1)} %bitcast.3), channel_id=1, source_target_pairs={{0,8},{8,0},{1,9},{9,1},{2,10},{10,2},{3,11},{11,3},{4,12},{12,4},... | collective-permute-start | bytes 1376264 | tf_op jit(solution)/shard_map/ppermute | solution.py:395
  92.2 1.4 %collective-permute-done.8.other_ref = bf16[1792,128]{1,0:T(8,128)(2,1)S(1)} collective-permute-done((bf16[1792,128]{1,0:T(8,128)(2,1)S(1)}, bf16[1792,128]{1,0:T(8,128)(2,1)S(1)}, u32[]{:S(2)}, u32[]{:S(2)}) %collective-permute-start.8) | collective-permute-done | bytes 458784 | tf_op jit(solution)/shard_map/ppermute | solution.py:395
  93.7 1.4 %unpack.1 = (f32[2,128,384]{2,1,0:T(8,128)}, f32[2,128,128]{2,1,0:T(8,128)}, f32[2,128,512]{2,1,0:T(8,128)}, f32[2,512,128]{2,1,0:T(8,128)}, f32[2,2,128]{2,1,0:T(2,128)}, /*index=5*/f32[2,4,64,64]{3,2,1,0:T(8,128)}) custom-call(s32[1]{0:T(128)} %bitcast.refs_12_.core_ref, bf16[1792,128]{1,0:T(8,128)(2,1)S(1)} %bitcast.4, ...), custom_call_target="tpu_custom_call" | custom-call | flops 1000000 | bytes 4000000 | tf_op jit(solution)/shard_map/unpack/pallas_call | solution.py:506
  (35 shorter events, 0.2 us)
Async XLA Ops:
  0.6 19.5 %copy-start.8 = (bf16[8,128,128]{2,1,0:T(8,128)(2,1)S(1)}, bf16[8,128,128]{2,1,0:T(8,128)(2,1)}, u32[]{:S(2)}) copy-start(bf16[8,128,128]{2,1,0:T(8,128)(2,1)} %refs_4_.5) | copy-start | bytes 786436
  0.6 13.6 %copy-start.9 = (f32[2,2,128]{2,1,0:T(2,128)S(1)}, f32[2,2,128]{2,1,0:T(2,128)}, u32[]{:S(2)}) copy-start(f32[2,2,128]{2,1,0:T(2,128)} %refs_10_.3) | copy-start | bytes 6148
  0.7 13.6 %copy-start.3 = (bf16[2,128,128]{2,1,0:T(8,128)(2,1)S(1)}, bf16[2,128,128]{2,1,0:T(8,128)(2,1)}, u32[]{:S(2)}) copy-start(bf16[2,128,128]{2,1,0:T(8,128)(2,1)} %refs_7_.7) | copy-start | bytes 196612
  0.7 13.6 %copy-start.2 = (bf16[2,128,384]{2,1,0:T(8,128)(2,1)S(1)}, bf16[2,128,384]{2,1,0:T(8,128)(2,1)}, u32[]{:S(2)}) copy-start(bf16[2,128,384]{2,1,0:T(8,128)(2,1)} %refs_6_.5) | copy-start | bytes 589828
  0.7 13.5 %copy-start.1 = (f32[2,4,64,64]{3,2,1,0:T(8,128)S(1)}, f32[2,4,64,64]{3,2,1,0:T(8,128)}, u32[]{:S(2)}) copy-start(f32[2,4,64,64]{3,2,1,0:T(8,128)} %bias_ref.5) | copy-start | bytes 393220
  0.7 13.5 %copy-start.6 = (bf16[2,512,128]{2,1,0:T(8,128)(2,1)S(1)}, bf16[2,512,128]{2,1,0:T(8,128)(2,1)}, u32[]{:S(2)}) copy-start(bf16[2,512,128]{2,1,0:T(8,128)(2,1)} %refs_9_.5) | copy-start | bytes 786436
  0.7 13.5 %copy-start.4 = (bf16[2,128,512]{2,1,0:T(8,128)(2,1)S(1)}, bf16[2,128,512]{2,1,0:T(8,128)(2,1)}, u32[]{:S(2)}) copy-start(bf16[2,128,512]{2,1,0:T(8,128)(2,1)} %refs_8_.5) | copy-start | bytes 786436
  0.7 13.5 %copy-start = (bf16[8,128,128]{2,1,0:T(8,128)(2,1)S(1)}, bf16[8,128,128]{2,1,0:T(8,128)(2,1)}, u32[]{:S(2)}) copy-start(bf16[8,128,128]{2,1,0:T(8,128)(2,1)} %x_ref.5) | copy-start | bytes 786436
  0.7 16.1 %collective-permute-start.1 = (bf16[8,128,128]{2,1,0:T(8,128)(2,1)}, bf16[8,128,128]{2,1,0:T(8,128)(2,1)S(1)}, u32[]{:S(2)}, u32[]{:S(2)}) collective-permute-start(bf16[8,128,128]{2,1,0:T(8,128)(2,1)} %refs_4_.5), channel_id=1, source_target_pairs={{0,248},{1,249},{2,250},{3,251},{4,252},{5,253},{6,254},{7,255},{8... | collective-permute-start | bytes 786440 | tf_op jit(solution)/shard_map/ppermute | solution.py:391
  7.9 8.8 %collective-permute-start = (bf16[4,64,128]{2,1,0:T(8,128)(2,1)}, bf16[4,64,128]{2,1,0:T(8,128)(2,1)S(1)}, u32[]{:S(2)}, u32[]{:S(2)}) collective-permute-start(bf16[4,64,128]{2,1,0:T(8,128)(2,1)} %get-tuple-element.33), channel_id=1, source_target_pairs={{0,248},{1,249},{2,250},{3,251},{4,252},{5,253},{6,254},{7,255},{8... | collective-permute-start | bytes 196616 | tf_op jit(solution)/shard_map/ppermute | solution.py:391
  16.0 8.1 %collective-permute-start.3 = (bf16[4,64,128]{2,1,0:T(8,128)(2,1)S(1)}, bf16[4,64,128]{2,1,0:T(8,128)(2,1)S(1)}, u32[]{:S(2)}, u32[]{:S(2)}) collective-permute-start(bf16[4,64,128]{2,1,0:T(8,128)(2,1)S(1)} %get-tuple-element.35), channel_id=1, source_target_pairs={{0,248},{1,249},{2,250},{3,251},{4,252},{5,253},{6,254},{7,255},{8... | collective-permute-start | bytes 196616 | tf_op jit(solution)/shard_map/ppermute | solution.py:391
  17.5 6.5 %collective-permute-start.2 = (bf16[16,8,128]{2,1,0:T(8,128)(2,1)S(1)}, bf16[16,8,128]{2,1,0:T(8,128)(2,1)S(1)}, u32[]{:S(2)}, u32[]{:S(2)}) collective-permute-start(bf16[16,8,128]{2,1,0:T(8,128)(2,1)S(1)} %pad_maximum_fusion), channel_id=1, source_target_pairs={{0,7},{1,0},{2,1},{3,2},{4,3},{5,4},{6,5},{7,6},{8,15},{9,8},{10,9... | collective-permute-start | bytes 98312 | tf_op jit(solution)/shard_map/ppermute | solution.py:391
  20.1 0.8 copy-start.10
  28.2 6.4 %copy-start.11 = (f32[1792,128]{1,0:T(8,128)}, f32[1792,128]{1,0:T(8,128)S(1)}, u32[]{:S(2)}) copy-start(f32[1792,128]{1,0:T(8,128)S(1)} %get-tuple-element.45.refs_11_) | copy-start | bytes 2752516
  28.3 6.4 %copy-start.13 = (bf16[4,128,128]{2,1,0:T(8,128)(2,1)}, bf16[4,128,128]{2,1,0:T(8,128)(2,1)S(1)}, u32[]{:S(2)}) copy-start(bf16[4,128,128]{2,1,0:T(8,128)(2,1)S(1)} %get-tuple-element.41.refs_0_) | copy-start | bytes 393220
  28.3 10.7 %collective-permute-start.4 = (bf16[4,128,128]{2,1,0:T(8,128)(2,1)S(1)}, bf16[4,128,128]{2,1,0:T(8,128)(2,1)}, u32[]{:S(2)}, u32[]{:S(2)}) collective-permute-start(bf16[4,128,128]{2,1,0:T(8,128)(2,1)S(1)} %get-tuple-element.42), channel_id=1, source_target_pairs={{0,8},{1,9},{2,10},{3,11},{4,12},{5,13},{6,14},{7,15},{8,16},{9,17... | collective-permute-start | bytes 393224 | tf_op jit(solution)/shard_map/ppermute | solution.py:391
  33.0 5.3 %collective-permute-start.5 = (bf16[4,8,128]{2,1,0:T(8,128)(2,1)}, bf16[4,8,128]{2,1,0:T(8,128)(2,1)}, u32[]{:S(2)}, u32[]{:S(2)}) collective-permute-start(bf16[4,8,128]{2,1,0:T(8,128)(2,1)} %get-tuple-element.43), channel_id=1, source_target_pairs={{0,1},{1,2},{2,3},{3,4},{4,5},{5,6},{6,7},{7,0},{8,9},{9,10},{10,1... | collective-permute-start | bytes 24584 | tf_op jit(solution)/shard_map/ppermute | solution.py:391
  33.1 5.9 %collective-permute-start.6 = (bf16[4,8,128]{2,1,0:T(8,128)(2,1)S(1)}, bf16[4,8,128]{2,1,0:T(8,128)(2,1)}, u32[]{:S(2)}, u32[]{:S(2)}) collective-permute-start(bf16[4,8,128]{2,1,0:T(8,128)(2,1)S(1)} %get-tuple-element.44), channel_id=1, source_target_pairs={{0,9},{1,10},{2,11},{3,12},{4,13},{5,14},{6,15},{7,8},{8,17},{9,18... | collective-permute-start | bytes 24584 | tf_op jit(solution)/shard_map/ppermute | solution.py:391
  38.9 1.0 %copy-start.5 = (bf16[2,128,512]{2,1,0:T(8,128)(2,1)S(1)}, bf16[2,128,512]{2,1,0:T(8,128)(2,1)}, u32[]{:S(2)}) copy-start(bf16[2,128,512]{2,1,0:T(8,128)(2,1)} %refs_8_.5) | copy-start | bytes 786436
  39.9 0.9 copy-start.7
  40.8 1.2 %copy-start.12 = (f32[1792,128]{1,0:T(8,128)S(1)}, f32[1792,128]{1,0:T(8,128)}, u32[]{:S(2)}) copy-start(f32[1792,128]{1,0:T(8,128)} %copy-done.11) | copy-start | bytes 2752516
  42.0 0.9 copy-start.14
  48.5 2.2 %collective-permute-start.7 = (bf16[1792,128]{1,0:T(8,128)(2,1)S(1)}, bf16[1792,128]{1,0:T(8,128)(2,1)S(1)}, u32[]{:S(2)}, u32[]{:S(2)}) collective-permute-start(bf16[1792,128]{1,0:T(8,128)(2,1)S(1)} %get-tuple-element.48), channel_id=1, source_target_pairs={{0,8},{8,0},{1,9},{9,1},{2,10},{10,2},{3,11},{11,3},{4,12},{12,4},... | collective-permute-start | bytes 1376264 | tf_op jit(solution)/shard_map/ppermute | solution.py:395
  87.7 6.0 %collective-permute-start.8 = (bf16[1792,128]{1,0:T(8,128)(2,1)S(1)}, bf16[1792,128]{1,0:T(8,128)(2,1)S(1)}, u32[]{:S(2)}, u32[]{:S(2)}) collective-permute-start(bf16[1792,128]{1,0:T(8,128)(2,1)S(1)} %bitcast.3), channel_id=1, source_target_pairs={{0,8},{8,0},{1,9},{9,1},{2,10},{10,2},{3,11},{11,3},{4,12},{12,4},... | collective-permute-start | bytes 1376264 | tf_op jit(solution)/shard_map/ppermute | solution.py:395

commit v8 on v7

--- a/solution.py
+++ b/solution.py
@@ -17,7 +17,7 @@
 SCALE = (CH // HEADS) ** -0.5
 F32 = jnp.float32
 BF16 = jnp.bfloat16
-VMEM_LIMIT = 32 * 1024 * 1024
+VMEM_LIMIT = 16 * 1024 * 1024
 FIRST_LIMIT = 57 * 1000 * 1000
 
 ROW_QKV, ROW_PROJ, ROW_UP, ROW_DOWN, ROW_BIAS, ROW_GAIN, ROWS = 0, 384, 512, 1024, 1536, 1664, 1792
@@ -160,8 +160,8 @@
     return h, (hat1, inv1, a1, p, o, hat2, inv2, a2), qkv
 
 
-def backward(gy, kept, w_qkv, w_proj, w_up, w_down, g1, g2, mask, group):
-    hat1, inv1, a1, p, o, hat2, inv2, a2, qkv = kept
+def backward(gy, kept, qkv, w_qkv, w_proj, w_up, w_down, g1, g2, mask, group):
+    hat1, inv1, a1, p, o, hat2, inv2, a2 = kept
     m, slope = gelu_and_slope(nn(a2, w_up))
     m = m.astype(BF16)
     du = (nt(gy, w_down) * slope).astype(BF16)
@@ -253,7 +253,7 @@
     low_ref[...] = tile[HALF:].astype(BF16)
 
 
-KEPT = (CH, CH, CH, HEADS * LEN, CH, CH, CH, CH, 3 * CH)
+KEPT = (CH, CH, CH, HEADS * LEN, CH, CH, CH, CH)
 
 
 def kept_slices():
@@ -264,8 +264,7 @@
 def keep_kernel(part, x_ref, w_qkv_ref, w_proj_ref, gain_ref, bias_ref, kept_ref):
     wide = x_ref.shape[1] // 2
     x = to_windows(x_ref[:, part * wide : (part + 1) * wide].astype(F32))
-    _, kept, qkv = forward(x, at(w_qkv_ref, 0), at(w_proj_ref, 0), at(gain_ref, 0), at(bias_ref, 0), head_mask(), 8)
-    kept += (qkv,)
+    _, kept, _ = forward(x, at(w_qkv_ref, 0), at(w_proj_ref, 0), at(gain_ref, 0), at(bias_ref, 0), head_mask(), 8)
     for place, value, width in zip(kept_slices(), kept, KEPT):
         kept_ref[:, place] = jnp.broadcast_to(value, (x.shape[0], width)).astype(BF16)
 
@@ -277,7 +276,7 @@
     )
     w_qkv, w_proj, w_up, w_down = w_qkv_ref[1], w_proj_ref[1], w_up_ref[1], w_down_ref[1]
     g1, g2 = gain_ref[1, 0:1], gain_ref[1, 1:2]
-    return backward(to_windows(gy).astype(BF16), (*kept, qkv), w_qkv, w_proj, w_up, w_down, g1, g2, mask, group)
+    return backward(to_windows(gy).astype(BF16), kept, qkv, w_qkv, w_proj, w_up, w_down, g1, g2, mask, group)
 
 
 def second_kernel(*refs):
@@ -337,7 +336,7 @@
     kept = [v.astype(F32) if i in (0, 1, 5, 6) else v for i, v in enumerate(kept)]
     g1, g2 = gain_ref[0, 0:1], gain_ref[0, 1:2]
     dx, grads, bias, gain1, gain2 = backward(
-        gy, kept, w_qkv_ref[0], w_proj_ref[0], w_up_ref[0], w_down_ref[0], g1, g2, head_mask(), 16
+        gy, kept, nn(kept[2], w_qkv_ref[0]).astype(BF16), w_qkv_ref[0], w_proj_ref[0], w_up_ref[0], w_down_ref[0], g1, g2, head_mask(), 8
     )
     dx_ref[...] = from_windows(dx).astype(BF16)
     pack(pack_ref, grads, bias, gain1, gain2)

time: 95.5 us -> 92 us (0.963)
  local copies, waits for them, and re-layouts: 4.97 us -> 2.88 us
    unnamed x30 -> x28, local copies, waits for them, and re-layouts: 4.87 us -> 2.78 us
  transfers between devices with their start and end apart: 9 -> 9, of which waited for: 4 -> 4; matrix products, arithmetic and copies ran while one was open for 1% -> 0% of each run, Pallas kernels for 12% -> 12%
where the time goes in v8:
time: 92 us; the launch traced here: 91.8 us
  blocking collectives  36.9 us (40%)
  starting transfers between devices  22.3 us (24%)
  Pallas kernels  21.4 us (23%)
  waiting for transfers between devices  7.1 us (8%)
  local copies, waits for them, and re-layouts  2.88 us (3%)
    all_to_all x2, blocking collectives, collect(): return lax.all_to_all(spread, axis, 0, 0)  24.1 us
    ppermute x7, starting transfers between devices, shift(): return lax.ppermute(value, AXES, pairs)  17 us
    all_to_all x1, blocking collectives, scatter_sum(): return jnp.sum(lax.all_to_all(pieces, axis, 0, 0).astype(F32), axis=0)  12.8 us
    ppermute x2, starting transfers between devices, swap_core(): return lax.ppermute(value, 'core', [(0, 1), (1, 0)])  5.29 us
    pallas_call x1, Pallas kernels, body(): pl.pallas_call(last_kernel, out_shape=(jax.ShapeDtypeStruct(latent.shape,...  5.22 us
    ppermute x7, waiting for transfers between devices, shift(): return lax.ppermute(value, AXES, pairs)  4.21 us
    pallas_call x1, Pallas kernels, body(): pl.pallas_call(first_kernel, out_shape=(side, side, corner), in_specs=[pl...  3.9 us
    pallas_call x1, Pallas kernels, body(): pl.pallas_call(third_kernel, out_shape=(half, half, small, small, packed)...  3.59 us
  transfers between devices with their start and end apart: 9, of which 4 were waited for; matrix products, arithmetic and copies ran while one was open for 0% of the time, Pallas kernels for 12%

profile of v8, /device:TPU:1, one launch (start us, length us, event | category | flops | bytes accessed | tf_op | source)
XLA Modules:
  0.0 91.8 jit_solution(1219703129969448508)
XLA Ops:
  0.7 3.3 %collective-permute-start.1 = (bf16[8,128,128]{2,1,0:T(8,128)(2,1)}, bf16[8,128,128]{2,1,0:T(8,128)(2,1)S(1)}, u32[]{:S(2)}, u32[]{:S(2)}) collective-permute-start(bf16[8,128,128]{2,1,0:T(8,128)(2,1)} %refs_4_.5), channel_id=1, source_target_pairs={{0,248},{1,249},{2,250},{3,251},{4,252},{5,253},{6,254},{7,255},{8... | collective-permute-start | bytes 786440 | tf_op jit(solution)/shard_map/ppermute | solution.py:390
  4.0 3.9 %forward_first.1 = (bf16[4,64,128]{2,1,0:T(8,128)(2,1)}, bf16[4,64,128]{2,1,0:T(8,128)(2,1)}, bf16[8,8,128]{2,1,0:T(8,128)(2,1)}) custom-call(bf16[8,128,128]{2,1,0:T(8,128)(2,1)} %x_ref.5, bf16[2,128,384]{2,1,0:T(8,128)(2,1)} %refs_6_.5, bf16[2,128,128]{2,1,0:T(8,128)(2,1)} %refs_7_.7, bf16[2,128,512]{2,1,0:T(8,128)(2,1)} %refs_8_.5, ...), custom_call_target="tpu_custom_call" | custom-call | flops 300000000 | bytes 1500000 | tf_op jit(solution)/shard_map/forward_first/pallas_call | solution.py:430
  7.9 0.0 copy-start.13
  8.0 0.0 copy-start.8
  8.0 6.3 %collective-permute-start = (bf16[4,64,128]{2,1,0:T(8,128)(2,1)}, bf16[4,64,128]{2,1,0:T(8,128)(2,1)S(1)}, u32[]{:S(2)}, u32[]{:S(2)}) collective-permute-start(bf16[4,64,128]{2,1,0:T(8,128)(2,1)} %get-tuple-element.33), channel_id=1, source_target_pairs={{0,248},{1,249},{2,250},{3,251},{4,252},{5,253},{6,254},{7,255},{8... | collective-permute-start | bytes 196616 | tf_op jit(solution)/shard_map/ppermute | solution.py:390
  14.3 1.8 %forward_next.1 = (bf16[4,64,128]{2,1,0:T(8,128)(2,1)S(1)}, bf16[4,64,128]{2,1,0:T(8,128)(2,1)S(1)}) custom-call(bf16[8,128,128]{2,1,0:T(8,128)(2,1)S(1)} %copy-done, bf16[2,128,384]{2,1,0:T(8,128)(2,1)S(1)} %copy-done.2, bf16[2,128,128]{2,1,0:T(8,128)(2,1)S(1)} %copy-done.3, bf16[2,128,512]{2,1,0:T(8,128)(2,1)S(1)} %copy-done.4, ...), custom_call_target="tpu_custom_call" | custom-call | flops 300000000 | bytes 1500000 | tf_op jit(solution)/shard_map/forward_next/pallas_call | solution.py:443
  16.0 0.8 collective-permute-start.3
  16.8 2.9 %collective-permute-start.2 = (bf16[16,8,128]{2,1,0:T(8,128)(2,1)S(1)}, bf16[16,8,128]{2,1,0:T(8,128)(2,1)S(1)}, u32[]{:S(2)}, u32[]{:S(2)}) collective-permute-start(bf16[16,8,128]{2,1,0:T(8,128)(2,1)S(1)} %pad_maximum_fusion), channel_id=1, source_target_pairs={{0,7},{1,0},{2,1},{3,2},{4,3},{5,4},{6,5},{7,6},{8,15},{9,8},{10,9... | collective-permute-start | bytes 98312 | tf_op jit(solution)/shard_map/ppermute | solution.py:390
  19.7 3.1 %backward_second.1 = (bf16[448,128]{1,0:T(8,128)(2,1)S(1)}, f32[1792,128]{1,0:T(8,128)S(1)}) custom-call(bf16[4,64,128]{2,1,0:T(8,128)(2,1)S(1)} %copy-done.8, bf16[4,64,128]{2,1,0:T(8,128)(2,1)S(1)} %collective-permute-done.refs_1_.refs_2_, bf16[8,128,128]{2,1,0:T(8,128)(2,1)S(1)} %copy-done.6, ...), custom_call_target="tpu_custom_call" | custom-call | flops 700000000 | bytes 3000000 | tf_op jit(solution)/shard_map/backward_second/pallas_call | solution.py:456
  22.8 3.6 %backward_third.1 = (bf16[4,128,128]{2,1,0:T(8,128)(2,1)S(1)}, bf16[4,128,128]{2,1,0:T(8,128)(2,1)S(1)}, bf16[4,8,128]{2,1,0:T(8,128)(2,1)S(1)}, bf16[4,8,128]{2,1,0:T(8,128)(2,1)S(1)}, f32[1792,128]{1,0:T(8,128)S(1)}) custom-call(bf16[4,64,128]{2,1,0:T(8,128)(2,1)S(1)} %copy-done.8, bf16[4,64,128]{2,1,0:T(8,128)(2,1)S(1)} %get-tuple-element.32.refs_1_, ...), custom_call_target="tpu_custom_call" | custom-call | flops 800000000 | bytes 3000000 | tf_op jit(solution)/shard_map/backward_third/pallas_call | solution.py:467
  26.4 0.6 copy-done.11
  27.1 3.5 %collective-permute-start.4 = (bf16[4,128,128]{2,1,0:T(8,128)(2,1)S(1)}, bf16[4,128,128]{2,1,0:T(8,128)(2,1)S(1)}, u32[]{:S(2)}, u32[]{:S(2)}) collective-permute-start(bf16[4,128,128]{2,1,0:T(8,128)(2,1)S(1)} %get-tuple-element.42), channel_id=1, source_target_pairs={{0,8},{1,9},{2,10},{3,11},{4,12},{5,13},{6,14},{7,15},{8,16},{9,17... | collective-permute-start | bytes 393224 | tf_op jit(solution)/shard_map/ppermute | solution.py:390
  30.5 1.2 %keep_first.3.refs_5_ = bf16[512,1152]{1,0:T(8,128)(2,1)S(1)} custom-call(bf16[8,128,128]{2,1,0:T(8,128)(2,1)S(1)} %copy-done, bf16[2,128,384]{2,1,0:T(8,128)(2,1)S(1)} %copy-done.2, bf16[2,128,128]{2,1,0:T(8,128)(2,1)S(1)} %copy-done.3, f32[2,2,128]{2,1,0:T(2,128)S(1)} %copy-done.7, f32[2,4,64,64]{3,2,1,0:T(8,128)S(1)} %copy-done.1), custom_call_target="tpu_custom_call" | custom-call | flops 300000000 | bytes 2000000 | tf_op jit(solution)/shard_map/keep_first/pallas_call | solution.py:480
  31.8 0.1 collective-permute-start.5
  31.9 0.3 collective-permute-start.6
  32.2 1.2 %keep_first.2.refs_4_ = bf16[512,1152]{1,0:T(8,128)(2,1)S(1)} custom-call(bf16[8,128,128]{2,1,0:T(8,128)(2,1)S(1)} %copy-done, bf16[2,128,384]{2,1,0:T(8,128)(2,1)S(1)} %copy-done.2, bf16[2,128,128]{2,1,0:T(8,128)(2,1)S(1)} %copy-done.3, f32[2,2,128]{2,1,0:T(2,128)S(1)} %copy-done.7, f32[2,4,64,64]{3,2,1,0:T(8,128)S(1)} %copy-done.1), custom_call_target="tpu_custom_call" | custom-call | flops 300000000 | bytes 2000000 | tf_op jit(solution)/shard_map/keep_first/pallas_call | solution.py:480
  33.5 3.3 %collective-permute-done.5.refs_2_ = bf16[4,8,128]{2,1,0:T(8,128)(2,1)S(1)} collective-permute-done((bf16[4,8,128]{2,1,0:T(8,128)(2,1)S(1)}, bf16[4,8,128]{2,1,0:T(8,128)(2,1)S(1)}, u32[]{:S(2)}, u32[]{:S(2)}) %collective-permute-start.5) | collective-permute-done | bytes 8224 | tf_op jit(solution)/shard_map/ppermute | solution.py:390
  36.8 0.9 collective-permute-done.6.refs_3_
  37.7 1.2 %copy-done.10 = f32[1792,128]{1,0:T(8,128)S(1)} copy-done((f32[1792,128]{1,0:T(8,128)S(1)}, f32[1792,128]{1,0:T(8,128)}, u32[]{:S(2)}) %copy-start.10) | copy-done | bytes 917528
  38.9 0.9 copy-done.12
  39.8 5.2 %backward_first.1 = (bf16[8,128,128]{2,1,0:T(8,128)(2,1)}, f32[1792,128]{1,0:T(8,128)S(1)}, bf16[1792,128]{1,0:T(8,128)(2,1)S(1)}) custom-call(bf16[4,128,128]{2,1,0:T(8,128)(2,1)S(1)} %copy-done.12, bf16[4,128,128]{2,1,0:T(8,128)(2,1)S(1)} %collective-permute-done.4.refs_1_, bf16[4,8,128]{2,1,0:T(8,128)(2,1)S(1)} %collective-permute-done.5.refs_2_, ...), custom_call_target="tpu_custom_call" | custom-call | flops 1500000000 | bytes 4000000 | tf_op jit(solution)/shard_map/backward_first/pallas_call | solution.py:490
  45.0 0.8 collective-permute-start.7
  45.7 1.4 %collective-permute-done.7 = bf16[1792,128]{1,0:T(8,128)(2,1)S(1)} collective-permute-done((bf16[1792,128]{1,0:T(8,128)(2,1)S(1)}, bf16[1792,128]{1,0:T(8,128)(2,1)S(1)}, u32[]{:S(2)}, u32[]{:S(2)}) %collective-permute-start.7) | collective-permute-done | bytes 458784 | tf_op jit(solution)/shard_map/ppermute | solution.py:394
  47.2 0.1 add_convert_fusion
  47.3 12.8 %all_to_all.15 = bf16[16,112,128]{2,1,0:T(8,128)(2,1)S(1)} all-to-all(bf16[16,112,128]{2,1,0:T(8,128)(2,1)S(1)} %bitcast.5), channel_id=1, replica_groups=mesh['z'=8,'yh'=2,'core'=2,'x'=4,'yl'=2] {'yh','x','yl'}, dimensions={0} | all-to-all | bytes 917504 | tf_op jit(solution)/shard_map/all_to_all | solution.py:399
  60.0 0.1 reduce_sum.24
  60.2 12.5 %all_to_all.16 = bf16[8,112,128]{2,1,0:T(8,128)(2,1)S(1)} all-to-all(bf16[8,112,128]{2,1,0:T(8,128)(2,1)S(1)} %broadcast_in_dim.4), channel_id=1, replica_groups=mesh['z'=8,'yh'=2,'core'=2,'x'=4,'yl'=2] {'z'}, dimensions={0} | all-to-all | bytes 458752 | tf_op jit(solution)/shard_map/all_to_all | solution.py:404
  72.6 0.1 broadcast_in_dim.5
  72.7 11.7 %all_to_all.17 = bf16[16,112,128]{2,1,0:T(8,128)(2,1)S(1)} all-to-all(bf16[16,112,128]{2,1,0:T(8,128)(2,1)S(1)} %broadcast_in_dim.5), channel_id=1, replica_groups=mesh['z'=8,'yh'=2,'core'=2,'x'=4,'yl'=2] {'yh','x','yl'}, dimensions={0} | all-to-all | bytes 917504 | tf_op jit(solution)/shard_map/all_to_all | solution.py:404
  84.4 4.5 %collective-permute-start.8 = (bf16[1792,128]{1,0:T(8,128)(2,1)S(1)}, bf16[1792,128]{1,0:T(8,128)(2,1)S(1)}, u32[]{:S(2)}, u32[]{:S(2)}) collective-permute-start(bf16[1792,128]{1,0:T(8,128)(2,1)S(1)} %bitcast.3), channel_id=1, source_target_pairs={{0,8},{8,0},{1,9},{9,1},{2,10},{10,2},{3,11},{11,3},{4,12},{12,4},... | collective-permute-start | bytes 1376264 | tf_op jit(solution)/shard_map/ppermute | solution.py:394
  88.9 1.4 %collective-permute-done.8.other_ref = bf16[1792,128]{1,0:T(8,128)(2,1)S(1)} collective-permute-done((bf16[1792,128]{1,0:T(8,128)(2,1)S(1)}, bf16[1792,128]{1,0:T(8,128)(2,1)S(1)}, u32[]{:S(2)}, u32[]{:S(2)}) %collective-permute-start.8) | collective-permute-done | bytes 458784 | tf_op jit(solution)/shard_map/ppermute | solution.py:394
  90.4 1.4 %unpack.1 = (f32[2,128,384]{2,1,0:T(8,128)}, f32[2,128,128]{2,1,0:T(8,128)}, f32[2,128,512]{2,1,0:T(8,128)}, f32[2,512,128]{2,1,0:T(8,128)}, f32[2,2,128]{2,1,0:T(2,128)}, /*index=5*/f32[2,4,64,64]{3,2,1,0:T(8,128)}) custom-call(s32[1]{0:T(128)} %bitcast.refs_12_.core_ref, bf16[1792,128]{1,0:T(8,128)(2,1)S(1)} %bitcast.4, ...), custom_call_target="tpu_custom_call" | custom-call | flops 1000000 | bytes 4000000 | tf_op jit(solution)/shard_map/unpack/pallas_call | solution.py:505
  (33 shorter events, 0.1 us)
Async XLA Ops:
  0.6 19.1 %copy-start.6 = (bf16[8,128,128]{2,1,0:T(8,128)(2,1)S(1)}, bf16[8,128,128]{2,1,0:T(8,128)(2,1)}, u32[]{:S(2)}) copy-start(bf16[8,128,128]{2,1,0:T(8,128)(2,1)} %refs_4_.5) | copy-start | bytes 786436
  0.6 13.6 %copy-start.7 = (f32[2,2,128]{2,1,0:T(2,128)S(1)}, f32[2,2,128]{2,1,0:T(2,128)}, u32[]{:S(2)}) copy-start(f32[2,2,128]{2,1,0:T(2,128)} %refs_10_.3) | copy-start | bytes 6148
  0.7 13.6 %copy-start.3 = (bf16[2,128,128]{2,1,0:T(8,128)(2,1)S(1)}, bf16[2,128,128]{2,1,0:T(8,128)(2,1)}, u32[]{:S(2)}) copy-start(bf16[2,128,128]{2,1,0:T(8,128)(2,1)} %refs_7_.7) | copy-start | bytes 196612
  0.7 13.6 %copy-start.2 = (bf16[2,128,384]{2,1,0:T(8,128)(2,1)S(1)}, bf16[2,128,384]{2,1,0:T(8,128)(2,1)}, u32[]{:S(2)}) copy-start(bf16[2,128,384]{2,1,0:T(8,128)(2,1)} %refs_6_.5) | copy-start | bytes 589828
  0.7 13.6 %copy-start.1 = (f32[2,4,64,64]{3,2,1,0:T(8,128)S(1)}, f32[2,4,64,64]{3,2,1,0:T(8,128)}, u32[]{:S(2)}) copy-start(f32[2,4,64,64]{3,2,1,0:T(8,128)} %bias_ref.5) | copy-start | bytes 393220
  0.7 13.6 %copy-start.5 = (bf16[2,512,128]{2,1,0:T(8,128)(2,1)S(1)}, bf16[2,512,128]{2,1,0:T(8,128)(2,1)}, u32[]{:S(2)}) copy-start(bf16[2,512,128]{2,1,0:T(8,128)(2,1)} %refs_9_.5) | copy-start | bytes 786436
  0.7 13.6 %copy-start.4 = (bf16[2,128,512]{2,1,0:T(8,128)(2,1)S(1)}, bf16[2,128,512]{2,1,0:T(8,128)(2,1)}, u32[]{:S(2)}) copy-start(bf16[2,128,512]{2,1,0:T(8,128)(2,1)} %refs_8_.5) | copy-start | bytes 786436
  0.7 13.6 %copy-start = (bf16[8,128,128]{2,1,0:T(8,128)(2,1)S(1)}, bf16[8,128,128]{2,1,0:T(8,128)(2,1)}, u32[]{:S(2)}) copy-start(bf16[8,128,128]{2,1,0:T(8,128)(2,1)} %x_ref.5) | copy-start | bytes 786436
  0.7 16.1 %collective-permute-start.1 = (bf16[8,128,128]{2,1,0:T(8,128)(2,1)}, bf16[8,128,128]{2,1,0:T(8,128)(2,1)S(1)}, u32[]{:S(2)}, u32[]{:S(2)}) collective-permute-start(bf16[8,128,128]{2,1,0:T(8,128)(2,1)} %refs_4_.5), channel_id=1, source_target_pairs={{0,248},{1,249},{2,250},{3,251},{4,252},{5,253},{6,254},{7,255},{8... | collective-permute-start | bytes 786440 | tf_op jit(solution)/shard_map/ppermute | solution.py:390
  7.9 8.9 %copy-start.13 = (bf16[8,8,128]{2,1,0:T(8,128)(2,1)S(1)}, bf16[8,8,128]{2,1,0:T(8,128)(2,1)}, u32[]{:S(2)}) copy-start(bf16[8,8,128]{2,1,0:T(8,128)(2,1)} %get-tuple-element.34) | copy-start | bytes 49156
  8.0 11.7 %copy-start.8 = (bf16[4,64,128]{2,1,0:T(8,128)(2,1)S(1)}, bf16[4,64,128]{2,1,0:T(8,128)(2,1)}, u32[]{:S(2)}) copy-start(bf16[4,64,128]{2,1,0:T(8,128)(2,1)} %get-tuple-element.31.refs_0_) | copy-start | bytes 196612
  8.0 8.8 %collective-permute-start = (bf16[4,64,128]{2,1,0:T(8,128)(2,1)}, bf16[4,64,128]{2,1,0:T(8,128)(2,1)S(1)}, u32[]{:S(2)}, u32[]{:S(2)}) collective-permute-start(bf16[4,64,128]{2,1,0:T(8,128)(2,1)} %get-tuple-element.33), channel_id=1, source_target_pairs={{0,248},{1,249},{2,250},{3,251},{4,252},{5,253},{6,254},{7,255},{8... | collective-permute-start | bytes 196616 | tf_op jit(solution)/shard_map/ppermute | solution.py:390
  16.0 6.8 %collective-permute-start.3 = (bf16[4,64,128]{2,1,0:T(8,128)(2,1)S(1)}, bf16[4,64,128]{2,1,0:T(8,128)(2,1)S(1)}, u32[]{:S(2)}, u32[]{:S(2)}) collective-permute-start(bf16[4,64,128]{2,1,0:T(8,128)(2,1)S(1)} %get-tuple-element.35), channel_id=1, source_target_pairs={{0,248},{1,249},{2,250},{3,251},{4,252},{5,253},{6,254},{7,255},{8... | collective-permute-start | bytes 196616 | tf_op jit(solution)/shard_map/ppermute | solution.py:390
  16.8 6.0 %collective-permute-start.2 = (bf16[16,8,128]{2,1,0:T(8,128)(2,1)S(1)}, bf16[16,8,128]{2,1,0:T(8,128)(2,1)S(1)}, u32[]{:S(2)}, u32[]{:S(2)}) collective-permute-start(bf16[16,8,128]{2,1,0:T(8,128)(2,1)S(1)} %pad_maximum_fusion), channel_id=1, source_target_pairs={{0,7},{1,0},{2,1},{3,2},{4,3},{5,4},{6,5},{7,6},{8,15},{9,8},{10,9... | collective-permute-start | bytes 98312 | tf_op jit(solution)/shard_map/ppermute | solution.py:390
  26.4 0.7 copy-start.11
  27.1 6.4 %copy-start.9 = (f32[1792,128]{1,0:T(8,128)}, f32[1792,128]{1,0:T(8,128)S(1)}, u32[]{:S(2)}) copy-start(f32[1792,128]{1,0:T(8,128)S(1)} %get-tuple-element.45.refs_11_) | copy-start | bytes 2752516
  27.1 10.6 %collective-permute-start.4 = (bf16[4,128,128]{2,1,0:T(8,128)(2,1)S(1)}, bf16[4,128,128]{2,1,0:T(8,128)(2,1)S(1)}, u32[]{:S(2)}, u32[]{:S(2)}) collective-permute-start(bf16[4,128,128]{2,1,0:T(8,128)(2,1)S(1)} %get-tuple-element.42), channel_id=1, source_target_pairs={{0,8},{1,9},{2,10},{3,11},{4,12},{5,13},{6,14},{7,15},{8,16},{9,17... | collective-permute-start | bytes 393224 | tf_op jit(solution)/shard_map/ppermute | solution.py:390
  31.8 5.0 %collective-permute-start.5 = (bf16[4,8,128]{2,1,0:T(8,128)(2,1)S(1)}, bf16[4,8,128]{2,1,0:T(8,128)(2,1)S(1)}, u32[]{:S(2)}, u32[]{:S(2)}) collective-permute-start(bf16[4,8,128]{2,1,0:T(8,128)(2,1)S(1)} %get-tuple-element.43), channel_id=1, source_target_pairs={{0,1},{1,2},{2,3},{3,4},{4,5},{5,6},{6,7},{7,0},{8,9},{9,10},{10,1... | collective-permute-start | bytes 24584 | tf_op jit(solution)/shard_map/ppermute | solution.py:390
  31.9 5.8 %collective-permute-start.6 = (bf16[4,8,128]{2,1,0:T(8,128)(2,1)S(1)}, bf16[4,8,128]{2,1,0:T(8,128)(2,1)S(1)}, u32[]{:S(2)}, u32[]{:S(2)}) collective-permute-start(bf16[4,8,128]{2,1,0:T(8,128)(2,1)S(1)} %get-tuple-element.44), channel_id=1, source_target_pairs={{0,9},{1,10},{2,11},{3,12},{4,13},{5,14},{6,15},{7,8},{8,17},{9,18... | collective-permute-start | bytes 24584 | tf_op jit(solution)/shard_map/ppermute | solution.py:390
  37.7 1.2 %copy-start.10 = (f32[1792,128]{1,0:T(8,128)S(1)}, f32[1792,128]{1,0:T(8,128)}, u32[]{:S(2)}) copy-start(f32[1792,128]{1,0:T(8,128)} %copy-done.9) | copy-start | bytes 2752516
  38.9 0.9 copy-start.12
  45.0 2.2 %collective-permute-start.7 = (bf16[1792,128]{1,0:T(8,128)(2,1)S(1)}, bf16[1792,128]{1,0:T(8,128)(2,1)S(1)}, u32[]{:S(2)}, u32[]{:S(2)}) collective-permute-start(bf16[1792,128]{1,0:T(8,128)(2,1)S(1)} %get-tuple-element.48), channel_id=1, source_target_pairs={{0,8},{8,0},{1,9},{9,1},{2,10},{10,2},{3,11},{11,3},{4,12},{12,4},... | collective-permute-start | bytes 1376264 | tf_op jit(solution)/shard_map/ppermute | solution.py:394
  84.4 6.0 %collective-permute-start.8 = (bf16[1792,128]{1,0:T(8,128)(2,1)S(1)}, bf16[1792,128]{1,0:T(8,128)(2,1)S(1)}, u32[]{:S(2)}, u32[]{:S(2)}) collective-permute-start(bf16[1792,128]{1,0:T(8,128)(2,1)S(1)} %bitcast.3), channel_id=1, source_target_pairs={{0,8},{8,0},{1,9},{9,1},{2,10},{10,2},{3,11},{11,3},{4,12},{12,4},... | collective-permute-start | bytes 1376264 | tf_op jit(solution)/shard_map/ppermute | solution.py:394

commit v9 on v8

--- a/solution.py
+++ b/solution.py
@@ -261,7 +261,10 @@
     return [slice(start, start + width) for start, width in zip(starts, KEPT)]
 
 
-def keep_kernel(part, x_ref, w_qkv_ref, w_proj_ref, gain_ref, bias_ref, kept_ref):
+def keep_kernel(part, x_ref, w_qkv_ref, w_proj_ref, gain_ref, bias_ref, *refs):
+    kept_ref = refs[len(refs) // 2]
+    for source, target in zip(refs[: len(refs) // 2], refs[len(refs) // 2 + 1 :]):
+        target[...] = source[...]
     wide = x_ref.shape[1] // 2
     x = to_windows(x_ref[:, part * wide : (part + 1) * wide].astype(F32))
     _, kept, _ = forward(x, at(w_qkv_ref, 0), at(w_proj_ref, 0), at(gain_ref, 0), at(bias_ref, 0), head_mask(), 8)
@@ -353,24 +356,26 @@
         send_ref[...] = pack_ref[...].astype(BF16)
 
 
-def unpack_kernel(core_ref, own_ref, other_ref, *refs):
-    qkv_ref, proj_ref, up_ref, down_ref, gain_ref, bias_ref, whole_ref = refs
-    at = pl.multiple_of(core_ref[0] * ROWS, ROWS)
-    whole_ref[pl.ds(at, ROWS)] = own_ref[...].astype(F32)
-    whole_ref[pl.ds(ROWS - at, ROWS)] = other_ref[...].astype(F32)
-    for b in range(2):
-        at = b * ROWS
-        for j in range(3):
-            qkv_ref[b, :, CH * j : CH * (j + 1)] = whole_ref[at + ROW_QKV + CH * j : at + ROW_QKV + CH * (j + 1)]
-        proj_ref[b] = whole_ref[at + ROW_PROJ : at + ROW_PROJ + CH]
-        for j in range(4):
-            up_ref[b, :, CH * j : CH * (j + 1)] = whole_ref[at + ROW_UP + CH * j : at + ROW_UP + CH * (j + 1)]
-        down_ref[b] = whole_ref[at + ROW_DOWN : at + ROW_DOWN + FFN]
-        for j in range(2):
-            turned = whole_ref[at + ROW_BIAS + LEN * j : at + ROW_BIAS + LEN * (j + 1)].T
-            bias_ref[b, 2 * j] = turned[:LEN]
-            bias_ref[b, 2 * j + 1] = turned[LEN:]
-        gain_ref[b] = whole_ref[at + ROW_GAIN : at + ROW_GAIN + 2]
+def unpack_kernel(mine, core_ref, part_ref, *refs):
+    outs, places, sem = refs[-13:-7], refs[-7:-1], refs[-1]
+    qkv, proj, up, down, gain, bias = places
+    for j in range(3):
+        qkv[:, CH * j : CH * (j + 1)] = part_ref[ROW_QKV + CH * j : ROW_QKV + CH * (j + 1)].astype(F32)
+    proj[...] = part_ref[ROW_PROJ : ROW_PROJ + CH].astype(F32)
+    for j in range(4):
+        up[:, CH * j : CH * (j + 1)] = part_ref[ROW_UP + CH * j : ROW_UP + CH * (j + 1)].astype(F32)
+    down[...] = part_ref[ROW_DOWN : ROW_DOWN + FFN].astype(F32)
+    for j in range(2):
+        turned = part_ref[ROW_BIAS + LEN * j : ROW_BIAS + LEN * (j + 1)].astype(F32).T
+        bias[2 * j] = turned[:LEN]
+        bias[2 * j + 1] = turned[LEN:]
+    gain[...] = part_ref[ROW_GAIN : ROW_GAIN + 16].astype(F32)[0:2]
+    block = core_ref[0] if mine else 1 - core_ref[0]
+    copies = [pltpu.make_async_copy(a, b.at[block], sem.at[i]) for i, (a, b) in enumerate(zip(places, outs))]
+    for copy in copies:
+        copy.start()
+    for copy in copies:
+        copy.wait()
 
 
 def vmem(count):
@@ -475,18 +480,22 @@
         name="backward_third",
     )(low_a, low_b, below_a, below_b, cotangent, g_below, edge, *weights, dx_a, pack_a)
     d_above, d_left, d_corner = shift(d_low, 1, 0), shift(d_edge, 0, 1), shift(d_corner, 1, 1)
-    kept = []
-    for part in range(2):
-        made = pl.pallas_call(
+    passed = ()
+    for part, arrays in enumerate(((), (pack_two, d_top))):
+        arrays = (*passed, *arrays)
+        passed = pl.pallas_call(
             functools.partial(keep_kernel, part),
-            out_shape=jax.ShapeDtypeStruct((WIN * wide, sum(KEPT)), BF16),
-            in_specs=vmem(5),
-            out_specs=vmem(1)[0],
+            out_shape=(
+                jax.ShapeDtypeStruct((WIN * wide, sum(KEPT)), BF16),
+                *[jax.ShapeDtypeStruct(a.shape, a.dtype) for a in arrays],
+            ),
+            in_specs=vmem(5 + len(arrays)),
+            out_specs=vmem(1 + len(arrays)),
             compiler_params=params,
             cost_estimate=cost(300_000_000, 2_000_000),
             name="keep_first",
-        )(latent, w_qkv, w_proj, gains, attn_bias)
-        kept.append(made)
+        )(latent, w_qkv, w_proj, gains, attn_bias, *arrays)
+    kept_b, kept_a, pack_two, d_top = passed
     dx, keep, send = pl.pallas_call(
         last_kernel,
         out_shape=(
@@ -500,25 +509,25 @@
         compiler_params=params,
         cost_estimate=cost(1_500_000_000, 4_000_000),
         name="backward_first",
-    )(d_top, d_above, d_left, d_corner, *kept, *weights[:5], pack_two, core)
+    )(d_top, d_above, d_left, d_corner, kept_a, kept_b, *weights[:5], pack_two, core)
     parts = sum_over_devices(keep, send)
-    qkv, proj, up, down, gain, bias = pl.pallas_call(
-        unpack_kernel,
-        out_shape=(
-            jax.ShapeDtypeStruct((2, CH, 3 * CH), F32),
-            jax.ShapeDtypeStruct((2, CH, CH), F32),
-            jax.ShapeDtypeStruct((2, CH, FFN), F32),
-            jax.ShapeDtypeStruct((2, FFN, CH), F32),
-            jax.ShapeDtypeStruct((2, 2, CH), F32),
-            jax.ShapeDtypeStruct((2, HEADS, LEN, LEN), F32),
-        ),
-        in_specs=[pl.BlockSpec(memory_space=pltpu.SMEM)] + vmem(2),
-        out_specs=vmem(6),
-        scratch_shapes=[pltpu.VMEM((2 * ROWS, CH), F32)],
-        compiler_params=params,
-        cost_estimate=cost(1_000_000, 4_000_000),
-        name="unpack",
-    )(core, *parts)
+    shapes = ((CH, 3 * CH), (CH, CH), (CH, FFN), (FFN, CH), (2, CH), (HEADS, LEN, LEN))
+    outs = ()
+    for mine, part in zip((True, False), parts):
+        outs = pl.pallas_call(
+            functools.partial(unpack_kernel, mine),
+            out_shape=[jax.ShapeDtypeStruct((2, *shape), F32) for shape in shapes],
+            in_specs=[pl.BlockSpec(memory_space=pltpu.SMEM)]
+            + vmem(1)
+            + [pl.BlockSpec(memory_space=pl.ANY)] * len(outs),
+            out_specs=[pl.BlockSpec(memory_space=pl.ANY)] * 6,
+            scratch_shapes=[pltpu.VMEM(shape, F32) for shape in shapes] + [pltpu.SemaphoreType.DMA((6,))],
+            input_output_aliases={2 + i: i for i in range(len(outs))},
+            compiler_params=params,
+            cost_estimate=cost(1_000_000, 2_000_000),
+            name="unpack",
+        )(core, part, *outs)
+    qkv, proj, up, down, gain, bias = outs
     return dx, qkv, proj, up, down, gain, bias
 
 

time: 92 us -> 89.1 us (0.968)
  local copies, waits for them, and re-layouts: 2.88 us -> 0.15 us
  waiting for transfers between devices: 7.1 us -> 6.05 us
    unnamed x28 -> x20, local copies, waits for them, and re-layouts: 2.78 us -> 0.05 us
    ppermute x2, waiting for transfers between devices: 2.89 us -> 1.89 us  [swap_core(): return lax.ppermute(value, 'core', [(0, 1), (1, 0)])]
    pallas_call x3 -> x4, Pallas kernels: 3.88 us -> 4.53 us  [the longest x2 2.56 us: body(): pl.pallas_call(functools.partial(keep_kernel, part), out_shape=(jax.Shape...]
  transfers between devices with their start and end apart: 9 -> 9, of which waited for: 4 -> 4; matrix products, arithmetic and copies ran while one was open for 0% -> 0% of each run, Pallas kernels for 12% -> 14%
where the time goes in v9:
time: 89.1 us; the launch traced here: 88.9 us
  blocking collectives  36.9 us (41%)
  starting transfers between devices  22.4 us (25%)
  Pallas kernels  22.2 us (25%)
  waiting for transfers between devices  6.05 us (7%)
  between operations  1.06 us (1%)
    all_to_all x2, blocking collectives, collect(): return lax.all_to_all(spread, axis, 0, 0)  24.1 us
    ppermute x7, starting transfers between devices, shift(): return lax.ppermute(value, AXES, pairs)  17.1 us
    all_to_all x1, blocking collectives, scatter_sum(): return jnp.sum(lax.all_to_all(pieces, axis, 0, 0).astype(F32), axis=0)  12.8 us
    ppermute x2, starting transfers between devices, swap_core(): return lax.ppermute(value, 'core', [(0, 1), (1, 0)])  5.3 us
    pallas_call x1, Pallas kernels, body(): pl.pallas_call(last_kernel, out_shape=(jax.ShapeDtypeStruct(latent.shape,...  5.27 us
    ppermute x7, waiting for transfers between devices, shift(): return lax.ppermute(value, AXES, pairs)  4.16 us
    pallas_call x1, Pallas kernels, body(): pl.pallas_call(first_kernel, out_shape=(side, side, corner), in_specs=[pl...  3.9 us
    pallas_call x1, Pallas kernels, body(): pl.pallas_call(third_kernel, out_shape=(half, half, small, small, packed)...  3.59 us
  transfers between devices with their start and end apart: 9, of which 4 were waited for; matrix products, arithmetic and copies ran while one was open for 0% of the time, Pallas kernels for 14%

profile of v9, /device:TPU:1, one launch (start us, length us, event | category | flops | bytes accessed | tf_op | source)
XLA Modules:
  0.0 88.9 jit_solution(4272070918733462712)
XLA Ops:
  0.7 3.3 %collective-permute-start.1 = (bf16[8,128,128]{2,1,0:T(8,128)(2,1)}, bf16[8,128,128]{2,1,0:T(8,128)(2,1)S(1)}, u32[]{:S(2)}, u32[]{:S(2)}) collective-permute-start(bf16[8,128,128]{2,1,0:T(8,128)(2,1)} %refs_4_.5), channel_id=1, source_target_pairs={{0,248},{1,249},{2,250},{3,251},{4,252},{5,253},{6,254},{7,255},{8... | collective-permute-start | bytes 786440 | tf_op jit(solution)/shard_map/ppermute | solution.py:395
  4.0 3.9 %forward_first.1 = (bf16[4,64,128]{2,1,0:T(8,128)(2,1)}, bf16[4,64,128]{2,1,0:T(8,128)(2,1)}, bf16[8,8,128]{2,1,0:T(8,128)(2,1)}) custom-call(bf16[8,128,128]{2,1,0:T(8,128)(2,1)} %x_ref.5, bf16[2,128,384]{2,1,0:T(8,128)(2,1)} %refs_6_.5, bf16[2,128,128]{2,1,0:T(8,128)(2,1)} %refs_7_.7, bf16[2,128,512]{2,1,0:T(8,128)(2,1)} %refs_8_.5, ...), custom_call_target="tpu_custom_call" | custom-call | flops 300000000 | bytes 1500000 | tf_op jit(solution)/shard_map/forward_first/pallas_call | solution.py:435
  7.9 0.0 copy-start.9
  8.0 0.0 copy-start.8
  8.0 6.3 %collective-permute-start = (bf16[4,64,128]{2,1,0:T(8,128)(2,1)}, bf16[4,64,128]{2,1,0:T(8,128)(2,1)S(1)}, u32[]{:S(2)}, u32[]{:S(2)}) collective-permute-start(bf16[4,64,128]{2,1,0:T(8,128)(2,1)} %get-tuple-element.43), channel_id=1, source_target_pairs={{0,248},{1,249},{2,250},{3,251},{4,252},{5,253},{6,254},{7,255},{8... | collective-permute-start | bytes 196616 | tf_op jit(solution)/shard_map/ppermute | solution.py:395
  14.3 1.8 %forward_next.1 = (bf16[4,64,128]{2,1,0:T(8,128)(2,1)S(1)}, bf16[4,64,128]{2,1,0:T(8,128)(2,1)S(1)}) custom-call(bf16[8,128,128]{2,1,0:T(8,128)(2,1)S(1)} %copy-done, bf16[2,128,384]{2,1,0:T(8,128)(2,1)S(1)} %copy-done.2, bf16[2,128,128]{2,1,0:T(8,128)(2,1)S(1)} %copy-done.3, bf16[2,128,512]{2,1,0:T(8,128)(2,1)S(1)} %copy-done.4, ...), custom_call_target="tpu_custom_call" | custom-call | flops 300000000 | bytes 1500000 | tf_op jit(solution)/shard_map/forward_next/pallas_call | solution.py:448
  16.0 0.8 collective-permute-start.3
  16.8 0.0 collective-permute-done.refs_1_.refs_2_
  16.8 0.0 collective-permute-done.1.refs_3_.refs_5_
  16.8 2.8 %collective-permute-start.2 = (bf16[16,8,128]{2,1,0:T(8,128)(2,1)S(1)}, bf16[16,8,128]{2,1,0:T(8,128)(2,1)S(1)}, u32[]{:S(2)}, u32[]{:S(2)}) collective-permute-start(bf16[16,8,128]{2,1,0:T(8,128)(2,1)S(1)} %pad_maximum_fusion), channel_id=1, source_target_pairs={{0,7},{1,0},{2,1},{3,2},{4,3},{5,4},{6,5},{7,6},{8,15},{9,8},{10,9... | collective-permute-start | bytes 98312 | tf_op jit(solution)/shard_map/ppermute | solution.py:395
  19.7 3.1 %backward_second.1 = (bf16[448,128]{1,0:T(8,128)(2,1)S(1)}, f32[1792,128]{1,0:T(8,128)S(1)}) custom-call(bf16[4,64,128]{2,1,0:T(8,128)(2,1)S(1)} %copy-done.8, bf16[4,64,128]{2,1,0:T(8,128)(2,1)S(1)} %collective-permute-done.refs_1_.refs_2_, bf16[8,128,128]{2,1,0:T(8,128)(2,1)S(1)} %copy-done.6, ...), custom_call_target="tpu_custom_call" | custom-call | flops 700000000 | bytes 3000000 | tf_op jit(solution)/shard_map/backward_second/pallas_call | solution.py:461
  22.8 3.6 %backward_third.1 = (bf16[4,128,128]{2,1,0:T(8,128)(2,1)S(1)}, bf16[4,128,128]{2,1,0:T(8,128)(2,1)S(1)}, bf16[4,8,128]{2,1,0:T(8,128)(2,1)S(1)}, bf16[4,8,128]{2,1,0:T(8,128)(2,1)S(1)}, f32[1792,128]{1,0:T(8,128)S(1)}) custom-call(bf16[4,64,128]{2,1,0:T(8,128)(2,1)S(1)} %copy-done.8, bf16[4,64,128]{2,1,0:T(8,128)(2,1)S(1)} %get-tuple-element.42.refs_1_, ...), custom_call_target="tpu_custom_call" | custom-call | flops 800000000 | bytes 3000000 | tf_op jit(solution)/shard_map/backward_third/pallas_call | solution.py:472
  26.4 3.5 %collective-permute-start.4 = (bf16[4,128,128]{2,1,0:T(8,128)(2,1)S(1)}, bf16[4,128,128]{2,1,0:T(8,128)(2,1)S(1)}, u32[]{:S(2)}, u32[]{:S(2)}) collective-permute-start(bf16[4,128,128]{2,1,0:T(8,128)(2,1)S(1)} %get-tuple-element.54), channel_id=1, source_target_pairs={{0,8},{1,9},{2,10},{3,11},{4,12},{5,13},{6,14},{7,15},{8,16},{9,17... | collective-permute-start | bytes 393224 | tf_op jit(solution)/shard_map/ppermute | solution.py:395
  30.0 1.2 %keep_first.2.refs_0_ = bf16[512,1152]{1,0:T(8,128)(2,1)S(1)} custom-call(bf16[8,128,128]{2,1,0:T(8,128)(2,1)S(1)} %copy-done, bf16[2,128,384]{2,1,0:T(8,128)(2,1)S(1)} %copy-done.2, bf16[2,128,128]{2,1,0:T(8,128)(2,1)S(1)} %copy-done.3, f32[2,2,128]{2,1,0:T(2,128)S(1)} %copy-done.7, f32[2,4,64,64]{3,2,1,0:T(8,128)S(1)} %copy-done.1), custom_call_target="tpu_custom_call" | custom-call | flops 300000000 | bytes 2000000 | tf_op jit(solution)/shard_map/keep_first/pallas_call | solution.py:486
  31.2 0.1 collective-permute-start.5
  31.3 0.3 collective-permute-start.6
  31.6 1.3 %keep_first.3 = (bf16[512,1152]{1,0:T(8,128)(2,1)S(1)}, bf16[512,1152]{1,0:T(8,128)(2,1)S(1)}, f32[1792,128]{1,0:T(8,128)S(1)}, bf16[4,128,128]{2,1,0:T(8,128)(2,1)S(1)}) custom-call(bf16[8,128,128]{2,1,0:T(8,128)(2,1)S(1)} %copy-done, bf16[2,128,384]{2,1,0:T(8,128)(2,1)S(1)} %copy-done.2, bf16[2,128,128]{2,1,0:T(8,128)(2,1)S(1)} %copy-done.3, ...), custom_call_target="tpu_custom_call" | custom-call | flops 300000000 | bytes 2000000 | tf_op jit(solution)/shard_map/keep_first/pallas_call | solution.py:486
  32.9 3.3 %collective-permute-done.5.refs_2_ = bf16[4,8,128]{2,1,0:T(8,128)(2,1)S(1)} collective-permute-done((bf16[4,8,128]{2,1,0:T(8,128)(2,1)S(1)}, bf16[4,8,128]{2,1,0:T(8,128)(2,1)S(1)}, u32[]{:S(2)}, u32[]{:S(2)}) %collective-permute-start.5) | collective-permute-done | bytes 8224 | tf_op jit(solution)/shard_map/ppermute | solution.py:395
  36.2 0.9 collective-permute-done.6.refs_3_
  37.1 5.3 %backward_first.1 = (bf16[8,128,128]{2,1,0:T(8,128)(2,1)}, f32[1792,128]{1,0:T(8,128)S(1)}, bf16[1792,128]{1,0:T(8,128)(2,1)S(1)}) custom-call(bf16[4,128,128]{2,1,0:T(8,128)(2,1)S(1)} %get-tuple-element.53.refs_0_, bf16[4,128,128]{2,1,0:T(8,128)(2,1)S(1)} %collective-permute-done.4.refs_1_, bf16[4,8,128]{2,1,0:T(8,128)(2,1)S(1)} %collective-permute-done.5.refs_2_, ...), custom_call_target="tpu_custom_call" | custom-call | flops 1500000000 | bytes 4000000 | tf_op jit(solution)/shard_map/backward_first/pallas_call | solution.py:499
  42.4 0.8 collective-permute-start.7
  43.1 1.4 %collective-permute-done.7 = bf16[1792,128]{1,0:T(8,128)(2,1)S(1)} collective-permute-done((bf16[1792,128]{1,0:T(8,128)(2,1)S(1)}, bf16[1792,128]{1,0:T(8,128)(2,1)S(1)}, u32[]{:S(2)}, u32[]{:S(2)}) %collective-permute-start.7) | collective-permute-done | bytes 458784 | tf_op jit(solution)/shard_map/ppermute | solution.py:399
  44.6 0.1 add_convert_fusion
  44.7 12.8 %all_to_all.15 = bf16[16,112,128]{2,1,0:T(8,128)(2,1)S(1)} all-to-all(bf16[16,112,128]{2,1,0:T(8,128)(2,1)S(1)} %bitcast.5), channel_id=1, replica_groups=mesh['z'=8,'yh'=2,'core'=2,'x'=4,'yl'=2] {'yh','x','yl'}, dimensions={0} | all-to-all | bytes 917504 | tf_op jit(solution)/shard_map/all_to_all | solution.py:404
  57.4 0.1 reduce_sum.24
  57.5 12.4 %all_to_all.16 = bf16[8,112,128]{2,1,0:T(8,128)(2,1)S(1)} all-to-all(bf16[8,112,128]{2,1,0:T(8,128)(2,1)S(1)} %broadcast_in_dim.4), channel_id=1, replica_groups=mesh['z'=8,'yh'=2,'core'=2,'x'=4,'yl'=2] {'z'}, dimensions={0} | all-to-all | bytes 458752 | tf_op jit(solution)/shard_map/all_to_all | solution.py:409
  70.0 0.1 broadcast_in_dim.5
  70.1 11.7 %all_to_all.17 = bf16[16,112,128]{2,1,0:T(8,128)(2,1)S(1)} all-to-all(bf16[16,112,128]{2,1,0:T(8,128)(2,1)S(1)} %broadcast_in_dim.5), channel_id=1, replica_groups=mesh['z'=8,'yh'=2,'core'=2,'x'=4,'yl'=2] {'yh','x','yl'}, dimensions={0} | all-to-all | bytes 917504 | tf_op jit(solution)/shard_map/all_to_all | solution.py:409
  81.8 4.5 %collective-permute-start.8 = (bf16[1792,128]{1,0:T(8,128)(2,1)S(1)}, bf16[1792,128]{1,0:T(8,128)(2,1)S(1)}, u32[]{:S(2)}, u32[]{:S(2)}) collective-permute-start(bf16[1792,128]{1,0:T(8,128)(2,1)S(1)} %bitcast.3), channel_id=1, source_target_pairs={{0,8},{8,0},{1,9},{9,1},{2,10},{10,2},{3,11},{11,3},{4,12},{12,4},... | collective-permute-start | bytes 1376264 | tf_op jit(solution)/shard_map/ppermute | solution.py:399
  86.3 1.0 %unpack.2 = (f32[2,128,384]{2,1,0:T(8,128)}, f32[2,128,128]{2,1,0:T(8,128)}, f32[2,128,512]{2,1,0:T(8,128)}, f32[2,512,128]{2,1,0:T(8,128)}, f32[2,2,128]{2,1,0:T(2,128)}, /*index=5*/f32[2,4,64,64]{3,2,1,0:T(8,128)}) custom-call(s32[1]{0:T(128)} %bitcast.refs_12_.core_ref, bf16[1792,128]{1,0:T(8,128)(2,1)S(1)} %bitcast.4), custom_call_target="tpu_custom_call" | custom-call | flops 1000000 | bytes 2000000 | tf_op jit(solution)/shard_map/unpack/pallas_call | solution.py:517
  87.3 0.4 collective-permute-done.8.part_ref
  87.7 1.0 %unpack.3 = (f32[2,128,384]{2,1,0:T(8,128)}, f32[2,128,128]{2,1,0:T(8,128)}, f32[2,128,512]{2,1,0:T(8,128)}, f32[2,512,128]{2,1,0:T(8,128)}, f32[2,2,128]{2,1,0:T(2,128)}, /*index=5*/f32[2,4,64,64]{3,2,1,0:T(8,128)}) custom-call(s32[1]{0:T(128)} %bitcast.refs_12_.core_ref, ...), custom_call_target="tpu_custom_call", output_to_operand_aliasing={{0}: (2, {}), {1}: (3, {}), {2}: (4, {}), {3}: (5, {}), {4}... | custom-call | flops 1000000 | bytes 2000000 | tf_op jit(solution)/shard_map/unpack/pallas_call | solution.py:517
  (26 shorter events, 0.1 us)
Async XLA Ops:
  0.6 19.1 %copy-start.6 = (bf16[8,128,128]{2,1,0:T(8,128)(2,1)S(1)}, bf16[8,128,128]{2,1,0:T(8,128)(2,1)}, u32[]{:S(2)}) copy-start(bf16[8,128,128]{2,1,0:T(8,128)(2,1)} %refs_4_.5) | copy-start | bytes 786436
  0.6 13.6 %copy-start.2 = (bf16[2,128,384]{2,1,0:T(8,128)(2,1)S(1)}, bf16[2,128,384]{2,1,0:T(8,128)(2,1)}, u32[]{:S(2)}) copy-start(bf16[2,128,384]{2,1,0:T(8,128)(2,1)} %refs_6_.5) | copy-start | bytes 589828
  0.7 13.6 %copy-start.3 = (bf16[2,128,128]{2,1,0:T(8,128)(2,1)S(1)}, bf16[2,128,128]{2,1,0:T(8,128)(2,1)}, u32[]{:S(2)}) copy-start(bf16[2,128,128]{2,1,0:T(8,128)(2,1)} %refs_7_.7) | copy-start | bytes 196612
  0.7 13.6 %copy-start.4 = (bf16[2,128,512]{2,1,0:T(8,128)(2,1)S(1)}, bf16[2,128,512]{2,1,0:T(8,128)(2,1)}, u32[]{:S(2)}) copy-start(bf16[2,128,512]{2,1,0:T(8,128)(2,1)} %refs_8_.5) | copy-start | bytes 786436
  0.7 13.6 %copy-start.5 = (bf16[2,512,128]{2,1,0:T(8,128)(2,1)S(1)}, bf16[2,512,128]{2,1,0:T(8,128)(2,1)}, u32[]{:S(2)}) copy-start(bf16[2,512,128]{2,1,0:T(8,128)(2,1)} %refs_9_.5) | copy-start | bytes 786436
  0.7 13.6 %copy-start.7 = (f32[2,2,128]{2,1,0:T(2,128)S(1)}, f32[2,2,128]{2,1,0:T(2,128)}, u32[]{:S(2)}) copy-start(f32[2,2,128]{2,1,0:T(2,128)} %refs_10_.3) | copy-start | bytes 6148
  0.7 13.6 %copy-start.1 = (f32[2,4,64,64]{3,2,1,0:T(8,128)S(1)}, f32[2,4,64,64]{3,2,1,0:T(8,128)}, u32[]{:S(2)}) copy-start(f32[2,4,64,64]{3,2,1,0:T(8,128)} %bias_ref.5) | copy-start | bytes 393220
  0.7 13.6 %copy-start = (bf16[8,128,128]{2,1,0:T(8,128)(2,1)S(1)}, bf16[8,128,128]{2,1,0:T(8,128)(2,1)}, u32[]{:S(2)}) copy-start(bf16[8,128,128]{2,1,0:T(8,128)(2,1)} %x_ref.5) | copy-start | bytes 786436
  0.7 16.1 %collective-permute-start.1 = (bf16[8,128,128]{2,1,0:T(8,128)(2,1)}, bf16[8,128,128]{2,1,0:T(8,128)(2,1)S(1)}, u32[]{:S(2)}, u32[]{:S(2)}) collective-permute-start(bf16[8,128,128]{2,1,0:T(8,128)(2,1)} %refs_4_.5), channel_id=1, source_target_pairs={{0,248},{1,249},{2,250},{3,251},{4,252},{5,253},{6,254},{7,255},{8... | collective-permute-start | bytes 786440 | tf_op jit(solution)/shard_map/ppermute | solution.py:395
  7.9 8.9 %copy-start.9 = (bf16[8,8,128]{2,1,0:T(8,128)(2,1)S(1)}, bf16[8,8,128]{2,1,0:T(8,128)(2,1)}, u32[]{:S(2)}) copy-start(bf16[8,8,128]{2,1,0:T(8,128)(2,1)} %get-tuple-element.44) | copy-start | bytes 49156
  8.0 11.7 %copy-start.8 = (bf16[4,64,128]{2,1,0:T(8,128)(2,1)S(1)}, bf16[4,64,128]{2,1,0:T(8,128)(2,1)}, u32[]{:S(2)}) copy-start(bf16[4,64,128]{2,1,0:T(8,128)(2,1)} %get-tuple-element.41.refs_0_) | copy-start | bytes 196612
  8.0 8.8 %collective-permute-start = (bf16[4,64,128]{2,1,0:T(8,128)(2,1)}, bf16[4,64,128]{2,1,0:T(8,128)(2,1)S(1)}, u32[]{:S(2)}, u32[]{:S(2)}) collective-permute-start(bf16[4,64,128]{2,1,0:T(8,128)(2,1)} %get-tuple-element.43), channel_id=1, source_target_pairs={{0,248},{1,249},{2,250},{3,251},{4,252},{5,253},{6,254},{7,255},{8... | collective-permute-start | bytes 196616 | tf_op jit(solution)/shard_map/ppermute | solution.py:395
  16.0 6.8 %collective-permute-start.3 = (bf16[4,64,128]{2,1,0:T(8,128)(2,1)S(1)}, bf16[4,64,128]{2,1,0:T(8,128)(2,1)S(1)}, u32[]{:S(2)}, u32[]{:S(2)}) collective-permute-start(bf16[4,64,128]{2,1,0:T(8,128)(2,1)S(1)} %get-tuple-element.45), channel_id=1, source_target_pairs={{0,248},{1,249},{2,250},{3,251},{4,252},{5,253},{6,254},{7,255},{8... | collective-permute-start | bytes 196616 | tf_op jit(solution)/shard_map/ppermute | solution.py:395
  16.8 6.0 %collective-permute-start.2 = (bf16[16,8,128]{2,1,0:T(8,128)(2,1)S(1)}, bf16[16,8,128]{2,1,0:T(8,128)(2,1)S(1)}, u32[]{:S(2)}, u32[]{:S(2)}) collective-permute-start(bf16[16,8,128]{2,1,0:T(8,128)(2,1)S(1)} %pad_maximum_fusion), channel_id=1, source_target_pairs={{0,7},{1,0},{2,1},{3,2},{4,3},{5,4},{6,5},{7,6},{8,15},{9,8},{10,9... | collective-permute-start | bytes 98312 | tf_op jit(solution)/shard_map/ppermute | solution.py:395
  26.4 10.7 %collective-permute-start.4 = (bf16[4,128,128]{2,1,0:T(8,128)(2,1)S(1)}, bf16[4,128,128]{2,1,0:T(8,128)(2,1)S(1)}, u32[]{:S(2)}, u32[]{:S(2)}) collective-permute-start(bf16[4,128,128]{2,1,0:T(8,128)(2,1)S(1)} %get-tuple-element.54), channel_id=1, source_target_pairs={{0,8},{1,9},{2,10},{3,11},{4,12},{5,13},{6,14},{7,15},{8,16},{9,17... | collective-permute-start | bytes 393224 | tf_op jit(solution)/shard_map/ppermute | solution.py:395
  31.2 5.0 %collective-permute-start.5 = (bf16[4,8,128]{2,1,0:T(8,128)(2,1)S(1)}, bf16[4,8,128]{2,1,0:T(8,128)(2,1)S(1)}, u32[]{:S(2)}, u32[]{:S(2)}) collective-permute-start(bf16[4,8,128]{2,1,0:T(8,128)(2,1)S(1)} %get-tuple-element.55), channel_id=1, source_target_pairs={{0,1},{1,2},{2,3},{3,4},{4,5},{5,6},{6,7},{7,0},{8,9},{9,10},{10,1... | collective-permute-start | bytes 24584 | tf_op jit(solution)/shard_map/ppermute | solution.py:395
  31.3 5.8 %collective-permute-start.6 = (bf16[4,8,128]{2,1,0:T(8,128)(2,1)S(1)}, bf16[4,8,128]{2,1,0:T(8,128)(2,1)S(1)}, u32[]{:S(2)}, u32[]{:S(2)}) collective-permute-start(bf16[4,8,128]{2,1,0:T(8,128)(2,1)S(1)} %get-tuple-element.56), channel_id=1, source_target_pairs={{0,9},{1,10},{2,11},{3,12},{4,13},{5,14},{6,15},{7,8},{8,17},{9,18... | collective-permute-start | bytes 24584 | tf_op jit(solution)/shard_map/ppermute | solution.py:395
  42.4 2.2 %collective-permute-start.7 = (bf16[1792,128]{1,0:T(8,128)(2,1)S(1)}, bf16[1792,128]{1,0:T(8,128)(2,1)S(1)}, u32[]{:S(2)}, u32[]{:S(2)}) collective-permute-start(bf16[1792,128]{1,0:T(8,128)(2,1)S(1)} %get-tuple-element.62), channel_id=1, source_target_pairs={{0,8},{8,0},{1,9},{9,1},{2,10},{10,2},{3,11},{11,3},{4,12},{12,4},... | collective-permute-start | bytes 1376264 | tf_op jit(solution)/shard_map/ppermute | solution.py:399
  81.8 6.0 %collective-permute-start.8 = (bf16[1792,128]{1,0:T(8,128)(2,1)S(1)}, bf16[1792,128]{1,0:T(8,128)(2,1)S(1)}, u32[]{:S(2)}, u32[]{:S(2)}) collective-permute-start(bf16[1792,128]{1,0:T(8,128)(2,1)S(1)} %bitcast.3), channel_id=1, source_target_pairs={{0,8},{8,0},{1,9},{9,1},{2,10},{10,2},{3,11},{11,3},{4,12},{12,4},... | collective-permute-start | bytes 1376264 | tf_op jit(solution)/shard_map/ppermute | solution.py:399

commit v10 on v9

--- a/solution.py
+++ b/solution.py
@@ -492,7 +492,7 @@
             in_specs=vmem(5 + len(arrays)),
             out_specs=vmem(1 + len(arrays)),
             compiler_params=params,
-            cost_estimate=cost(300_000_000, 2_000_000),
+            cost_estimate=cost(30_000_000, 200_000),
             name="keep_first",
         )(latent, w_qkv, w_proj, gains, attn_bias, *arrays)
     kept_b, kept_a, pack_two, d_top = passed

time: 89.1 us -> 87.9 us (0.987)
  waiting for transfers between devices: 6.05 us -> 4.54 us
  starting transfers between devices: 22.4 us -> 23.5 us
  blocking collectives: 36.9 us -> 36 us
    ppermute x2, starting transfers between devices: 5.3 us -> 6.82 us  [swap_core(): return lax.ppermute(value, 'core', [(0, 1), (1, 0)])]
    ppermute x7, waiting for transfers between devices: 4.16 us -> 2.65 us  [shift(): return lax.ppermute(value, AXES, pairs)]
    all_to_all x2, blocking collectives: 24.1 us -> 23.1 us  [collect(): return lax.all_to_all(spread, axis, 0, 0)]
where the time goes in v10:
time: 87.9 us; the launch traced here: 87.7 us
  blocking collectives  36 us (41%)
  starting transfers between devices  23.5 us (27%)
  Pallas kernels  22.1 us (25%)
  waiting for transfers between devices  4.54 us (5%)
  between operations  1.05 us (1%)
    all_to_all x2, blocking collectives, collect(): return lax.all_to_all(spread, axis, 0, 0)  23.1 us
    ppermute x7, starting transfers between devices, shift(): return lax.ppermute(value, AXES, pairs)  16.7 us
    all_to_all x1, blocking collectives, scatter_sum(): return jnp.sum(lax.all_to_all(pieces, axis, 0, 0).astype(F32), axis=0)  12.9 us
    ppermute x2, starting transfers between devices, swap_core(): return lax.ppermute(value, 'core', [(0, 1), (1, 0)])  6.82 us
    pallas_call x1, Pallas kernels, body(): pl.pallas_call(last_kernel, out_shape=(jax.ShapeDtypeStruct(latent.shape,...  5.27 us
    pallas_call x1, Pallas kernels, body(): pl.pallas_call(first_kernel, out_shape=(side, side, corner), in_specs=[pl...  3.9 us
    pallas_call x1, Pallas kernels, body(): pl.pallas_call(third_kernel, out_shape=(half, half, small, small, packed)...  3.59 us
    pallas_call x1, Pallas kernels, body(): pl.pallas_call(second_kernel, out_shape=(jax.ShapeDtypeStruct((part_a, CH...  3.11 us
  transfers between devices with their start and end apart: 9, of which 4 were waited for; matrix products, arithmetic and copies ran while one was open for 0% of the time, Pallas kernels for 14%

profile of v10, /device:TPU:1, one launch (start us, length us, event | category | flops | bytes accessed | tf_op | source)
XLA Modules:
  0.0 87.7 jit_solution(13194975447394343571)
XLA Ops:
  0.7 3.3 %collective-permute-start.1 = (bf16[8,128,128]{2,1,0:T(8,128)(2,1)}, bf16[8,128,128]{2,1,0:T(8,128)(2,1)S(1)}, u32[]{:S(2)}, u32[]{:S(2)}) collective-permute-start(bf16[8,128,128]{2,1,0:T(8,128)(2,1)} %refs_4_.5), channel_id=1, source_target_pairs={{0,248},{1,249},{2,250},{3,251},{4,252},{5,253},{6,254},{7,255},{8... | collective-permute-start | bytes 786440 | tf_op jit(solution)/shard_map/ppermute | solution.py:395
  4.0 3.9 %forward_first.1 = (bf16[4,64,128]{2,1,0:T(8,128)(2,1)}, bf16[4,64,128]{2,1,0:T(8,128)(2,1)}, bf16[8,8,128]{2,1,0:T(8,128)(2,1)}) custom-call(bf16[8,128,128]{2,1,0:T(8,128)(2,1)} %x_ref.5, bf16[2,128,384]{2,1,0:T(8,128)(2,1)} %refs_6_.5, bf16[2,128,128]{2,1,0:T(8,128)(2,1)} %refs_7_.7, bf16[2,128,512]{2,1,0:T(8,128)(2,1)} %refs_8_.5, ...), custom_call_target="tpu_custom_call" | custom-call | flops 300000000 | bytes 1500000 | tf_op jit(solution)/shard_map/forward_first/pallas_call | solution.py:435
  7.9 0.0 copy-start.9
  8.0 0.0 copy-start.8
  8.0 6.3 %collective-permute-start = (bf16[4,64,128]{2,1,0:T(8,128)(2,1)}, bf16[4,64,128]{2,1,0:T(8,128)(2,1)S(1)}, u32[]{:S(2)}, u32[]{:S(2)}) collective-permute-start(bf16[4,64,128]{2,1,0:T(8,128)(2,1)} %get-tuple-element.43), channel_id=1, source_target_pairs={{0,248},{1,249},{2,250},{3,251},{4,252},{5,253},{6,254},{7,255},{8... | collective-permute-start | bytes 196616 | tf_op jit(solution)/shard_map/ppermute | solution.py:395
  14.3 1.8 %forward_next.1 = (bf16[4,64,128]{2,1,0:T(8,128)(2,1)S(1)}, bf16[4,64,128]{2,1,0:T(8,128)(2,1)S(1)}) custom-call(bf16[8,128,128]{2,1,0:T(8,128)(2,1)S(1)} %copy-done, bf16[2,128,384]{2,1,0:T(8,128)(2,1)S(1)} %copy-done.2, bf16[2,128,128]{2,1,0:T(8,128)(2,1)S(1)} %copy-done.3, bf16[2,128,512]{2,1,0:T(8,128)(2,1)S(1)} %copy-done.4, ...), custom_call_target="tpu_custom_call" | custom-call | flops 300000000 | bytes 1500000 | tf_op jit(solution)/shard_map/forward_next/pallas_call | solution.py:448
  16.0 0.8 collective-permute-start.3
  16.8 0.0 collective-permute-done.refs_1_.refs_2_
  16.8 0.0 collective-permute-done.1.refs_3_.refs_5_
  16.8 2.8 %collective-permute-start.2 = (bf16[16,8,128]{2,1,0:T(8,128)(2,1)S(1)}, bf16[16,8,128]{2,1,0:T(8,128)(2,1)S(1)}, u32[]{:S(2)}, u32[]{:S(2)}) collective-permute-start(bf16[16,8,128]{2,1,0:T(8,128)(2,1)S(1)} %pad_maximum_fusion), channel_id=1, source_target_pairs={{0,7},{1,0},{2,1},{3,2},{4,3},{5,4},{6,5},{7,6},{8,15},{9,8},{10,9... | collective-permute-start | bytes 98312 | tf_op jit(solution)/shard_map/ppermute | solution.py:395
  19.7 3.1 %backward_second.1 = (bf16[448,128]{1,0:T(8,128)(2,1)S(1)}, f32[1792,128]{1,0:T(8,128)S(1)}) custom-call(bf16[4,64,128]{2,1,0:T(8,128)(2,1)S(1)} %copy-done.8, bf16[4,64,128]{2,1,0:T(8,128)(2,1)S(1)} %collective-permute-done.refs_1_.refs_2_, bf16[8,128,128]{2,1,0:T(8,128)(2,1)S(1)} %copy-done.6, ...), custom_call_target="tpu_custom_call" | custom-call | flops 700000000 | bytes 3000000 | tf_op jit(solution)/shard_map/backward_second/pallas_call | solution.py:461
  22.8 0.0 collective-permute-done.2.refs_6_
  22.8 3.6 %backward_third.1 = (bf16[4,128,128]{2,1,0:T(8,128)(2,1)S(1)}, bf16[4,128,128]{2,1,0:T(8,128)(2,1)S(1)}, bf16[4,8,128]{2,1,0:T(8,128)(2,1)S(1)}, bf16[4,8,128]{2,1,0:T(8,128)(2,1)S(1)}, f32[1792,128]{1,0:T(8,128)S(1)}) custom-call(bf16[4,64,128]{2,1,0:T(8,128)(2,1)S(1)} %copy-done.8, bf16[4,64,128]{2,1,0:T(8,128)(2,1)S(1)} %get-tuple-element.42.refs_1_, ...), custom_call_target="tpu_custom_call" | custom-call | flops 800000000 | bytes 3000000 | tf_op jit(solution)/shard_map/backward_third/pallas_call | solution.py:472
  26.4 3.5 %collective-permute-start.4 = (bf16[4,128,128]{2,1,0:T(8,128)(2,1)S(1)}, bf16[4,128,128]{2,1,0:T(8,128)(2,1)S(1)}, u32[]{:S(2)}, u32[]{:S(2)}) collective-permute-start(bf16[4,128,128]{2,1,0:T(8,128)(2,1)S(1)} %get-tuple-element.54), channel_id=1, source_target_pairs={{0,8},{1,9},{2,10},{3,11},{4,12},{5,13},{6,14},{7,15},{8,16},{9,17... | collective-permute-start | bytes 393224 | tf_op jit(solution)/shard_map/ppermute | solution.py:395
  30.0 0.0 collective-permute-start.6
  30.0 1.2 %keep_first.2.refs_0_ = bf16[512,1152]{1,0:T(8,128)(2,1)S(1)} custom-call(bf16[8,128,128]{2,1,0:T(8,128)(2,1)S(1)} %copy-done, bf16[2,128,384]{2,1,0:T(8,128)(2,1)S(1)} %copy-done.2, bf16[2,128,128]{2,1,0:T(8,128)(2,1)S(1)} %copy-done.3, f32[2,2,128]{2,1,0:T(2,128)S(1)} %copy-done.7, f32[2,4,64,64]{3,2,1,0:T(8,128)S(1)} %copy-done.1), custom_call_target="tpu_custom_call" | custom-call | flops 30000000 | bytes 200000 | tf_op jit(solution)/shard_map/keep_first/pallas_call | solution.py:486
  31.2 1.3 %keep_first.3 = (bf16[512,1152]{1,0:T(8,128)(2,1)S(1)}, bf16[512,1152]{1,0:T(8,128)(2,1)S(1)}, f32[1792,128]{1,0:T(8,128)S(1)}, bf16[4,128,128]{2,1,0:T(8,128)(2,1)S(1)}) custom-call(bf16[8,128,128]{2,1,0:T(8,128)(2,1)S(1)} %copy-done, bf16[2,128,384]{2,1,0:T(8,128)(2,1)S(1)} %copy-done.2, bf16[2,128,128]{2,1,0:T(8,128)(2,1)S(1)} %copy-done.3, ...), custom_call_target="tpu_custom_call" | custom-call | flops 30000000 | bytes 200000 | tf_op jit(solution)/shard_map/keep_first/pallas_call | solution.py:486
  32.5 2.3 %collective-permute-done.5.refs_2_ = bf16[4,8,128]{2,1,0:T(8,128)(2,1)S(1)} collective-permute-done((bf16[4,8,128]{2,1,0:T(8,128)(2,1)S(1)}, bf16[4,8,128]{2,1,0:T(8,128)(2,1)S(1)}, u32[]{:S(2)}, u32[]{:S(2)}) %collective-permute-start.5) | collective-permute-done | bytes 8224 | tf_op jit(solution)/shard_map/ppermute | solution.py:395
  34.9 0.3 collective-permute-done.6.refs_3_
  35.2 5.3 %backward_first.1 = (bf16[8,128,128]{2,1,0:T(8,128)(2,1)}, f32[1792,128]{1,0:T(8,128)S(1)}, bf16[1792,128]{1,0:T(8,128)(2,1)S(1)}) custom-call(bf16[4,128,128]{2,1,0:T(8,128)(2,1)S(1)} %get-tuple-element.53.refs_0_, bf16[4,128,128]{2,1,0:T(8,128)(2,1)S(1)} %collective-permute-done.4.refs_1_, bf16[4,8,128]{2,1,0:T(8,128)(2,1)S(1)} %collective-permute-done.5.refs_2_, ...), custom_call_target="tpu_custom_call" | custom-call | flops 1500000000 | bytes 4000000 | tf_op jit(solution)/shard_map/backward_first/pallas_call | solution.py:499
  40.5 2.4 %collective-permute-start.7 = (bf16[1792,128]{1,0:T(8,128)(2,1)S(1)}, bf16[1792,128]{1,0:T(8,128)(2,1)S(1)}, u32[]{:S(2)}, u32[]{:S(2)}) collective-permute-start(bf16[1792,128]{1,0:T(8,128)(2,1)S(1)} %get-tuple-element.62), channel_id=1, source_target_pairs={{0,8},{8,0},{1,9},{9,1},{2,10},{10,2},{3,11},{11,3},{4,12},{12,4},... | collective-permute-start | bytes 1376264 | tf_op jit(solution)/shard_map/ppermute | solution.py:399
  42.8 1.4 %collective-permute-done.7 = bf16[1792,128]{1,0:T(8,128)(2,1)S(1)} collective-permute-done((bf16[1792,128]{1,0:T(8,128)(2,1)S(1)}, bf16[1792,128]{1,0:T(8,128)(2,1)S(1)}, u32[]{:S(2)}, u32[]{:S(2)}) %collective-permute-start.7) | collective-permute-done | bytes 458784 | tf_op jit(solution)/shard_map/ppermute | solution.py:399
  44.3 0.1 add_convert_fusion
  44.4 12.9 %all_to_all.15 = bf16[16,112,128]{2,1,0:T(8,128)(2,1)S(1)} all-to-all(bf16[16,112,128]{2,1,0:T(8,128)(2,1)S(1)} %bitcast.5), channel_id=1, replica_groups=mesh['z'=8,'yh'=2,'core'=2,'x'=4,'yl'=2] {'yh','x','yl'}, dimensions={0} | all-to-all | bytes 917504 | tf_op jit(solution)/shard_map/all_to_all | solution.py:404
  57.3 0.1 reduce_sum.24
  57.4 11.3 %all_to_all.16 = bf16[8,112,128]{2,1,0:T(8,128)(2,1)S(1)} all-to-all(bf16[8,112,128]{2,1,0:T(8,128)(2,1)S(1)} %broadcast_in_dim.4), channel_id=1, replica_groups=mesh['z'=8,'yh'=2,'core'=2,'x'=4,'yl'=2] {'z'}, dimensions={0} | all-to-all | bytes 458752 | tf_op jit(solution)/shard_map/all_to_all | solution.py:409
  68.7 0.1 broadcast_in_dim.5
  68.8 11.8 %all_to_all.17 = bf16[16,112,128]{2,1,0:T(8,128)(2,1)S(1)} all-to-all(bf16[16,112,128]{2,1,0:T(8,128)(2,1)S(1)} %broadcast_in_dim.5), channel_id=1, replica_groups=mesh['z'=8,'yh'=2,'core'=2,'x'=4,'yl'=2] {'yh','x','yl'}, dimensions={0} | all-to-all | bytes 917504 | tf_op jit(solution)/shard_map/all_to_all | solution.py:409
  80.6 4.4 %collective-permute-start.8 = (bf16[1792,128]{1,0:T(8,128)(2,1)S(1)}, bf16[1792,128]{1,0:T(8,128)(2,1)S(1)}, u32[]{:S(2)}, u32[]{:S(2)}) collective-permute-start(bf16[1792,128]{1,0:T(8,128)(2,1)S(1)} %bitcast.3), channel_id=1, source_target_pairs={{0,8},{8,0},{1,9},{9,1},{2,10},{10,2},{3,11},{11,3},{4,12},{12,4},... | collective-permute-start | bytes 1376264 | tf_op jit(solution)/shard_map/ppermute | solution.py:399
  85.0 1.0 %unpack.2 = (f32[2,128,384]{2,1,0:T(8,128)}, f32[2,128,128]{2,1,0:T(8,128)}, f32[2,128,512]{2,1,0:T(8,128)}, f32[2,512,128]{2,1,0:T(8,128)}, f32[2,2,128]{2,1,0:T(2,128)}, /*index=5*/f32[2,4,64,64]{3,2,1,0:T(8,128)}) custom-call(s32[1]{0:T(128)} %bitcast.refs_12_.core_ref, bf16[1792,128]{1,0:T(8,128)(2,1)S(1)} %bitcast.4), custom_call_target="tpu_custom_call" | custom-call | flops 1000000 | bytes 2000000 | tf_op jit(solution)/shard_map/unpack/pallas_call | solution.py:517
  86.0 0.4 collective-permute-done.8.part_ref
  86.5 1.0 %unpack.3 = (f32[2,128,384]{2,1,0:T(8,128)}, f32[2,128,128]{2,1,0:T(8,128)}, f32[2,128,512]{2,1,0:T(8,128)}, f32[2,512,128]{2,1,0:T(8,128)}, f32[2,2,128]{2,1,0:T(2,128)}, /*index=5*/f32[2,4,64,64]{3,2,1,0:T(8,128)}) custom-call(s32[1]{0:T(128)} %bitcast.refs_12_.core_ref, ...), custom_call_target="tpu_custom_call", output_to_operand_aliasing={{0}: (2, {}), {1}: (3, {}), {2}: (4, {}), {3}: (5, {}), {4}... | custom-call | flops 1000000 | bytes 2000000 | tf_op jit(solution)/shard_map/unpack/pallas_call | solution.py:517
  (26 shorter events, 0.1 us)
Async XLA Ops:
  0.6 19.1 %copy-start.6 = (bf16[8,128,128]{2,1,0:T(8,128)(2,1)S(1)}, bf16[8,128,128]{2,1,0:T(8,128)(2,1)}, u32[]{:S(2)}) copy-start(bf16[8,128,128]{2,1,0:T(8,128)(2,1)} %refs_4_.5) | copy-start | bytes 786436
  0.6 13.6 %copy-start.2 = (bf16[2,128,384]{2,1,0:T(8,128)(2,1)S(1)}, bf16[2,128,384]{2,1,0:T(8,128)(2,1)}, u32[]{:S(2)}) copy-start(bf16[2,128,384]{2,1,0:T(8,128)(2,1)} %refs_6_.5) | copy-start | bytes 589828
  0.7 13.6 %copy-start.3 = (bf16[2,128,128]{2,1,0:T(8,128)(2,1)S(1)}, bf16[2,128,128]{2,1,0:T(8,128)(2,1)}, u32[]{:S(2)}) copy-start(bf16[2,128,128]{2,1,0:T(8,128)(2,1)} %refs_7_.7) | copy-start | bytes 196612
  0.7 13.6 %copy-start.4 = (bf16[2,128,512]{2,1,0:T(8,128)(2,1)S(1)}, bf16[2,128,512]{2,1,0:T(8,128)(2,1)}, u32[]{:S(2)}) copy-start(bf16[2,128,512]{2,1,0:T(8,128)(2,1)} %refs_8_.5) | copy-start | bytes 786436
  0.7 13.6 %copy-start.5 = (bf16[2,512,128]{2,1,0:T(8,128)(2,1)S(1)}, bf16[2,512,128]{2,1,0:T(8,128)(2,1)}, u32[]{:S(2)}) copy-start(bf16[2,512,128]{2,1,0:T(8,128)(2,1)} %refs_9_.5) | copy-start | bytes 786436
  0.7 13.6 %copy-start.7 = (f32[2,2,128]{2,1,0:T(2,128)S(1)}, f32[2,2,128]{2,1,0:T(2,128)}, u32[]{:S(2)}) copy-start(f32[2,2,128]{2,1,0:T(2,128)} %refs_10_.3) | copy-start | bytes 6148
  0.7 13.6 %copy-start.1 = (f32[2,4,64,64]{3,2,1,0:T(8,128)S(1)}, f32[2,4,64,64]{3,2,1,0:T(8,128)}, u32[]{:S(2)}) copy-start(f32[2,4,64,64]{3,2,1,0:T(8,128)} %bias_ref.5) | copy-start | bytes 393220
  0.7 13.6 %copy-start = (bf16[8,128,128]{2,1,0:T(8,128)(2,1)S(1)}, bf16[8,128,128]{2,1,0:T(8,128)(2,1)}, u32[]{:S(2)}) copy-start(bf16[8,128,128]{2,1,0:T(8,128)(2,1)} %x_ref.5) | copy-start | bytes 786436
  0.7 16.1 %collective-permute-start.1 = (bf16[8,128,128]{2,1,0:T(8,128)(2,1)}, bf16[8,128,128]{2,1,0:T(8,128)(2,1)S(1)}, u32[]{:S(2)}, u32[]{:S(2)}) collective-permute-start(bf16[8,128,128]{2,1,0:T(8,128)(2,1)} %refs_4_.5), channel_id=1, source_target_pairs={{0,248},{1,249},{2,250},{3,251},{4,252},{5,253},{6,254},{7,255},{8... | collective-permute-start | bytes 786440 | tf_op jit(solution)/shard_map/ppermute | solution.py:395
  7.9 8.9 %copy-start.9 = (bf16[8,8,128]{2,1,0:T(8,128)(2,1)S(1)}, bf16[8,8,128]{2,1,0:T(8,128)(2,1)}, u32[]{:S(2)}) copy-start(bf16[8,8,128]{2,1,0:T(8,128)(2,1)} %get-tuple-element.44) | copy-start | bytes 49156
  8.0 11.7 %copy-start.8 = (bf16[4,64,128]{2,1,0:T(8,128)(2,1)S(1)}, bf16[4,64,128]{2,1,0:T(8,128)(2,1)}, u32[]{:S(2)}) copy-start(bf16[4,64,128]{2,1,0:T(8,128)(2,1)} %get-tuple-element.41.refs_0_) | copy-start | bytes 196612
  8.0 8.8 %collective-permute-start = (bf16[4,64,128]{2,1,0:T(8,128)(2,1)}, bf16[4,64,128]{2,1,0:T(8,128)(2,1)S(1)}, u32[]{:S(2)}, u32[]{:S(2)}) collective-permute-start(bf16[4,64,128]{2,1,0:T(8,128)(2,1)} %get-tuple-element.43), channel_id=1, source_target_pairs={{0,248},{1,249},{2,250},{3,251},{4,252},{5,253},{6,254},{7,255},{8... | collective-permute-start | bytes 196616 | tf_op jit(solution)/shard_map/ppermute | solution.py:395
  16.0 6.8 %collective-permute-start.3 = (bf16[4,64,128]{2,1,0:T(8,128)(2,1)S(1)}, bf16[4,64,128]{2,1,0:T(8,128)(2,1)S(1)}, u32[]{:S(2)}, u32[]{:S(2)}) collective-permute-start(bf16[4,64,128]{2,1,0:T(8,128)(2,1)S(1)} %get-tuple-element.45), channel_id=1, source_target_pairs={{0,248},{1,249},{2,250},{3,251},{4,252},{5,253},{6,254},{7,255},{8... | collective-permute-start | bytes 196616 | tf_op jit(solution)/shard_map/ppermute | solution.py:395
  16.8 6.0 %collective-permute-start.2 = (bf16[16,8,128]{2,1,0:T(8,128)(2,1)S(1)}, bf16[16,8,128]{2,1,0:T(8,128)(2,1)S(1)}, u32[]{:S(2)}, u32[]{:S(2)}) collective-permute-start(bf16[16,8,128]{2,1,0:T(8,128)(2,1)S(1)} %pad_maximum_fusion), channel_id=1, source_target_pairs={{0,7},{1,0},{2,1},{3,2},{4,3},{5,4},{6,5},{7,6},{8,15},{9,8},{10,9... | collective-permute-start | bytes 98312 | tf_op jit(solution)/shard_map/ppermute | solution.py:395
  26.4 8.8 %collective-permute-start.4 = (bf16[4,128,128]{2,1,0:T(8,128)(2,1)S(1)}, bf16[4,128,128]{2,1,0:T(8,128)(2,1)S(1)}, u32[]{:S(2)}, u32[]{:S(2)}) collective-permute-start(bf16[4,128,128]{2,1,0:T(8,128)(2,1)S(1)} %get-tuple-element.54), channel_id=1, source_target_pairs={{0,8},{1,9},{2,10},{3,11},{4,12},{5,13},{6,14},{7,15},{8,16},{9,17... | collective-permute-start | bytes 393224 | tf_op jit(solution)/shard_map/ppermute | solution.py:395
  30.0 4.9 %collective-permute-start.5 = (bf16[4,8,128]{2,1,0:T(8,128)(2,1)S(1)}, bf16[4,8,128]{2,1,0:T(8,128)(2,1)S(1)}, u32[]{:S(2)}, u32[]{:S(2)}) collective-permute-start(bf16[4,8,128]{2,1,0:T(8,128)(2,1)S(1)} %get-tuple-element.55), channel_id=1, source_target_pairs={{0,1},{1,2},{2,3},{3,4},{4,5},{5,6},{6,7},{7,0},{8,9},{9,10},{10,1... | collective-permute-start | bytes 24584 | tf_op jit(solution)/shard_map/ppermute | solution.py:395
  30.0 5.2 %collective-permute-start.6 = (bf16[4,8,128]{2,1,0:T(8,128)(2,1)S(1)}, bf16[4,8,128]{2,1,0:T(8,128)(2,1)S(1)}, u32[]{:S(2)}, u32[]{:S(2)}) collective-permute-start(bf16[4,8,128]{2,1,0:T(8,128)(2,1)S(1)} %get-tuple-element.56), channel_id=1, source_target_pairs={{0,9},{1,10},{2,11},{3,12},{4,13},{5,14},{6,15},{7,8},{8,17},{9,18... | collective-permute-start | bytes 24584 | tf_op jit(solution)/shard_map/ppermute | solution.py:395
  40.5 3.8 %collective-permute-start.7 = (bf16[1792,128]{1,0:T(8,128)(2,1)S(1)}, bf16[1792,128]{1,0:T(8,128)(2,1)S(1)}, u32[]{:S(2)}, u32[]{:S(2)}) collective-permute-start(bf16[1792,128]{1,0:T(8,128)(2,1)S(1)} %get-tuple-element.62), channel_id=1, source_target_pairs={{0,8},{8,0},{1,9},{9,1},{2,10},{10,2},{3,11},{11,3},{4,12},{12,4},... | collective-permute-start | bytes 1376264 | tf_op jit(solution)/shard_map/ppermute | solution.py:399
  80.6 5.9 %collective-permute-start.8 = (bf16[1792,128]{1,0:T(8,128)(2,1)S(1)}, bf16[1792,128]{1,0:T(8,128)(2,1)S(1)}, u32[]{:S(2)}, u32[]{:S(2)}) collective-permute-start(bf16[1792,128]{1,0:T(8,128)(2,1)S(1)} %bitcast.3), channel_id=1, source_target_pairs={{0,8},{8,0},{1,9},{9,1},{2,10},{10,2},{3,11},{11,3},{4,12},{12,4},... | collective-permute-start | bytes 1376264 | tf_op jit(solution)/shard_map/ppermute | solution.py:399

commit v11 on v10

--- a/solution.py
+++ b/solution.py
@@ -46,8 +46,11 @@
 
 
 def normalise(v):
-    centre = v - jnp.mean(v, axis=-1, keepdims=True)
-    spread = jnp.mean(centre * centre, axis=-1, keepdims=True)
+    centre = v - nn(v.astype(BF16), jnp.full((CH, CH), 1.0 / CH, BF16))
+    square = centre * centre
+    high = square.astype(BF16)
+    low = (square - high.astype(F32)).astype(BF16)
+    spread = nn(jnp.concatenate([high, low], axis=1), jnp.full((2 * CH, CH), 1.0 / CH, BF16))
     inv = lax.rsqrt(spread + EPS)
     return centre * inv, inv
 

time: 87.9 us -> 88.3 us (level)
  transfers between devices with their start and end apart: 9 -> 9, of which waited for: 4 -> 4; matrix products, arithmetic and copies ran while one was open for 0% -> 0% of each run, Pallas kernels for 14% -> 15%
where the time goes in v11:
time: 88.3 us; the launch traced here: 88.1 us
  blocking collectives  36 us (41%)
  starting transfers between devices  23.2 us (26%)
  Pallas kernels  22.9 us (26%)
  waiting for transfers between devices  4.57 us (5%)
  between operations  1.04 us (1%)
    all_to_all x2, blocking collectives, collect(): return lax.all_to_all(spread, axis, 0, 0)  23.1 us
    ppermute x7, starting transfers between devices, shift(): return lax.ppermute(value, AXES, pairs)  16.7 us
    all_to_all x1, blocking collectives, scatter_sum(): return jnp.sum(lax.all_to_all(pieces, axis, 0, 0).astype(F32), axis=0)  12.9 us
    ppermute x2, starting transfers between devices, swap_core(): return lax.ppermute(value, 'core', [(0, 1), (1, 0)])  6.48 us
    pallas_call x1, Pallas kernels, body(): pl.pallas_call(last_kernel, out_shape=(jax.ShapeDtypeStruct(latent.shape,...  5.27 us
    pallas_call x1, Pallas kernels, body(): pl.pallas_call(first_kernel, out_shape=(side, side, corner), in_specs=[pl...  4.25 us
    pallas_call x1, Pallas kernels, body(): pl.pallas_call(third_kernel, out_shape=(half, half, small, small, packed)...  3.66 us
    pallas_call x1, Pallas kernels, body(): pl.pallas_call(second_kernel, out_shape=(jax.ShapeDtypeStruct((part_a, CH...  3.16 us
  transfers between devices with their start and end apart: 9, of which 4 were waited for; matrix products, arithmetic and copies ran while one was open for 0% of the time, Pallas kernels for 15%

profile of v11, /device:TPU:1, one launch (start us, length us, event | category | flops | bytes accessed | tf_op | source)
XLA Modules:
  0.0 88.1 jit_solution(9568282632575913968)
XLA Ops:
  0.7 3.3 %collective-permute-start.1 = (bf16[8,128,128]{2,1,0:T(8,128)(2,1)}, bf16[8,128,128]{2,1,0:T(8,128)(2,1)S(1)}, u32[]{:S(2)}, u32[]{:S(2)}) collective-permute-start(bf16[8,128,128]{2,1,0:T(8,128)(2,1)} %refs_4_.5), channel_id=1, source_target_pairs={{0,248},{1,249},{2,250},{3,251},{4,252},{5,253},{6,254},{7,255},{8... | collective-permute-start | bytes 786440 | tf_op jit(solution)/shard_map/ppermute | solution.py:398
  4.0 4.3 %forward_first.1 = (bf16[4,64,128]{2,1,0:T(8,128)(2,1)}, bf16[4,64,128]{2,1,0:T(8,128)(2,1)}, bf16[8,8,128]{2,1,0:T(8,128)(2,1)}) custom-call(bf16[8,128,128]{2,1,0:T(8,128)(2,1)} %x_ref.5, bf16[2,128,384]{2,1,0:T(8,128)(2,1)} %refs_6_.5, bf16[2,128,128]{2,1,0:T(8,128)(2,1)} %refs_7_.7, bf16[2,128,512]{2,1,0:T(8,128)(2,1)} %refs_8_.5, ...), custom_call_target="tpu_custom_call" | custom-call | flops 300000000 | bytes 1500000 | tf_op jit(solution)/shard_map/forward_first/pallas_call | solution.py:438
  8.3 0.0 copy-start.9
  8.3 0.0 copy-start.8
  8.3 6.3 %collective-permute-start = (bf16[4,64,128]{2,1,0:T(8,128)(2,1)}, bf16[4,64,128]{2,1,0:T(8,128)(2,1)S(1)}, u32[]{:S(2)}, u32[]{:S(2)}) collective-permute-start(bf16[4,64,128]{2,1,0:T(8,128)(2,1)} %get-tuple-element.43), channel_id=1, source_target_pairs={{0,248},{1,249},{2,250},{3,251},{4,252},{5,253},{6,254},{7,255},{8... | collective-permute-start | bytes 196616 | tf_op jit(solution)/shard_map/ppermute | solution.py:398
  14.6 1.7 %forward_next.1 = (bf16[4,64,128]{2,1,0:T(8,128)(2,1)S(1)}, bf16[4,64,128]{2,1,0:T(8,128)(2,1)S(1)}) custom-call(bf16[8,128,128]{2,1,0:T(8,128)(2,1)S(1)} %copy-done, bf16[2,128,384]{2,1,0:T(8,128)(2,1)S(1)} %copy-done.2, bf16[2,128,128]{2,1,0:T(8,128)(2,1)S(1)} %copy-done.3, bf16[2,128,512]{2,1,0:T(8,128)(2,1)S(1)} %copy-done.4, ...), custom_call_target="tpu_custom_call" | custom-call | flops 300000000 | bytes 1500000 | tf_op jit(solution)/shard_map/forward_next/pallas_call | solution.py:451
  16.4 0.8 collective-permute-start.3
  17.1 0.0 collective-permute-done.refs_1_.refs_2_
  17.1 0.0 collective-permute-done.1.refs_3_.refs_5_
  17.2 2.9 %collective-permute-start.2 = (bf16[16,8,128]{2,1,0:T(8,128)(2,1)S(1)}, bf16[16,8,128]{2,1,0:T(8,128)(2,1)S(1)}, u32[]{:S(2)}, u32[]{:S(2)}) collective-permute-start(bf16[16,8,128]{2,1,0:T(8,128)(2,1)S(1)} %pad_maximum_fusion), channel_id=1, source_target_pairs={{0,7},{1,0},{2,1},{3,2},{4,3},{5,4},{6,5},{7,6},{8,15},{9,8},{10,9... | collective-permute-start | bytes 98312 | tf_op jit(solution)/shard_map/ppermute | solution.py:398
  20.0 3.2 %backward_second.1 = (bf16[448,128]{1,0:T(8,128)(2,1)S(1)}, f32[1792,128]{1,0:T(8,128)S(1)}) custom-call(bf16[4,64,128]{2,1,0:T(8,128)(2,1)S(1)} %copy-done.8, bf16[4,64,128]{2,1,0:T(8,128)(2,1)S(1)} %collective-permute-done.refs_1_.refs_2_, bf16[8,128,128]{2,1,0:T(8,128)(2,1)S(1)} %copy-done.6, ...), custom_call_target="tpu_custom_call" | custom-call | flops 700000000 | bytes 3000000 | tf_op jit(solution)/shard_map/backward_second/pallas_call | solution.py:464
  23.2 3.7 %backward_third.1 = (bf16[4,128,128]{2,1,0:T(8,128)(2,1)S(1)}, bf16[4,128,128]{2,1,0:T(8,128)(2,1)S(1)}, bf16[4,8,128]{2,1,0:T(8,128)(2,1)S(1)}, bf16[4,8,128]{2,1,0:T(8,128)(2,1)S(1)}, f32[1792,128]{1,0:T(8,128)S(1)}) custom-call(bf16[4,64,128]{2,1,0:T(8,128)(2,1)S(1)} %copy-done.8, bf16[4,64,128]{2,1,0:T(8,128)(2,1)S(1)} %get-tuple-element.42.refs_1_, ...), custom_call_target="tpu_custom_call" | custom-call | flops 800000000 | bytes 3000000 | tf_op jit(solution)/shard_map/backward_third/pallas_call | solution.py:475
  26.9 3.5 %collective-permute-start.4 = (bf16[4,128,128]{2,1,0:T(8,128)(2,1)S(1)}, bf16[4,128,128]{2,1,0:T(8,128)(2,1)S(1)}, u32[]{:S(2)}, u32[]{:S(2)}) collective-permute-start(bf16[4,128,128]{2,1,0:T(8,128)(2,1)S(1)} %get-tuple-element.54), channel_id=1, source_target_pairs={{0,8},{1,9},{2,10},{3,11},{4,12},{5,13},{6,14},{7,15},{8,16},{9,17... | collective-permute-start | bytes 393224 | tf_op jit(solution)/shard_map/ppermute | solution.py:398
  30.4 0.0 collective-permute-start.6
  30.4 1.3 %keep_first.2.refs_0_ = bf16[512,1152]{1,0:T(8,128)(2,1)S(1)} custom-call(bf16[8,128,128]{2,1,0:T(8,128)(2,1)S(1)} %copy-done, bf16[2,128,384]{2,1,0:T(8,128)(2,1)S(1)} %copy-done.2, bf16[2,128,128]{2,1,0:T(8,128)(2,1)S(1)} %copy-done.3, f32[2,2,128]{2,1,0:T(2,128)S(1)} %copy-done.7, f32[2,4,64,64]{3,2,1,0:T(8,128)S(1)} %copy-done.1), custom_call_target="tpu_custom_call" | custom-call | flops 30000000 | bytes 200000 | tf_op jit(solution)/shard_map/keep_first/pallas_call | solution.py:489
  31.8 1.5 %keep_first.3 = (bf16[512,1152]{1,0:T(8,128)(2,1)S(1)}, bf16[512,1152]{1,0:T(8,128)(2,1)S(1)}, f32[1792,128]{1,0:T(8,128)S(1)}, bf16[4,128,128]{2,1,0:T(8,128)(2,1)S(1)}) custom-call(bf16[8,128,128]{2,1,0:T(8,128)(2,1)S(1)} %copy-done, bf16[2,128,384]{2,1,0:T(8,128)(2,1)S(1)} %copy-done.2, bf16[2,128,128]{2,1,0:T(8,128)(2,1)S(1)} %copy-done.3, ...), custom_call_target="tpu_custom_call" | custom-call | flops 30000000 | bytes 200000 | tf_op jit(solution)/shard_map/keep_first/pallas_call | solution.py:489
  33.3 2.1 %collective-permute-done.5.refs_2_ = bf16[4,8,128]{2,1,0:T(8,128)(2,1)S(1)} collective-permute-done((bf16[4,8,128]{2,1,0:T(8,128)(2,1)S(1)}, bf16[4,8,128]{2,1,0:T(8,128)(2,1)S(1)}, u32[]{:S(2)}, u32[]{:S(2)}) %collective-permute-start.5) | collective-permute-done | bytes 8224 | tf_op jit(solution)/shard_map/ppermute | solution.py:398
  35.3 0.6 collective-permute-done.6.refs_3_
  35.9 0.0 collective-permute-done.4.refs_1_
  35.9 5.3 %backward_first.1 = (bf16[8,128,128]{2,1,0:T(8,128)(2,1)}, f32[1792,128]{1,0:T(8,128)S(1)}, bf16[1792,128]{1,0:T(8,128)(2,1)S(1)}) custom-call(bf16[4,128,128]{2,1,0:T(8,128)(2,1)S(1)} %get-tuple-element.53.refs_0_, bf16[4,128,128]{2,1,0:T(8,128)(2,1)S(1)} %collective-permute-done.4.refs_1_, bf16[4,8,128]{2,1,0:T(8,128)(2,1)S(1)} %collective-permute-done.5.refs_2_, ...), custom_call_target="tpu_custom_call" | custom-call | flops 1500000000 | bytes 4000000 | tf_op jit(solution)/shard_map/backward_first/pallas_call | solution.py:502
  41.2 2.0 %collective-permute-start.7 = (bf16[1792,128]{1,0:T(8,128)(2,1)S(1)}, bf16[1792,128]{1,0:T(8,128)(2,1)S(1)}, u32[]{:S(2)}, u32[]{:S(2)}) collective-permute-start(bf16[1792,128]{1,0:T(8,128)(2,1)S(1)} %get-tuple-element.62), channel_id=1, source_target_pairs={{0,8},{8,0},{1,9},{9,1},{2,10},{10,2},{3,11},{11,3},{4,12},{12,4},... | collective-permute-start | bytes 1376264 | tf_op jit(solution)/shard_map/ppermute | solution.py:402
  43.3 1.4 %collective-permute-done.7 = bf16[1792,128]{1,0:T(8,128)(2,1)S(1)} collective-permute-done((bf16[1792,128]{1,0:T(8,128)(2,1)S(1)}, bf16[1792,128]{1,0:T(8,128)(2,1)S(1)}, u32[]{:S(2)}, u32[]{:S(2)}) %collective-permute-start.7) | collective-permute-done | bytes 458784 | tf_op jit(solution)/shard_map/ppermute | solution.py:402
  44.7 0.1 add_convert_fusion
  44.8 12.9 %all_to_all.15 = bf16[16,112,128]{2,1,0:T(8,128)(2,1)S(1)} all-to-all(bf16[16,112,128]{2,1,0:T(8,128)(2,1)S(1)} %bitcast.5), channel_id=1, replica_groups=mesh['z'=8,'yh'=2,'core'=2,'x'=4,'yl'=2] {'yh','x','yl'}, dimensions={0} | all-to-all | bytes 917504 | tf_op jit(solution)/shard_map/all_to_all | solution.py:407
  57.7 0.1 reduce_sum.24
  57.8 11.3 %all_to_all.16 = bf16[8,112,128]{2,1,0:T(8,128)(2,1)S(1)} all-to-all(bf16[8,112,128]{2,1,0:T(8,128)(2,1)S(1)} %broadcast_in_dim.4), channel_id=1, replica_groups=mesh['z'=8,'yh'=2,'core'=2,'x'=4,'yl'=2] {'z'}, dimensions={0} | all-to-all | bytes 458752 | tf_op jit(solution)/shard_map/all_to_all | solution.py:412
  69.1 0.1 broadcast_in_dim.5
  69.2 11.8 %all_to_all.17 = bf16[16,112,128]{2,1,0:T(8,128)(2,1)S(1)} all-to-all(bf16[16,112,128]{2,1,0:T(8,128)(2,1)S(1)} %broadcast_in_dim.5), channel_id=1, replica_groups=mesh['z'=8,'yh'=2,'core'=2,'x'=4,'yl'=2] {'yh','x','yl'}, dimensions={0} | all-to-all | bytes 917504 | tf_op jit(solution)/shard_map/all_to_all | solution.py:412
  81.0 4.4 %collective-permute-start.8 = (bf16[1792,128]{1,0:T(8,128)(2,1)S(1)}, bf16[1792,128]{1,0:T(8,128)(2,1)S(1)}, u32[]{:S(2)}, u32[]{:S(2)}) collective-permute-start(bf16[1792,128]{1,0:T(8,128)(2,1)S(1)} %bitcast.3), channel_id=1, source_target_pairs={{0,8},{8,0},{1,9},{9,1},{2,10},{10,2},{3,11},{11,3},{4,12},{12,4},... | collective-permute-start | bytes 1376264 | tf_op jit(solution)/shard_map/ppermute | solution.py:402
  85.5 1.0 %unpack.2 = (f32[2,128,384]{2,1,0:T(8,128)}, f32[2,128,128]{2,1,0:T(8,128)}, f32[2,128,512]{2,1,0:T(8,128)}, f32[2,512,128]{2,1,0:T(8,128)}, f32[2,2,128]{2,1,0:T(2,128)}, /*index=5*/f32[2,4,64,64]{3,2,1,0:T(8,128)}) custom-call(s32[1]{0:T(128)} %bitcast.refs_12_.core_ref, bf16[1792,128]{1,0:T(8,128)(2,1)S(1)} %bitcast.4), custom_call_target="tpu_custom_call" | custom-call | flops 1000000 | bytes 2000000 | tf_op jit(solution)/shard_map/unpack/pallas_call | solution.py:520
  86.5 0.4 collective-permute-done.8.part_ref
  86.9 1.0 %unpack.3 = (f32[2,128,384]{2,1,0:T(8,128)}, f32[2,128,128]{2,1,0:T(8,128)}, f32[2,128,512]{2,1,0:T(8,128)}, f32[2,512,128]{2,1,0:T(8,128)}, f32[2,2,128]{2,1,0:T(2,128)}, /*index=5*/f32[2,4,64,64]{3,2,1,0:T(8,128)}) custom-call(s32[1]{0:T(128)} %bitcast.refs_12_.core_ref, ...), custom_call_target="tpu_custom_call", output_to_operand_aliasing={{0}: (2, {}), {1}: (3, {}), {2}: (4, {}), {3}: (5, {}), {4}... | custom-call | flops 1000000 | bytes 2000000 | tf_op jit(solution)/shard_map/unpack/pallas_call | solution.py:520
  (26 shorter events, 0.1 us)
Async XLA Ops:
  0.6 19.4 %copy-start.6 = (bf16[8,128,128]{2,1,0:T(8,128)(2,1)S(1)}, bf16[8,128,128]{2,1,0:T(8,128)(2,1)}, u32[]{:S(2)}) copy-start(bf16[8,128,128]{2,1,0:T(8,128)(2,1)} %refs_4_.5) | copy-start | bytes 786436
  0.6 13.9 %copy-start.2 = (bf16[2,128,384]{2,1,0:T(8,128)(2,1)S(1)}, bf16[2,128,384]{2,1,0:T(8,128)(2,1)}, u32[]{:S(2)}) copy-start(bf16[2,128,384]{2,1,0:T(8,128)(2,1)} %refs_6_.5) | copy-start | bytes 589828
  0.7 13.9 %copy-start.3 = (bf16[2,128,128]{2,1,0:T(8,128)(2,1)S(1)}, bf16[2,128,128]{2,1,0:T(8,128)(2,1)}, u32[]{:S(2)}) copy-start(bf16[2,128,128]{2,1,0:T(8,128)(2,1)} %refs_7_.7) | copy-start | bytes 196612
  0.7 13.9 %copy-start.4 = (bf16[2,128,512]{2,1,0:T(8,128)(2,1)S(1)}, bf16[2,128,512]{2,1,0:T(8,128)(2,1)}, u32[]{:S(2)}) copy-start(bf16[2,128,512]{2,1,0:T(8,128)(2,1)} %refs_8_.5) | copy-start | bytes 786436
  0.7 13.9 %copy-start.5 = (bf16[2,512,128]{2,1,0:T(8,128)(2,1)S(1)}, bf16[2,512,128]{2,1,0:T(8,128)(2,1)}, u32[]{:S(2)}) copy-start(bf16[2,512,128]{2,1,0:T(8,128)(2,1)} %refs_9_.5) | copy-start | bytes 786436
  0.7 13.9 %copy-start.7 = (f32[2,2,128]{2,1,0:T(2,128)S(1)}, f32[2,2,128]{2,1,0:T(2,128)}, u32[]{:S(2)}) copy-start(f32[2,2,128]{2,1,0:T(2,128)} %refs_10_.3) | copy-start | bytes 6148
  0.7 13.9 %copy-start.1 = (f32[2,4,64,64]{3,2,1,0:T(8,128)S(1)}, f32[2,4,64,64]{3,2,1,0:T(8,128)}, u32[]{:S(2)}) copy-start(f32[2,4,64,64]{3,2,1,0:T(8,128)} %bias_ref.5) | copy-start | bytes 393220
  0.7 13.9 %copy-start = (bf16[8,128,128]{2,1,0:T(8,128)(2,1)S(1)}, bf16[8,128,128]{2,1,0:T(8,128)(2,1)}, u32[]{:S(2)}) copy-start(bf16[8,128,128]{2,1,0:T(8,128)(2,1)} %x_ref.5) | copy-start | bytes 786436
  0.7 16.4 %collective-permute-start.1 = (bf16[8,128,128]{2,1,0:T(8,128)(2,1)}, bf16[8,128,128]{2,1,0:T(8,128)(2,1)S(1)}, u32[]{:S(2)}, u32[]{:S(2)}) collective-permute-start(bf16[8,128,128]{2,1,0:T(8,128)(2,1)} %refs_4_.5), channel_id=1, source_target_pairs={{0,248},{1,249},{2,250},{3,251},{4,252},{5,253},{6,254},{7,255},{8... | collective-permute-start | bytes 786440 | tf_op jit(solution)/shard_map/ppermute | solution.py:398
  8.3 8.9 %copy-start.9 = (bf16[8,8,128]{2,1,0:T(8,128)(2,1)S(1)}, bf16[8,8,128]{2,1,0:T(8,128)(2,1)}, u32[]{:S(2)}) copy-start(bf16[8,8,128]{2,1,0:T(8,128)(2,1)} %get-tuple-element.44) | copy-start | bytes 49156
  8.3 11.7 %copy-start.8 = (bf16[4,64,128]{2,1,0:T(8,128)(2,1)S(1)}, bf16[4,64,128]{2,1,0:T(8,128)(2,1)}, u32[]{:S(2)}) copy-start(bf16[4,64,128]{2,1,0:T(8,128)(2,1)} %get-tuple-element.41.refs_0_) | copy-start | bytes 196612
  8.3 8.8 %collective-permute-start = (bf16[4,64,128]{2,1,0:T(8,128)(2,1)}, bf16[4,64,128]{2,1,0:T(8,128)(2,1)S(1)}, u32[]{:S(2)}, u32[]{:S(2)}) collective-permute-start(bf16[4,64,128]{2,1,0:T(8,128)(2,1)} %get-tuple-element.43), channel_id=1, source_target_pairs={{0,248},{1,249},{2,250},{3,251},{4,252},{5,253},{6,254},{7,255},{8... | collective-permute-start | bytes 196616 | tf_op jit(solution)/shard_map/ppermute | solution.py:398
  16.4 6.8 %collective-permute-start.3 = (bf16[4,64,128]{2,1,0:T(8,128)(2,1)S(1)}, bf16[4,64,128]{2,1,0:T(8,128)(2,1)S(1)}, u32[]{:S(2)}, u32[]{:S(2)}) collective-permute-start(bf16[4,64,128]{2,1,0:T(8,128)(2,1)S(1)} %get-tuple-element.45), channel_id=1, source_target_pairs={{0,248},{1,249},{2,250},{3,251},{4,252},{5,253},{6,254},{7,255},{8... | collective-permute-start | bytes 196616 | tf_op jit(solution)/shard_map/ppermute | solution.py:398
  17.2 6.0 %collective-permute-start.2 = (bf16[16,8,128]{2,1,0:T(8,128)(2,1)S(1)}, bf16[16,8,128]{2,1,0:T(8,128)(2,1)S(1)}, u32[]{:S(2)}, u32[]{:S(2)}) collective-permute-start(bf16[16,8,128]{2,1,0:T(8,128)(2,1)S(1)} %pad_maximum_fusion), channel_id=1, source_target_pairs={{0,7},{1,0},{2,1},{3,2},{4,3},{5,4},{6,5},{7,6},{8,15},{9,8},{10,9... | collective-permute-start | bytes 98312 | tf_op jit(solution)/shard_map/ppermute | solution.py:398
  26.9 9.0 %collective-permute-start.4 = (bf16[4,128,128]{2,1,0:T(8,128)(2,1)S(1)}, bf16[4,128,128]{2,1,0:T(8,128)(2,1)S(1)}, u32[]{:S(2)}, u32[]{:S(2)}) collective-permute-start(bf16[4,128,128]{2,1,0:T(8,128)(2,1)S(1)} %get-tuple-element.54), channel_id=1, source_target_pairs={{0,8},{1,9},{2,10},{3,11},{4,12},{5,13},{6,14},{7,15},{8,16},{9,17... | collective-permute-start | bytes 393224 | tf_op jit(solution)/shard_map/ppermute | solution.py:398
  30.4 4.9 %collective-permute-start.5 = (bf16[4,8,128]{2,1,0:T(8,128)(2,1)S(1)}, bf16[4,8,128]{2,1,0:T(8,128)(2,1)S(1)}, u32[]{:S(2)}, u32[]{:S(2)}) collective-permute-start(bf16[4,8,128]{2,1,0:T(8,128)(2,1)S(1)} %get-tuple-element.55), channel_id=1, source_target_pairs={{0,1},{1,2},{2,3},{3,4},{4,5},{5,6},{6,7},{7,0},{8,9},{9,10},{10,1... | collective-permute-start | bytes 24584 | tf_op jit(solution)/shard_map/ppermute | solution.py:398
  30.4 5.5 %collective-permute-start.6 = (bf16[4,8,128]{2,1,0:T(8,128)(2,1)S(1)}, bf16[4,8,128]{2,1,0:T(8,128)(2,1)S(1)}, u32[]{:S(2)}, u32[]{:S(2)}) collective-permute-start(bf16[4,8,128]{2,1,0:T(8,128)(2,1)S(1)} %get-tuple-element.56), channel_id=1, source_target_pairs={{0,9},{1,10},{2,11},{3,12},{4,13},{5,14},{6,15},{7,8},{8,17},{9,18... | collective-permute-start | bytes 24584 | tf_op jit(solution)/shard_map/ppermute | solution.py:398
  41.2 3.5 %collective-permute-start.7 = (bf16[1792,128]{1,0:T(8,128)(2,1)S(1)}, bf16[1792,128]{1,0:T(8,128)(2,1)S(1)}, u32[]{:S(2)}, u32[]{:S(2)}) collective-permute-start(bf16[1792,128]{1,0:T(8,128)(2,1)S(1)} %get-tuple-element.62), channel_id=1, source_target_pairs={{0,8},{8,0},{1,9},{9,1},{2,10},{10,2},{3,11},{11,3},{4,12},{12,4},... | collective-permute-start | bytes 1376264 | tf_op jit(solution)/shard_map/ppermute | solution.py:402
  81.0 5.9 %collective-permute-start.8 = (bf16[1792,128]{1,0:T(8,128)(2,1)S(1)}, bf16[1792,128]{1,0:T(8,128)(2,1)S(1)}, u32[]{:S(2)}, u32[]{:S(2)}) collective-permute-start(bf16[1792,128]{1,0:T(8,128)(2,1)S(1)} %bitcast.3), channel_id=1, source_target_pairs={{0,8},{8,0},{1,9},{9,1},{2,10},{10,2},{3,11},{11,3},{4,12},{12,4},... | collective-permute-start | bytes 1376264 | tf_op jit(solution)/shard_map/ppermute | solution.py:402
